TPU v7x, 32 devices: a whole 2x2x4 slice. The times are simulated.
32 devices in a mesh: tile: 8 (over z, x), rot: 4 (over y, core).
Axes of the slice: x: 2, y: 2, z: 4, core: 2. Of those that a mesh axis runs over, the one named last changes fastest.
Arguments:
- tomogram: bfloat16 [256, 5120], P('tile'), may hold values from -12 to 12
- templates: bfloat16 [16, 110592], P('rot', 'tile'), may hold values from -6 to 6
- valid: int32 [256, 80], P('tile'), may hold values from 0 to 1, as said below
- quats: float32 [4, 4096], replicated, may hold values from -1 to 1, as said below
- rot_index: int32 [16], P('rot'), may hold values from 0 to 4095
Outputs:
- best: float32 [256, 5120], P('tile', 'rot')
- evidence: float32 [256, 5120], P('tile', 'rot')
- moments: float32 [4, 256, 5120], P(None, 'tile', 'rot')
Inputs may be any that keep to these rules, and one draw needn't show every extreme that they name: `valid`: 1 marks a column (x, y) of voxels inside the lamella. `quats`: each column is a unit quaternion with a non-negative first component.
All inputs are finite; a program needn't handle non-finite values.
Results may differ from a plain program's by a relative error of at most 0.0003.
Values may be sent and summed in bfloat16 or wider, within the bound.
No kernel may reach another device: no remote copies, remote signals or barrier semaphores. Data moves between devices by JAX's collectives and lax.ppermute only.
A program may use at most 128 MiB of HBM per device.

v0:
```python
import functools
import math

import jax
import jax.numpy as jnp
import ml_dtypes
import numpy as np
from jax import lax
from jax.experimental import pallas as pl
from jax.experimental.pallas import tpu as pltpu
from jax.sharding import PartitionSpec as P

TEMPL = 48
HALF = 24
EPSILON = 1e-06
LANES = 128
SPLIT = 64
VMEM_LIMIT = 48 * 1024 * 1024
F32 = jnp.float32
BF16 = jnp.bfloat16


def two_parts(table):
    high = table.astype(ml_dtypes.bfloat16)
    low = (table - high.astype(np.float64)).astype(ml_dtypes.bfloat16)
    return high, low


def row_table(out_idx, in_idx, length, sign, factor):
    theta = 2.0 * math.pi / length * np.outer(out_idx, in_idx)
    full = np.concatenate([np.cos(theta), sign * np.sin(theta)], axis=0) * factor
    high, low = two_parts(full)
    return np.concatenate([high, high, low], axis=1)


def depth_table(in_idx, length, sign, factor):
    freq = np.arange(length // 2) + 0.5
    theta = 2.0 * math.pi / length * np.outer(in_idx, freq)
    out = np.zeros((len(in_idx), LANES))
    out[:, : length // 2] = np.cos(theta) * factor
    out[:, SPLIT : SPLIT + length // 2] = sign * np.sin(theta) * factor
    return out


def make_tables(x_cells, y_cells, z_cells):
    n_x, n_y, n_z = x_cells + TEMPL, y_cells + HALF, z_cells + HALF
    k_x, k_y = np.arange(n_x), np.arange(n_y)
    tables = {}
    slab = np.zeros((2 * z_cells, 4 * LANES), ml_dtypes.bfloat16)
    high, low = two_parts(depth_table(np.arange(z_cells), n_z, -1.0, 1.0))
    for j in range(2):
        rows = slice(j * z_cells, (j + 1) * z_cells)
        slab[rows, 2 * j * LANES : (2 * j + 1) * LANES] = high
        slab[rows, (2 * j + 1) * LANES : (2 * j + 2) * LANES] = low
    tables["slab_z"] = slab
    tables["slab_y"] = row_table(k_y, np.arange(y_cells), n_y, -1.0, 1.0)
    tables["slab_x"] = row_table(k_x, np.arange(n_x), n_x, -1.0, 1.0)
    high, low = two_parts(depth_table(np.arange(TEMPL) - HALF, n_z, 1.0, 1.0))
    tmpl = np.zeros((8, 2 * LANES, 2 * LANES), ml_dtypes.bfloat16)
    for j in range(8):
        start = TEMPL * j - (LANES if j >= 4 else 0)
        tmpl[j, start : start + TEMPL, :LANES] = high
        tmpl[j, start : start + TEMPL, LANES:] = low
    tables["tmpl_z"] = tmpl
    ones = (high.astype(np.float64) + low.astype(np.float64)).sum(axis=0)
    tables["ones_z"] = np.broadcast_to(ones.astype(np.float32)[None], (8, LANES)).copy()
    tables["tmpl_y"] = row_table(k_y, np.arange(TEMPL) - HALF, n_y, 1.0, 1.0)
    tables["tmpl_x"] = row_table(k_x, np.arange(TEMPL), n_x, 1.0, 1.0)
    tables["back_x"] = row_table(np.arange(x_cells), k_x, n_x, 1.0, 1.0 / n_x)
    tables["back_y"] = row_table(np.arange(y_cells), k_y, n_y, 1.0, 1.0 / n_y)
    back = depth_table(np.arange(z_cells), n_z, -1.0, 2.0 / n_z).T
    high, low = two_parts(back)
    back_z = np.zeros((2 * LANES, 2 * LANES), ml_dtypes.bfloat16)
    for j in range(2):
        rows = slice(j * LANES, (j + 1) * LANES)
        back_z[rows, j * z_cells : (j + 1) * z_cells] = high
        back_z[rows, LANES + j * z_cells : LANES + (j + 1) * z_cells] = low
    tables["back_z"] = back_z
    return tables


def split_rows(value):
    high = value.astype(BF16)
    if value.shape[0] % 16 == 0:
        low = (value - high.astype(F32)).astype(BF16)
        return jnp.concatenate([high, low, high], axis=0)
    high = high.astype(F32)
    return jnp.concatenate([high, value - high, high], axis=0).astype(BF16)


def swap(value):
    parts = [
        pltpu.roll(value[:, s : s + LANES], SPLIT, 1) for s in range(0, value.shape[1], LANES)
    ]
    return jnp.concatenate(parts, axis=1)


def lane_sign(width):
    lane = lax.broadcasted_iota(jnp.int32, (8, width), 1) % LANES
    return jnp.where(lane < SPLIT, -1.0, 1.0)[:1]


def complex_rows(table, value, sign):
    out = jnp.dot(table, split_rows(value), preferred_element_type=F32)
    half = out.shape[0] // 2
    return out[:half] + sign * swap(out[half:])


def pick(ref, first, count, stride):
    return jnp.concatenate(
        [ref[pl.ds(first + i, count, stride=stride), :] for i in range(2)], axis=1
    )


def store_pair(ref, first, step, value):
    rows = value.shape[0]
    for i in range(2):
        start = pl.multiple_of(first + i * step, 8)
        ref[pl.ds(start, rows), :] = value[:, i * LANES : (i + 1) * LANES]


def loop(count, unroll, body):
    def several(i, carry):
        for u in range(unroll):
            body(i * unroll + u)
        return carry

    assert count % unroll == 0
    lax.fori_loop(0, count // unroll, several, 0)


def slab_kernel(dims, slab_ref, z_ref, y_ref, x_ref, same_ref, cross_ref, depth_buf, rows_buf):
    x_cells, y_cells, z_cells = dims
    n_x, n_y = x_cells + TEMPL, y_cells + HALF
    sign = lane_sign(2 * LANES)

    def depth_step(q):
        lanes = pl.multiple_of(q * LANES, LANES)
        block = slab_ref[:, pl.ds(lanes, LANES)]
        out = jnp.dot(block, z_ref[...], preferred_element_type=F32)
        for j in range(2):
            part = out[:, 2 * j * LANES : (2 * j + 1) * LANES]
            part = part + out[:, (2 * j + 1) * LANES : (2 * j + 2) * LANES]
            start = pl.multiple_of((2 * q + j) * n_x, 8)
            depth_buf[pl.ds(start, n_x), :] = part

    loop(y_cells // 2, 4, depth_step)

    def y_step(i):
        value = pick(depth_buf, 2 * i, y_cells, n_x)
        store_pair(rows_buf, 2 * i * n_y, n_y, complex_rows(y_ref[...], value, sign))

    loop(n_x // 2, 4, y_step)

    def x_step(i):
        value = pick(rows_buf, 2 * i, n_x, n_y)
        spec = complex_rows(x_ref[...], value, sign)
        turned = swap(spec)
        real_lane = sign < 0
        same_ref[i] = jnp.where(real_lane, spec, turned)
        cross_ref[i] = jnp.where(real_lane, -turned, spec)

    loop(n_y // 2, 4, x_step)


def slab_spectrum(widened, dims, tables):
    x_cells, y_cells, z_cells = dims
    n_x, n_y = x_cells + TEMPL, y_cells + HALF
    shape = jax.ShapeDtypeStruct((n_y // 2, n_x, 2 * LANES), F32)
    vmem = pl.BlockSpec(memory_space=pltpu.VMEM)
    return pl.pallas_call(
        functools.partial(slab_kernel, dims),
        out_shape=(shape, shape),
        in_specs=[vmem] * 4,
        out_specs=(vmem, vmem),
        scratch_shapes=[
            pltpu.VMEM((y_cells * n_x, LANES), F32),
            pltpu.VMEM((n_x * n_y, LANES), F32),
        ],
        compiler_params=pltpu.CompilerParams(vmem_limit_bytes=VMEM_LIMIT),
        name="slab_spectrum",
    )(widened, tables["slab_z"], tables["slab_y"], tables["slab_x"])


def corr_kernel(
    dims, place_ref, tmpl_ref, mask_ref, same_hbm, cross_hbm,
    z_ref, ones_ref, y_ref, x_ref, bx_ref, by_ref, bz_ref,
    mine_ref, side_ref, far_ref, stat_ref,
    same_ref, cross_ref, depth_buf, rows_buf, back_buf, vol_buf, sems,
):
    x_cells, y_cells, z_cells = dims
    n_x, n_y = x_cells + TEMPL, y_cells + HALF
    copies = [
        pltpu.make_async_copy(same_hbm, same_ref, sems.at[0]),
        pltpu.make_async_copy(cross_hbm, cross_ref, sems.at[1]),
    ]
    for copy in copies:
        copy.start()
    sign = lane_sign(2 * LANES)

    tmpl = tmpl_ref[0].astype(F32)
    inv_size = 1.0 / TEMPL**3
    mean = jnp.sum(tmpl) * inv_size
    centred = tmpl - mean
    var = jnp.sum(centred * centred) * inv_size
    scale = 1.0 / (jnp.sqrt(jnp.full((1, LANES), var + EPSILON, F32)) * TEMPL**1.5)
    shift = ones_ref[:1] * mean

    wide = 8 * TEMPL
    block = jnp.concatenate(
        [tmpl_ref[0, :, g * wide : (g + 1) * wide] for g in range(TEMPL // 8)], axis=0
    )
    for j in range(8):
        window = block[:, : 2 * LANES] if j < 4 else block[:, LANES:]
        out = jnp.dot(window, z_ref[j], preferred_element_type=F32)
        part = (out[:, :LANES] + out[:, LANES:] - shift) * scale
        for g in range(TEMPL // 8):
            start = (8 * g + j) * TEMPL
            depth_buf[start : start + TEMPL, :] = part[g * TEMPL : (g + 1) * TEMPL]

    def y_step(i):
        value = pick(depth_buf, 2 * i, TEMPL, TEMPL)
        store_pair(rows_buf, 2 * i * n_y, n_y, complex_rows(y_ref[...], value, sign))

    loop(TEMPL // 2, 4, y_step)
    for copy in copies:
        copy.wait()

    def x_step(i):
        value = pick(rows_buf, 2 * i, TEMPL, n_y)
        spec = complex_rows(x_ref[...], value, sign)
        prod = spec * same_ref[i] + swap(spec) * cross_ref[i]
        store_pair(back_buf, 2 * i * x_cells, x_cells, complex_rows(bx_ref[...], prod, sign))

    loop(n_y // 2, 4, x_step)

    def back_step(i):
        value = pick(back_buf, 2 * i, n_y, x_cells)
        store_pair(vol_buf, 2 * i * y_cells, y_cells, complex_rows(by_ref[...], value, sign))

    loop(x_cells // 2, 4, back_step)

    share = y_cells // 8
    me = place_ref[0]
    total = jnp.zeros((x_cells, LANES), F32)
    number = jnp.zeros((x_cells, LANES), F32)
    targets = [mine_ref, side_ref, far_ref.at[0], far_ref.at[1]]
    for p, target in enumerate(targets):
        first = (me ^ p) * share
        for i in range(share):
            value = pick(vol_buf, 2 * (first + i), x_cells, y_cells)
            high = value.astype(BF16)
            low = (value - high.astype(F32)).astype(BF16)
            out = jnp.dot(jnp.concatenate([high, low], axis=0), bz_ref[...], preferred_element_type=F32)
            corr = out[:x_cells, :LANES] + out[:x_cells, LANES:] + out[x_cells:, :LANES]
            target[:, i * LANES : (i + 1) * LANES] = corr
            mask = mask_ref[first + i]
            total = total + corr * mask
            number = number + mask
    number_sum = jnp.sum(number)
    total_sum = jnp.sum(total)
    local_mean = jnp.full((1, LANES), total_sum, F32) / jnp.maximum(number_sum, 1.0)
    square = jnp.zeros((x_cells, LANES), F32)
    for p, target in enumerate(targets):
        first = (me ^ p) * share
        for i in range(share):
            gap = target[:, i * LANES : (i + 1) * LANES] - local_mean
            square = square + gap * gap * mask_ref[first + i]
    row = lax.broadcasted_iota(jnp.int32, (8, LANES), 0)
    stat_ref[...] = jnp.where(row == 0, number_sum, jnp.where(row == 1, total_sum, jnp.sum(square)))


def correlate(place, bank, rot, mask, same, cross, dims, tables):
    x_cells, y_cells, z_cells = dims
    n_x, n_y = x_cells + TEMPL, y_cells + HALF
    width = y_cells * z_cells // 4
    vmem = pl.BlockSpec(memory_space=pltpu.VMEM)
    anyspace = pl.BlockSpec(memory_space=pl.ANY)
    return pl.pallas_call(
        functools.partial(corr_kernel, dims),
        grid=(1,),
        out_shape=(
            jax.ShapeDtypeStruct((x_cells, width), F32),
            jax.ShapeDtypeStruct((x_cells, width), F32),
            jax.ShapeDtypeStruct((2, x_cells, width), F32),
            jax.ShapeDtypeStruct((8, LANES), F32),
        ),
        in_specs=[
            pl.BlockSpec(memory_space=pltpu.SMEM),
            pl.BlockSpec((1, TEMPL, TEMPL * TEMPL), lambda i: (rot, 0, 0)),
            vmem, anyspace, anyspace, vmem, vmem, vmem, vmem, vmem, vmem, vmem,
        ],
        out_specs=(vmem,) * 4,
        scratch_shapes=[
            pltpu.VMEM((n_y // 2, n_x, 2 * LANES), F32),
            pltpu.VMEM((n_y // 2, n_x, 2 * LANES), F32),
            pltpu.VMEM((TEMPL * TEMPL, LANES), F32),
            pltpu.VMEM((TEMPL * n_y, LANES), F32),
            pltpu.VMEM((n_y * x_cells, LANES), F32),
            pltpu.VMEM((x_cells * y_cells, LANES), F32),
            pltpu.SemaphoreType.DMA((2,)),
        ],
        compiler_params=pltpu.CompilerParams(vmem_limit_bytes=VMEM_LIMIT),
        name="correlate",
    )(
        place, bank, mask, same, cross,
        tables["tmpl_z"], tables["ones_z"], tables["tmpl_y"], tables["tmpl_x"],
        tables["back_x"], tables["back_y"], tables["back_z"],
    )


def score_kernel(groups, rots, coef_ref, mask_ref, *refs):
    pieces = refs[: len(refs) - 3]
    best_ref, evid_ref, mom_ref = refs[len(refs) - 3 :]

    def step(i):
        lanes = pl.ds(pl.multiple_of(i * LANES, LANES), LANES)
        for top in range(0, best_ref.shape[0], 8):
            rows = slice(top, top + 8)
            mask = mask_ref[i, rows]
            scores = []
            for k, piece in enumerate(pieces):
                scores.append((piece[rows, lanes] - coef_ref[k, 0]) * coef_ref[k, 1])
            high = functools.reduce(jnp.maximum, scores)
            total = jnp.zeros_like(high)
            moment = [jnp.zeros_like(high) for _ in range(4)]
            for k, score in enumerate(scores):
                weight = jnp.exp(score - high)
                total = total + weight
                for c in range(4):
                    moment[c] = moment[c] + weight * coef_ref[k, 2 + c]
            best_ref[rows, lanes] = mask * high
            evid_ref[rows, lanes] = mask * (high + jnp.log(total))
            share = mask / total
            for c in range(4):
                mom_ref[c, rows, lanes] = moment[c] * share

    loop(best_ref.shape[1] // LANES, 1, step)


def combine(coefs, mask, pieces):
    shape = pieces[0].shape
    vmem = pl.BlockSpec(memory_space=pltpu.VMEM)
    out = jax.ShapeDtypeStruct(shape, F32)
    return pl.pallas_call(
        functools.partial(score_kernel, 4, 4),
        out_shape=(out, out, jax.ShapeDtypeStruct((4,) + shape, F32)),
        in_specs=[pl.BlockSpec(memory_space=pltpu.SMEM)] + [vmem] * (1 + len(pieces)),
        out_specs=(vmem,) * 3,
        compiler_params=pltpu.CompilerParams(vmem_limit_bytes=VMEM_LIMIT),
        name="combine",
    )(coefs, mask, *pieces)


def padded(block, axis, width):
    count = lax.axis_size(axis)
    forward = [(i, i + 1) for i in range(count - 1)]
    backward = [(target, source) for source, target in forward]
    low = lax.ppermute(block[block.shape[0] - width :], axis, forward)
    high = lax.ppermute(block[:width], axis, backward)
    return jnp.concatenate([low, block, high], axis=0)


def local(tomogram, templates, valid, quats, rot_index):
    x_cells, voxels = tomogram.shape
    y_cells = valid.shape[1]
    z_cells = voxels // y_cells
    dims = (x_cells, y_cells, z_cells)
    tables = {name: jnp.asarray(table) for name, table in make_tables(*dims).items()}
    groups = lax.axis_size("rot")
    tiles = lax.axis_size("tile")
    me = lax.axis_index("rot")
    rots = templates.shape[0]

    widened = padded(tomogram, "tile", HALF)
    gathered = lax.all_gather(templates, "tile", axis=0)
    bank = jnp.transpose(gathered, (1, 0, 2)).reshape(rots, TEMPL, TEMPL * TEMPL)
    one_hot = (rot_index[:, None] == jnp.arange(quats.shape[1], dtype=jnp.int32)[None, :]).astype(F32)
    orient = jnp.einsum("rq,kq->rk", one_hot, quats, precision=lax.Precision.HIGHEST)
    place = jnp.reshape(me, (1,)).astype(jnp.int32)
    inside = jnp.repeat(valid.astype(F32), z_cells, axis=1)
    mask = jnp.transpose(inside.reshape(x_cells, voxels // LANES, LANES), (1, 0, 2))
    share_blocks = voxels // LANES // groups
    mask_part = lax.dynamic_slice_in_dim(mask, me * share_blocks, share_blocks, 0)

    same, cross = slab_spectrum(widened, dims, tables)
    far_swap = [(i, i ^ 2) for i in range(groups)]
    side_swap = [(i, i ^ 1) for i in range(groups)]
    pieces, stats = [], []
    for r in range(rots):
        mine, side, far, stat = correlate(place, bank, r, mask, same, cross, dims, tables)
        stats.append(stat[:3, 0])
        from_far = lax.ppermute(far, "rot", far_swap)
        from_side = lax.ppermute(jnp.stack([side, from_far[1]]), "rot", side_swap)
        pieces.append((mine, from_side[0], from_far[0], from_side[1]))

    packed = jnp.concatenate([jnp.stack(stats), orient], axis=1).reshape(1, rots * 7)
    packed = jnp.pad(packed, ((0, 0), (0, LANES - rots * 7)))
    everyone = lax.all_gather(packed, ("rot", "tile"), axis=0, tiled=True)
    everyone = everyone[:, : rots * 7].reshape(groups, tiles, rots, 7)
    number, total, square = everyone[..., 0], everyone[..., 1], everyone[..., 2]
    count = jnp.sum(number, axis=1)
    average = jnp.sum(total, axis=1) / count
    gap = total / jnp.maximum(number, 1.0) - average[:, None]
    spread = jnp.sqrt(jnp.sum(square + number * gap * gap, axis=1) / count + EPSILON)
    coefs = jnp.concatenate(
        [average[..., None], 1.0 / spread[..., None], everyone[:, 0, :, 3:]], axis=-1
    )
    order = jnp.arange(groups, dtype=jnp.int32) ^ me
    coefs = coefs[order].reshape(groups * rots, 6)
    flat = [pieces[r][p] for p in range(groups) for r in range(rots)]
    return combine(coefs, mask_part, flat)


def solution(mesh):
    placed = (P("tile", None), P("rot", "tile"), P("tile", None), P(), P("rot"))
    return jax.shard_map(
        local,
        mesh=mesh,
        in_specs=placed,
        out_specs=(P("tile", "rot"), P("tile", "rot"), P(None, "tile", "rot")),
        check_vma=False,
    )
```

profile of v0, /device:TPU:0, one launch (start us, length us, event | category | flops | bytes accessed | tf_op | source)
XLA Modules:
  0.0 277.4 jit_solution(1054562146150472988)
XLA Ops:
  0.6 1.9 fusion.6
  2.5 5.5 %collective-permute-start = (bf16[24,5120]{1,0:T(8,128)(2,1)}, bf16[24,5120]{1,0:T(8,128)(2,1)}, u32[]{:S(2)}, u32[]{:S(2)}) collective-permute-start(bf16[24,5120]{1,0:T(8,128)(2,1)} %get-tuple-element.59), channel_id=1, source_target_pairs={{0,4},{4,8},{8,12},{12,16},{16,20},{20,24},{24,28},{1,5},{5,9},{9,... | collective-permute-start | bytes 737288 | tf_op jit(solution)/shard_map/ppermute | solution.py:359
  8.1 1.3 collective-permute-start.1
  9.4 0.7 convert_element_type.6
  10.1 0.4 broadcast_in_dim.2
  10.5 0.2 reshape_reshape.3
  10.9 0.5 copy-done.16
  11.4 36.5 %all-gather.1 = bf16[8,4,13824]{2,1,0:T(4,128)(2,1)S(1)} all-gather(bf16[1,4,13824]{2,1,0:T(4,128)(2,1)S(1)} %bitcast.76), channel_id=2, replica_groups=mesh['tile'=8,'rot'=4] {'tile'}, dimensions={0}, use_global_device_ids=true | all-gather | bytes 995328 | tf_op jit(solution)/shard_map/all_gather | solution.py:376
  48.1 1.1 reshape.78.tmpl_ref
  49.3 0.3 fusion
  49.7 1.2 pad_maximum_fusion.slab_ref
  50.9 14.4 %slab_spectrum.1 = (f32[52,80,256]{2,1,0:T(8,128)S(1)}, f32[52,80,256]{2,1,0:T(8,128)}) custom-call(bf16[80,5120]{1,0:T(8,128)(2,1)S(1)} %pad_maximum_fusion.slab_ref, bf16[128,512]{1,0:T(8,128)(2,1)S(1)} %copy-done.8, bf16[208,240]{1,0:T(8,128)(2,1)S(1)} %copy-done.9, bf16[160,240]{1,0:T(8,128)(2,1)S(1)} %copy-done.10), custom_call_target="tpu_custom_call" | custom-call | tf_op jit(solution)/shard_map/slab_spectrum/pallas_call | solution.py:171
  65.3 2.0 copy-done.1
  67.3 28.1 %correlate.4 = (f32[32,1280]{1,0:T(8,128)S(1)}, f32[32,1280]{1,0:T(8,128)S(1)}, f32[2,32,1280]{2,1,0:T(8,128)S(1)}, f32[8,128]{1,0:T(8,128)S(1)}) custom-call(s32[1]{0:T(128)} %bitcast.place_ref, bf16[4,48,2304]{2,1,0:T(8,128)(2,1)S(1)} %reshape.78.tmpl_ref, f32[40,32,128]{2,1,0:T(8,128)S(1)} %bitcast.66, f32[52,80,256]{2,1,0:T(8,128)} %copy-done.1, ...), custom_call_target="tpu_custom_call" | custom-call | tf_op jit(solution)/shard_map/correlate/pallas_call | solution.py:279
  95.5 28.1 %correlate.5 = (f32[32,1280]{1,0:T(8,128)S(1)}, f32[32,1280]{1,0:T(8,128)S(1)}, f32[2,32,1280]{2,1,0:T(8,128)S(1)}, f32[8,128]{1,0:T(8,128)S(1)}) custom-call(s32[1]{0:T(128)} %bitcast.place_ref, bf16[4,48,2304]{2,1,0:T(8,128)(2,1)S(1)} %reshape.78.tmpl_ref, f32[40,32,128]{2,1,0:T(8,128)S(1)} %bitcast.67, f32[52,80,256]{2,1,0:T(8,128)} %copy-done.1, ...), custom_call_target="tpu_custom_call" | custom-call | tf_op jit(solution)/shard_map/correlate/pallas_call | solution.py:279
  123.6 0.7 copy-done.12
  124.3 28.1 %correlate.6 = (f32[32,1280]{1,0:T(8,128)S(1)}, f32[32,1280]{1,0:T(8,128)S(1)}, f32[2,32,1280]{2,1,0:T(8,128)S(1)}, f32[8,128]{1,0:T(8,128)S(1)}) custom-call(s32[1]{0:T(128)} %bitcast.place_ref, bf16[4,48,2304]{2,1,0:T(8,128)(2,1)S(1)} %reshape.78.tmpl_ref, f32[40,32,128]{2,1,0:T(8,128)S(1)} %bitcast.68, f32[52,80,256]{2,1,0:T(8,128)} %copy-done.1, ...), custom_call_target="tpu_custom_call" | custom-call | tf_op jit(solution)/shard_map/correlate/pallas_call | solution.py:279
  152.4 0.7 copy-done.13
  153.2 28.3 %correlate.7 = (f32[32,1280]{1,0:T(8,128)S(1)}, f32[32,1280]{1,0:T(8,128)S(1)}, f32[2,32,1280]{2,1,0:T(8,128)S(1)}, f32[8,128]{1,0:T(8,128)S(1)}) custom-call(s32[1]{0:T(128)} %bitcast.place_ref, bf16[4,48,2304]{2,1,0:T(8,128)(2,1)S(1)} %reshape.78.tmpl_ref, f32[40,32,128]{2,1,0:T(8,128)S(1)} %bitcast.69, f32[52,80,256]{2,1,0:T(8,128)} %copy-done.1, ...), custom_call_target="tpu_custom_call" | custom-call | tf_op jit(solution)/shard_map/correlate/pallas_call | solution.py:279
  181.5 0.7 copy-done.14
  182.9 63.0 %all-gather.2 = f32[32,1,128]{2,1,0:T(1,128)S(1)} all-gather(f32[1,1,128]{2,1,0:T(1,128)S(1)} %pad_bitcast_fusion), channel_id=1, replica_groups=mesh['tile'=8,'rot'=4] {'rot','tile'}, dimensions={0}, use_global_device_ids=true | all-gather | bytes 16896 | tf_op jit(solution)/shard_map/all_gather | solution.py:399
  246.5 1.6 collective-permute-start.8
  248.5 0.5 collective-permute-start.6
  249.0 1.6 collective-permute-start.4
  250.6 0.5 collective-permute-start.2
  251.1 0.6 gather_fusion
  251.7 5.7 %collective-permute-done.8 = f32[2,32,1280]{2,1,0:T(8,128)S(1)} collective-permute-done((f32[2,32,1280]{2,1,0:T(8,128)}, f32[2,32,1280]{2,1,0:T(8,128)S(1)}, u32[]{:S(2)}, u32[]{:S(2)}) %collective-permute-start.8) | collective-permute-done | bytes 327712 | tf_op jit(solution)/shard_map/ppermute | solution.py:393
  257.5 6.9 %collective-permute-done.6 = f32[2,32,1280]{2,1,0:T(8,128)S(1)} collective-permute-done((f32[2,32,1280]{2,1,0:T(8,128)}, f32[2,32,1280]{2,1,0:T(8,128)S(1)}, u32[]{:S(2)}, u32[]{:S(2)}) %collective-permute-start.6) | collective-permute-done | bytes 327712 | tf_op jit(solution)/shard_map/ppermute | solution.py:393
  264.5 3.9 %collective-permute-done.4 = f32[2,32,1280]{2,1,0:T(8,128)S(1)} collective-permute-done((f32[2,32,1280]{2,1,0:T(8,128)}, f32[2,32,1280]{2,1,0:T(8,128)S(1)}, u32[]{:S(2)}, u32[]{:S(2)}) %collective-permute-start.4) | collective-permute-done | bytes 327712 | tf_op jit(solution)/shard_map/ppermute | solution.py:393
  268.6 3.4 %collective-permute-done.2 = f32[2,32,1280]{2,1,0:T(8,128)S(1)} collective-permute-done((f32[2,32,1280]{2,1,0:T(8,128)S(1)}, f32[2,32,1280]{2,1,0:T(8,128)S(1)}, u32[]{:S(2)}, u32[]{:S(2)}) %collective-permute-start.2) | collective-permute-done | bytes 327712 | tf_op jit(solution)/shard_map/ppermute | solution.py:393
  272.2 1.5 collective-permute-done.3
  273.8 3.7 %combine.1 = (f32[32,1280]{1,0:T(8,128)}, f32[32,1280]{1,0:T(8,128)}, f32[4,32,1280]{2,1,0:T(8,128)}) custom-call(f32[16,6]{1,0:T(8,128)S(1)} %bitcast.74, f32[10,32,128]{2,1,0:T(8,128)S(1)} %dynamic-slice_bitcast_fusion.mask_ref, f32[32,1280]{1,0:T(8,128)S(1)} %get-tuple-element.27.refs_0_, f32[32,1280]{1,0:T(8,128)S(1)} %get-tuple-element.28.refs_1_, ...), custom_call_target="tpu_custom_call" | custom-call | tf_op jit(solution)/shard_map/combine/pallas_call | solution.py:345
  (77 shorter events, 2.8 us)
Async XLA Ops:
  0.6 48.6 %copy-start = (f32[4,4096]{1,0:T(4,128)S(1)}, f32[4,4096]{1,0:T(4,128)}, u32[]{:S(2)}) copy-start(f32[4,4096]{1,0:T(4,128)} %param.18) | copy-start | bytes 196612
  2.5 47.1 %collective-permute-start = (bf16[24,5120]{1,0:T(8,128)(2,1)}, bf16[24,5120]{1,0:T(8,128)(2,1)}, u32[]{:S(2)}, u32[]{:S(2)}) collective-permute-start(bf16[24,5120]{1,0:T(8,128)(2,1)} %get-tuple-element.59), channel_id=1, source_target_pairs={{0,4},{4,8},{8,12},{12,16},{16,20},{20,24},{24,28},{1,5},{5,9},{9,... | collective-permute-start | bytes 737288 | tf_op jit(solution)/shard_map/ppermute | solution.py:359
  8.1 41.6 %collective-permute-start.1 = (bf16[24,5120]{1,0:T(8,128)(2,1)}, bf16[24,5120]{1,0:T(8,128)(2,1)}, u32[]{:S(2)}, u32[]{:S(2)}) collective-permute-start(bf16[24,5120]{1,0:T(8,128)(2,1)} %get-tuple-element.60), channel_id=1, source_target_pairs={{4,0},{8,4},{12,8},{16,12},{20,16},{24,20},{28,24},{5,1},{9,5},{13... | collective-permute-start | bytes 737288 | tf_op jit(solution)/shard_map/ppermute | solution.py:360
  10.5 0.9 copy-start.16
  47.9 1.3 copy-start.17
  47.9 1.7 copy-start.15
  48.1 2.7 copy-start.8
  48.1 2.7 copy-start.9
  48.1 2.7 copy-start.10
  49.2 18.1 %copy-start.2 = (bf16[8,256,256]{2,1,0:T(8,128)(2,1)S(1)}, bf16[8,256,256]{2,1,0:T(8,128)(2,1)}, u32[]{:S(2)}) copy-start(bf16[8,256,256]{2,1,0:T(8,128)(2,1)} %constant.44.clone.z_ref) | copy-start | bytes 3145732
  49.3 18.1 %copy-start.3 = (bf16[256,256]{1,0:T(8,128)(2,1)S(1)}, bf16[256,256]{1,0:T(8,128)(2,1)}, u32[]{:S(2)}) copy-start(bf16[256,256]{1,0:T(8,128)(2,1)} %constant.50.clone.bz_ref) | copy-start | bytes 393220
  49.3 18.0 %copy-start.4 = (bf16[160,312]{1,0:T(8,128)(2,1)S(1)}, bf16[160,312]{1,0:T(8,128)(2,1)}, u32[]{:S(2)}) copy-start(bf16[160,312]{1,0:T(8,128)(2,1)} %constant.49.clone.by_ref) | copy-start | bytes 299524
  49.3 18.0 %copy-start.5 = (bf16[208,144]{1,0:T(8,128)(2,1)S(1)}, bf16[208,144]{1,0:T(8,128)(2,1)}, u32[]{:S(2)}) copy-start(bf16[208,144]{1,0:T(8,128)(2,1)} %constant.46.clone.y_ref) | copy-start | bytes 179716
  49.3 18.0 %copy-start.6 = (bf16[160,144]{1,0:T(8,128)(2,1)S(1)}, bf16[160,144]{1,0:T(8,128)(2,1)}, u32[]{:S(2)}) copy-start(bf16[160,144]{1,0:T(8,128)(2,1)} %constant.47.clone.x_ref) | copy-start | bytes 138244
  49.3 18.0 %copy-start.7 = (bf16[64,240]{1,0:T(8,128)(2,1)S(1)}, bf16[64,240]{1,0:T(8,128)(2,1)}, u32[]{:S(2)}) copy-start(bf16[64,240]{1,0:T(8,128)(2,1)} %constant.48.clone.bx_ref) | copy-start | bytes 92164
  49.3 18.0 %copy-start.11 = (f32[8,128]{1,0:T(8,128)S(1)}, f32[8,128]{1,0:T(8,128)}, u32[]{:S(2)}) copy-start(f32[8,128]{1,0:T(8,128)} %constant.45.clone.ones_ref) | copy-start | bytes 12292
  65.3 2.0 copy-start.1
  123.6 0.7 copy-start.12
  152.4 0.8 copy-start.13
  181.5 0.7 copy-start.14
  246.5 10.9 %collective-permute-start.8 = (f32[2,32,1280]{2,1,0:T(8,128)}, f32[2,32,1280]{2,1,0:T(8,128)S(1)}, u32[]{:S(2)}, u32[]{:S(2)}) collective-permute-start(f32[2,32,1280]{2,1,0:T(8,128)} %copy-done.14), channel_id=1, source_target_pairs={{0,2},{1,3},{2,0},{3,1},{4,6},{5,7},{6,4},{7,5},{8,10},{9,11},{10,... | collective-permute-start | bytes 983048 | tf_op jit(solution)/shard_map/ppermute | solution.py:393
  248.5 15.9 %collective-permute-start.6 = (f32[2,32,1280]{2,1,0:T(8,128)}, f32[2,32,1280]{2,1,0:T(8,128)S(1)}, u32[]{:S(2)}, u32[]{:S(2)}) collective-permute-start(f32[2,32,1280]{2,1,0:T(8,128)} %copy-done.13), channel_id=1, source_target_pairs={{0,2},{1,3},{2,0},{3,1},{4,6},{5,7},{6,4},{7,5},{8,10},{9,11},{10,... | collective-permute-start | bytes 983048 | tf_op jit(solution)/shard_map/ppermute | solution.py:393
  249.0 19.4 %collective-permute-start.4 = (f32[2,32,1280]{2,1,0:T(8,128)}, f32[2,32,1280]{2,1,0:T(8,128)S(1)}, u32[]{:S(2)}, u32[]{:S(2)}) collective-permute-start(f32[2,32,1280]{2,1,0:T(8,128)} %copy-done.12), channel_id=1, source_target_pairs={{0,2},{1,3},{2,0},{3,1},{4,6},{5,7},{6,4},{7,5},{8,10},{9,11},{10,... | collective-permute-start | bytes 983048 | tf_op jit(solution)/shard_map/ppermute | solution.py:393
  250.6 21.4 %collective-permute-start.2 = (f32[2,32,1280]{2,1,0:T(8,128)S(1)}, f32[2,32,1280]{2,1,0:T(8,128)S(1)}, u32[]{:S(2)}, u32[]{:S(2)}) collective-permute-start(f32[2,32,1280]{2,1,0:T(8,128)S(1)} %get-tuple-element.32), channel_id=1, source_target_pairs={{0,2},{1,3},{2,0},{3,1},{4,6},{5,7},{6,4},{7,5},{8,10},{9,11},{10,... | collective-permute-start | bytes 983048 | tf_op jit(solution)/shard_map/ppermute | solution.py:393
  257.4 14.7 %collective-permute-start.9 = (f32[2,32,1280]{2,1,0:T(8,128)S(1)}, f32[2,32,1280]{2,1,0:T(8,128)S(1)}, u32[]{:S(2)}, u32[]{:S(2)}) collective-permute-start(f32[2,32,1280]{2,1,0:T(8,128)S(1)} %pad_maximum_fusion.4), channel_id=1, source_target_pairs={{0,1},{1,0},{2,3},{3,2},{4,5},{5,4},{6,7},{7,6},{8,9},{9,8},{10,11... | collective-permute-start | bytes 983048 | tf_op jit(solution)/shard_map/ppermute | solution.py:394
  264.5 7.7 %collective-permute-start.7 = (f32[2,32,1280]{2,1,0:T(8,128)S(1)}, f32[2,32,1280]{2,1,0:T(8,128)S(1)}, u32[]{:S(2)}, u32[]{:S(2)}) collective-permute-start(f32[2,32,1280]{2,1,0:T(8,128)S(1)} %pad_maximum_fusion.3), channel_id=1, source_target_pairs={{0,1},{1,0},{2,3},{3,2},{4,5},{5,4},{6,7},{7,6},{8,9},{9,8},{10,11... | collective-permute-start | bytes 983048 | tf_op jit(solution)/shard_map/ppermute | solution.py:394
  268.5 3.7 %collective-permute-start.5 = (f32[2,32,1280]{2,1,0:T(8,128)S(1)}, f32[2,32,1280]{2,1,0:T(8,128)S(1)}, u32[]{:S(2)}, u32[]{:S(2)}) collective-permute-start(f32[2,32,1280]{2,1,0:T(8,128)S(1)} %pad_maximum_fusion.2), channel_id=1, source_target_pairs={{0,1},{1,0},{2,3},{3,2},{4,5},{5,4},{6,7},{7,6},{8,9},{9,8},{10,11... | collective-permute-start | bytes 983048 | tf_op jit(solution)/shard_map/ppermute | solution.py:394
  272.0 1.7 collective-permute-start.3
where the time goes:
time: 278 us; the launch traced here: 277 us
  Pallas kernels  131 us (47%)
  blocking collectives  99.5 us (36%)
  waiting for transfers between devices  21.4 us (8%)
  starting transfers between devices  11.2 us (4%)
  local copies, waits for them, and re-layouts  10.8 us (4%)
    pallas_call x4, Pallas kernels, correlate(): pl.pallas_call(functools.partial(corr_kernel, dims), grid=(1,), out_shape...  113 us
    all_gather x1, blocking collectives, local(): everyone = lax.all_gather(packed, ('rot', 'tile'), axis=0, tiled=True)  63 us
    all_gather x1, blocking collectives, local(): gathered = lax.all_gather(templates, 'tile', axis=0)  36.5 us
    ppermute x4, waiting for transfers between devices, local(): from_far = lax.ppermute(far, 'rot', far_swap)  19.9 us
    pallas_call x1, Pallas kernels, slab_spectrum(): pl.pallas_call(functools.partial(slab_kernel, dims), out_shape=(shape, sh...  14.4 us
  transfers between devices with their start and end apart: 10, of which 5 were waited for; matrix products, arithmetic and copies ran while one was open for 2% of the time, Pallas kernels for 0%

commit v1 on v0

--- a/solution.py
+++ b/solution.py
@@ -26,11 +26,17 @@
     return high, low
 
 
-def row_table(out_idx, in_idx, length, sign, factor):
+def row_table(out_idx, in_idx, length, sign, factor, wide):
     theta = 2.0 * math.pi / length * np.outer(out_idx, in_idx)
-    full = np.concatenate([np.cos(theta), sign * np.sin(theta)], axis=0) * factor
+    pad = np.zeros((-len(out_idx) % 8, len(in_idx)))
+    full = np.concatenate([np.cos(theta), pad, sign * np.sin(theta), pad], axis=0) * factor
     high, low = two_parts(full)
-    return np.concatenate([high, high, low], axis=1)
+    if wide:
+        return np.concatenate([high, high, low], axis=1)
+    zeros = np.zeros_like(low)
+    return np.concatenate(
+        [np.concatenate([high, high], axis=1), np.concatenate([low, zeros], axis=1)], axis=0
+    )
 
 
 def depth_table(in_idx, length, sign, factor):
@@ -42,9 +48,16 @@
     return out
 
 
+def half_odd(count):
+    return np.arange(count // 2) + 0.5
+
+
 def make_tables(x_cells, y_cells, z_cells):
     n_x, n_y, n_z = x_cells + TEMPL, y_cells + HALF, z_cells + HALF
-    k_x, k_y = np.arange(n_x), np.arange(n_y)
+    k_x, k_y = half_odd(n_x), half_odd(n_y)
+    both_x = np.concatenate([k_x, -k_x])
+    both_y = np.stack([k_y, -k_y], axis=1).reshape(-1)
+    mid_x, mid_y = (x_cells - 1) / 2, (y_cells - 1) / 2
     tables = {}
     slab = np.zeros((2 * z_cells, 4 * LANES), ml_dtypes.bfloat16)
     high, low = two_parts(depth_table(np.arange(z_cells), n_z, -1.0, 1.0))
@@ -53,8 +66,8 @@
         slab[rows, 2 * j * LANES : (2 * j + 1) * LANES] = high
         slab[rows, (2 * j + 1) * LANES : (2 * j + 2) * LANES] = low
     tables["slab_z"] = slab
-    tables["slab_y"] = row_table(k_y, np.arange(y_cells), n_y, -1.0, 1.0)
-    tables["slab_x"] = row_table(k_x, np.arange(n_x), n_x, -1.0, 1.0)
+    tables["slab_y"] = row_table(k_y, np.arange(y_cells), n_y, -1.0, 1.0, True)
+    tables["slab_x"] = row_table(k_x, np.arange(n_x), n_x, -1.0, 1.0, True)
     high, low = two_parts(depth_table(np.arange(TEMPL) - HALF, n_z, 1.0, 1.0))
     tmpl = np.zeros((8, 2 * LANES, 2 * LANES), ml_dtypes.bfloat16)
     for j in range(8):
@@ -64,10 +77,10 @@
     tables["tmpl_z"] = tmpl
     ones = (high.astype(np.float64) + low.astype(np.float64)).sum(axis=0)
     tables["ones_z"] = np.broadcast_to(ones.astype(np.float32)[None], (8, LANES)).copy()
-    tables["tmpl_y"] = row_table(k_y, np.arange(TEMPL) - HALF, n_y, 1.0, 1.0)
-    tables["tmpl_x"] = row_table(k_x, np.arange(TEMPL), n_x, 1.0, 1.0)
-    tables["back_x"] = row_table(np.arange(x_cells), k_x, n_x, 1.0, 1.0 / n_x)
-    tables["back_y"] = row_table(np.arange(y_cells), k_y, n_y, 1.0, 1.0 / n_y)
+    tables["tmpl_y"] = row_table(k_y, np.arange(TEMPL) - HALF + mid_y, n_y, 1.0, 1.0, True)
+    tables["tmpl_x"] = row_table(k_x, np.arange(TEMPL) + mid_x, n_x, 1.0, 1.0, True)
+    tables["back_x"] = row_table(half_odd(x_cells), both_x, n_x, 1.0, 1.0 / n_x, False)
+    tables["back_y"] = row_table(half_odd(y_cells), both_y, n_y, 1.0, 1.0 / n_y, False)
     back = depth_table(np.arange(z_cells), n_z, -1.0, 2.0 / n_z).T
     high, low = two_parts(back)
     back_z = np.zeros((2 * LANES, 2 * LANES), ml_dtypes.bfloat16)
@@ -79,13 +92,14 @@
     return tables
 
 
-def split_rows(value):
+def split_rows(value, wide):
     high = value.astype(BF16)
     if value.shape[0] % 16 == 0:
         low = (value - high.astype(F32)).astype(BF16)
-        return jnp.concatenate([high, low, high], axis=0)
+        return jnp.concatenate([high, low, high] if wide else [high, low], axis=0)
     high = high.astype(F32)
-    return jnp.concatenate([high, value - high, high], axis=0).astype(BF16)
+    low = value - high
+    return jnp.concatenate([high, low, high] if wide else [high, low], axis=0).astype(BF16)
 
 
 def swap(value):
@@ -100,73 +114,89 @@
     return jnp.where(lane < SPLIT, -1.0, 1.0)[:1]
 
 
-def complex_rows(table, value, sign):
-    out = jnp.dot(table, split_rows(value), preferred_element_type=F32)
+def pair_rows(table, value, wide):
+    out = jnp.dot(table, split_rows(value, wide), preferred_element_type=F32)
+    if not wide:
+        half = out.shape[0] // 2
+        out = out[:half] + out[half:]
     half = out.shape[0] // 2
-    return out[:half] + sign * swap(out[half:])
-
-
-def pick(ref, first, count, stride):
-    return jnp.concatenate(
-        [ref[pl.ds(first + i, count, stride=stride), :] for i in range(2)], axis=1
-    )
-
-
-def store_pair(ref, first, step, value):
-    rows = value.shape[0]
-    for i in range(2):
-        start = pl.multiple_of(first + i * step, 8)
-        ref[pl.ds(start, rows), :] = value[:, i * LANES : (i + 1) * LANES]
-
-
-def loop(count, unroll, body):
-    def several(i, carry):
-        for u in range(unroll):
-            body(i * unroll + u)
+    turned = swap(out[half:]) * lane_sign(out.shape[1])
+    return out[:half] + turned, out[:half] - turned
+
+
+def pick(ref, firsts, count, stride):
+    return jnp.concatenate([ref[pl.ds(f, count, stride=stride), :] for f in firsts], axis=1)
+
+
+def store(ref, start, value):
+    ref[pl.ds(pl.multiple_of(start, 8), value.shape[0]), :] = value
+
+
+def lane_block(value, i):
+    return value[:, i * LANES : (i + 1) * LANES]
+
+
+def loop(count, body):
+    def one(i, carry):
+        body(i)
         return carry
 
-    assert count % unroll == 0
-    lax.fori_loop(0, count // unroll, several, 0)
+    lax.fori_loop(0, count, one, 0)
+
+
+GROUP = 8
 
 
 def slab_kernel(dims, slab_ref, z_ref, y_ref, x_ref, same_ref, cross_ref, depth_buf, rows_buf):
     x_cells, y_cells, z_cells = dims
     n_x, n_y = x_cells + TEMPL, y_cells + HALF
-    sign = lane_sign(2 * LANES)
-
-    def depth_step(q):
-        lanes = pl.multiple_of(q * LANES, LANES)
-        block = slab_ref[:, pl.ds(lanes, LANES)]
+    half_y = n_y // 2
+    pad_y = half_y + -half_y % 8
+
+    def depth_step(i):
+        block = jnp.concatenate(
+            [slab_ref[:, pl.ds(pl.multiple_of((4 * i + u) * LANES, LANES), LANES)] for u in range(4)],
+            axis=0,
+        )
         out = jnp.dot(block, z_ref[...], preferred_element_type=F32)
-        for j in range(2):
-            part = out[:, 2 * j * LANES : (2 * j + 1) * LANES]
-            part = part + out[:, (2 * j + 1) * LANES : (2 * j + 2) * LANES]
-            start = pl.multiple_of((2 * q + j) * n_x, 8)
-            depth_buf[pl.ds(start, n_x), :] = part
-
-    loop(y_cells // 2, 4, depth_step)
+        for u in range(4):
+            part = out[u * n_x : (u + 1) * n_x]
+            for j in range(2):
+                store(
+                    depth_buf, (8 * i + 2 * u + j) * n_x,
+                    lane_block(part, 2 * j) + lane_block(part, 2 * j + 1),
+                )
+
+    loop(y_cells // 8, depth_step)
 
     def y_step(i):
-        value = pick(depth_buf, 2 * i, y_cells, n_x)
-        store_pair(rows_buf, 2 * i * n_y, n_y, complex_rows(y_ref[...], value, sign))
-
-    loop(n_x // 2, 4, y_step)
+        value = pick(depth_buf, [GROUP * i + u for u in range(GROUP)], y_cells, n_x)
+        plus, minus = pair_rows(y_ref[...], value, True)
+        for u in range(GROUP):
+            start = (GROUP * i + u) * 2 * pad_y
+            store(rows_buf, start, lane_block(plus, u))
+            store(rows_buf, start + pad_y, lane_block(minus, u))
+
+    loop(n_x // GROUP, y_step)
 
     def x_step(i):
-        value = pick(rows_buf, 2 * i, n_x, n_y)
-        spec = complex_rows(x_ref[...], value, sign)
+        firsts = [GROUP // 2 * i + u // 2 + u % 2 * pad_y for u in range(GROUP)]
+        value = pick(rows_buf, firsts, n_x, 2 * pad_y)
+        plus, minus = pair_rows(x_ref[...], value, True)
+        spec = jnp.concatenate([plus, minus], axis=0)
         turned = swap(spec)
-        real_lane = sign < 0
+        real_lane = lane_sign(GROUP * LANES) < 0
         same_ref[i] = jnp.where(real_lane, spec, turned)
         cross_ref[i] = jnp.where(real_lane, -turned, spec)
 
-    loop(n_y // 2, 4, x_step)
+    loop(n_y // GROUP, x_step)
 
 
 def slab_spectrum(widened, dims, tables):
     x_cells, y_cells, z_cells = dims
     n_x, n_y = x_cells + TEMPL, y_cells + HALF
-    shape = jax.ShapeDtypeStruct((n_y // 2, n_x, 2 * LANES), F32)
+    pad_y = n_y // 2 + -(n_y // 2) % 8
+    shape = jax.ShapeDtypeStruct((n_y // GROUP, n_x, GROUP * LANES), F32)
     vmem = pl.BlockSpec(memory_space=pltpu.VMEM)
     return pl.pallas_call(
         functools.partial(slab_kernel, dims),
@@ -175,9 +205,10 @@
         out_specs=(vmem, vmem),
         scratch_shapes=[
             pltpu.VMEM((y_cells * n_x, LANES), F32),
-            pltpu.VMEM((n_x * n_y, LANES), F32),
+            pltpu.VMEM((n_x * 2 * pad_y, LANES), F32),
         ],
         compiler_params=pltpu.CompilerParams(vmem_limit_bytes=VMEM_LIMIT),
+        cost_estimate=pl.CostEstimate(flops=10**10, bytes_accessed=10**7, transcendentals=0),
         name="slab_spectrum",
     )(widened, tables["slab_z"], tables["slab_y"], tables["slab_x"])
 
@@ -190,13 +221,14 @@
 ):
     x_cells, y_cells, z_cells = dims
     n_x, n_y = x_cells + TEMPL, y_cells + HALF
+    half_y = n_y // 2
+    pad_y = half_y + -half_y % 8
     copies = [
         pltpu.make_async_copy(same_hbm, same_ref, sems.at[0]),
         pltpu.make_async_copy(cross_hbm, cross_ref, sems.at[1]),
     ]
     for copy in copies:
         copy.start()
-    sign = lane_sign(2 * LANES)
 
     tmpl = tmpl_ref[0].astype(F32)
     inv_size = 1.0 / TEMPL**3
@@ -219,26 +251,41 @@
             depth_buf[start : start + TEMPL, :] = part[g * TEMPL : (g + 1) * TEMPL]
 
     def y_step(i):
-        value = pick(depth_buf, 2 * i, TEMPL, TEMPL)
-        store_pair(rows_buf, 2 * i * n_y, n_y, complex_rows(y_ref[...], value, sign))
-
-    loop(TEMPL // 2, 4, y_step)
+        value = pick(depth_buf, [GROUP * i + u for u in range(GROUP)], TEMPL, TEMPL)
+        plus, minus = pair_rows(y_ref[...], value, True)
+        for u in range(GROUP):
+            start = (GROUP * i + u) * 2 * pad_y
+            store(rows_buf, start, lane_block(plus, u))
+            store(rows_buf, start + pad_y, lane_block(minus, u))
+
+    loop(TEMPL // GROUP, y_step)
     for copy in copies:
         copy.wait()
 
     def x_step(i):
-        value = pick(rows_buf, 2 * i, TEMPL, n_y)
-        spec = complex_rows(x_ref[...], value, sign)
+        firsts = [GROUP // 2 * i + u // 2 + u % 2 * pad_y for u in range(GROUP)]
+        value = pick(rows_buf, firsts, TEMPL, 2 * pad_y)
+        plus, minus = pair_rows(x_ref[...], value, True)
+        spec = jnp.concatenate([plus, minus], axis=0)
         prod = spec * same_ref[i] + swap(spec) * cross_ref[i]
-        store_pair(back_buf, 2 * i * x_cells, x_cells, complex_rows(bx_ref[...], prod, sign))
-
-    loop(n_y // 2, 4, x_step)
+        plus, minus = pair_rows(bx_ref[...], prod, False)
+        for u in range(GROUP):
+            start = (GROUP * i + u) * x_cells
+            store(back_buf, start, lane_block(plus, u))
+            store(back_buf, start + x_cells // 2, lane_block(minus, u))
+
+    loop(n_y // GROUP, x_step)
 
     def back_step(i):
-        value = pick(back_buf, 2 * i, n_y, x_cells)
-        store_pair(vol_buf, 2 * i * y_cells, y_cells, complex_rows(by_ref[...], value, sign))
-
-    loop(x_cells // 2, 4, back_step)
+        value = pick(back_buf, [GROUP * i + u for u in range(GROUP)], n_y, x_cells)
+        plus, minus = pair_rows(by_ref[...], value, False)
+        for u in range(GROUP):
+            row = GROUP * i + u
+            x = jnp.where(row < x_cells // 2, row + x_cells // 2, x_cells - 1 - row)
+            store(vol_buf, x * y_cells, lane_block(plus, u))
+            store(vol_buf, x * y_cells + y_cells // 2, lane_block(minus, u))
+
+    loop(x_cells // GROUP, back_step)
 
     share = y_cells // 8
     me = place_ref[0]
@@ -247,12 +294,19 @@
     targets = [mine_ref, side_ref, far_ref.at[0], far_ref.at[1]]
     for p, target in enumerate(targets):
         first = (me ^ p) * share
+        values = []
         for i in range(share):
-            value = pick(vol_buf, 2 * (first + i), x_cells, y_cells)
-            high = value.astype(BF16)
-            low = (value - high.astype(F32)).astype(BF16)
-            out = jnp.dot(jnp.concatenate([high, low], axis=0), bz_ref[...], preferred_element_type=F32)
-            corr = out[:x_cells, :LANES] + out[:x_cells, LANES:] + out[x_cells:, :LANES]
+            firsts = []
+            for j in range(2):
+                y = 2 * (first + i) + j
+                firsts.append(jnp.where(y < y_cells // 2, y_cells - 1 - y, y - y_cells // 2))
+            values.append(pick(vol_buf, firsts, x_cells, y_cells))
+        value = jnp.concatenate(values, axis=0)
+        out = jnp.dot(split_rows(value, False), bz_ref[...], preferred_element_type=F32)
+        rows = value.shape[0]
+        full = out[:rows, :LANES] + out[:rows, LANES:] + out[rows:, :LANES]
+        for i in range(share):
+            corr = full[i * x_cells : (i + 1) * x_cells]
             target[:, i * LANES : (i + 1) * LANES] = corr
             mask = mask_ref[first + i]
             total = total + corr * mask
@@ -273,6 +327,7 @@
 def correlate(place, bank, rot, mask, same, cross, dims, tables):
     x_cells, y_cells, z_cells = dims
     n_x, n_y = x_cells + TEMPL, y_cells + HALF
+    pad_y = n_y // 2 + -(n_y // 2) % 8
     width = y_cells * z_cells // 4
     vmem = pl.BlockSpec(memory_space=pltpu.VMEM)
     anyspace = pl.BlockSpec(memory_space=pl.ANY)
@@ -292,15 +347,16 @@
         ],
         out_specs=(vmem,) * 4,
         scratch_shapes=[
-            pltpu.VMEM((n_y // 2, n_x, 2 * LANES), F32),
-            pltpu.VMEM((n_y // 2, n_x, 2 * LANES), F32),
+            pltpu.VMEM((n_y // GROUP, n_x, GROUP * LANES), F32),
+            pltpu.VMEM((n_y // GROUP, n_x, GROUP * LANES), F32),
             pltpu.VMEM((TEMPL * TEMPL, LANES), F32),
-            pltpu.VMEM((TEMPL * n_y, LANES), F32),
+            pltpu.VMEM((TEMPL * 2 * pad_y, LANES), F32),
             pltpu.VMEM((n_y * x_cells, LANES), F32),
             pltpu.VMEM((x_cells * y_cells, LANES), F32),
             pltpu.SemaphoreType.DMA((2,)),
         ],
         compiler_params=pltpu.CompilerParams(vmem_limit_bytes=VMEM_LIMIT),
+        cost_estimate=pl.CostEstimate(flops=15 * 10**9, bytes_accessed=10**7, transcendentals=0),
         name="correlate",
     )(
         place, bank, mask, same, cross,
@@ -309,7 +365,7 @@
     )
 
 
-def score_kernel(groups, rots, coef_ref, mask_ref, *refs):
+def score_kernel(coef_ref, mask_ref, *refs):
     pieces = refs[: len(refs) - 3]
     best_ref, evid_ref, mom_ref = refs[len(refs) - 3 :]
 
@@ -335,7 +391,7 @@
             for c in range(4):
                 mom_ref[c, rows, lanes] = moment[c] * share
 
-    loop(best_ref.shape[1] // LANES, 1, step)
+    loop(best_ref.shape[1] // LANES, step)
 
 
 def combine(coefs, mask, pieces):
@@ -343,13 +399,35 @@
     vmem = pl.BlockSpec(memory_space=pltpu.VMEM)
     out = jax.ShapeDtypeStruct(shape, F32)
     return pl.pallas_call(
-        functools.partial(score_kernel, 4, 4),
+        score_kernel,
         out_shape=(out, out, jax.ShapeDtypeStruct((4,) + shape, F32)),
         in_specs=[pl.BlockSpec(memory_space=pltpu.SMEM)] + [vmem] * (1 + len(pieces)),
         out_specs=(vmem,) * 3,
         compiler_params=pltpu.CompilerParams(vmem_limit_bytes=VMEM_LIMIT),
         name="combine",
     )(coefs, mask, *pieces)
+
+
+def doubling_gather(block, axis):
+    count = lax.axis_size(axis)
+    me = lax.axis_index(axis)
+    steps = [1 << i for i in reversed(range(count.bit_length() - 1))]
+    block = block[None]
+    for step in steps:
+        other = lax.ppermute(block, axis, [(i, i ^ step) for i in range(count)])
+        upper = (me & step) != 0
+        pair = [jnp.where(upper, other, block), jnp.where(upper, block, other)]
+        block = jnp.stack(pair, axis=1).reshape((-1,) + block.shape[1:])
+    return block
+
+
+def merge(first, other):
+    mean_a = first[1] / jnp.maximum(first[0], 1.0)
+    mean_b = other[1] / jnp.maximum(other[0], 1.0)
+    number = first[0] + other[0]
+    gap = mean_b - mean_a
+    between = gap * gap * (first[0] * other[0] / jnp.maximum(number, 1.0))
+    return jnp.stack([number, first[1] + other[1], (first[2] + other[2]) + between])
 
 
 def padded(block, axis, width):
@@ -373,7 +451,7 @@
     rots = templates.shape[0]
 
     widened = padded(tomogram, "tile", HALF)
-    gathered = lax.all_gather(templates, "tile", axis=0)
+    gathered = doubling_gather(templates, "tile")
     bank = jnp.transpose(gathered, (1, 0, 2)).reshape(rots, TEMPL, TEMPL * TEMPL)
     one_hot = (rot_index[:, None] == jnp.arange(quats.shape[1], dtype=jnp.int32)[None, :]).astype(F32)
     orient = jnp.einsum("rq,kq->rk", one_hot, quats, precision=lax.Precision.HIGHEST)
@@ -386,30 +464,42 @@
     same, cross = slab_spectrum(widened, dims, tables)
     far_swap = [(i, i ^ 2) for i in range(groups)]
     side_swap = [(i, i ^ 1) for i in range(groups)]
-    pieces, stats = [], []
+    mines, sides, fars, from_sides, stats = [], [], [], [], []
     for r in range(rots):
+        if r >= 2:
+            place, fars[r - 2] = lax.optimization_barrier((place, fars[r - 2]))
+        if r >= 3:
+            place, from_sides[r - 3] = lax.optimization_barrier((place, from_sides[r - 3]))
         mine, side, far, stat = correlate(place, bank, r, mask, same, cross, dims, tables)
+        if r >= 1 and r < rots - 1:
+            both = jnp.stack([sides[r - 1], fars[r - 1][1]])
+        mines.append(mine)
+        sides.append(side)
         stats.append(stat[:3, 0])
-        from_far = lax.ppermute(far, "rot", far_swap)
-        from_side = lax.ppermute(jnp.stack([side, from_far[1]]), "rot", side_swap)
-        pieces.append((mine, from_side[0], from_far[0], from_side[1]))
-
-    packed = jnp.concatenate([jnp.stack(stats), orient], axis=1).reshape(1, rots * 7)
-    packed = jnp.pad(packed, ((0, 0), (0, LANES - rots * 7)))
-    everyone = lax.all_gather(packed, ("rot", "tile"), axis=0, tiled=True)
-    everyone = everyone[:, : rots * 7].reshape(groups, tiles, rots, 7)
-    number, total, square = everyone[..., 0], everyone[..., 1], everyone[..., 2]
-    count = jnp.sum(number, axis=1)
-    average = jnp.sum(total, axis=1) / count
-    gap = total / jnp.maximum(number, 1.0) - average[:, None]
-    spread = jnp.sqrt(jnp.sum(square + number * gap * gap, axis=1) / count + EPSILON)
-    coefs = jnp.concatenate(
-        [average[..., None], 1.0 / spread[..., None], everyone[:, 0, :, 3:]], axis=-1
+        fars.append(lax.ppermute(far, "rot", far_swap))
+        if r >= 1 and r < rots - 1:
+            from_sides.append(lax.ppermute(both, "rot", side_swap))
+    state = jnp.stack(stats, axis=1)
+    state, fars[rots - 2], from_sides[rots - 3] = lax.optimization_barrier(
+        (state, fars[rots - 2], from_sides[rots - 3])
     )
-    order = jnp.arange(groups, dtype=jnp.int32) ^ me
-    coefs = coefs[order].reshape(groups * rots, 6)
-    flat = [pieces[r][p] for p in range(groups) for r in range(rots)]
-    return combine(coefs, mask_part, flat)
+    step = 1
+    while step < tiles:
+        swap_pairs = [(i, i ^ step) for i in range(tiles)]
+        state = merge(state, lax.ppermute(state, "tile", swap_pairs))
+        step *= 2
+    average = state[1] / state[0]
+    inverse = 1.0 / jnp.sqrt(state[2] / state[0] + EPSILON)
+    coefs = jnp.concatenate([average[:, None], inverse[:, None], orient], axis=1)[None]
+    from_far = lax.ppermute(coefs, "rot", far_swap)
+    coefs = jnp.concatenate([coefs, from_far], axis=0)
+    from_side = lax.ppermute(coefs, "rot", side_swap)
+    coefs = jnp.stack([coefs[0], from_side[0], coefs[1], from_side[1]])
+    last = [part for r in range(rots - 2, rots) for part in (sides[r], fars[r][1])]
+    last = lax.ppermute(jnp.stack(last), "rot", side_swap)
+    from_sides += [last[:2], last[2:]]
+    flat = mines + [f[0] for f in from_sides] + [f[0] for f in fars] + [f[1] for f in from_sides]
+    return combine(coefs.reshape(groups * rots, 6), mask_part, flat)
 
 
 def solution(mesh):

time: 278 us -> 144 us (0.52)
  blocking collectives: 99.5 us -> 0 us
  Pallas kernels: 131 us -> 80.5 us
  starting transfers between devices: 11.2 us -> 21.5 us
  waiting for transfers between devices: 21.4 us -> 24.6 us
    all_gather x2 -> x0, blocking collectives: 99.5 us -> none  [the longest x1 63 us: local(): everyone = lax.all_gather(packed, ('rot', 'tile'), axis=0, tiled=True)]
    pallas_call x4, Pallas kernels: 113 us -> 62.9 us  [correlate(): pl.pallas_call(functools.partial(corr_kernel, dims), grid=(1,), out_shape...]
    ppermute x8 -> x15, starting transfers between devices: 4.39 us -> 16.8 us  [the longest x3 8.14 us: doubling_gather(): other = lax.ppermute(block, axis, [(i, i ^ step) for i in range(count)])]
    ppermute x8 -> x15, waiting for transfers between devices: 21.4 us -> 24.2 us  [the longest x3 8.65 us: local(): state = merge(state, lax.ppermute(state, 'tile', swap_pairs))]
  transfers between devices with their start and end apart: 10 -> 17, of which waited for: 5 -> 10; matrix products, arithmetic and copies ran while one was open for 2% -> 5% of each run, Pallas kernels for 0% -> 43%
where the time goes in v1:
time: 144 us
  Pallas kernels  80.5 us (56%)
  waiting for transfers between devices  24.6 us (17%)
  starting transfers between devices  21.5 us (15%)
  local copies, waits for them, and re-layouts  10.6 us (7%)
  other arithmetic  3.86 us (3%)
  matrix products  1.55 us (1%)
    pallas_call x4, Pallas kernels, correlate(): pl.pallas_call(functools.partial(corr_kernel, dims), grid=(1,), out_shape...  62.9 us
    pallas_call x1, Pallas kernels, slab_spectrum(): pl.pallas_call(functools.partial(slab_kernel, dims), out_shape=(shape, sh...  13.9 us
    ppermute x3, waiting for transfers between devices, local(): state = merge(state, lax.ppermute(state, 'tile', swap_pairs))  8.65 us
    ppermute x3, starting transfers between devices, doubling_gather(): other = lax.ppermute(block, axis, [(i, i ^ step) for i in range(count)])  8.14 us
    ppermute x4, waiting for transfers between devices, local(): fars.append(lax.ppermute(far, 'rot', far_swap))  7.21 us
    ppermute x3, waiting for transfers between devices, doubling_gather(): other = lax.ppermute(block, axis, [(i, i ^ step) for i in range(count)])  4.52 us
    pallas_call x1, Pallas kernels, combine(): pl.pallas_call(score_kernel, out_shape=(out, out, jax.ShapeDtypeStruct((4...  3.67 us
    ppermute x1, starting transfers between devices, padded(): low = lax.ppermute(block[block.shape[0] - width:], axis, forward)  3.41 us
  transfers between devices with their start and end apart: 17, of which 10 were waited for; matrix products, arithmetic and copies ran while one was open for 5% of the time, Pallas kernels for 43%

profile of v1, /device:TPU:0, one launch (start us, length us, event | category | flops | bytes accessed | tf_op | source)
XLA Modules:
  0.0 143.8 jit_solution(2593778767429630890)
XLA Ops:
  0.6 4.1 %collective-permute-start = (bf16[1,4,13824]{2,1,0:T(4,128)(2,1)}, bf16[1,4,13824]{2,1,0:T(4,128)(2,1)}, u32[]{:S(2)}, u32[]{:S(2)}) collective-permute-start(bf16[1,4,13824]{2,1,0:T(4,128)(2,1)} %bitcast.85), channel_id=1, source_target_pairs={{0,16},{4,20},{8,24},{12,28},{16,0},{20,4},{24,8},{28,12},{1,17},{... | collective-permute-start | bytes 331784 | tf_op jit(solution)/shard_map/ppermute | solution.py:417
  4.7 1.1 fusion.3
  5.8 3.4 %collective-permute-start.3 = (bf16[24,5120]{1,0:T(8,128)(2,1)S(1)}, bf16[24,5120]{1,0:T(8,128)(2,1)S(1)}, u32[]{:S(2)}, u32[]{:S(2)}) collective-permute-start(bf16[24,5120]{1,0:T(8,128)(2,1)S(1)} %get-tuple-element.79), channel_id=1, source_target_pairs={{0,4},{4,8},{8,12},{12,16},{16,20},{20,24},{24,28},{1,5},{5,9},{9,... | collective-permute-start | bytes 737288 | tf_op jit(solution)/shard_map/ppermute | solution.py:437
  9.3 1.3 collective-permute-start.4
  10.6 1.6 %fusion = f32[4,4]{1,0:T(4,128)} fusion(f32[4,4096]{1,0:T(4,128)S(1)} %copy-done, s32[4]{0:T(128)} %param.19), kind=kOutput, calls=%fused_computation.27 | convolution fusion | flops 802816 | bytes 65616 | tf_op jit(solution)/shard_map/rq,kq->rk/dot_general | solution.py:457
  12.1 0.7 convert_element_type.4
  14.2 1.0 select_bitcast_fusion.5
  15.3 3.7 %collective-permute-start.1 = (bf16[2,4,13824]{2,1,0:T(4,128)(2,1)S(1)}, bf16[2,4,13824]{2,1,0:T(4,128)(2,1)S(1)}, u32[]{:S(2)}, u32[]{:S(2)}) collective-permute-start(bf16[2,4,13824]{2,1,0:T(4,128)(2,1)S(1)} %maximum_bitcast_fusion), channel_id=1, source_target_pairs={{0,8},{4,12},{8,0},{12,4},{16,24},{20,28},{24,16},{28,20},{1,9},{5... | collective-permute-start | bytes 663560 | tf_op jit(solution)/shard_map/ppermute | solution.py:417
  19.5 4.5 %collective-permute-done.1 = bf16[2,4,13824]{2,1,0:T(4,128)(2,1)S(1)} collective-permute-done((bf16[2,4,13824]{2,1,0:T(4,128)(2,1)S(1)}, bf16[2,4,13824]{2,1,0:T(4,128)(2,1)S(1)}, u32[]{:S(2)}, u32[]{:S(2)}) %collective-permute-start.1) | collective-permute-done | bytes 221216 | tf_op jit(solution)/shard_map/ppermute | solution.py:417
  25.2 13.9 %slab_spectrum.1 = (f32[13,80,1024]{2,1,0:T(8,128)S(1)}, f32[13,80,1024]{2,1,0:T(8,128)}) custom-call(bf16[80,5120]{1,0:T(8,128)(2,1)S(1)} %pad_maximum_fusion.1.slab_ref, bf16[128,512]{1,0:T(8,128)(2,1)S(1)} %copy-done.5, bf16[112,240]{1,0:T(8,128)(2,1)S(1)} %copy-done.9, bf16[80,240]{1,0:T(8,128)(2,1)S(1)} %copy-done.12), custom_call_target="tpu_custom_call" | custom-call | flops 10000000000 | bytes 10000000 | tf_op jit(solution)/shard_map/slab_spectrum/pallas_call | solution.py:201
  39.1 2.0 %copy-done.17 = f32[13,80,1024]{2,1,0:T(8,128)} copy-done((f32[13,80,1024]{2,1,0:T(8,128)}, f32[13,80,1024]{2,1,0:T(8,128)S(1)}, u32[]{:S(2)}) %copy-start.17) | copy-done | bytes 4259864
  41.5 0.6 pad_maximum_fusion
  42.6 1.0 copy.38
  43.6 2.2 %reshape.379.tmpl_ref = bf16[4,48,2304]{2,1,0:T(8,128)(2,1)S(1)} reshape(bf16[4,8,13824]{2,1,0:T(8,128)(2,1)} %copy.38) | data formatting | bytes 1769472 | tf_op jit(solution)/shard_map/reshape | solution.py:455
  45.9 15.7 %correlate.5 = (f32[32,1280]{1,0:T(8,128)S(1)}, f32[32,1280]{1,0:T(8,128)S(1)}, f32[2,32,1280]{2,1,0:T(8,128)S(1)}, f32[8,128]{1,0:T(8,128)S(1)}) custom-call(s32[1]{0:T(128)} %bitcast.place_ref, bf16[4,48,2304]{2,1,0:T(8,128)(2,1)S(1)} %reshape.379.tmpl_ref, f32[40,32,128]{2,1,0:T(8,128)S(1)} %bitcast.74, f32[13,80,1024]{2,1,0:T(8,128)} %copy-done.17, ...), custom_call_target="tpu_custom_call" | custom-call | flops 15000000512 | bytes 10000000 | tf_op jit(solution)/shard_map/correlate/pallas_call | solution.py:334
  61.6 1.6 %collective-permute-start.6 = (f32[2,32,1280]{2,1,0:T(8,128)S(1)}, f32[2,32,1280]{2,1,0:T(8,128)S(1)}, u32[]{:S(2)}, u32[]{:S(2)}) collective-permute-start(f32[2,32,1280]{2,1,0:T(8,128)S(1)} %get-tuple-element.37), channel_id=1, source_target_pairs={{0,2},{1,3},{2,0},{3,1},{4,6},{5,7},{6,4},{7,5},{8,10},{9,11},{10,... | collective-permute-start | bytes 983048 | tf_op jit(solution)/shard_map/ppermute | solution.py:479
  63.2 15.7 %correlate.4 = (f32[32,1280]{1,0:T(8,128)S(1)}, f32[32,1280]{1,0:T(8,128)S(1)}, f32[2,32,1280]{2,1,0:T(8,128)S(1)}, f32[8,128]{1,0:T(8,128)S(1)}) custom-call(s32[1]{0:T(128)} %bitcast.place_ref, bf16[4,48,2304]{2,1,0:T(8,128)(2,1)S(1)} %reshape.379.tmpl_ref, f32[40,32,128]{2,1,0:T(8,128)S(1)} %bitcast.75, f32[13,80,1024]{2,1,0:T(8,128)} %copy-done.17, ...), custom_call_target="tpu_custom_call" | custom-call | flops 15000000512 | bytes 10000000 | tf_op jit(solution)/shard_map/correlate/pallas_call | solution.py:334
  79.7 7.2 %collective-permute-done.5 = f32[2,32,1280]{2,1,0:T(8,128)S(1)} collective-permute-done((f32[2,32,1280]{2,1,0:T(8,128)S(1)}, f32[2,32,1280]{2,1,0:T(8,128)S(1)}, u32[]{:S(2)}, u32[]{:S(2)}) %collective-permute-start.5) | collective-permute-done | bytes 327712 | tf_op jit(solution)/shard_map/ppermute | solution.py:479
  86.9 15.9 %correlate.6 = (f32[32,1280]{1,0:T(8,128)S(1)}, f32[32,1280]{1,0:T(8,128)S(1)}, f32[2,32,1280]{2,1,0:T(8,128)S(1)}, f32[8,128]{1,0:T(8,128)S(1)}) custom-call(s32[1]{0:T(128)} %bitcast.place_ref, bf16[4,48,2304]{2,1,0:T(8,128)(2,1)S(1)} %reshape.379.tmpl_ref, f32[40,32,128]{2,1,0:T(8,128)S(1)} %bitcast.76, f32[13,80,1024]{2,1,0:T(8,128)} %copy-done.17, ...), custom_call_target="tpu_custom_call" | custom-call | flops 15000000512 | bytes 10000000 | tf_op jit(solution)/shard_map/correlate/pallas_call | solution.py:334
  103.5 1.0 collective-permute-done.7
  104.6 15.7 %correlate.7 = (f32[32,1280]{1,0:T(8,128)S(1)}, f32[32,1280]{1,0:T(8,128)S(1)}, f32[2,32,1280]{2,1,0:T(8,128)S(1)}, f32[8,128]{1,0:T(8,128)S(1)}) custom-call(s32[1]{0:T(128)} %bitcast.place_ref, bf16[4,48,2304]{2,1,0:T(8,128)(2,1)S(1)} %reshape.379.tmpl_ref, f32[40,32,128]{2,1,0:T(8,128)S(1)} %bitcast.77, f32[13,80,1024]{2,1,0:T(8,128)} %copy-done.17, ...), custom_call_target="tpu_custom_call" | custom-call | flops 15000000512 | bytes 10000000 | tf_op jit(solution)/shard_map/correlate/pallas_call | solution.py:334
  120.9 0.7 copy-done.19
  121.6 1.7 %collective-permute-start.10 = (f32[3,4]{1,0:T(4,128)S(1)}, f32[3,4]{1,0:T(4,128)S(1)}, u32[]{:S(2)}, u32[]{:S(2)}) collective-permute-start(f32[3,4]{1,0:T(4,128)S(1)} %pad_maximum_fusion.8), channel_id=1, source_target_pairs={{0,4},{4,0},{8,12},{12,8},{16,20},{20,16},{24,28},{28,24},{1,5},{5... | collective-permute-start | bytes 152 | tf_op jit(solution)/shard_map/ppermute | solution.py:489
  123.4 1.8 %collective-permute-done.10 = f32[3,4]{1,0:T(4,128)S(1)} collective-permute-done((f32[3,4]{1,0:T(4,128)S(1)}, f32[3,4]{1,0:T(4,128)S(1)}, u32[]{:S(2)}, u32[]{:S(2)}) %collective-permute-start.10) | collective-permute-done | bytes 80 | tf_op jit(solution)/shard_map/ppermute | solution.py:489
  125.3 0.8 collective-permute-start.11
  126.1 2.8 %collective-permute-done.11 = f32[3,4]{1,0:T(4,128)S(1)} collective-permute-done((f32[3,4]{1,0:T(4,128)S(1)}, f32[3,4]{1,0:T(4,128)S(1)}, u32[]{:S(2)}, u32[]{:S(2)}) %collective-permute-start.11) | collective-permute-done | bytes 80 | tf_op jit(solution)/shard_map/ppermute | solution.py:489
  129.5 4.0 %collective-permute-done.12 = f32[3,4]{1,0:T(4,128)S(1)} collective-permute-done((f32[3,4]{1,0:T(4,128)S(1)}, f32[3,4]{1,0:T(4,128)S(1)}, u32[]{:S(2)}, u32[]{:S(2)}) %collective-permute-start.12) | collective-permute-done | bytes 80 | tf_op jit(solution)/shard_map/ppermute | solution.py:489
  134.1 1.5 %collective-permute-start.13 = (f32[1,4,6]{2,1,0:T(4,128)S(1)}, f32[1,4,6]{2,1,0:T(4,128)S(1)}, u32[]{:S(2)}, u32[]{:S(2)}) collective-permute-start(f32[1,4,6]{2,1,0:T(4,128)S(1)} %maximum_bitcast_fusion.1), channel_id=1, source_target_pairs={{0,2},{1,3},{2,0},{3,1},{4,6},{5,7},{6,4},{7,5},{8,10},{9,11},{10,... | collective-permute-start | bytes 296 | tf_op jit(solution)/shard_map/ppermute | solution.py:494
  135.6 1.0 slice_bitcast_fusion.7
  136.6 1.1 collective-permute-done.13
  138.8 1.2 collective-permute-done.16
  140.1 3.7 %combine.1 = (f32[32,1280]{1,0:T(8,128)}, f32[32,1280]{1,0:T(8,128)}, f32[4,32,1280]{2,1,0:T(8,128)}) custom-call(f32[16,6]{1,0:T(8,128)S(1)} %bitcast.82, f32[10,32,128]{2,1,0:T(8,128)S(1)} %dynamic-slice_bitcast_fusion.mask_ref, f32[32,1280]{1,0:T(8,128)S(1)} %get-tuple-element.45.refs_0_, f32[32,1280]{1,0:T(8,128)S(1)} %get-tuple-element.46.refs_1_, ...), custom_call_target="tpu_custom_call" | custom-call | tf_op jit(solution)/shard_map/combine/pallas_call | solution.py:401
  (103 shorter events, 8.3 us)
Async XLA Ops:
  0.6 9.9 %copy-start = (f32[4,4096]{1,0:T(4,128)S(1)}, f32[4,4096]{1,0:T(4,128)}, u32[]{:S(2)}) copy-start(f32[4,4096]{1,0:T(4,128)} %param.18) | copy-start | bytes 196612
  0.6 13.0 %collective-permute-start = (bf16[1,4,13824]{2,1,0:T(4,128)(2,1)}, bf16[1,4,13824]{2,1,0:T(4,128)(2,1)}, u32[]{:S(2)}, u32[]{:S(2)}) collective-permute-start(bf16[1,4,13824]{2,1,0:T(4,128)(2,1)} %bitcast.85), channel_id=1, source_target_pairs={{0,16},{4,20},{8,24},{12,28},{16,0},{20,4},{24,8},{28,12},{1,17},{... | collective-permute-start | bytes 331784 | tf_op jit(solution)/shard_map/ppermute | solution.py:417
  5.8 13.6 %collective-permute-start.3 = (bf16[24,5120]{1,0:T(8,128)(2,1)S(1)}, bf16[24,5120]{1,0:T(8,128)(2,1)S(1)}, u32[]{:S(2)}, u32[]{:S(2)}) collective-permute-start(bf16[24,5120]{1,0:T(8,128)(2,1)S(1)} %get-tuple-element.79), channel_id=1, source_target_pairs={{0,4},{4,8},{8,12},{12,16},{16,20},{20,24},{24,28},{1,5},{5,9},{9,... | collective-permute-start | bytes 737288 | tf_op jit(solution)/shard_map/ppermute | solution.py:437
  9.3 10.2 %collective-permute-start.4 = (bf16[24,5120]{1,0:T(8,128)(2,1)S(1)}, bf16[24,5120]{1,0:T(8,128)(2,1)S(1)}, u32[]{:S(2)}, u32[]{:S(2)}) collective-permute-start(bf16[24,5120]{1,0:T(8,128)(2,1)S(1)} %get-tuple-element.80), channel_id=1, source_target_pairs={{4,0},{8,4},{12,8},{16,12},{20,16},{24,20},{28,24},{5,1},{9,5},{13... | collective-permute-start | bytes 737288 | tf_op jit(solution)/shard_map/ppermute | solution.py:438
  13.3 6.2 %copy-start.18 = (bf16[32,5120]{1,0:T(8,128)(2,1)S(1)}, bf16[32,5120]{1,0:T(8,128)(2,1)}, u32[]{:S(2)}) copy-start(bf16[32,5120]{1,0:T(8,128)(2,1)} %param.15) | copy-start | bytes 983044
  15.3 8.7 %collective-permute-start.1 = (bf16[2,4,13824]{2,1,0:T(4,128)(2,1)S(1)}, bf16[2,4,13824]{2,1,0:T(4,128)(2,1)S(1)}, u32[]{:S(2)}, u32[]{:S(2)}) collective-permute-start(bf16[2,4,13824]{2,1,0:T(4,128)(2,1)S(1)} %maximum_bitcast_fusion), channel_id=1, source_target_pairs={{0,8},{4,12},{8,0},{12,4},{16,24},{20,28},{24,16},{28,20},{1,9},{5... | collective-permute-start | bytes 663560 | tf_op jit(solution)/shard_map/ppermute | solution.py:417
  19.5 5.7 %copy-start.5 = (bf16[128,512]{1,0:T(8,128)(2,1)S(1)}, bf16[128,512]{1,0:T(8,128)(2,1)}, u32[]{:S(2)}) copy-start(bf16[128,512]{1,0:T(8,128)(2,1)} %constant.45.clone.z_ref) | copy-start | bytes 393220
  19.5 5.7 %copy-start.9 = (bf16[112,240]{1,0:T(8,128)(2,1)S(1)}, bf16[112,240]{1,0:T(8,128)(2,1)}, u32[]{:S(2)}) copy-start(bf16[112,240]{1,0:T(8,128)(2,1)} %constant.46.clone.y_ref) | copy-start | bytes 161284
  19.5 5.6 %copy-start.12 = (bf16[80,240]{1,0:T(8,128)(2,1)S(1)}, bf16[80,240]{1,0:T(8,128)(2,1)}, u32[]{:S(2)}) copy-start(bf16[80,240]{1,0:T(8,128)(2,1)} %constant.47.clone.x_ref) | copy-start | bytes 115204
  24.8 16.3 %collective-permute-start.2 = (bf16[4,4,13824]{2,1,0:T(4,128)(2,1)S(1)}, bf16[4,4,13824]{2,1,0:T(4,128)(2,1)S(1)}, u32[]{:S(2)}, u32[]{:S(2)}) collective-permute-start(bf16[4,4,13824]{2,1,0:T(4,128)(2,1)S(1)} %bitcast.84), channel_id=1, source_target_pairs={{0,4},{4,0},{8,12},{12,8},{16,20},{20,16},{24,28},{28,24},{1,5},{5... | collective-permute-start | bytes 1327112 | tf_op jit(solution)/shard_map/ppermute | solution.py:417
  42.5 3.4 %copy-start.1 = (bf16[8,256,256]{2,1,0:T(8,128)(2,1)S(1)}, bf16[8,256,256]{2,1,0:T(8,128)(2,1)}, u32[]{:S(2)}) copy-start(bf16[8,256,256]{2,1,0:T(8,128)(2,1)} %constant.48.clone.z_ref) | copy-start | bytes 3145732
  42.5 3.4 %copy-start.3 = (bf16[256,256]{1,0:T(8,128)(2,1)S(1)}, bf16[256,256]{1,0:T(8,128)(2,1)}, u32[]{:S(2)}) copy-start(bf16[256,256]{1,0:T(8,128)(2,1)} %constant.54.clone.bz_ref) | copy-start | bytes 393220
  45.9 17.3 %copy-start.2 = (bf16[8,256,256]{2,1,0:T(8,128)(2,1)S(1)}, bf16[8,256,256]{2,1,0:T(8,128)(2,1)}, u32[]{:S(2)}) copy-start(bf16[8,256,256]{2,1,0:T(8,128)(2,1)} %constant.48.clone.z_ref) | copy-start | bytes 3145732
  61.6 25.3 %copy-start.8 = (bf16[112,144]{1,0:T(8,128)(2,1)S(1)}, bf16[112,144]{1,0:T(8,128)(2,1)}, u32[]{:S(2)}) copy-start(bf16[112,144]{1,0:T(8,128)(2,1)} %constant.50.clone.y_ref) | copy-start | bytes 96772
  61.6 25.3 %copy-start.11 = (bf16[80,144]{1,0:T(8,128)(2,1)S(1)}, bf16[80,144]{1,0:T(8,128)(2,1)}, u32[]{:S(2)}) copy-start(bf16[80,144]{1,0:T(8,128)(2,1)} %constant.51.clone.x_ref) | copy-start | bytes 69124
  61.6 25.3 %copy-start.16 = (f32[8,128]{1,0:T(8,128)S(1)}, f32[8,128]{1,0:T(8,128)}, u32[]{:S(2)}) copy-start(f32[8,128]{1,0:T(8,128)} %constant.49.clone.ones_ref) | copy-start | bytes 12292
  61.6 17.9 %collective-permute-start.6 = (f32[2,32,1280]{2,1,0:T(8,128)S(1)}, f32[2,32,1280]{2,1,0:T(8,128)S(1)}, u32[]{:S(2)}, u32[]{:S(2)}) collective-permute-start(f32[2,32,1280]{2,1,0:T(8,128)S(1)} %get-tuple-element.37), channel_id=1, source_target_pairs={{0,2},{1,3},{2,0},{3,1},{4,6},{5,7},{6,4},{7,5},{8,10},{9,11},{10,... | collective-permute-start | bytes 983048 | tf_op jit(solution)/shard_map/ppermute | solution.py:479
  78.9 8.0 %collective-permute-start.5 = (f32[2,32,1280]{2,1,0:T(8,128)S(1)}, f32[2,32,1280]{2,1,0:T(8,128)S(1)}, u32[]{:S(2)}, u32[]{:S(2)}) collective-permute-start(f32[2,32,1280]{2,1,0:T(8,128)S(1)} %get-tuple-element.34), channel_id=1, source_target_pairs={{0,2},{1,3},{2,0},{3,1},{4,6},{5,7},{6,4},{7,5},{8,10},{9,11},{10,... | collective-permute-start | bytes 983048 | tf_op jit(solution)/shard_map/ppermute | solution.py:479
  79.6 25.0 %copy-start.4 = (bf16[256,256]{1,0:T(8,128)(2,1)S(1)}, bf16[256,256]{1,0:T(8,128)(2,1)}, u32[]{:S(2)}) copy-start(bf16[256,256]{1,0:T(8,128)(2,1)} %constant.54.clone.bz_ref) | copy-start | bytes 393220
  79.6 25.0 %copy-start.14 = (bf16[64,160]{1,0:T(8,128)(2,1)S(1)}, bf16[64,160]{1,0:T(8,128)(2,1)}, u32[]{:S(2)}) copy-start(bf16[64,160]{1,0:T(8,128)(2,1)} %constant.52.clone.bx_ref) | copy-start | bytes 61444
  79.6 41.3 %collective-permute-start.9 = (f32[2,32,1280]{2,1,0:T(8,128)S(1)}, f32[2,32,1280]{2,1,0:T(8,128)S(1)}, u32[]{:S(2)}, u32[]{:S(2)}) collective-permute-start(f32[2,32,1280]{2,1,0:T(8,128)S(1)} %pad_maximum_fusion.5), channel_id=1, source_target_pairs={{0,1},{1,0},{2,3},{3,2},{4,5},{5,4},{6,7},{7,6},{8,9},{9,8},{10,11... | collective-permute-start | bytes 983048 | tf_op jit(solution)/shard_map/ppermute | solution.py:481
  102.9 1.7 %collective-permute-start.7 = (f32[2,32,1280]{2,1,0:T(8,128)S(1)}, f32[2,32,1280]{2,1,0:T(8,128)S(1)}, u32[]{:S(2)}, u32[]{:S(2)}) collective-permute-start(f32[2,32,1280]{2,1,0:T(8,128)S(1)} %pad_maximum_fusion.4), channel_id=1, source_target_pairs={{0,1},{1,0},{2,3},{3,2},{4,5},{5,4},{6,7},{7,6},{8,9},{9,8},{10,11... | collective-permute-start | bytes 983048 | tf_op jit(solution)/shard_map/ppermute | solution.py:481
  102.9 18.0 %collective-permute-start.8 = (f32[2,32,1280]{2,1,0:T(8,128)S(1)}, f32[2,32,1280]{2,1,0:T(8,128)}, u32[]{:S(2)}, u32[]{:S(2)}) collective-permute-start(f32[2,32,1280]{2,1,0:T(8,128)S(1)} %get-tuple-element.42), channel_id=1, source_target_pairs={{0,2},{1,3},{2,0},{3,1},{4,6},{5,7},{6,4},{7,5},{8,10},{9,11},{10,... | collective-permute-start | bytes 983048 | tf_op jit(solution)/shard_map/ppermute | solution.py:479
  103.5 30.5 %copy-start.22 = (f32[4,4]{1,0:T(4,128)S(1)}, f32[4,4]{1,0:T(4,128)}, u32[]{:S(2)}) copy-start(f32[4,4]{1,0:T(4,128)} %fusion) | copy-start | bytes 196
  120.2 17.5 %collective-permute-start.15 = (f32[2,32,1280]{2,1,0:T(8,128)S(1)}, f32[2,32,1280]{2,1,0:T(8,128)S(1)}, u32[]{:S(2)}, u32[]{:S(2)}) collective-permute-start(f32[2,32,1280]{2,1,0:T(8,128)S(1)} %get-tuple-element.54), channel_id=1, source_target_pairs={{0,2},{1,3},{2,0},{3,1},{4,6},{5,7},{6,4},{7,5},{8,10},{9,11},{10,... | collective-permute-start | bytes 983048 | tf_op jit(solution)/shard_map/ppermute | solution.py:479
  121.6 3.6 %collective-permute-start.10 = (f32[3,4]{1,0:T(4,128)S(1)}, f32[3,4]{1,0:T(4,128)S(1)}, u32[]{:S(2)}, u32[]{:S(2)}) collective-permute-start(f32[3,4]{1,0:T(4,128)S(1)} %pad_maximum_fusion.8), channel_id=1, source_target_pairs={{0,4},{4,0},{8,12},{12,8},{16,20},{20,16},{24,28},{28,24},{1,5},{5... | collective-permute-start | bytes 152 | tf_op jit(solution)/shard_map/ppermute | solution.py:489
  123.3 15.0 %copy-start.20 = (f32[2,32,1280]{2,1,0:T(8,128)S(1)}, f32[2,32,1280]{2,1,0:T(8,128)}, u32[]{:S(2)}) copy-start(f32[2,32,1280]{2,1,0:T(8,128)} %copy-done.19) | copy-start | bytes 983044
  125.3 3.7 %collective-permute-start.11 = (f32[3,4]{1,0:T(4,128)S(1)}, f32[3,4]{1,0:T(4,128)S(1)}, u32[]{:S(2)}, u32[]{:S(2)}) collective-permute-start(f32[3,4]{1,0:T(4,128)S(1)} %pad_maximum_fusion.9), channel_id=1, source_target_pairs={{0,8},{4,12},{8,0},{12,4},{16,24},{20,28},{24,16},{28,20},{1,9},{5... | collective-permute-start | bytes 152 | tf_op jit(solution)/shard_map/ppermute | solution.py:489
  128.9 4.5 %collective-permute-start.12 = (f32[3,4]{1,0:T(4,128)S(1)}, f32[3,4]{1,0:T(4,128)S(1)}, u32[]{:S(2)}, u32[]{:S(2)}) collective-permute-start(f32[3,4]{1,0:T(4,128)S(1)} %pad_maximum_fusion.10), channel_id=1, source_target_pairs={{0,16},{4,20},{8,24},{12,28},{16,0},{20,4},{24,8},{28,12},{1,17},{... | collective-permute-start | bytes 152 | tf_op jit(solution)/shard_map/ppermute | solution.py:489
  134.1 3.6 %collective-permute-start.13 = (f32[1,4,6]{2,1,0:T(4,128)S(1)}, f32[1,4,6]{2,1,0:T(4,128)S(1)}, u32[]{:S(2)}, u32[]{:S(2)}) collective-permute-start(f32[1,4,6]{2,1,0:T(4,128)S(1)} %maximum_bitcast_fusion.1), channel_id=1, source_target_pairs={{0,2},{1,3},{2,0},{3,1},{4,6},{5,7},{6,4},{7,5},{8,10},{9,11},{10,... | collective-permute-start | bytes 296 | tf_op jit(solution)/shard_map/ppermute | solution.py:494
  137.7 1.2 collective-permute-start.14
  137.8 2.3 %collective-permute-start.16 = (f32[4,32,1280]{2,1,0:T(8,128)S(1)}, f32[4,32,1280]{2,1,0:T(8,128)S(1)}, u32[]{:S(2)}, u32[]{:S(2)}) collective-permute-start(f32[4,32,1280]{2,1,0:T(8,128)S(1)} %pad_maximum_fusion.2), channel_id=1, source_target_pairs={{0,1},{1,0},{2,3},{3,2},{4,5},{5,4},{6,7},{7,6},{8,9},{9,8},{10,11... | collective-permute-start | bytes 1966088 | tf_op jit(solution)/shard_map/ppermute | solution.py:499
  (8 other events, 20.5 us)

commit v2 on v1

--- a/solution.py
+++ b/solution.py
@@ -67,7 +67,9 @@
         slab[rows, (2 * j + 1) * LANES : (2 * j + 2) * LANES] = low
     tables["slab_z"] = slab
     tables["slab_y"] = row_table(k_y, np.arange(y_cells), n_y, -1.0, 1.0, True)
-    tables["slab_x"] = row_table(k_x, np.arange(n_x), n_x, -1.0, 1.0, True)
+    own = np.arange(HALF, HALF + x_cells)
+    halo = np.concatenate([np.arange(HALF), np.arange(HALF + x_cells, n_x)])
+    tables["slab_x"] = row_table(k_x, np.concatenate([own, halo]), n_x, -1.0, 1.0, True)
     high, low = two_parts(depth_table(np.arange(TEMPL) - HALF, n_z, 1.0, 1.0))
     tmpl = np.zeros((8, 2 * LANES, 2 * LANES), ml_dtypes.bfloat16)
     for j in range(8):
@@ -115,7 +117,11 @@
 
 
 def pair_rows(table, value, wide):
-    out = jnp.dot(table, split_rows(value, wide), preferred_element_type=F32)
+    return pair_dot(table, split_rows(value, wide), wide)
+
+
+def pair_dot(table, parts, wide):
+    out = jnp.dot(table, parts, preferred_element_type=F32)
     if not wide:
         half = out.shape[0] // 2
         out = out[:half] + out[half:]
@@ -147,90 +153,116 @@
 GROUP = 8
 
 
-def slab_kernel(dims, slab_ref, z_ref, y_ref, x_ref, same_ref, cross_ref, depth_buf, rows_buf):
+def slab_rows_kernel(dims, *refs):
+    slab_refs, (z_ref, y_ref, rows_ref, depth_buf) = refs[:-4], refs[-4:]
     x_cells, y_cells, z_cells = dims
-    n_x, n_y = x_cells + TEMPL, y_cells + HALF
-    half_y = n_y // 2
-    pad_y = half_y + -half_y % 8
+    count = sum(ref.shape[0] for ref in slab_refs)
+    n_y = y_cells + HALF
+    pad_y = n_y // 2 + -(n_y // 2) % 8
+    many = 4
 
     def depth_step(i):
-        block = jnp.concatenate(
-            [slab_ref[:, pl.ds(pl.multiple_of((4 * i + u) * LANES, LANES), LANES)] for u in range(4)],
-            axis=0,
-        )
-        out = jnp.dot(block, z_ref[...], preferred_element_type=F32)
-        for u in range(4):
-            part = out[u * n_x : (u + 1) * n_x]
-            for j in range(2):
-                store(
-                    depth_buf, (8 * i + 2 * u + j) * n_x,
-                    lane_block(part, 2 * j) + lane_block(part, 2 * j + 1),
-                )
-
-    loop(y_cells // 8, depth_step)
+        top = 0
+        for ref in slab_refs:
+            size = ref.shape[0]
+            lanes = [pl.ds(pl.multiple_of((many * i + u) * LANES, LANES), LANES) for u in range(many)]
+            block = jnp.concatenate([ref[:, l].astype(F32) for l in lanes], axis=0).astype(BF16)
+            out = jnp.dot(block, z_ref[...], preferred_element_type=F32)
+            for u in range(many):
+                part = out[u * size : (u + 1) * size]
+                for j in range(2):
+                    store(
+                        depth_buf, (2 * many * i + 2 * u + j) * count + top,
+                        lane_block(part, 2 * j) + lane_block(part, 2 * j + 1),
+                    )
+            top += size
+
+    loop(y_cells // (2 * many), depth_step)
 
     def y_step(i):
-        value = pick(depth_buf, [GROUP * i + u for u in range(GROUP)], y_cells, n_x)
+        value = pick(depth_buf, [GROUP * i + u for u in range(GROUP)], y_cells, count)
         plus, minus = pair_rows(y_ref[...], value, True)
         for u in range(GROUP):
             start = (GROUP * i + u) * 2 * pad_y
-            store(rows_buf, start, lane_block(plus, u))
-            store(rows_buf, start + pad_y, lane_block(minus, u))
-
-    loop(n_x // GROUP, y_step)
+            store(rows_ref, start, lane_block(plus, u))
+            store(rows_ref, start + pad_y, lane_block(minus, u))
+
+    loop(count // GROUP, y_step)
+
+
+def slab_rows(blocks, dims, tables, name):
+    x_cells, y_cells, z_cells = dims
+    count = sum(block.shape[0] for block in blocks)
+    n_y = y_cells + HALF
+    pad_y = n_y // 2 + -(n_y // 2) % 8
+    vmem = pl.BlockSpec(memory_space=pltpu.VMEM)
+    return pl.pallas_call(
+        functools.partial(slab_rows_kernel, dims),
+        out_shape=jax.ShapeDtypeStruct((count * 2 * pad_y, LANES), F32),
+        in_specs=[vmem] * (2 + len(blocks)),
+        out_specs=vmem,
+        scratch_shapes=[pltpu.VMEM((y_cells * count, LANES), F32)],
+        compiler_params=pltpu.CompilerParams(vmem_limit_bytes=VMEM_LIMIT),
+        cost_estimate=pl.CostEstimate(flops=count * 10**8, bytes_accessed=10**6, transcendentals=0),
+        name=name,
+    )(*blocks, tables["slab_z"], tables["slab_y"])
+
+
+def slab_x_kernel(dims, own_ref, halo_ref, x_ref, spec_ref):
+    x_cells, y_cells, z_cells = dims
+    n_y = y_cells + HALF
+    pad_y = n_y // 2 + -(n_y // 2) % 8
 
     def x_step(i):
         firsts = [GROUP // 2 * i + u // 2 + u % 2 * pad_y for u in range(GROUP)]
-        value = pick(rows_buf, firsts, n_x, 2 * pad_y)
+        value = jnp.concatenate(
+            [
+                pick(own_ref, firsts, x_cells, 2 * pad_y),
+                pick(halo_ref, firsts, TEMPL, 2 * pad_y),
+            ],
+            axis=0,
+        )
         plus, minus = pair_rows(x_ref[...], value, True)
         spec = jnp.concatenate([plus, minus], axis=0)
         turned = swap(spec)
         real_lane = lane_sign(GROUP * LANES) < 0
-        same_ref[i] = jnp.where(real_lane, spec, turned)
-        cross_ref[i] = jnp.where(real_lane, -turned, spec)
+        spec_ref[i, 0] = jnp.where(real_lane, spec, turned)
+        spec_ref[i, 1] = jnp.where(real_lane, -turned, spec)
 
     loop(n_y // GROUP, x_step)
 
 
-def slab_spectrum(widened, dims, tables):
+def slab_x(own, halo, dims, tables):
     x_cells, y_cells, z_cells = dims
     n_x, n_y = x_cells + TEMPL, y_cells + HALF
-    pad_y = n_y // 2 + -(n_y // 2) % 8
-    shape = jax.ShapeDtypeStruct((n_y // GROUP, n_x, GROUP * LANES), F32)
     vmem = pl.BlockSpec(memory_space=pltpu.VMEM)
     return pl.pallas_call(
-        functools.partial(slab_kernel, dims),
-        out_shape=(shape, shape),
-        in_specs=[vmem] * 4,
-        out_specs=(vmem, vmem),
-        scratch_shapes=[
-            pltpu.VMEM((y_cells * n_x, LANES), F32),
-            pltpu.VMEM((n_x * 2 * pad_y, LANES), F32),
-        ],
+        functools.partial(slab_x_kernel, dims),
+        out_shape=jax.ShapeDtypeStruct((n_y // GROUP, 2, n_x, GROUP * LANES), F32),
+        in_specs=[vmem] * 3,
+        out_specs=vmem,
         compiler_params=pltpu.CompilerParams(vmem_limit_bytes=VMEM_LIMIT),
-        cost_estimate=pl.CostEstimate(flops=10**10, bytes_accessed=10**7, transcendentals=0),
-        name="slab_spectrum",
-    )(widened, tables["slab_z"], tables["slab_y"], tables["slab_x"])
+        cost_estimate=pl.CostEstimate(flops=5 * 10**9, bytes_accessed=10**6, transcendentals=0),
+        name="slab_x",
+    )(own, halo, tables["slab_x"])
 
 
 def corr_kernel(
-    dims, place_ref, tmpl_ref, mask_ref, same_hbm, cross_hbm,
+    dims, rot, place_ref, tmpl_ref, mask_ref, spec_hbm,
     z_ref, ones_ref, y_ref, x_ref, bx_ref, by_ref, bz_ref,
     mine_ref, side_ref, far_ref, stat_ref,
-    same_ref, cross_ref, depth_buf, rows_buf, back_buf, vol_buf, sems,
+    spec_ref, depth_buf, rows_buf, first_buf, second_buf, back_buf, vol_buf, sem,
 ):
     x_cells, y_cells, z_cells = dims
     n_x, n_y = x_cells + TEMPL, y_cells + HALF
     half_y = n_y // 2
     pad_y = half_y + -half_y % 8
-    copies = [
-        pltpu.make_async_copy(same_hbm, same_ref, sems.at[0]),
-        pltpu.make_async_copy(cross_hbm, cross_ref, sems.at[1]),
-    ]
-    for copy in copies:
-        copy.start()
-
-    tmpl = tmpl_ref[0].astype(F32)
+    copy = pltpu.make_async_copy(spec_hbm, spec_ref, sem)
+    copy.start()
+
+    each = TEMPL // 8
+    rows = slice(rot * each, (rot + 1) * each)
+    tmpl = jnp.concatenate([tmpl_ref[t, rows, :] for t in range(8)], axis=0)
     inv_size = 1.0 / TEMPL**3
     mean = jnp.sum(tmpl) * inv_size
     centred = tmpl - mean
@@ -239,8 +271,9 @@
     shift = ones_ref[:1] * mean
 
     wide = 8 * TEMPL
+    narrow = tmpl.astype(BF16)
     block = jnp.concatenate(
-        [tmpl_ref[0, :, g * wide : (g + 1) * wide] for g in range(TEMPL // 8)], axis=0
+        [narrow[:, g * wide : (g + 1) * wide] for g in range(TEMPL // 8)], axis=0
     )
     for j in range(8):
         window = block[:, : 2 * LANES] if j < 4 else block[:, LANES:]
@@ -251,41 +284,60 @@
             depth_buf[start : start + TEMPL, :] = part[g * TEMPL : (g + 1) * TEMPL]
 
     def y_step(i):
-        value = pick(depth_buf, [GROUP * i + u for u in range(GROUP)], TEMPL, TEMPL)
-        plus, minus = pair_rows(y_ref[...], value, True)
-        for u in range(GROUP):
-            start = (GROUP * i + u) * 2 * pad_y
-            store(rows_buf, start, lane_block(plus, u))
-            store(rows_buf, start + pad_y, lane_block(minus, u))
-
-    loop(TEMPL // GROUP, y_step)
-    for copy in copies:
-        copy.wait()
-
-    def x_step(i):
+        for i in (2 * i, 2 * i + 1):
+            value = pick(depth_buf, [GROUP * i + u for u in range(GROUP)], TEMPL, TEMPL)
+            plus, minus = pair_rows(y_ref[...], value, True)
+            for u in range(GROUP):
+                start = (GROUP * i + u) * 2 * pad_y
+                store(rows_buf, start, lane_block(plus, u))
+                store(rows_buf, start + pad_y, lane_block(minus, u))
+
+    loop(TEMPL // GROUP // 2, y_step)
+    copy.wait()
+
+    def gather_rows(i):
         firsts = [GROUP // 2 * i + u // 2 + u % 2 * pad_y for u in range(GROUP)]
-        value = pick(rows_buf, firsts, TEMPL, 2 * pad_y)
-        plus, minus = pair_rows(x_ref[...], value, True)
+        first_buf[...] = split_rows(pick(rows_buf, firsts, TEMPL, 2 * pad_y), True)
+
+    def multiply(i):
+        plus, minus = pair_dot(x_ref[...], first_buf[...], True)
         spec = jnp.concatenate([plus, minus], axis=0)
-        prod = spec * same_ref[i] + swap(spec) * cross_ref[i]
-        plus, minus = pair_rows(bx_ref[...], prod, False)
+        prod = spec * spec_ref[i, 0] + swap(spec) * spec_ref[i, 1]
+        second_buf[...] = split_rows(prod, False)
+
+    def back_x(i):
+        plus, minus = pair_dot(bx_ref[...], second_buf[...], False)
         for u in range(GROUP):
             start = (GROUP * i + u) * x_cells
             store(back_buf, start, lane_block(plus, u))
             store(back_buf, start + x_cells // 2, lane_block(minus, u))
 
-    loop(n_y // GROUP, x_step)
+    steps = n_y // GROUP
+    gather_rows(0)
+    multiply(0)
+    gather_rows(1)
+
+    def pipelined(i):
+        back_x(i)
+        multiply(i + 1)
+        gather_rows(i + 2)
+
+    loop(steps - 2, pipelined)
+    back_x(steps - 2)
+    multiply(steps - 1)
+    back_x(steps - 1)
 
     def back_step(i):
-        value = pick(back_buf, [GROUP * i + u for u in range(GROUP)], n_y, x_cells)
-        plus, minus = pair_rows(by_ref[...], value, False)
-        for u in range(GROUP):
-            row = GROUP * i + u
-            x = jnp.where(row < x_cells // 2, row + x_cells // 2, x_cells - 1 - row)
-            store(vol_buf, x * y_cells, lane_block(plus, u))
-            store(vol_buf, x * y_cells + y_cells // 2, lane_block(minus, u))
-
-    loop(x_cells // GROUP, back_step)
+        for i in (2 * i, 2 * i + 1):
+            value = pick(back_buf, [GROUP * i + u for u in range(GROUP)], n_y, x_cells)
+            plus, minus = pair_rows(by_ref[...], value, False)
+            for u in range(GROUP):
+                row = GROUP * i + u
+                x = jnp.where(row < x_cells // 2, row + x_cells // 2, x_cells - 1 - row)
+                store(vol_buf, x * y_cells, lane_block(plus, u))
+                store(vol_buf, x * y_cells + y_cells // 2, lane_block(minus, u))
+
+    loop(x_cells // GROUP // 2, back_step)
 
     share = y_cells // 8
     me = place_ref[0]
@@ -324,42 +376,38 @@
     stat_ref[...] = jnp.where(row == 0, number_sum, jnp.where(row == 1, total_sum, jnp.sum(square)))
 
 
-def correlate(place, bank, rot, mask, same, cross, dims, tables):
+def correlate(place, bank, rot, mask, spec, dims, tables):
     x_cells, y_cells, z_cells = dims
     n_x, n_y = x_cells + TEMPL, y_cells + HALF
     pad_y = n_y // 2 + -(n_y // 2) % 8
     width = y_cells * z_cells // 4
     vmem = pl.BlockSpec(memory_space=pltpu.VMEM)
-    anyspace = pl.BlockSpec(memory_space=pl.ANY)
     return pl.pallas_call(
-        functools.partial(corr_kernel, dims),
-        grid=(1,),
+        functools.partial(corr_kernel, dims, rot),
         out_shape=(
             jax.ShapeDtypeStruct((x_cells, width), F32),
             jax.ShapeDtypeStruct((x_cells, width), F32),
             jax.ShapeDtypeStruct((2, x_cells, width), F32),
             jax.ShapeDtypeStruct((8, LANES), F32),
         ),
-        in_specs=[
-            pl.BlockSpec(memory_space=pltpu.SMEM),
-            pl.BlockSpec((1, TEMPL, TEMPL * TEMPL), lambda i: (rot, 0, 0)),
-            vmem, anyspace, anyspace, vmem, vmem, vmem, vmem, vmem, vmem, vmem,
-        ],
+        in_specs=[pl.BlockSpec(memory_space=pltpu.SMEM), vmem, vmem]
+        + [pl.BlockSpec(memory_space=pl.ANY)] + [vmem] * 7,
         out_specs=(vmem,) * 4,
         scratch_shapes=[
-            pltpu.VMEM((n_y // GROUP, n_x, GROUP * LANES), F32),
-            pltpu.VMEM((n_y // GROUP, n_x, GROUP * LANES), F32),
+            pltpu.VMEM(spec.shape, F32),
             pltpu.VMEM((TEMPL * TEMPL, LANES), F32),
             pltpu.VMEM((TEMPL * 2 * pad_y, LANES), F32),
+            pltpu.VMEM((3 * TEMPL, GROUP * LANES), BF16),
+            pltpu.VMEM((2 * n_x, GROUP * LANES), BF16),
             pltpu.VMEM((n_y * x_cells, LANES), F32),
             pltpu.VMEM((x_cells * y_cells, LANES), F32),
-            pltpu.SemaphoreType.DMA((2,)),
+            pltpu.SemaphoreType.DMA,
         ],
         compiler_params=pltpu.CompilerParams(vmem_limit_bytes=VMEM_LIMIT),
         cost_estimate=pl.CostEstimate(flops=15 * 10**9, bytes_accessed=10**7, transcendentals=0),
         name="correlate",
     )(
-        place, bank, mask, same, cross,
+        place, bank, mask, spec,
         tables["tmpl_z"], tables["ones_z"], tables["tmpl_y"], tables["tmpl_x"],
         tables["back_x"], tables["back_y"], tables["back_z"],
     )
@@ -408,17 +456,16 @@
     )(coefs, mask, *pieces)
 
 
-def doubling_gather(block, axis):
+def gather_steps(count):
+    return [1 << i for i in reversed(range(count.bit_length() - 1))]
+
+
+def gather_step(block, axis, step):
     count = lax.axis_size(axis)
-    me = lax.axis_index(axis)
-    steps = [1 << i for i in reversed(range(count.bit_length() - 1))]
-    block = block[None]
-    for step in steps:
-        other = lax.ppermute(block, axis, [(i, i ^ step) for i in range(count)])
-        upper = (me & step) != 0
-        pair = [jnp.where(upper, other, block), jnp.where(upper, block, other)]
-        block = jnp.stack(pair, axis=1).reshape((-1,) + block.shape[1:])
-    return block
+    other = lax.ppermute(block, axis, [(i, i ^ step) for i in range(count)])
+    upper = (lax.axis_index(axis) & step) != 0
+    pair = [jnp.where(upper, other, block), jnp.where(upper, block, other)]
+    return jnp.stack(pair, axis=1).reshape((-1,) + block.shape[1:])
 
 
 def merge(first, other):
@@ -430,13 +477,13 @@
     return jnp.stack([number, first[1] + other[1], (first[2] + other[2]) + between])
 
 
-def padded(block, axis, width):
+def halos(block, axis, width):
     count = lax.axis_size(axis)
     forward = [(i, i + 1) for i in range(count - 1)]
     backward = [(target, source) for source, target in forward]
     low = lax.ppermute(block[block.shape[0] - width :], axis, forward)
     high = lax.ppermute(block[:width], axis, backward)
-    return jnp.concatenate([low, block, high], axis=0)
+    return low, high
 
 
 def local(tomogram, templates, valid, quats, rot_index):
@@ -450,9 +497,15 @@
     me = lax.axis_index("rot")
     rots = templates.shape[0]
 
-    widened = padded(tomogram, "tile", HALF)
-    gathered = doubling_gather(templates, "tile")
-    bank = jnp.transpose(gathered, (1, 0, 2)).reshape(rots, TEMPL, TEMPL * TEMPL)
+    low, high = halos(tomogram, "tile", HALF)
+    row = TEMPL * TEMPL
+    chunk = templates.shape[1]
+    whole_rows = chunk % row == 0
+    block = templates.reshape(rots * chunk // row, row) if whole_rows else templates
+    block = block[None]
+    steps = gather_steps(tiles)
+    for step in steps[:-1]:
+        block = gather_step(block, "tile", step)
     one_hot = (rot_index[:, None] == jnp.arange(quats.shape[1], dtype=jnp.int32)[None, :]).astype(F32)
     orient = jnp.einsum("rq,kq->rk", one_hot, quats, precision=lax.Precision.HIGHEST)
     place = jnp.reshape(me, (1,)).astype(jnp.int32)
@@ -461,7 +514,14 @@
     share_blocks = voxels // LANES // groups
     mask_part = lax.dynamic_slice_in_dim(mask, me * share_blocks, share_blocks, 0)
 
-    same, cross = slab_spectrum(widened, dims, tables)
+    own = slab_rows([tomogram], dims, tables, "slab_own")
+    halo = slab_rows([low, high], dims, tables, "slab_halo")
+    spec = slab_x(own, halo, dims, tables)
+    block = gather_step(block, "tile", steps[-1])
+    if not whole_rows:
+        block = jnp.transpose(block, (1, 0, 2)).reshape(rots, 8, TEMPL // 8, row)
+        block = jnp.transpose(block, (1, 0, 2, 3))
+    bank = block.reshape(8, rots * (TEMPL // 8), row).astype(F32)
     far_swap = [(i, i ^ 2) for i in range(groups)]
     side_swap = [(i, i ^ 1) for i in range(groups)]
     mines, sides, fars, from_sides, stats = [], [], [], [], []
@@ -470,7 +530,9 @@
             place, fars[r - 2] = lax.optimization_barrier((place, fars[r - 2]))
         if r >= 3:
             place, from_sides[r - 3] = lax.optimization_barrier((place, from_sides[r - 3]))
-        mine, side, far, stat = correlate(place, bank, r, mask, same, cross, dims, tables)
+        mine, side, far, stat = correlate(place, bank, r, mask, spec, dims, tables)
+        if r >= 1:
+            stat, fars[r - 1] = lax.optimization_barrier((stat, fars[r - 1]))
         if r >= 1 and r < rots - 1:
             both = jnp.stack([sides[r - 1], fars[r - 1][1]])
         mines.append(mine)

time: 144 us -> 124 us (0.86)
  waiting for transfers between devices: 24.6 us -> 13.6 us
  Pallas kernels: 80.5 us -> 72.9 us
  starting transfers between devices: 21.5 us -> 23.9 us
  local copies, waits for them, and re-layouts: 10.6 us -> 8.71 us
  other arithmetic: 3.86 us -> 2.42 us
    pallas_call x5 -> x7, Pallas kernels: 76.8 us -> 69.2 us  [the longest x4 52.5 us: correlate(): pl.pallas_call(functools.partial(corr_kernel, dims, rot), out_shape=(jax....]
    ppermute x4, waiting for transfers between devices: 7.21 us -> 0.01 us  [local(): fars.append(lax.ppermute(far, 'rot', far_swap))]
    ppermute x5, waiting for transfers between devices: 4.96 us -> 0.85 us  [the longest x3 0.84 us: gather_step(): other = lax.ppermute(block, axis, [(i, i ^ step) for i in range(count)])]
    reshape x1 -> x0, local copies, waits for them, and re-layouts: 2.22 us -> none  [local(): jnp.transpose(gathered, (1, 0, 2)).reshape(rots, TEMPL, TEMPL * TEMPL)]
    another operation x2, local copies, waits for them, and re-layouts: 0.37 us -> 2.29 us  [local(): inside.reshape(x_cells, voxels // LANES, LANES)]
    ppermute x1, waiting for transfers between devices: 1.09 us -> 3.01 us  [local(): from_far = lax.ppermute(coefs, 'rot', far_swap)]
    ppermute x4, starting transfers between devices: 3.36 us -> 5.17 us  [local(): fars.append(lax.ppermute(far, 'rot', far_swap))]
    unnamed x46 -> x34, local copies, waits for them, and re-layouts: 3.38 us -> 2.41 us
  transfers between devices with their start and end apart: 17 -> 17, of which waited for: 10 -> 8; matrix products, arithmetic and copies ran while one was open for 5% -> 6% of each run, Pallas kernels for 43% -> 46%
where the time goes in v2:
time: 124 us; the launch traced here: 123 us
  Pallas kernels  72.9 us (59%)
  starting transfers between devices  23.9 us (19%)
  waiting for transfers between devices  13.6 us (11%)
  local copies, waits for them, and re-layouts  8.71 us (7%)
  other arithmetic  2.42 us (2%)
    pallas_call x4, Pallas kernels, correlate(): pl.pallas_call(functools.partial(corr_kernel, dims, rot), out_shape=(jax....  52.5 us
    pallas_call x1, Pallas kernels, slab_x(): pl.pallas_call(functools.partial(slab_x_kernel, dims), out_shape=jax.Shap...  9.03 us
    ppermute x3, starting transfers between devices, gather_step(): other = lax.ppermute(block, axis, [(i, i ^ step) for i in range(count)])  8.62 us
    ppermute x3, waiting for transfers between devices, local(): state = merge(state, lax.ppermute(state, 'tile', swap_pairs))  8.05 us
    pallas_call x2, Pallas kernels, slab_rows(): pl.pallas_call(functools.partial(slab_rows_kernel, dims), out_shape=jax.S...  7.72 us
    ppermute x4, starting transfers between devices, local(): fars.append(lax.ppermute(far, 'rot', far_swap))  5.17 us
    ppermute x3, starting transfers between devices, local(): state = merge(state, lax.ppermute(state, 'tile', swap_pairs))  3.7 us
    pallas_call x1, Pallas kernels, combine(): pl.pallas_call(score_kernel, out_shape=(out, out, jax.ShapeDtypeStruct((4...  3.67 us
  transfers between devices with their start and end apart: 17, of which 8 were waited for; matrix products, arithmetic and copies ran while one was open for 6% of the time, Pallas kernels for 46%

profile of v2, /device:TPU:0, one launch (start us, length us, event | category | flops | bytes accessed | tf_op | source)
XLA Modules:
  0.0 123.0 jit_solution(5273561294494946730)
XLA Ops:
  0.6 1.0 broadcast_in_dim_reshape.3
  1.7 4.1 %collective-permute-start = (bf16[1,24,2304]{2,1,0:T(8,128)(2,1)S(1)}, bf16[1,24,2304]{2,1,0:T(8,128)(2,1)}, u32[]{:S(2)}, u32[]{:S(2)}) collective-permute-start(bf16[1,24,2304]{2,1,0:T(8,128)(2,1)S(1)} %broadcast_in_dim_reshape.3), channel_id=1, source_target_pairs={{0,16},{4,20},{8,24},{12,28},{16,0},{20,4},{24,8},{28,12},{1,17},{... | collective-permute-start | bytes 331784 | tf_op jit(solution)/shard_map/ppermute | solution.py:465
  5.8 1.9 %fusion.3 = (bf16[24,5120]{1,0:T(8,128)(2,1)}, bf16[24,5120]{1,0:T(8,128)(2,1)}) fusion(bf16[32,5120]{1,0:T(8,128)(2,1)} %refs_0_.1), kind=kLoop, calls=%fused_computation.50 | loop fusion | bytes 983040 | tf_op jit(solution)/shard_map/slice | solution.py:485
  7.7 3.4 %collective-permute-start.3 = (bf16[24,5120]{1,0:T(8,128)(2,1)}, bf16[24,5120]{1,0:T(8,128)(2,1)S(1)}, u32[]{:S(2)}, u32[]{:S(2)}) collective-permute-start(bf16[24,5120]{1,0:T(8,128)(2,1)} %get-tuple-element.88), channel_id=1, source_target_pairs={{0,4},{4,8},{8,12},{12,16},{16,20},{20,24},{24,28},{1,5},{5,9},{9,... | collective-permute-start | bytes 737288 | tf_op jit(solution)/shard_map/ppermute | solution.py:484
  11.1 1.3 %collective-permute-start.4 = (bf16[24,5120]{1,0:T(8,128)(2,1)}, bf16[24,5120]{1,0:T(8,128)(2,1)S(1)}, u32[]{:S(2)}, u32[]{:S(2)}) collective-permute-start(bf16[24,5120]{1,0:T(8,128)(2,1)} %get-tuple-element.87), channel_id=1, source_target_pairs={{4,0},{8,4},{12,8},{16,12},{20,16},{24,20},{28,24},{5,1},{9,5},{13... | collective-permute-start | bytes 737288 | tf_op jit(solution)/shard_map/ppermute | solution.py:485
  12.4 0.7 convert_element_type.11
  13.5 1.1 reshape_reshape.3
  14.6 1.2 copy.40
  15.9 3.5 %slab_own.1.own_ref = f32[3584,128]{1,0:T(8,128)S(1)} custom-call(bf16[32,5120]{1,0:T(8,128)(2,1)S(1)} %copy-done.1, bf16[128,512]{1,0:T(8,128)(2,1)S(1)} %copy-done.4, bf16[112,240]{1,0:T(8,128)(2,1)S(1)} %copy-done.7), custom_call_target="tpu_custom_call" | custom-call | flops 3200000000 | bytes 1000000 | tf_op jit(solution)/shard_map/slab_own/pallas_call | solution.py:199
  19.4 1.3 %copy-done.12 = f32[3584,128]{1,0:T(8,128)} copy-done((f32[3584,128]{1,0:T(8,128)}, f32[3584,128]{1,0:T(8,128)S(1)}, u32[]{:S(2)}) %copy-start.12) | copy-done | bytes 1835032
  21.1 0.9 select_bitcast_fusion.5
  22.0 3.7 %collective-permute-start.1 = (bf16[2,24,2304]{2,1,0:T(8,128)(2,1)S(1)}, bf16[2,24,2304]{2,1,0:T(8,128)(2,1)S(1)}, u32[]{:S(2)}, u32[]{:S(2)}) collective-permute-start(bf16[2,24,2304]{2,1,0:T(8,128)(2,1)S(1)} %maximum_bitcast_fusion), channel_id=1, source_target_pairs={{0,8},{4,12},{8,0},{12,4},{16,24},{20,28},{24,16},{28,20},{1,9},{5... | collective-permute-start | bytes 663560 | tf_op jit(solution)/shard_map/ppermute | solution.py:465
  25.7 4.2 %slab_halo.1.halo_ref = f32[5376,128]{1,0:T(8,128)S(1)} custom-call(bf16[24,5120]{1,0:T(8,128)(2,1)S(1)} %collective-permute-done.3.refs_0_, bf16[24,5120]{1,0:T(8,128)(2,1)S(1)} %collective-permute-done.4.refs_1_, bf16[128,512]{1,0:T(8,128)(2,1)S(1)} %copy-done.4, bf16[112,240]{1,0:T(8,128)(2,1)S(1)} %copy-done.7), custom_call_target="tpu_custom_call" | custom-call | flops 4800000000 | bytes 1000000 | tf_op jit(solution)/shard_map/slab_halo/pallas_call | solution.py:199
  30.4 0.8 collective-permute-start.2
  31.4 9.0 %slab_x.1.spec_hbm = f32[13,2,80,1024]{3,2,1,0:T(8,128)} custom-call(f32[3584,128]{1,0:T(8,128)S(1)} %copy-done.13, f32[5376,128]{1,0:T(8,128)S(1)} %slab_halo.1.halo_ref, bf16[80,240]{1,0:T(8,128)(2,1)S(1)} %copy-done.9), custom_call_target="tpu_custom_call" | custom-call | flops 5000000000 | bytes 1000000 | tf_op jit(solution)/shard_map/slab_x/pallas_call | solution.py:239
  41.4 0.9 copy-done.2
  42.3 13.1 %correlate.4 = (f32[32,1280]{1,0:T(8,128)S(1)}, f32[32,1280]{1,0:T(8,128)S(1)}, f32[2,32,1280]{2,1,0:T(8,128)S(1)}, f32[8,128]{1,0:T(8,128)S(1)}) custom-call(s32[1]{0:T(128)} %bitcast.place_ref, f32[8,24,2304]{2,1,0:T(8,128)S(1)} %bitcast_convert_fusion.tmpl_ref, f32[40,32,128]{2,1,0:T(8,128)S(1)} %bitcast.73, f32[13,2,80,1024]{3,2,1,0:T(8,128)} %slab_x.1.spec_hbm, ...), custom_call_target="tpu_custom_call" | custom-call | flops 15000000512 | bytes 10000000 | tf_op jit(solution)/shard_map/correlate/pallas_call | solution.py:385
  55.4 1.6 %collective-permute-start.5 = (f32[2,32,1280]{2,1,0:T(8,128)S(1)}, f32[2,32,1280]{2,1,0:T(8,128)S(1)}, u32[]{:S(2)}, u32[]{:S(2)}) collective-permute-start(f32[2,32,1280]{2,1,0:T(8,128)S(1)} %get-tuple-element.36), channel_id=1, source_target_pairs={{0,2},{1,3},{2,0},{3,1},{4,6},{5,7},{6,4},{7,5},{8,10},{9,11},{10,... | collective-permute-start | bytes 983048 | tf_op jit(solution)/shard_map/ppermute | solution.py:541
  56.9 13.1 %correlate.5 = (f32[32,1280]{1,0:T(8,128)S(1)}, f32[32,1280]{1,0:T(8,128)S(1)}, f32[2,32,1280]{2,1,0:T(8,128)S(1)}, f32[8,128]{1,0:T(8,128)S(1)}) custom-call(s32[1]{0:T(128)} %bitcast.place_ref, f32[8,24,2304]{2,1,0:T(8,128)S(1)} %bitcast_convert_fusion.tmpl_ref, f32[40,32,128]{2,1,0:T(8,128)S(1)} %bitcast.74, f32[13,2,80,1024]{3,2,1,0:T(8,128)} %slab_x.1.spec_hbm, ...), custom_call_target="tpu_custom_call" | custom-call | flops 15000000512 | bytes 10000000 | tf_op jit(solution)/shard_map/correlate/pallas_call | solution.py:385
  70.6 13.3 %correlate.6 = (f32[32,1280]{1,0:T(8,128)S(1)}, f32[32,1280]{1,0:T(8,128)S(1)}, f32[2,32,1280]{2,1,0:T(8,128)S(1)}, f32[8,128]{1,0:T(8,128)S(1)}) custom-call(s32[1]{0:T(128)} %bitcast.place_ref, f32[8,24,2304]{2,1,0:T(8,128)S(1)} %bitcast_convert_fusion.tmpl_ref, f32[40,32,128]{2,1,0:T(8,128)S(1)} %bitcast.75, f32[13,2,80,1024]{3,2,1,0:T(8,128)} %slab_x.1.spec_hbm, ...), custom_call_target="tpu_custom_call" | custom-call | flops 15000000512 | bytes 10000000 | tf_op jit(solution)/shard_map/correlate/pallas_call | solution.py:385
  84.7 1.5 %collective-permute-start.8 = (f32[2,32,1280]{2,1,0:T(8,128)S(1)}, f32[2,32,1280]{2,1,0:T(8,128)S(1)}, u32[]{:S(2)}, u32[]{:S(2)}) collective-permute-start(f32[2,32,1280]{2,1,0:T(8,128)S(1)} %get-tuple-element.48), channel_id=1, source_target_pairs={{0,2},{1,3},{2,0},{3,1},{4,6},{5,7},{6,4},{7,5},{8,10},{9,11},{10,... | collective-permute-start | bytes 983048 | tf_op jit(solution)/shard_map/ppermute | solution.py:541
  86.2 13.0 %correlate.7 = (f32[32,1280]{1,0:T(8,128)S(1)}, f32[32,1280]{1,0:T(8,128)S(1)}, f32[2,32,1280]{2,1,0:T(8,128)S(1)}, f32[8,128]{1,0:T(8,128)S(1)}) custom-call(s32[1]{0:T(128)} %bitcast.place_ref, f32[8,24,2304]{2,1,0:T(8,128)S(1)} %bitcast_convert_fusion.tmpl_ref, f32[40,32,128]{2,1,0:T(8,128)S(1)} %bitcast.76, f32[13,2,80,1024]{3,2,1,0:T(8,128)} %slab_x.1.spec_hbm, ...), custom_call_target="tpu_custom_call" | custom-call | flops 15000000512 | bytes 10000000 | tf_op jit(solution)/shard_map/correlate/pallas_call | solution.py:385
  99.4 1.5 %collective-permute-start.15 = (f32[2,32,1280]{2,1,0:T(8,128)S(1)}, f32[2,32,1280]{2,1,0:T(8,128)S(1)}, u32[]{:S(2)}, u32[]{:S(2)}) collective-permute-start(f32[2,32,1280]{2,1,0:T(8,128)S(1)} %get-tuple-element.62), channel_id=1, source_target_pairs={{0,2},{1,3},{2,0},{3,1},{4,6},{5,7},{6,4},{7,5},{8,10},{9,11},{10,... | collective-permute-start | bytes 983048 | tf_op jit(solution)/shard_map/ppermute | solution.py:541
  100.9 0.6 collective-permute-start.10
  101.5 2.9 %collective-permute-done.10 = f32[3,4]{1,0:T(4,128)S(1)} collective-permute-done((f32[3,4]{1,0:T(4,128)S(1)}, f32[3,4]{1,0:T(4,128)S(1)}, u32[]{:S(2)}, u32[]{:S(2)}) %collective-permute-start.10) | collective-permute-done | bytes 80 | tf_op jit(solution)/shard_map/ppermute | solution.py:551
  104.5 1.5 %collective-permute-start.11 = (f32[3,4]{1,0:T(4,128)S(1)}, f32[3,4]{1,0:T(4,128)S(1)}, u32[]{:S(2)}, u32[]{:S(2)}) collective-permute-start(f32[3,4]{1,0:T(4,128)S(1)} %pad_maximum_fusion.8), channel_id=1, source_target_pairs={{0,8},{4,12},{8,0},{12,4},{16,24},{20,28},{24,16},{28,20},{1,9},{5... | collective-permute-start | bytes 152 | tf_op jit(solution)/shard_map/ppermute | solution.py:551
  106.0 2.1 %collective-permute-done.11 = f32[3,4]{1,0:T(4,128)S(1)} collective-permute-done((f32[3,4]{1,0:T(4,128)S(1)}, f32[3,4]{1,0:T(4,128)S(1)}, u32[]{:S(2)}, u32[]{:S(2)}) %collective-permute-start.11) | collective-permute-done | bytes 80 | tf_op jit(solution)/shard_map/ppermute | solution.py:551
  108.2 1.5 %collective-permute-start.12 = (f32[3,4]{1,0:T(4,128)S(1)}, f32[3,4]{1,0:T(4,128)S(1)}, u32[]{:S(2)}, u32[]{:S(2)}) collective-permute-start(f32[3,4]{1,0:T(4,128)S(1)} %pad_maximum_fusion.9), channel_id=1, source_target_pairs={{0,16},{4,20},{8,24},{12,28},{16,0},{20,4},{24,8},{28,12},{1,17},{... | collective-permute-start | bytes 152 | tf_op jit(solution)/shard_map/ppermute | solution.py:551
  109.7 3.0 %collective-permute-done.12 = f32[3,4]{1,0:T(4,128)S(1)} collective-permute-done((f32[3,4]{1,0:T(4,128)S(1)}, f32[3,4]{1,0:T(4,128)S(1)}, u32[]{:S(2)}, u32[]{:S(2)}) %collective-permute-start.12) | collective-permute-done | bytes 80 | tf_op jit(solution)/shard_map/ppermute | solution.py:551
  113.9 3.0 %collective-permute-done.13 = f32[1,4,6]{2,1,0:T(4,128)S(1)} collective-permute-done((f32[1,4,6]{2,1,0:T(4,128)S(1)}, f32[1,4,6]{2,1,0:T(4,128)S(1)}, u32[]{:S(2)}, u32[]{:S(2)}) %collective-permute-start.13) | collective-permute-done | bytes 128 | tf_op jit(solution)/shard_map/ppermute | solution.py:556
  118.1 1.2 collective-permute-done.16
  119.3 3.7 %combine.1 = (f32[32,1280]{1,0:T(8,128)}, f32[32,1280]{1,0:T(8,128)}, f32[4,32,1280]{2,1,0:T(8,128)}) custom-call(f32[16,6]{1,0:T(8,128)S(1)} %bitcast.81, f32[10,32,128]{2,1,0:T(8,128)S(1)} %dynamic-slice_bitcast_fusion.mask_ref, f32[32,1280]{1,0:T(8,128)S(1)} %get-tuple-element.53.refs_0_, f32[32,1280]{1,0:T(8,128)S(1)} %get-tuple-element.54.refs_1_, ...), custom_call_target="tpu_custom_call" | custom-call | tf_op jit(solution)/shard_map/combine/pallas_call | solution.py:449
  (91 shorter events, 6.1 us)
Async XLA Ops:
  0.6 20.1 %copy-start = (f32[4,4096]{1,0:T(4,128)S(1)}, f32[4,4096]{1,0:T(4,128)}, u32[]{:S(2)}) copy-start(f32[4,4096]{1,0:T(4,128)} %param.18) | copy-start | bytes 196612
  1.6 13.0 %copy-start.14 = (bf16[1,24,2304]{2,1,0:T(8,128)(2,1)}, bf16[1,24,2304]{2,1,0:T(8,128)(2,1)S(1)}, u32[]{:S(2)}) copy-start(bf16[1,24,2304]{2,1,0:T(8,128)(2,1)S(1)} %broadcast_in_dim_reshape.3) | copy-start | bytes 331780
  1.7 19.4 %collective-permute-start = (bf16[1,24,2304]{2,1,0:T(8,128)(2,1)S(1)}, bf16[1,24,2304]{2,1,0:T(8,128)(2,1)}, u32[]{:S(2)}, u32[]{:S(2)}) collective-permute-start(bf16[1,24,2304]{2,1,0:T(8,128)(2,1)S(1)} %broadcast_in_dim_reshape.3), channel_id=1, source_target_pairs={{0,16},{4,20},{8,24},{12,28},{16,0},{20,4},{24,8},{28,12},{1,17},{... | collective-permute-start | bytes 331784 | tf_op jit(solution)/shard_map/ppermute | solution.py:465
  7.7 18.1 %collective-permute-start.3 = (bf16[24,5120]{1,0:T(8,128)(2,1)}, bf16[24,5120]{1,0:T(8,128)(2,1)S(1)}, u32[]{:S(2)}, u32[]{:S(2)}) collective-permute-start(bf16[24,5120]{1,0:T(8,128)(2,1)} %get-tuple-element.88), channel_id=1, source_target_pairs={{0,4},{4,8},{8,12},{12,16},{16,20},{20,24},{24,28},{1,5},{5,9},{9,... | collective-permute-start | bytes 737288 | tf_op jit(solution)/shard_map/ppermute | solution.py:484
  11.1 14.7 %collective-permute-start.4 = (bf16[24,5120]{1,0:T(8,128)(2,1)}, bf16[24,5120]{1,0:T(8,128)(2,1)S(1)}, u32[]{:S(2)}, u32[]{:S(2)}) collective-permute-start(bf16[24,5120]{1,0:T(8,128)(2,1)} %get-tuple-element.87), channel_id=1, source_target_pairs={{4,0},{8,4},{12,8},{16,12},{20,16},{24,20},{28,24},{5,1},{9,5},{13... | collective-permute-start | bytes 737288 | tf_op jit(solution)/shard_map/ppermute | solution.py:485
  13.5 2.3 %copy-start.1 = (bf16[32,5120]{1,0:T(8,128)(2,1)S(1)}, bf16[32,5120]{1,0:T(8,128)(2,1)}, u32[]{:S(2)}) copy-start(bf16[32,5120]{1,0:T(8,128)(2,1)} %refs_0_.1) | copy-start | bytes 983044
  13.5 2.3 %copy-start.4 = (bf16[128,512]{1,0:T(8,128)(2,1)S(1)}, bf16[128,512]{1,0:T(8,128)(2,1)}, u32[]{:S(2)}) copy-start(bf16[128,512]{1,0:T(8,128)(2,1)} %constant.45.clone.refs_1_.refs_2_) | copy-start | bytes 393220
  13.5 2.3 %copy-start.7 = (bf16[112,240]{1,0:T(8,128)(2,1)S(1)}, bf16[112,240]{1,0:T(8,128)(2,1)}, u32[]{:S(2)}) copy-start(bf16[112,240]{1,0:T(8,128)(2,1)} %constant.46.clone.refs_2_.refs_3_) | copy-start | bytes 161284
  15.9 4.8 %copy-start.16 = (s32[4]{0:T(128)S(1)}, s32[4]{0:T(128)}, u32[]{:S(2)}) copy-start(s32[4]{0:T(128)} %param.19) | copy-start | bytes 52
  15.9 5.2 %copy-start.15 = (bf16[1,24,2304]{2,1,0:T(8,128)(2,1)S(1)}, bf16[1,24,2304]{2,1,0:T(8,128)(2,1)}, u32[]{:S(2)}) copy-start(bf16[1,24,2304]{2,1,0:T(8,128)(2,1)} %copy-done.14) | copy-start | bytes 331780
  19.4 1.3 %copy-start.12 = (f32[3584,128]{1,0:T(8,128)}, f32[3584,128]{1,0:T(8,128)S(1)}, u32[]{:S(2)}) copy-start(f32[3584,128]{1,0:T(8,128)S(1)} %slab_own.1.own_ref) | copy-start | bytes 5505028
  22.0 8.3 %collective-permute-start.1 = (bf16[2,24,2304]{2,1,0:T(8,128)(2,1)S(1)}, bf16[2,24,2304]{2,1,0:T(8,128)(2,1)S(1)}, u32[]{:S(2)}, u32[]{:S(2)}) collective-permute-start(bf16[2,24,2304]{2,1,0:T(8,128)(2,1)S(1)} %maximum_bitcast_fusion), channel_id=1, source_target_pairs={{0,8},{4,12},{8,0},{12,4},{16,24},{20,28},{24,16},{28,20},{1,9},{5... | collective-permute-start | bytes 663560 | tf_op jit(solution)/shard_map/ppermute | solution.py:465
  29.9 1.4 %copy-start.9 = (bf16[80,240]{1,0:T(8,128)(2,1)S(1)}, bf16[80,240]{1,0:T(8,128)(2,1)}, u32[]{:S(2)}) copy-start(bf16[80,240]{1,0:T(8,128)(2,1)} %constant.47.clone.x_ref) | copy-start | bytes 115204
  29.9 1.5 %copy-start.13 = (f32[3584,128]{1,0:T(8,128)S(1)}, f32[3584,128]{1,0:T(8,128)}, u32[]{:S(2)}) copy-start(f32[3584,128]{1,0:T(8,128)} %copy-done.12) | copy-start | bytes 5505028
  30.4 10.5 %collective-permute-start.2 = (bf16[4,24,2304]{2,1,0:T(8,128)(2,1)S(1)}, bf16[4,24,2304]{2,1,0:T(8,128)(2,1)S(1)}, u32[]{:S(2)}, u32[]{:S(2)}) collective-permute-start(bf16[4,24,2304]{2,1,0:T(8,128)(2,1)S(1)} %bitcast.82), channel_id=1, source_target_pairs={{0,4},{4,0},{8,12},{12,8},{16,20},{20,16},{24,28},{28,24},{1,5},{5... | collective-permute-start | bytes 1327112 | tf_op jit(solution)/shard_map/ppermute | solution.py:465
  41.0 1.2 copy-start.2
  41.0 1.2 copy-start.3
  41.0 1.2 copy-start.5
  41.1 1.2 copy-start.6
  41.1 1.2 copy-start.8
  55.4 15.3 %collective-permute-start.5 = (f32[2,32,1280]{2,1,0:T(8,128)S(1)}, f32[2,32,1280]{2,1,0:T(8,128)S(1)}, u32[]{:S(2)}, u32[]{:S(2)}) collective-permute-start(f32[2,32,1280]{2,1,0:T(8,128)S(1)} %get-tuple-element.36), channel_id=1, source_target_pairs={{0,2},{1,3},{2,0},{3,1},{4,6},{5,7},{6,4},{7,5},{8,10},{9,11},{10,... | collective-permute-start | bytes 983048 | tf_op jit(solution)/shard_map/ppermute | solution.py:541
  70.0 13.9 %collective-permute-start.6 = (f32[2,32,1280]{2,1,0:T(8,128)S(1)}, f32[2,32,1280]{2,1,0:T(8,128)S(1)}, u32[]{:S(2)}, u32[]{:S(2)}) collective-permute-start(f32[2,32,1280]{2,1,0:T(8,128)S(1)} %get-tuple-element.41), channel_id=1, source_target_pairs={{0,2},{1,3},{2,0},{3,1},{4,6},{5,7},{6,4},{7,5},{8,10},{9,11},{10,... | collective-permute-start | bytes 983048 | tf_op jit(solution)/shard_map/ppermute | solution.py:541
  84.0 15.4 %collective-permute-start.9 = (f32[2,32,1280]{2,1,0:T(8,128)S(1)}, f32[2,32,1280]{2,1,0:T(8,128)S(1)}, u32[]{:S(2)}, u32[]{:S(2)}) collective-permute-start(f32[2,32,1280]{2,1,0:T(8,128)S(1)} %pad_maximum_fusion.4), channel_id=1, source_target_pairs={{0,1},{1,0},{2,3},{3,2},{4,5},{5,4},{6,7},{7,6},{8,9},{9,8},{10,11... | collective-permute-start | bytes 983048 | tf_op jit(solution)/shard_map/ppermute | solution.py:543
  84.1 2.1 %collective-permute-start.7 = (f32[2,32,1280]{2,1,0:T(8,128)S(1)}, f32[2,32,1280]{2,1,0:T(8,128)S(1)}, u32[]{:S(2)}, u32[]{:S(2)}) collective-permute-start(f32[2,32,1280]{2,1,0:T(8,128)S(1)} %pad_maximum_fusion.3), channel_id=1, source_target_pairs={{0,1},{1,0},{2,3},{3,2},{4,5},{5,4},{6,7},{7,6},{8,9},{9,8},{10,11... | collective-permute-start | bytes 983048 | tf_op jit(solution)/shard_map/ppermute | solution.py:543
  84.7 14.6 %collective-permute-start.8 = (f32[2,32,1280]{2,1,0:T(8,128)S(1)}, f32[2,32,1280]{2,1,0:T(8,128)S(1)}, u32[]{:S(2)}, u32[]{:S(2)}) collective-permute-start(f32[2,32,1280]{2,1,0:T(8,128)S(1)} %get-tuple-element.48), channel_id=1, source_target_pairs={{0,2},{1,3},{2,0},{3,1},{4,6},{5,7},{6,4},{7,5},{8,10},{9,11},{10,... | collective-permute-start | bytes 983048 | tf_op jit(solution)/shard_map/ppermute | solution.py:541
  99.4 17.5 %collective-permute-start.15 = (f32[2,32,1280]{2,1,0:T(8,128)S(1)}, f32[2,32,1280]{2,1,0:T(8,128)S(1)}, u32[]{:S(2)}, u32[]{:S(2)}) collective-permute-start(f32[2,32,1280]{2,1,0:T(8,128)S(1)} %get-tuple-element.62), channel_id=1, source_target_pairs={{0,2},{1,3},{2,0},{3,1},{4,6},{5,7},{6,4},{7,5},{8,10},{9,11},{10,... | collective-permute-start | bytes 983048 | tf_op jit(solution)/shard_map/ppermute | solution.py:541
  100.9 3.6 %collective-permute-start.10 = (f32[3,4]{1,0:T(4,128)S(1)}, f32[3,4]{1,0:T(4,128)S(1)}, u32[]{:S(2)}, u32[]{:S(2)}) collective-permute-start(f32[3,4]{1,0:T(4,128)S(1)} %pad_maximum_fusion.7), channel_id=1, source_target_pairs={{0,4},{4,0},{8,12},{12,8},{16,20},{20,16},{24,28},{28,24},{1,5},{5... | collective-permute-start | bytes 152 | tf_op jit(solution)/shard_map/ppermute | solution.py:551
  104.5 3.7 %collective-permute-start.11 = (f32[3,4]{1,0:T(4,128)S(1)}, f32[3,4]{1,0:T(4,128)S(1)}, u32[]{:S(2)}, u32[]{:S(2)}) collective-permute-start(f32[3,4]{1,0:T(4,128)S(1)} %pad_maximum_fusion.8), channel_id=1, source_target_pairs={{0,8},{4,12},{8,0},{12,4},{16,24},{20,28},{24,16},{28,20},{1,9},{5... | collective-permute-start | bytes 152 | tf_op jit(solution)/shard_map/ppermute | solution.py:551
  108.2 4.5 %collective-permute-start.12 = (f32[3,4]{1,0:T(4,128)S(1)}, f32[3,4]{1,0:T(4,128)S(1)}, u32[]{:S(2)}, u32[]{:S(2)}) collective-permute-start(f32[3,4]{1,0:T(4,128)S(1)} %pad_maximum_fusion.9), channel_id=1, source_target_pairs={{0,16},{4,20},{8,24},{12,28},{16,0},{20,4},{24,8},{28,12},{1,17},{... | collective-permute-start | bytes 152 | tf_op jit(solution)/shard_map/ppermute | solution.py:551
  113.3 3.6 %collective-permute-start.13 = (f32[1,4,6]{2,1,0:T(4,128)S(1)}, f32[1,4,6]{2,1,0:T(4,128)S(1)}, u32[]{:S(2)}, u32[]{:S(2)}) collective-permute-start(f32[1,4,6]{2,1,0:T(4,128)S(1)} %maximum_bitcast_fusion.1), channel_id=1, source_target_pairs={{0,2},{1,3},{2,0},{3,1},{4,6},{5,7},{6,4},{7,5},{8,10},{9,11},{10,... | collective-permute-start | bytes 296 | tf_op jit(solution)/shard_map/ppermute | solution.py:556
  116.9 1.2 collective-permute-start.14
  117.0 2.3 %collective-permute-start.16 = (f32[4,32,1280]{2,1,0:T(8,128)S(1)}, f32[4,32,1280]{2,1,0:T(8,128)S(1)}, u32[]{:S(2)}, u32[]{:S(2)}) collective-permute-start(f32[4,32,1280]{2,1,0:T(8,128)S(1)} %pad_maximum_fusion.1), channel_id=1, source_target_pairs={{0,1},{1,0},{2,3},{3,2},{4,5},{5,4},{6,7},{7,6},{8,9},{9,8},{10,11... | collective-permute-start | bytes 1966088 | tf_op jit(solution)/shard_map/ppermute | solution.py:561
  (2 other events, 2.4 us)

commit v3 on v2

--- a/solution.py
+++ b/solution.py
@@ -15,7 +15,6 @@
 EPSILON = 1e-06
 LANES = 128
 SPLIT = 64
-VMEM_LIMIT = 48 * 1024 * 1024
 F32 = jnp.float32
 BF16 = jnp.bfloat16
 
@@ -153,21 +152,57 @@
 GROUP = 8
 
 
-def slab_rows_kernel(dims, *refs):
-    slab_refs, (z_ref, y_ref, rows_ref, depth_buf) = refs[:-4], refs[-4:]
+def pipeline(steps, stages, width):
+    blocks = -(-steps // width)
+    depth = len(stages)
+
+    def turn(t, static):
+        for s in reversed(range(depth)):
+            if static and not 0 <= t - s < blocks:
+                continue
+            for slot in range(width):
+                step = (t - s) * width + slot
+                if not static or step < steps:
+                    stages[s](step, slot)
+
+    full = steps // width
+    first, last = depth - 1, max(full, depth - 1)
+    for t in range(first):
+        turn(t, True)
+    if last - first >= 2:
+        loop(last - first, lambda i: turn(i + first, False))
+    else:
+        last = first
+    for t in range(last, blocks + depth - 1):
+        turn(t, True)
+
+
+def slab_rows_kernel(dims, row_slices, *refs):
+    parts = len(row_slices)
+    slab_refs, refs = refs[:parts], refs[parts:]
+    if parts == 1:
+        valid_ref, z_ref, y_ref, rows_ref, mask_ref, depth_buf, parts_buf = refs
+    else:
+        z_ref, y_ref, rows_ref, depth_buf, parts_buf = refs
     x_cells, y_cells, z_cells = dims
-    count = sum(ref.shape[0] for ref in slab_refs)
+    count = sum(stop - start for start, stop in row_slices)
     n_y = y_cells + HALF
     pad_y = n_y // 2 + -(n_y // 2) % 8
     many = 4
 
+    if parts == 1:
+        valid = valid_ref[...].astype(F32)
+        low_lane = lax.broadcasted_iota(jnp.int32, (x_cells, LANES), 1) < z_cells
+        for q in range(y_cells // 2):
+            mask_ref[q] = jnp.where(low_lane, valid[:, 2 * q : 2 * q + 1], valid[:, 2 * q + 1 : 2 * q + 2])
+
     def depth_step(i):
         top = 0
-        for ref in slab_refs:
-            size = ref.shape[0]
+        for ref, (start, stop) in zip(slab_refs, row_slices):
+            size = stop - start
             lanes = [pl.ds(pl.multiple_of((many * i + u) * LANES, LANES), LANES) for u in range(many)]
-            block = jnp.concatenate([ref[:, l].astype(F32) for l in lanes], axis=0).astype(BF16)
-            out = jnp.dot(block, z_ref[...], preferred_element_type=F32)
+            block = jnp.concatenate([ref[:, l].astype(F32)[start:stop] for l in lanes], axis=0)
+            out = jnp.dot(block.astype(BF16), z_ref[...], preferred_element_type=F32)
             for u in range(many):
                 part = out[u * size : (u + 1) * size]
                 for j in range(2):
@@ -179,41 +214,55 @@
 
     loop(y_cells // (2 * many), depth_step)
 
-    def y_step(i):
+    def gather_rows(i, slot):
         value = pick(depth_buf, [GROUP * i + u for u in range(GROUP)], y_cells, count)
-        plus, minus = pair_rows(y_ref[...], value, True)
+        parts_buf[slot] = split_rows(value, True)
+
+    def y_step(i, slot):
+        plus, minus = pair_dot(y_ref[...], parts_buf[slot], True)
         for u in range(GROUP):
             start = (GROUP * i + u) * 2 * pad_y
             store(rows_ref, start, lane_block(plus, u))
             store(rows_ref, start + pad_y, lane_block(minus, u))
 
-    loop(count // GROUP, y_step)
-
-
-def slab_rows(blocks, dims, tables, name):
+    pipeline(count // GROUP, [gather_rows, y_step], 2)
+
+
+def slab_rows(blocks, row_slices, valid, dims, tables, name):
     x_cells, y_cells, z_cells = dims
-    count = sum(block.shape[0] for block in blocks)
+    count = sum(stop - start for start, stop in row_slices)
     n_y = y_cells + HALF
     pad_y = n_y // 2 + -(n_y // 2) % 8
     vmem = pl.BlockSpec(memory_space=pltpu.VMEM)
+    out_shape = [jax.ShapeDtypeStruct((count * 2 * pad_y, LANES), F32)]
+    if valid is not None:
+        blocks = blocks + [valid]
+        out_shape.append(jax.ShapeDtypeStruct((y_cells // 2, x_cells, LANES), F32))
     return pl.pallas_call(
-        functools.partial(slab_rows_kernel, dims),
-        out_shape=jax.ShapeDtypeStruct((count * 2 * pad_y, LANES), F32),
+        functools.partial(slab_rows_kernel, dims, row_slices),
+        out_shape=tuple(out_shape),
         in_specs=[vmem] * (2 + len(blocks)),
-        out_specs=vmem,
-        scratch_shapes=[pltpu.VMEM((y_cells * count, LANES), F32)],
-        compiler_params=pltpu.CompilerParams(vmem_limit_bytes=VMEM_LIMIT),
+        out_specs=(vmem,) * len(out_shape),
+        scratch_shapes=[
+            pltpu.VMEM((y_cells * count, LANES), F32),
+            pltpu.VMEM((2, 3 * y_cells, GROUP * LANES), BF16),
+        ],
+        compiler_params=pltpu.CompilerParams(vmem_limit_bytes=20 * 1024 * 1024),
         cost_estimate=pl.CostEstimate(flops=count * 10**8, bytes_accessed=10**6, transcendentals=0),
         name=name,
     )(*blocks, tables["slab_z"], tables["slab_y"])
 
 
-def slab_x_kernel(dims, own_ref, halo_ref, x_ref, spec_ref):
+def slab_x_kernel(dims, own_ref, halo_ref, x_ref, out_hbm, spec_buf, parts_buf, sems):
     x_cells, y_cells, z_cells = dims
     n_y = y_cells + HALF
     pad_y = n_y // 2 + -(n_y // 2) % 8
-
-    def x_step(i):
+    steps = n_y // GROUP
+
+    def send(i):
+        return pltpu.make_async_copy(spec_buf.at[i], out_hbm.at[i], sems.at[i])
+
+    def gather_rows(i, slot):
         firsts = [GROUP // 2 * i + u // 2 + u % 2 * pad_y for u in range(GROUP)]
         value = jnp.concatenate(
             [
@@ -222,26 +271,38 @@
             ],
             axis=0,
         )
-        plus, minus = pair_rows(x_ref[...], value, True)
+        parts_buf[slot] = split_rows(value, True)
+
+    def x_step(i, slot):
+        plus, minus = pair_dot(x_ref[...], parts_buf[slot], True)
         spec = jnp.concatenate([plus, minus], axis=0)
         turned = swap(spec)
         real_lane = lane_sign(GROUP * LANES) < 0
-        spec_ref[i, 0] = jnp.where(real_lane, spec, turned)
-        spec_ref[i, 1] = jnp.where(real_lane, -turned, spec)
-
-    loop(n_y // GROUP, x_step)
+        spec_buf[i, 0] = jnp.where(real_lane, spec, turned)
+        spec_buf[i, 1] = jnp.where(real_lane, -turned, spec)
+        send(i).start()
+
+    pipeline(steps, [gather_rows, x_step], 2)
+    loop(steps, lambda i: send(i).wait())
 
 
 def slab_x(own, halo, dims, tables):
     x_cells, y_cells, z_cells = dims
     n_x, n_y = x_cells + TEMPL, y_cells + HALF
+    steps = n_y // GROUP
     vmem = pl.BlockSpec(memory_space=pltpu.VMEM)
+    shape = (steps, 2, n_x, GROUP * LANES)
     return pl.pallas_call(
         functools.partial(slab_x_kernel, dims),
-        out_shape=jax.ShapeDtypeStruct((n_y // GROUP, 2, n_x, GROUP * LANES), F32),
+        out_shape=jax.ShapeDtypeStruct(shape, F32),
         in_specs=[vmem] * 3,
-        out_specs=vmem,
-        compiler_params=pltpu.CompilerParams(vmem_limit_bytes=VMEM_LIMIT),
+        out_specs=pl.BlockSpec(memory_space=pl.ANY),
+        scratch_shapes=[
+            pltpu.VMEM(shape, F32),
+            pltpu.VMEM((2, 3 * n_x, GROUP * LANES), BF16),
+            pltpu.SemaphoreType.DMA((steps,)),
+        ],
+        compiler_params=pltpu.CompilerParams(vmem_limit_bytes=24 * 1024 * 1024),
         cost_estimate=pl.CostEstimate(flops=5 * 10**9, bytes_accessed=10**6, transcendentals=0),
         name="slab_x",
     )(own, halo, tables["slab_x"])
@@ -251,7 +312,7 @@
     dims, rot, place_ref, tmpl_ref, mask_ref, spec_hbm,
     z_ref, ones_ref, y_ref, x_ref, bx_ref, by_ref, bz_ref,
     mine_ref, side_ref, far_ref, stat_ref,
-    spec_ref, depth_buf, rows_buf, first_buf, second_buf, back_buf, vol_buf, sem,
+    spec_ref, depth_buf, rows_buf, first_buf, second_buf, third_buf, back_buf, vol_buf, sem,
 ):
     x_cells, y_cells, z_cells = dims
     n_x, n_y = x_cells + TEMPL, y_cells + HALF
@@ -278,66 +339,57 @@
     for j in range(8):
         window = block[:, : 2 * LANES] if j < 4 else block[:, LANES:]
         out = jnp.dot(window, z_ref[j], preferred_element_type=F32)
-        part = (out[:, :LANES] + out[:, LANES:] - shift) * scale
+        part = out[:, :LANES] + out[:, LANES:] - shift
         for g in range(TEMPL // 8):
             start = (8 * g + j) * TEMPL
             depth_buf[start : start + TEMPL, :] = part[g * TEMPL : (g + 1) * TEMPL]
 
-    def y_step(i):
-        for i in (2 * i, 2 * i + 1):
-            value = pick(depth_buf, [GROUP * i + u for u in range(GROUP)], TEMPL, TEMPL)
-            plus, minus = pair_rows(y_ref[...], value, True)
-            for u in range(GROUP):
-                start = (GROUP * i + u) * 2 * pad_y
-                store(rows_buf, start, lane_block(plus, u))
-                store(rows_buf, start + pad_y, lane_block(minus, u))
-
-    loop(TEMPL // GROUP // 2, y_step)
+    def gather_a(i, slot):
+        value = pick(depth_buf, [GROUP * i + u for u in range(GROUP)], TEMPL, TEMPL)
+        first_buf[slot] = split_rows(value, True)
+
+    def y_step(i, slot):
+        plus, minus = pair_dot(y_ref[...], first_buf[slot], True)
+        for u in range(GROUP):
+            start = (GROUP * i + u) * 2 * pad_y
+            store(rows_buf, start, lane_block(plus, u))
+            store(rows_buf, start + pad_y, lane_block(minus, u))
+
+    pipeline(TEMPL // GROUP, [gather_a, y_step], 2)
     copy.wait()
 
-    def gather_rows(i):
+    def gather_ky(i, slot):
         firsts = [GROUP // 2 * i + u // 2 + u % 2 * pad_y for u in range(GROUP)]
-        first_buf[...] = split_rows(pick(rows_buf, firsts, TEMPL, 2 * pad_y), True)
-
-    def multiply(i):
-        plus, minus = pair_dot(x_ref[...], first_buf[...], True)
+        first_buf[slot] = split_rows(pick(rows_buf, firsts, TEMPL, 2 * pad_y), True)
+
+    def multiply(i, slot):
+        plus, minus = pair_dot(x_ref[...], first_buf[slot], True)
         spec = jnp.concatenate([plus, minus], axis=0)
         prod = spec * spec_ref[i, 0] + swap(spec) * spec_ref[i, 1]
-        second_buf[...] = split_rows(prod, False)
-
-    def back_x(i):
-        plus, minus = pair_dot(bx_ref[...], second_buf[...], False)
+        second_buf[slot] = split_rows(prod, False)
+
+    def back_x(i, slot):
+        plus, minus = pair_dot(bx_ref[...], second_buf[slot], False)
         for u in range(GROUP):
             start = (GROUP * i + u) * x_cells
             store(back_buf, start, lane_block(plus, u))
             store(back_buf, start + x_cells // 2, lane_block(minus, u))
 
-    steps = n_y // GROUP
-    gather_rows(0)
-    multiply(0)
-    gather_rows(1)
-
-    def pipelined(i):
-        back_x(i)
-        multiply(i + 1)
-        gather_rows(i + 2)
-
-    loop(steps - 2, pipelined)
-    back_x(steps - 2)
-    multiply(steps - 1)
-    back_x(steps - 1)
-
-    def back_step(i):
-        for i in (2 * i, 2 * i + 1):
-            value = pick(back_buf, [GROUP * i + u for u in range(GROUP)], n_y, x_cells)
-            plus, minus = pair_rows(by_ref[...], value, False)
-            for u in range(GROUP):
-                row = GROUP * i + u
-                x = jnp.where(row < x_cells // 2, row + x_cells // 2, x_cells - 1 - row)
-                store(vol_buf, x * y_cells, lane_block(plus, u))
-                store(vol_buf, x * y_cells + y_cells // 2, lane_block(minus, u))
-
-    loop(x_cells // GROUP // 2, back_step)
+    pipeline(n_y // GROUP, [gather_ky, multiply, back_x], 2)
+
+    def gather_x(i, slot):
+        value = pick(back_buf, [GROUP * i + u for u in range(GROUP)], n_y, x_cells)
+        third_buf[slot] = split_rows(value, False)
+
+    def back_y(i, slot):
+        plus, minus = pair_dot(by_ref[...], third_buf[slot], False)
+        for u in range(GROUP):
+            row = GROUP * i + u
+            x = jnp.where(row < x_cells // 2, row + x_cells // 2, x_cells - 1 - row)
+            store(vol_buf, x * y_cells, lane_block(plus, u))
+            store(vol_buf, x * y_cells + y_cells // 2, lane_block(minus, u))
+
+    pipeline(x_cells // GROUP, [gather_x, back_y], 2)
 
     share = y_cells // 8
     me = place_ref[0]
@@ -358,7 +410,7 @@
         rows = value.shape[0]
         full = out[:rows, :LANES] + out[:rows, LANES:] + out[rows:, :LANES]
         for i in range(share):
-            corr = full[i * x_cells : (i + 1) * x_cells]
+            corr = full[i * x_cells : (i + 1) * x_cells] * scale
             target[:, i * LANES : (i + 1) * LANES] = corr
             mask = mask_ref[first + i]
             total = total + corr * mask
@@ -397,13 +449,14 @@
             pltpu.VMEM(spec.shape, F32),
             pltpu.VMEM((TEMPL * TEMPL, LANES), F32),
             pltpu.VMEM((TEMPL * 2 * pad_y, LANES), F32),
-            pltpu.VMEM((3 * TEMPL, GROUP * LANES), BF16),
-            pltpu.VMEM((2 * n_x, GROUP * LANES), BF16),
+            pltpu.VMEM((2, 3 * TEMPL, GROUP * LANES), BF16),
+            pltpu.VMEM((2, 2 * n_x, GROUP * LANES), BF16),
+            pltpu.VMEM((2, 2 * n_y, GROUP * LANES), BF16),
             pltpu.VMEM((n_y * x_cells, LANES), F32),
             pltpu.VMEM((x_cells * y_cells, LANES), F32),
             pltpu.SemaphoreType.DMA,
         ],
-        compiler_params=pltpu.CompilerParams(vmem_limit_bytes=VMEM_LIMIT),
+        compiler_params=pltpu.CompilerParams(vmem_limit_bytes=32 * 1024 * 1024),
         cost_estimate=pl.CostEstimate(flops=15 * 10**9, bytes_accessed=10**7, transcendentals=0),
         name="correlate",
     )(
@@ -413,15 +466,17 @@
     )
 
 
-def score_kernel(coef_ref, mask_ref, *refs):
+def score_kernel(place_ref, coef_ref, mask_ref, *refs):
     pieces = refs[: len(refs) - 3]
     best_ref, evid_ref, mom_ref = refs[len(refs) - 3 :]
+
+    blocks = best_ref.shape[1] // LANES
 
     def step(i):
         lanes = pl.ds(pl.multiple_of(i * LANES, LANES), LANES)
         for top in range(0, best_ref.shape[0], 8):
             rows = slice(top, top + 8)
-            mask = mask_ref[i, rows]
+            mask = mask_ref[place_ref[0] * blocks + i, rows]
             scores = []
             for k, piece in enumerate(pieces):
                 scores.append((piece[rows, lanes] - coef_ref[k, 0]) * coef_ref[k, 1])
@@ -439,21 +494,21 @@
             for c in range(4):
                 mom_ref[c, rows, lanes] = moment[c] * share
 
-    loop(best_ref.shape[1] // LANES, step)
-
-
-def combine(coefs, mask, pieces):
+    loop(blocks, step)
+
+
+def combine(place, coefs, mask, pieces):
     shape = pieces[0].shape
     vmem = pl.BlockSpec(memory_space=pltpu.VMEM)
     out = jax.ShapeDtypeStruct(shape, F32)
     return pl.pallas_call(
         score_kernel,
         out_shape=(out, out, jax.ShapeDtypeStruct((4,) + shape, F32)),
-        in_specs=[pl.BlockSpec(memory_space=pltpu.SMEM)] + [vmem] * (1 + len(pieces)),
+        in_specs=[pl.BlockSpec(memory_space=pltpu.SMEM)] * 2 + [vmem] * (1 + len(pieces)),
         out_specs=(vmem,) * 3,
-        compiler_params=pltpu.CompilerParams(vmem_limit_bytes=VMEM_LIMIT),
+        compiler_params=pltpu.CompilerParams(vmem_limit_bytes=16 * 1024 * 1024),
         name="combine",
-    )(coefs, mask, *pieces)
+    )(place, coefs, mask, *pieces)
 
 
 def gather_steps(count):
@@ -468,22 +523,27 @@
     return jnp.stack(pair, axis=1).reshape((-1,) + block.shape[1:])
 
 
-def merge(first, other):
-    mean_a = first[1] / jnp.maximum(first[0], 1.0)
-    mean_b = other[1] / jnp.maximum(other[0], 1.0)
-    number = first[0] + other[0]
-    gap = mean_b - mean_a
-    between = gap * gap * (first[0] * other[0] / jnp.maximum(number, 1.0))
-    return jnp.stack([number, first[1] + other[1], (first[2] + other[2]) + between])
-
-
-def halos(block, axis, width):
+def merge(parts):
+    number, total, square = parts[:, 0], parts[:, 1], parts[:, 2]
+    all_number = jnp.sum(number, axis=0)
+    all_total = jnp.sum(total, axis=0)
+    gap = total / jnp.maximum(number, 1.0) - all_total / jnp.maximum(all_number, 1.0)
+    return jnp.stack([all_number, all_total, jnp.sum(square + number * gap * gap, axis=0)])
+
+
+def exchange_all(block, axis, low, high):
+    count = lax.axis_size(axis)
+    parts = [block]
+    for step in range(low, high, low):
+        parts.append(lax.ppermute(block, axis, [(i, i ^ step) for i in range(count)]))
+    return jnp.stack(parts)
+
+
+def neighbours(block, axis):
     count = lax.axis_size(axis)
     forward = [(i, i + 1) for i in range(count - 1)]
     backward = [(target, source) for source, target in forward]
-    low = lax.ppermute(block[block.shape[0] - width :], axis, forward)
-    high = lax.ppermute(block[:width], axis, backward)
-    return low, high
+    return lax.ppermute(block, axis, forward), lax.ppermute(block, axis, backward)
 
 
 def local(tomogram, templates, valid, quats, rot_index):
@@ -497,25 +557,23 @@
     me = lax.axis_index("rot")
     rots = templates.shape[0]
 
-    low, high = halos(tomogram, "tile", HALF)
     row = TEMPL * TEMPL
     chunk = templates.shape[1]
     whole_rows = chunk % row == 0
     block = templates.reshape(rots * chunk // row, row) if whole_rows else templates
     block = block[None]
     steps = gather_steps(tiles)
-    for step in steps[:-1]:
+    block = gather_step(block, "tile", steps[0])
+    low, high = neighbours(tomogram, "tile")
+    for step in steps[1:-1]:
         block = gather_step(block, "tile", step)
     one_hot = (rot_index[:, None] == jnp.arange(quats.shape[1], dtype=jnp.int32)[None, :]).astype(F32)
     orient = jnp.einsum("rq,kq->rk", one_hot, quats, precision=lax.Precision.HIGHEST)
-    place = jnp.reshape(me, (1,)).astype(jnp.int32)
-    inside = jnp.repeat(valid.astype(F32), z_cells, axis=1)
-    mask = jnp.transpose(inside.reshape(x_cells, voxels // LANES, LANES), (1, 0, 2))
-    share_blocks = voxels // LANES // groups
-    mask_part = lax.dynamic_slice_in_dim(mask, me * share_blocks, share_blocks, 0)
-
-    own = slab_rows([tomogram], dims, tables, "slab_own")
-    halo = slab_rows([low, high], dims, tables, "slab_halo")
+    place = me_place = jnp.reshape(me, (1,)).astype(jnp.int32)
+    own, mask = slab_rows([tomogram], [(0, x_cells)], valid, dims, tables, "slab_own")
+    (halo,) = slab_rows(
+        [low, high], [(x_cells - HALF, x_cells), (0, HALF)], None, dims, tables, "slab_halo"
+    )
     spec = slab_x(own, halo, dims, tables)
     block = gather_step(block, "tile", steps[-1])
     if not whole_rows:
@@ -547,21 +605,18 @@
     )
     step = 1
     while step < tiles:
-        swap_pairs = [(i, i ^ step) for i in range(tiles)]
-        state = merge(state, lax.ppermute(state, "tile", swap_pairs))
-        step *= 2
+        following = min(step * 8, tiles)
+        state = merge(exchange_all(state, "tile", step, following))
+        step = following
     average = state[1] / state[0]
     inverse = 1.0 / jnp.sqrt(state[2] / state[0] + EPSILON)
-    coefs = jnp.concatenate([average[:, None], inverse[:, None], orient], axis=1)[None]
-    from_far = lax.ppermute(coefs, "rot", far_swap)
-    coefs = jnp.concatenate([coefs, from_far], axis=0)
-    from_side = lax.ppermute(coefs, "rot", side_swap)
-    coefs = jnp.stack([coefs[0], from_side[0], coefs[1], from_side[1]])
+    coefs = jnp.concatenate([average[:, None], inverse[:, None], orient], axis=1)
+    coefs = exchange_all(coefs, "rot", 1, groups)
     last = [part for r in range(rots - 2, rots) for part in (sides[r], fars[r][1])]
     last = lax.ppermute(jnp.stack(last), "rot", side_swap)
     from_sides += [last[:2], last[2:]]
     flat = mines + [f[0] for f in from_sides] + [f[0] for f in fars] + [f[1] for f in from_sides]
-    return combine(coefs.reshape(groups * rots, 6), mask_part, flat)
+    return combine(me_place, coefs.reshape(groups * rots, 6), mask, flat)
 
 
 def solution(mesh):

time: 124 us -> 119 us (0.960)
  Pallas kernels: 72.9 us -> 60.5 us
  starting transfers between devices: 23.9 us -> 30.3 us
  local copies, waits for them, and re-layouts: 8.71 us -> 10.7 us
    pallas_call x4, Pallas kernels: 52.5 us -> 40.7 us  [correlate(): pl.pallas_call(functools.partial(corr_kernel, dims, rot), out_shape=(jax....]
    ppermute x7 -> x12, starting transfers between devices: 8.95 us -> 19.7 us  [the longest x10 13.4 us: exchange_all(): lax.ppermute(block, axis, [(i, i ^ step) for i in range(count)])]
    ppermute x7 -> x12, waiting for transfers between devices: 11.5 us -> 4.24 us  [the longest x10 4.24 us: exchange_all(): lax.ppermute(block, axis, [(i, i ^ step) for i in range(count)])]
    ppermute x4, waiting for transfers between devices: 0.01 us -> 4.6 us  [local(): fars.append(lax.ppermute(far, 'rot', far_swap))]
    ppermute x3, waiting for transfers between devices: 0.84 us -> 4.9 us  [gather_step(): other = lax.ppermute(block, axis, [(i, i ^ step) for i in range(count)])]
    unnamed x34 -> x40, local copies, waits for them, and re-layouts: 2.41 us -> 6.34 us
    ppermute x3, starting transfers between devices: 8.62 us -> 4.83 us  [gather_step(): other = lax.ppermute(block, axis, [(i, i ^ step) for i in range(count)])]
    slice x2 -> x0, local copies, waits for them, and re-layouts: 1.89 us -> none  [the longest x1 1.89 us: halos(): high = lax.ppermute(block[:width], axis, backward)]
  transfers between devices with their start and end apart: 17 -> 22, of which waited for: 8 -> 6; matrix products, arithmetic and copies ran while one was open for 6% -> 4% of each run, Pallas kernels for 46% -> 39%
where the time goes in v3:
time: 119 us
  Pallas kernels  60.5 us (51%)
  starting transfers between devices  30.3 us (25%)
  waiting for transfers between devices  13.8 us (12%)
  local copies, waits for them, and re-layouts  10.7 us (9%)
  other arithmetic  2.02 us (2%)
    pallas_call x4, Pallas kernels, correlate(): pl.pallas_call(functools.partial(corr_kernel, dims, rot), out_shape=(jax....  40.7 us
    ppermute x10, starting transfers between devices, exchange_all(): lax.ppermute(block, axis, [(i, i ^ step) for i in range(count)])  13.4 us
    pallas_call x1, Pallas kernels, slab_x(): pl.pallas_call(functools.partial(slab_x_kernel, dims), out_shape=jax.Shap...  9.23 us
    pallas_call x2, Pallas kernels, slab_rows(): pl.pallas_call(functools.partial(slab_rows_kernel, dims, row_slices), out...  7.04 us
    unnamed x40, local copies, waits for them, and re-layouts  6.34 us
    ppermute x4, starting transfers between devices, local(): fars.append(lax.ppermute(far, 'rot', far_swap))  5.16 us
    ppermute x1, starting transfers between devices, neighbours(): lax.ppermute(block, axis, forward)  5 us
    ppermute x3, waiting for transfers between devices, gather_step(): other = lax.ppermute(block, axis, [(i, i ^ step) for i in range(count)])  4.9 us
  transfers between devices with their start and end apart: 22, of which 6 were waited for; matrix products, arithmetic and copies ran while one was open for 4% of the time, Pallas kernels for 39%

profile of v3, /device:TPU:0, one launch (start us, length us, event | category | flops | bytes accessed | tf_op | source)
XLA Modules:
  0.0 118.7 jit_solution(8801883877409104258)
XLA Ops:
  0.6 5.0 %collective-permute-start.3 = (bf16[32,5120]{1,0:T(8,128)(2,1)}, bf16[32,5120]{1,0:T(8,128)(2,1)S(1)}, u32[]{:S(2)}, u32[]{:S(2)}) collective-permute-start(bf16[32,5120]{1,0:T(8,128)(2,1)} %refs_0_.1), channel_id=1, source_target_pairs={{0,4},{4,8},{8,12},{12,16},{16,20},{20,24},{24,28},{1,5},{5,9},{9,... | collective-permute-start | bytes 983048 | tf_op jit(solution)/shard_map/ppermute | solution.py:546
  5.6 1.3 %collective-permute-start.4 = (bf16[32,5120]{1,0:T(8,128)(2,1)}, bf16[32,5120]{1,0:T(8,128)(2,1)S(1)}, u32[]{:S(2)}, u32[]{:S(2)}) collective-permute-start(bf16[32,5120]{1,0:T(8,128)(2,1)} %refs_0_.1), channel_id=1, source_target_pairs={{4,0},{8,4},{12,8},{16,12},{20,16},{24,20},{28,24},{5,1},{9,5},{13... | collective-permute-start | bytes 983048 | tf_op jit(solution)/shard_map/ppermute | solution.py:546
  6.9 1.0 broadcast_in_dim_reshape.3
  7.9 4.7 %collective-permute-start = (bf16[1,24,2304]{2,1,0:T(8,128)(2,1)S(1)}, bf16[1,24,2304]{2,1,0:T(8,128)(2,1)S(1)}, u32[]{:S(2)}, u32[]{:S(2)}) collective-permute-start(bf16[1,24,2304]{2,1,0:T(8,128)(2,1)S(1)} %broadcast_in_dim_reshape.3), channel_id=1, source_target_pairs={{0,16},{4,20},{8,24},{12,28},{16,0},{20,4},{24,8},{28,12},{1,17},{... | collective-permute-start | bytes 331784 | tf_op jit(solution)/shard_map/ppermute | solution.py:520
  12.6 1.0 copy-done.1
  14.3 0.9 copy-done.5
  16.0 3.4 %slab_own.1 = (f32[3584,128]{1,0:T(8,128)S(1)}, f32[40,32,128]{2,1,0:T(8,128)S(1)}) custom-call(bf16[32,5120]{1,0:T(8,128)(2,1)S(1)} %copy-done.1, s32[32,80]{1,0:T(8,128)S(1)} %copy-done.2, bf16[128,512]{1,0:T(8,128)(2,1)S(1)} %copy-done.5, bf16[112,240]{1,0:T(8,128)(2,1)S(1)} %copy-done.9), custom_call_target="tpu_custom_call" | custom-call | flops 3200000000 | bytes 1000000 | tf_op jit(solution)/shard_map/slab_own/pallas_call | solution.py:241
  19.5 1.3 %copy-done.15 = f32[3584,128]{1,0:T(8,128)} copy-done((f32[3584,128]{1,0:T(8,128)}, f32[3584,128]{1,0:T(8,128)S(1)}, u32[]{:S(2)}) %copy-start.15) | copy-done | bytes 1835032
  21.0 2.7 %collective-permute-done = bf16[1,24,2304]{2,1,0:T(8,128)(2,1)S(1)} collective-permute-done((bf16[1,24,2304]{2,1,0:T(8,128)(2,1)S(1)}, bf16[1,24,2304]{2,1,0:T(8,128)(2,1)S(1)}, u32[]{:S(2)}, u32[]{:S(2)}) %collective-permute-start) | collective-permute-done | bytes 110624 | tf_op jit(solution)/shard_map/ppermute | solution.py:520
  23.9 3.6 %slab_halo.1.halo_ref = f32[5376,128]{1,0:T(8,128)S(1)} custom-call(bf16[32,5120]{1,0:T(8,128)(2,1)S(1)} %collective-permute-done.3.refs_0_, bf16[32,5120]{1,0:T(8,128)(2,1)S(1)} %collective-permute-done.4.refs_1_, bf16[128,512]{1,0:T(8,128)(2,1)S(1)} %copy-done.6, bf16[112,240]{1,0:T(8,128)(2,1)S(1)} %copy-done.10), custom_call_target="tpu_custom_call" | custom-call | flops 4800000000 | bytes 1000000 | tf_op jit(solution)/shard_map/slab_halo/pallas_call | solution.py:241
  27.5 2.2 %collective-permute-done.1 = bf16[2,24,2304]{2,1,0:T(8,128)(2,1)S(1)} collective-permute-done((bf16[2,24,2304]{2,1,0:T(8,128)(2,1)S(1)}, bf16[2,24,2304]{2,1,0:T(8,128)(2,1)S(1)}, u32[]{:S(2)}, u32[]{:S(2)}) %collective-permute-start.1) | collective-permute-done | bytes 221216 | tf_op jit(solution)/shard_map/ppermute | solution.py:520
  30.0 9.2 %slab_x.1.spec_hbm = f32[13,2,80,1024]{3,2,1,0:T(8,128)S(1)} custom-call(f32[3584,128]{1,0:T(8,128)S(1)} %copy-done.16, f32[5376,128]{1,0:T(8,128)S(1)} %slab_halo.1.halo_ref, bf16[80,240]{1,0:T(8,128)(2,1)S(1)} %copy-done.12), custom_call_target="tpu_custom_call" | custom-call | flops 5000000000 | bytes 1000000 | tf_op jit(solution)/shard_map/slab_x/pallas_call | solution.py:295
  40.6 10.1 %correlate.4 = (f32[32,1280]{1,0:T(8,128)S(1)}, f32[32,1280]{1,0:T(8,128)S(1)}, f32[2,32,1280]{2,1,0:T(8,128)S(1)}, f32[8,128]{1,0:T(8,128)S(1)}) custom-call(s32[1]{0:T(128)} %bitcast.place_ref, f32[8,24,2304]{2,1,0:T(8,128)S(1)} %bitcast_convert_fusion.tmpl_ref, f32[40,32,128]{2,1,0:T(8,128)S(1)} %get-tuple-element.36.mask_ref, ...), custom_call_target="tpu_custom_call" | custom-call | flops 15000000512 | bytes 10000000 | tf_op jit(solution)/shard_map/correlate/pallas_call | solution.py:437
  50.7 1.6 %collective-permute-start.5 = (f32[2,32,1280]{2,1,0:T(8,128)S(1)}, f32[2,32,1280]{2,1,0:T(8,128)S(1)}, u32[]{:S(2)}, u32[]{:S(2)}) collective-permute-start(f32[2,32,1280]{2,1,0:T(8,128)S(1)} %get-tuple-element.40), channel_id=1, source_target_pairs={{0,2},{1,3},{2,0},{3,1},{4,6},{5,7},{6,4},{7,5},{8,10},{9,11},{10,... | collective-permute-start | bytes 983048 | tf_op jit(solution)/shard_map/ppermute | solution.py:599
  52.3 10.2 %correlate.5 = (f32[32,1280]{1,0:T(8,128)S(1)}, f32[32,1280]{1,0:T(8,128)S(1)}, f32[2,32,1280]{2,1,0:T(8,128)S(1)}, f32[8,128]{1,0:T(8,128)S(1)}) custom-call(s32[1]{0:T(128)} %bitcast.place_ref, f32[8,24,2304]{2,1,0:T(8,128)S(1)} %bitcast_convert_fusion.tmpl_ref, f32[40,32,128]{2,1,0:T(8,128)S(1)} %get-tuple-element.36.mask_ref, ...), custom_call_target="tpu_custom_call" | custom-call | flops 15000000512 | bytes 10000000 | tf_op jit(solution)/shard_map/correlate/pallas_call | solution.py:437
  63.1 10.1 %correlate.6 = (f32[32,1280]{1,0:T(8,128)S(1)}, f32[32,1280]{1,0:T(8,128)S(1)}, f32[2,32,1280]{2,1,0:T(8,128)S(1)}, f32[8,128]{1,0:T(8,128)S(1)}) custom-call(s32[1]{0:T(128)} %bitcast.place_ref, f32[8,24,2304]{2,1,0:T(8,128)S(1)} %bitcast_convert_fusion.tmpl_ref, f32[40,32,128]{2,1,0:T(8,128)S(1)} %get-tuple-element.36.mask_ref, ...), custom_call_target="tpu_custom_call" | custom-call | flops 15000000512 | bytes 10000000 | tf_op jit(solution)/shard_map/correlate/pallas_call | solution.py:437
  74.6 1.5 %collective-permute-start.8 = (f32[2,32,1280]{2,1,0:T(8,128)S(1)}, f32[2,32,1280]{2,1,0:T(8,128)S(1)}, u32[]{:S(2)}, u32[]{:S(2)}) collective-permute-start(f32[2,32,1280]{2,1,0:T(8,128)S(1)} %get-tuple-element.52), channel_id=1, source_target_pairs={{0,2},{1,3},{2,0},{3,1},{4,6},{5,7},{6,4},{7,5},{8,10},{9,11},{10,... | collective-permute-start | bytes 983048 | tf_op jit(solution)/shard_map/ppermute | solution.py:599
  76.2 10.3 %correlate.7 = (f32[32,1280]{1,0:T(8,128)S(1)}, f32[32,1280]{1,0:T(8,128)S(1)}, f32[2,32,1280]{2,1,0:T(8,128)S(1)}, f32[8,128]{1,0:T(8,128)S(1)}) custom-call(s32[1]{0:T(128)} %bitcast.place_ref, f32[8,24,2304]{2,1,0:T(8,128)S(1)} %bitcast_convert_fusion.tmpl_ref, f32[40,32,128]{2,1,0:T(8,128)S(1)} %get-tuple-element.36.mask_ref, ...), custom_call_target="tpu_custom_call" | custom-call | flops 15000000512 | bytes 10000000 | tf_op jit(solution)/shard_map/correlate/pallas_call | solution.py:437
  86.6 2.0 %collective-permute-start.10 = (f32[3,4]{1,0:T(4,128)S(1)}, f32[3,4]{1,0:T(4,128)S(1)}, u32[]{:S(2)}, u32[]{:S(2)}) collective-permute-start(f32[3,4]{1,0:T(4,128)S(1)} %pad_maximum_fusion.6), channel_id=1, source_target_pairs={{0,4},{4,0},{8,12},{12,8},{16,20},{20,16},{24,28},{28,24},{1,5},{5... | collective-permute-start | bytes 152 | tf_op jit(solution)/shard_map/ppermute | solution.py:538
  88.6 1.5 %collective-permute-start.12 = (f32[3,4]{1,0:T(4,128)S(1)}, f32[3,4]{1,0:T(4,128)S(1)}, u32[]{:S(2)}, u32[]{:S(2)}) collective-permute-start(f32[3,4]{1,0:T(4,128)S(1)} %pad_maximum_fusion.6), channel_id=1, source_target_pairs={{0,12},{4,8},{8,4},{12,0},{16,28},{20,24},{24,20},{28,16},{1,13},{... | collective-permute-start | bytes 152 | tf_op jit(solution)/shard_map/ppermute | solution.py:538
  90.2 1.0 collective-permute-start.13
  91.1 3.3 %collective-permute-start.14 = (f32[3,4]{1,0:T(4,128)S(1)}, f32[3,4]{1,0:T(4,128)S(1)}, u32[]{:S(2)}, u32[]{:S(2)}) collective-permute-start(f32[3,4]{1,0:T(4,128)S(1)} %pad_maximum_fusion.6), channel_id=1, source_target_pairs={{0,20},{4,16},{8,28},{12,24},{16,4},{20,0},{24,12},{28,8},{1,21},{... | collective-permute-start | bytes 152 | tf_op jit(solution)/shard_map/ppermute | solution.py:538
  94.6 1.1 slice_bitcast_fusion.6
  96.2 3.1 %collective-permute-start.16 = (f32[3,4]{1,0:T(4,128)S(1)}, f32[3,4]{1,0:T(4,128)S(1)}, u32[]{:S(2)}, u32[]{:S(2)}) collective-permute-start(f32[3,4]{1,0:T(4,128)S(1)} %pad_maximum_fusion.6), channel_id=1, source_target_pairs={{0,28},{4,24},{8,20},{12,16},{16,12},{20,8},{24,4},{28,0},{1,29},{... | collective-permute-start | bytes 152 | tf_op jit(solution)/shard_map/ppermute | solution.py:538
  99.4 1.5 %collective-permute-start.20 = (f32[2,32,1280]{2,1,0:T(8,128)S(1)}, f32[2,32,1280]{2,1,0:T(8,128)}, u32[]{:S(2)}, u32[]{:S(2)}) collective-permute-start(f32[2,32,1280]{2,1,0:T(8,128)S(1)} %get-tuple-element.66), channel_id=1, source_target_pairs={{0,2},{1,3},{2,0},{3,1},{4,6},{5,7},{6,4},{7,5},{8,10},{9,11},{10,... | collective-permute-start | bytes 983048 | tf_op jit(solution)/shard_map/ppermute | solution.py:599
  101.3 1.2 %collective-permute-done.16 = f32[3,4]{1,0:T(4,128)S(1)} collective-permute-done((f32[3,4]{1,0:T(4,128)S(1)}, f32[3,4]{1,0:T(4,128)S(1)}, u32[]{:S(2)}, u32[]{:S(2)}) %collective-permute-start.16) | collective-permute-done | bytes 80 | tf_op jit(solution)/shard_map/ppermute | solution.py:538
  102.9 4.6 %collective-permute-done.20 = f32[2,32,1280]{2,1,0:T(8,128)} collective-permute-done((f32[2,32,1280]{2,1,0:T(8,128)S(1)}, f32[2,32,1280]{2,1,0:T(8,128)}, u32[]{:S(2)}, u32[]{:S(2)}) %collective-permute-start.20) | collective-permute-done | bytes 327712 | tf_op jit(solution)/shard_map/ppermute | solution.py:599
  107.5 1.0 slice_bitcast_fusion.2
  110.4 1.5 %collective-permute-start.18 = (f32[4,6]{1,0:T(4,128)S(1)}, f32[4,6]{1,0:T(4,128)S(1)}, u32[]{:S(2)}, u32[]{:S(2)}) collective-permute-start(f32[4,6]{1,0:T(4,128)S(1)} %pad_maximum_fusion.7), channel_id=1, source_target_pairs={{0,2},{1,3},{2,0},{3,1},{4,6},{5,7},{6,4},{7,5},{8,10},{9,11},{10,... | collective-permute-start | bytes 296 | tf_op jit(solution)/shard_map/ppermute | solution.py:538
  112.1 1.9 %collective-permute-done.18 = f32[4,6]{1,0:T(4,128)S(1)} collective-permute-done((f32[4,6]{1,0:T(4,128)S(1)}, f32[4,6]{1,0:T(4,128)S(1)}, u32[]{:S(2)}, u32[]{:S(2)}) %collective-permute-start.18) | collective-permute-done | bytes 128 | tf_op jit(solution)/shard_map/ppermute | solution.py:538
  114.0 1.1 collective-permute-done.19
  115.1 3.6 %combine.1 = (f32[32,1280]{1,0:T(8,128)}, f32[32,1280]{1,0:T(8,128)}, f32[4,32,1280]{2,1,0:T(8,128)}) custom-call(s32[1]{0:T(128)} %bitcast.place_ref, f32[16,6]{1,0:T(8,128)S(1)} %bitcast.93, f32[40,32,128]{2,1,0:T(8,128)S(1)} %get-tuple-element.36.mask_ref, f32[32,1280]{1,0:T(8,128)S(1)} %get-tuple-element.57.refs_0_, ...), custom_call_target="tpu_custom_call" | custom-call | tf_op jit(solution)/shard_map/combine/pallas_call | solution.py:504
  (104 shorter events, 9.1 us)
Async XLA Ops:
  0.6 20.1 %copy-start = (f32[4,4096]{1,0:T(4,128)S(1)}, f32[4,4096]{1,0:T(4,128)}, u32[]{:S(2)}) copy-start(f32[4,4096]{1,0:T(4,128)} %param.18) | copy-start | bytes 196612
  0.6 23.2 %collective-permute-start.3 = (bf16[32,5120]{1,0:T(8,128)(2,1)}, bf16[32,5120]{1,0:T(8,128)(2,1)S(1)}, u32[]{:S(2)}, u32[]{:S(2)}) collective-permute-start(bf16[32,5120]{1,0:T(8,128)(2,1)} %refs_0_.1), channel_id=1, source_target_pairs={{0,4},{4,8},{8,12},{12,16},{16,20},{20,24},{24,28},{1,5},{5,9},{9,... | collective-permute-start | bytes 983048 | tf_op jit(solution)/shard_map/ppermute | solution.py:546
  5.6 18.2 %collective-permute-start.4 = (bf16[32,5120]{1,0:T(8,128)(2,1)}, bf16[32,5120]{1,0:T(8,128)(2,1)S(1)}, u32[]{:S(2)}, u32[]{:S(2)}) collective-permute-start(bf16[32,5120]{1,0:T(8,128)(2,1)} %refs_0_.1), channel_id=1, source_target_pairs={{4,0},{8,4},{12,8},{16,12},{20,16},{24,20},{28,24},{5,1},{9,5},{13... | collective-permute-start | bytes 983048 | tf_op jit(solution)/shard_map/ppermute | solution.py:546
  7.9 15.8 %collective-permute-start = (bf16[1,24,2304]{2,1,0:T(8,128)(2,1)S(1)}, bf16[1,24,2304]{2,1,0:T(8,128)(2,1)S(1)}, u32[]{:S(2)}, u32[]{:S(2)}) collective-permute-start(bf16[1,24,2304]{2,1,0:T(8,128)(2,1)S(1)} %broadcast_in_dim_reshape.3), channel_id=1, source_target_pairs={{0,16},{4,20},{8,24},{12,28},{16,0},{20,4},{24,8},{28,12},{1,17},{... | collective-permute-start | bytes 331784 | tf_op jit(solution)/shard_map/ppermute | solution.py:520
  16.0 4.7 %copy-start.19 = (s32[4]{0:T(128)S(1)}, s32[4]{0:T(128)}, u32[]{:S(2)}) copy-start(s32[4]{0:T(128)} %param.19) | copy-start | bytes 52
  16.0 7.8 %copy-start.6 = (bf16[128,512]{1,0:T(8,128)(2,1)S(1)}, bf16[128,512]{1,0:T(8,128)(2,1)}, u32[]{:S(2)}) copy-start(bf16[128,512]{1,0:T(8,128)(2,1)} %constant.44.clone.refs_2_) | copy-start | bytes 393220
  16.0 7.8 %copy-start.10 = (bf16[112,240]{1,0:T(8,128)(2,1)S(1)}, bf16[112,240]{1,0:T(8,128)(2,1)}, u32[]{:S(2)}) copy-start(bf16[112,240]{1,0:T(8,128)(2,1)} %constant.45.clone.refs_3_) | copy-start | bytes 161284
  19.4 1.3 %copy-start.15 = (f32[3584,128]{1,0:T(8,128)}, f32[3584,128]{1,0:T(8,128)S(1)}, u32[]{:S(2)}) copy-start(f32[3584,128]{1,0:T(8,128)S(1)} %get-tuple-element.37.own_ref) | copy-start | bytes 5505028
  23.8 6.0 %collective-permute-start.1 = (bf16[2,24,2304]{2,1,0:T(8,128)(2,1)S(1)}, bf16[2,24,2304]{2,1,0:T(8,128)(2,1)S(1)}, u32[]{:S(2)}, u32[]{:S(2)}) collective-permute-start(bf16[2,24,2304]{2,1,0:T(8,128)(2,1)S(1)} %maximum_bitcast_fusion), channel_id=1, source_target_pairs={{0,8},{4,12},{8,0},{12,4},{16,24},{20,28},{24,16},{28,20},{1,9},{5... | collective-permute-start | bytes 663560 | tf_op jit(solution)/shard_map/ppermute | solution.py:520
  27.5 2.4 %copy-start.12 = (bf16[80,240]{1,0:T(8,128)(2,1)S(1)}, bf16[80,240]{1,0:T(8,128)(2,1)}, u32[]{:S(2)}) copy-start(bf16[80,240]{1,0:T(8,128)(2,1)} %constant.46.clone.x_ref) | copy-start | bytes 115204
  27.5 2.4 %copy-start.16 = (f32[3584,128]{1,0:T(8,128)S(1)}, f32[3584,128]{1,0:T(8,128)}, u32[]{:S(2)}) copy-start(f32[3584,128]{1,0:T(8,128)} %copy-done.15) | copy-start | bytes 5505028
  29.9 9.3 %collective-permute-start.2 = (bf16[4,24,2304]{2,1,0:T(8,128)(2,1)S(1)}, bf16[4,24,2304]{2,1,0:T(8,128)(2,1)S(1)}, u32[]{:S(2)}, u32[]{:S(2)}) collective-permute-start(bf16[4,24,2304]{2,1,0:T(8,128)(2,1)S(1)} %bitcast.94), channel_id=1, source_target_pairs={{0,4},{4,0},{8,12},{12,8},{16,20},{20,16},{24,28},{28,24},{1,5},{5... | collective-permute-start | bytes 1327112 | tf_op jit(solution)/shard_map/ppermute | solution.py:520
  39.3 1.2 %copy-start.3 = (bf16[8,256,256]{2,1,0:T(8,128)(2,1)S(1)}, bf16[8,256,256]{2,1,0:T(8,128)(2,1)}, u32[]{:S(2)}) copy-start(bf16[8,256,256]{2,1,0:T(8,128)(2,1)} %constant.47.clone.z_ref) | copy-start | bytes 3145732
  39.4 1.2 %copy-start.7 = (bf16[160,208]{1,0:T(8,128)(2,1)S(1)}, bf16[160,208]{1,0:T(8,128)(2,1)}, u32[]{:S(2)}) copy-start(bf16[160,208]{1,0:T(8,128)(2,1)} %constant.52.clone.by_ref) | copy-start | bytes 199684
  50.7 12.4 %collective-permute-start.5 = (f32[2,32,1280]{2,1,0:T(8,128)S(1)}, f32[2,32,1280]{2,1,0:T(8,128)S(1)}, u32[]{:S(2)}, u32[]{:S(2)}) collective-permute-start(f32[2,32,1280]{2,1,0:T(8,128)S(1)} %get-tuple-element.40), channel_id=1, source_target_pairs={{0,2},{1,3},{2,0},{3,1},{4,6},{5,7},{6,4},{7,5},{8,10},{9,11},{10,... | collective-permute-start | bytes 983048 | tf_op jit(solution)/shard_map/ppermute | solution.py:599
  62.5 10.7 %collective-permute-start.6 = (f32[2,32,1280]{2,1,0:T(8,128)S(1)}, f32[2,32,1280]{2,1,0:T(8,128)S(1)}, u32[]{:S(2)}, u32[]{:S(2)}) collective-permute-start(f32[2,32,1280]{2,1,0:T(8,128)S(1)} %get-tuple-element.45), channel_id=1, source_target_pairs={{0,2},{1,3},{2,0},{3,1},{4,6},{5,7},{6,4},{7,5},{8,10},{9,11},{10,... | collective-permute-start | bytes 983048 | tf_op jit(solution)/shard_map/ppermute | solution.py:599
  74.0 12.6 %collective-permute-start.9 = (f32[2,32,1280]{2,1,0:T(8,128)S(1)}, f32[2,32,1280]{2,1,0:T(8,128)S(1)}, u32[]{:S(2)}, u32[]{:S(2)}) collective-permute-start(f32[2,32,1280]{2,1,0:T(8,128)S(1)} %pad_maximum_fusion.4), channel_id=1, source_target_pairs={{0,1},{1,0},{2,3},{3,2},{4,5},{5,4},{6,7},{7,6},{8,9},{9,8},{10,11... | collective-permute-start | bytes 983048 | tf_op jit(solution)/shard_map/ppermute | solution.py:601
  74.1 2.1 %collective-permute-start.7 = (f32[2,32,1280]{2,1,0:T(8,128)S(1)}, f32[2,32,1280]{2,1,0:T(8,128)S(1)}, u32[]{:S(2)}, u32[]{:S(2)}) collective-permute-start(f32[2,32,1280]{2,1,0:T(8,128)S(1)} %pad_maximum_fusion.3), channel_id=1, source_target_pairs={{0,1},{1,0},{2,3},{3,2},{4,5},{5,4},{6,7},{7,6},{8,9},{9,8},{10,11... | collective-permute-start | bytes 983048 | tf_op jit(solution)/shard_map/ppermute | solution.py:601
  74.6 11.9 %collective-permute-start.8 = (f32[2,32,1280]{2,1,0:T(8,128)S(1)}, f32[2,32,1280]{2,1,0:T(8,128)S(1)}, u32[]{:S(2)}, u32[]{:S(2)}) collective-permute-start(f32[2,32,1280]{2,1,0:T(8,128)S(1)} %get-tuple-element.52), channel_id=1, source_target_pairs={{0,2},{1,3},{2,0},{3,1},{4,6},{5,7},{6,4},{7,5},{8,10},{9,11},{10,... | collective-permute-start | bytes 983048 | tf_op jit(solution)/shard_map/ppermute | solution.py:599
  76.2 10.3 %copy-start.17 = (f32[2,32,1280]{2,1,0:T(8,128)}, f32[2,32,1280]{2,1,0:T(8,128)S(1)}, u32[]{:S(2)}) copy-start(f32[2,32,1280]{2,1,0:T(8,128)S(1)} %collective-permute-done.7) | copy-start | bytes 983044
  86.6 9.1 %collective-permute-start.10 = (f32[3,4]{1,0:T(4,128)S(1)}, f32[3,4]{1,0:T(4,128)S(1)}, u32[]{:S(2)}, u32[]{:S(2)}) collective-permute-start(f32[3,4]{1,0:T(4,128)S(1)} %pad_maximum_fusion.6), channel_id=1, source_target_pairs={{0,4},{4,0},{8,12},{12,8},{16,20},{20,16},{24,28},{28,24},{1,5},{5... | collective-permute-start | bytes 152 | tf_op jit(solution)/shard_map/ppermute | solution.py:538
  88.6 7.6 %collective-permute-start.11 = (f32[3,4]{1,0:T(4,128)S(1)}, f32[3,4]{1,0:T(4,128)S(1)}, u32[]{:S(2)}, u32[]{:S(2)}) collective-permute-start(f32[3,4]{1,0:T(4,128)S(1)} %pad_maximum_fusion.6), channel_id=1, source_target_pairs={{0,8},{4,12},{8,0},{12,4},{16,24},{20,28},{24,16},{28,20},{1,9},{5... | collective-permute-start | bytes 152 | tf_op jit(solution)/shard_map/ppermute | solution.py:538
  88.6 10.8 %collective-permute-start.12 = (f32[3,4]{1,0:T(4,128)S(1)}, f32[3,4]{1,0:T(4,128)S(1)}, u32[]{:S(2)}, u32[]{:S(2)}) collective-permute-start(f32[3,4]{1,0:T(4,128)S(1)} %pad_maximum_fusion.6), channel_id=1, source_target_pairs={{0,12},{4,8},{8,4},{12,0},{16,28},{20,24},{24,20},{28,16},{1,13},{... | collective-permute-start | bytes 152 | tf_op jit(solution)/shard_map/ppermute | solution.py:538
  90.2 10.8 %collective-permute-start.13 = (f32[3,4]{1,0:T(4,128)S(1)}, f32[3,4]{1,0:T(4,128)S(1)}, u32[]{:S(2)}, u32[]{:S(2)}) collective-permute-start(f32[3,4]{1,0:T(4,128)S(1)} %pad_maximum_fusion.6), channel_id=1, source_target_pairs={{0,16},{4,20},{8,24},{12,28},{16,0},{20,4},{24,8},{28,12},{1,17},{... | collective-permute-start | bytes 152 | tf_op jit(solution)/shard_map/ppermute | solution.py:538
  91.1 10.0 %collective-permute-start.14 = (f32[3,4]{1,0:T(4,128)S(1)}, f32[3,4]{1,0:T(4,128)S(1)}, u32[]{:S(2)}, u32[]{:S(2)}) collective-permute-start(f32[3,4]{1,0:T(4,128)S(1)} %pad_maximum_fusion.6), channel_id=1, source_target_pairs={{0,20},{4,16},{8,28},{12,24},{16,4},{20,0},{24,12},{28,8},{1,21},{... | collective-permute-start | bytes 152 | tf_op jit(solution)/shard_map/ppermute | solution.py:538
  95.7 5.5 %collective-permute-start.15 = (f32[3,4]{1,0:T(4,128)S(1)}, f32[3,4]{1,0:T(4,128)S(1)}, u32[]{:S(2)}, u32[]{:S(2)}) collective-permute-start(f32[3,4]{1,0:T(4,128)S(1)} %pad_maximum_fusion.6), channel_id=1, source_target_pairs={{0,24},{4,28},{8,16},{12,20},{16,8},{20,12},{24,0},{28,4},{1,25},{... | collective-permute-start | bytes 152 | tf_op jit(solution)/shard_map/ppermute | solution.py:538
  96.2 6.3 %collective-permute-start.16 = (f32[3,4]{1,0:T(4,128)S(1)}, f32[3,4]{1,0:T(4,128)S(1)}, u32[]{:S(2)}, u32[]{:S(2)}) collective-permute-start(f32[3,4]{1,0:T(4,128)S(1)} %pad_maximum_fusion.6), channel_id=1, source_target_pairs={{0,28},{4,24},{8,20},{12,16},{16,12},{20,8},{24,4},{28,0},{1,29},{... | collective-permute-start | bytes 152 | tf_op jit(solution)/shard_map/ppermute | solution.py:538
  99.4 8.1 %collective-permute-start.20 = (f32[2,32,1280]{2,1,0:T(8,128)S(1)}, f32[2,32,1280]{2,1,0:T(8,128)}, u32[]{:S(2)}, u32[]{:S(2)}) collective-permute-start(f32[2,32,1280]{2,1,0:T(8,128)S(1)} %get-tuple-element.66), channel_id=1, source_target_pairs={{0,2},{1,3},{2,0},{3,1},{4,6},{5,7},{6,4},{7,5},{8,10},{9,11},{10,... | collective-permute-start | bytes 983048 | tf_op jit(solution)/shard_map/ppermute | solution.py:599
  109.4 5.6 %collective-permute-start.21 = (f32[4,32,1280]{2,1,0:T(8,128)}, f32[4,32,1280]{2,1,0:T(8,128)S(1)}, u32[]{:S(2)}, u32[]{:S(2)}) collective-permute-start(f32[4,32,1280]{2,1,0:T(8,128)} %pad_maximum_fusion.1), channel_id=1, source_target_pairs={{0,1},{1,0},{2,3},{3,2},{4,5},{5,4},{6,7},{7,6},{8,9},{9,8},{10,11... | collective-permute-start | bytes 1966088 | tf_op jit(solution)/shard_map/ppermute | solution.py:616
  109.9 2.2 %collective-permute-start.17 = (f32[4,6]{1,0:T(4,128)S(1)}, f32[4,6]{1,0:T(4,128)S(1)}, u32[]{:S(2)}, u32[]{:S(2)}) collective-permute-start(f32[4,6]{1,0:T(4,128)S(1)} %pad_maximum_fusion.7), channel_id=1, source_target_pairs={{0,1},{1,0},{2,3},{3,2},{4,5},{5,4},{6,7},{7,6},{8,9},{9,8},{10,11... | collective-permute-start | bytes 296 | tf_op jit(solution)/shard_map/ppermute | solution.py:538
  110.4 3.6 %collective-permute-start.18 = (f32[4,6]{1,0:T(4,128)S(1)}, f32[4,6]{1,0:T(4,128)S(1)}, u32[]{:S(2)}, u32[]{:S(2)}) collective-permute-start(f32[4,6]{1,0:T(4,128)S(1)} %pad_maximum_fusion.7), channel_id=1, source_target_pairs={{0,2},{1,3},{2,0},{3,1},{4,6},{5,7},{6,4},{7,5},{8,10},{9,11},{10,... | collective-permute-start | bytes 296 | tf_op jit(solution)/shard_map/ppermute | solution.py:538
  112.0 3.0 %collective-permute-start.19 = (f32[4,6]{1,0:T(4,128)S(1)}, f32[4,6]{1,0:T(4,128)S(1)}, u32[]{:S(2)}, u32[]{:S(2)}) collective-permute-start(f32[4,6]{1,0:T(4,128)S(1)} %pad_maximum_fusion.7), channel_id=1, source_target_pairs={{0,3},{1,2},{2,1},{3,0},{4,7},{5,6},{6,5},{7,4},{8,11},{9,10},{10,... | collective-permute-start | bytes 296 | tf_op jit(solution)/shard_map/ppermute | solution.py:538
  (10 other events, 10.1 us)

commit v4 on v3

--- a/solution.py
+++ b/solution.py
@@ -134,7 +134,11 @@
 
 
 def store(ref, start, value):
-    ref[pl.ds(pl.multiple_of(start, 8), value.shape[0]), :] = value
+    ref[pl.ds(start, value.shape[0]), :] = value
+
+
+def odd(rows):
+    return rows + 1
 
 
 def lane_block(value, i):
@@ -179,11 +183,20 @@
 
 def slab_rows_kernel(dims, row_slices, *refs):
     parts = len(row_slices)
-    slab_refs, refs = refs[:parts], refs[parts:]
     if parts == 1:
-        valid_ref, z_ref, y_ref, rows_ref, mask_ref, depth_buf, parts_buf = refs
+        ins, (rows_ref, mask_ref), scratch = refs[:4], refs[4:6], refs[6:]
+        depth_buf, parts_buf, slab_buf, valid_ref, z_ref, y_ref, sems = scratch
+        slab_refs = [slab_buf]
+        copies = [
+            pltpu.make_async_copy(source, target, sems.at[i])
+            for i, (source, target) in enumerate(zip(ins, (slab_buf, valid_ref, z_ref, y_ref)))
+        ]
+        for copy in copies:
+            copy.start()
+        for copy in copies:
+            copy.wait()
     else:
-        z_ref, y_ref, rows_ref, depth_buf, parts_buf = refs
+        slab_refs, (z_ref, y_ref, rows_ref, depth_buf, parts_buf) = refs[:parts], refs[parts:]
     x_cells, y_cells, z_cells = dims
     count = sum(stop - start for start, stop in row_slices)
     n_y = y_cells + HALF
@@ -207,7 +220,7 @@
                 part = out[u * size : (u + 1) * size]
                 for j in range(2):
                     store(
-                        depth_buf, (2 * many * i + 2 * u + j) * count + top,
+                        depth_buf, (2 * many * i + 2 * u + j) * odd(count) + top,
                         lane_block(part, 2 * j) + lane_block(part, 2 * j + 1),
                     )
             top += size
@@ -215,13 +228,13 @@
     loop(y_cells // (2 * many), depth_step)
 
     def gather_rows(i, slot):
-        value = pick(depth_buf, [GROUP * i + u for u in range(GROUP)], y_cells, count)
+        value = pick(depth_buf, [GROUP * i + u for u in range(GROUP)], y_cells, odd(count))
         parts_buf[slot] = split_rows(value, True)
 
     def y_step(i, slot):
         plus, minus = pair_dot(y_ref[...], parts_buf[slot], True)
         for u in range(GROUP):
-            start = (GROUP * i + u) * 2 * pad_y
+            start = (GROUP * i + u) * odd(2 * pad_y)
             store(rows_ref, start, lane_block(plus, u))
             store(rows_ref, start + pad_y, lane_block(minus, u))
 
@@ -234,40 +247,43 @@
     n_y = y_cells + HALF
     pad_y = n_y // 2 + -(n_y // 2) % 8
     vmem = pl.BlockSpec(memory_space=pltpu.VMEM)
-    out_shape = [jax.ShapeDtypeStruct((count * 2 * pad_y, LANES), F32)]
+    out_shape = [jax.ShapeDtypeStruct((count * odd(2 * pad_y), LANES), F32)]
+    scratch = [
+        pltpu.VMEM((y_cells * odd(count), LANES), F32),
+        pltpu.VMEM((2, 3 * y_cells, GROUP * LANES), BF16),
+    ]
+    slab_z, slab_y = tables["slab_z"], tables["slab_y"]
+    source = vmem
     if valid is not None:
+        source = pl.BlockSpec(memory_space=pltpu.HBM)
+        for array in (blocks[0], valid, slab_z, slab_y):
+            scratch.append(pltpu.VMEM(array.shape, array.dtype))
+        scratch.append(pltpu.SemaphoreType.DMA((4,)))
         blocks = blocks + [valid]
         out_shape.append(jax.ShapeDtypeStruct((y_cells // 2, x_cells, LANES), F32))
     return pl.pallas_call(
         functools.partial(slab_rows_kernel, dims, row_slices),
         out_shape=tuple(out_shape),
-        in_specs=[vmem] * (2 + len(blocks)),
+        in_specs=[source] * (2 + len(blocks)),
         out_specs=(vmem,) * len(out_shape),
-        scratch_shapes=[
-            pltpu.VMEM((y_cells * count, LANES), F32),
-            pltpu.VMEM((2, 3 * y_cells, GROUP * LANES), BF16),
-        ],
+        scratch_shapes=scratch,
         compiler_params=pltpu.CompilerParams(vmem_limit_bytes=20 * 1024 * 1024),
         cost_estimate=pl.CostEstimate(flops=count * 10**8, bytes_accessed=10**6, transcendentals=0),
         name=name,
-    )(*blocks, tables["slab_z"], tables["slab_y"])
-
-
-def slab_x_kernel(dims, own_ref, halo_ref, x_ref, out_hbm, spec_buf, parts_buf, sems):
+    )(*blocks, slab_z, slab_y)
+
+
+def slab_x_kernel(dims, own_ref, halo_ref, x_ref, spec_ref, parts_buf):
     x_cells, y_cells, z_cells = dims
     n_y = y_cells + HALF
     pad_y = n_y // 2 + -(n_y // 2) % 8
-    steps = n_y // GROUP
-
-    def send(i):
-        return pltpu.make_async_copy(spec_buf.at[i], out_hbm.at[i], sems.at[i])
 
     def gather_rows(i, slot):
         firsts = [GROUP // 2 * i + u // 2 + u % 2 * pad_y for u in range(GROUP)]
         value = jnp.concatenate(
             [
-                pick(own_ref, firsts, x_cells, 2 * pad_y),
-                pick(halo_ref, firsts, TEMPL, 2 * pad_y),
+                pick(own_ref, firsts, x_cells, odd(2 * pad_y)),
+                pick(halo_ref, firsts, TEMPL, odd(2 * pad_y)),
             ],
             axis=0,
         )
@@ -278,12 +294,10 @@
         spec = jnp.concatenate([plus, minus], axis=0)
         turned = swap(spec)
         real_lane = lane_sign(GROUP * LANES) < 0
-        spec_buf[i, 0] = jnp.where(real_lane, spec, turned)
-        spec_buf[i, 1] = jnp.where(real_lane, -turned, spec)
-        send(i).start()
-
-    pipeline(steps, [gather_rows, x_step], 2)
-    loop(steps, lambda i: send(i).wait())
+        spec_ref[i, 0] = jnp.where(real_lane, spec, turned)
+        spec_ref[i, 1] = jnp.where(real_lane, -turned, spec)
+
+    pipeline(n_y // GROUP, [gather_rows, x_step], 2)
 
 
 def slab_x(own, halo, dims, tables):
@@ -296,31 +310,24 @@
         functools.partial(slab_x_kernel, dims),
         out_shape=jax.ShapeDtypeStruct(shape, F32),
         in_specs=[vmem] * 3,
-        out_specs=pl.BlockSpec(memory_space=pl.ANY),
-        scratch_shapes=[
-            pltpu.VMEM(shape, F32),
-            pltpu.VMEM((2, 3 * n_x, GROUP * LANES), BF16),
-            pltpu.SemaphoreType.DMA((steps,)),
-        ],
-        compiler_params=pltpu.CompilerParams(vmem_limit_bytes=24 * 1024 * 1024),
+        out_specs=vmem,
+        scratch_shapes=[pltpu.VMEM((2, 3 * n_x, GROUP * LANES), BF16)],
+        compiler_params=pltpu.CompilerParams(vmem_limit_bytes=20 * 1024 * 1024),
         cost_estimate=pl.CostEstimate(flops=5 * 10**9, bytes_accessed=10**6, transcendentals=0),
         name="slab_x",
     )(own, halo, tables["slab_x"])
 
 
 def corr_kernel(
-    dims, rot, place_ref, tmpl_ref, mask_ref, spec_hbm,
+    dims, rot, place_ref, tmpl_ref, mask_ref, spec_ref,
     z_ref, ones_ref, y_ref, x_ref, bx_ref, by_ref, bz_ref,
     mine_ref, side_ref, far_ref, stat_ref,
-    spec_ref, depth_buf, rows_buf, first_buf, second_buf, third_buf, back_buf, vol_buf, sem,
+    depth_buf, rows_buf, first_buf, second_buf, third_buf, back_buf, vol_buf,
 ):
     x_cells, y_cells, z_cells = dims
     n_x, n_y = x_cells + TEMPL, y_cells + HALF
     half_y = n_y // 2
     pad_y = half_y + -half_y % 8
-    copy = pltpu.make_async_copy(spec_hbm, spec_ref, sem)
-    copy.start()
-
     each = TEMPL // 8
     rows = slice(rot * each, (rot + 1) * each)
     tmpl = jnp.concatenate([tmpl_ref[t, rows, :] for t in range(8)], axis=0)
@@ -341,26 +348,25 @@
         out = jnp.dot(window, z_ref[j], preferred_element_type=F32)
         part = out[:, :LANES] + out[:, LANES:] - shift
         for g in range(TEMPL // 8):
-            start = (8 * g + j) * TEMPL
-            depth_buf[start : start + TEMPL, :] = part[g * TEMPL : (g + 1) * TEMPL]
+            start = (8 * g + j) * odd(TEMPL)
+            store(depth_buf, start, part[g * TEMPL : (g + 1) * TEMPL])
 
     def gather_a(i, slot):
-        value = pick(depth_buf, [GROUP * i + u for u in range(GROUP)], TEMPL, TEMPL)
+        value = pick(depth_buf, [GROUP * i + u for u in range(GROUP)], TEMPL, odd(TEMPL))
         first_buf[slot] = split_rows(value, True)
 
     def y_step(i, slot):
         plus, minus = pair_dot(y_ref[...], first_buf[slot], True)
         for u in range(GROUP):
-            start = (GROUP * i + u) * 2 * pad_y
+            start = (GROUP * i + u) * odd(2 * pad_y)
             store(rows_buf, start, lane_block(plus, u))
             store(rows_buf, start + pad_y, lane_block(minus, u))
 
     pipeline(TEMPL // GROUP, [gather_a, y_step], 2)
-    copy.wait()
 
     def gather_ky(i, slot):
         firsts = [GROUP // 2 * i + u // 2 + u % 2 * pad_y for u in range(GROUP)]
-        first_buf[slot] = split_rows(pick(rows_buf, firsts, TEMPL, 2 * pad_y), True)
+        first_buf[slot] = split_rows(pick(rows_buf, firsts, TEMPL, odd(2 * pad_y)), True)
 
     def multiply(i, slot):
         plus, minus = pair_dot(x_ref[...], first_buf[slot], True)
@@ -371,14 +377,14 @@
     def back_x(i, slot):
         plus, minus = pair_dot(bx_ref[...], second_buf[slot], False)
         for u in range(GROUP):
-            start = (GROUP * i + u) * x_cells
+            start = (GROUP * i + u) * odd(x_cells)
             store(back_buf, start, lane_block(plus, u))
             store(back_buf, start + x_cells // 2, lane_block(minus, u))
 
     pipeline(n_y // GROUP, [gather_ky, multiply, back_x], 2)
 
     def gather_x(i, slot):
-        value = pick(back_buf, [GROUP * i + u for u in range(GROUP)], n_y, x_cells)
+        value = pick(back_buf, [GROUP * i + u for u in range(GROUP)], n_y, odd(x_cells))
         third_buf[slot] = split_rows(value, False)
 
     def back_y(i, slot):
@@ -386,8 +392,8 @@
         for u in range(GROUP):
             row = GROUP * i + u
             x = jnp.where(row < x_cells // 2, row + x_cells // 2, x_cells - 1 - row)
-            store(vol_buf, x * y_cells, lane_block(plus, u))
-            store(vol_buf, x * y_cells + y_cells // 2, lane_block(minus, u))
+            store(vol_buf, x * odd(y_cells), lane_block(plus, u))
+            store(vol_buf, x * odd(y_cells) + y_cells // 2, lane_block(minus, u))
 
     pipeline(x_cells // GROUP, [gather_x, back_y], 2)
 
@@ -404,7 +410,7 @@
             for j in range(2):
                 y = 2 * (first + i) + j
                 firsts.append(jnp.where(y < y_cells // 2, y_cells - 1 - y, y - y_cells // 2))
-            values.append(pick(vol_buf, firsts, x_cells, y_cells))
+            values.append(pick(vol_buf, firsts, x_cells, odd(y_cells)))
         value = jnp.concatenate(values, axis=0)
         out = jnp.dot(split_rows(value, False), bz_ref[...], preferred_element_type=F32)
         rows = value.shape[0]
@@ -442,21 +448,18 @@
             jax.ShapeDtypeStruct((2, x_cells, width), F32),
             jax.ShapeDtypeStruct((8, LANES), F32),
         ),
-        in_specs=[pl.BlockSpec(memory_space=pltpu.SMEM), vmem, vmem]
-        + [pl.BlockSpec(memory_space=pl.ANY)] + [vmem] * 7,
+        in_specs=[pl.BlockSpec(memory_space=pltpu.SMEM)] + [vmem] * 10,
         out_specs=(vmem,) * 4,
         scratch_shapes=[
-            pltpu.VMEM(spec.shape, F32),
-            pltpu.VMEM((TEMPL * TEMPL, LANES), F32),
-            pltpu.VMEM((TEMPL * 2 * pad_y, LANES), F32),
+            pltpu.VMEM((TEMPL * odd(TEMPL), LANES), F32),
+            pltpu.VMEM((TEMPL * odd(2 * pad_y), LANES), F32),
             pltpu.VMEM((2, 3 * TEMPL, GROUP * LANES), BF16),
             pltpu.VMEM((2, 2 * n_x, GROUP * LANES), BF16),
             pltpu.VMEM((2, 2 * n_y, GROUP * LANES), BF16),
-            pltpu.VMEM((n_y * x_cells, LANES), F32),
-            pltpu.VMEM((x_cells * y_cells, LANES), F32),
-            pltpu.SemaphoreType.DMA,
+            pltpu.VMEM((n_y * odd(x_cells), LANES), F32),
+            pltpu.VMEM((x_cells * odd(y_cells), LANES), F32),
         ],
-        compiler_params=pltpu.CompilerParams(vmem_limit_bytes=32 * 1024 * 1024),
+        compiler_params=pltpu.CompilerParams(vmem_limit_bytes=24 * 1024 * 1024),
         cost_estimate=pl.CostEstimate(flops=15 * 10**9, bytes_accessed=10**7, transcendentals=0),
         name="correlate",
     )(
@@ -523,12 +526,13 @@
     return jnp.stack(pair, axis=1).reshape((-1,) + block.shape[1:])
 
 
-def merge(parts):
-    number, total, square = parts[:, 0], parts[:, 1], parts[:, 2]
-    all_number = jnp.sum(number, axis=0)
-    all_total = jnp.sum(total, axis=0)
-    gap = total / jnp.maximum(number, 1.0) - all_total / jnp.maximum(all_number, 1.0)
-    return jnp.stack([all_number, all_total, jnp.sum(square + number * gap * gap, axis=0)])
+def merge(first, other):
+    number_a, number_b = first[:1], other[:1]
+    mean_a = first[1:2] / jnp.maximum(number_a, 1.0)
+    mean_b = other[1:2] / jnp.maximum(number_b, 1.0)
+    gap = mean_b - mean_a
+    between = gap * gap * (number_a * number_b / jnp.maximum(number_a + number_b, 1.0))
+    return first + other + jnp.where(jnp.arange(3)[:, None] == 2, between, 0.0)
 
 
 def exchange_all(block, axis, low, high):
@@ -605,9 +609,9 @@
     )
     step = 1
     while step < tiles:
-        following = min(step * 8, tiles)
-        state = merge(exchange_all(state, "tile", step, following))
-        step = following
+        swap_pairs = [(i, i ^ step) for i in range(tiles)]
+        state = merge(state, lax.ppermute(state, "tile", swap_pairs))
+        step *= 2
     average = state[1] / state[0]
     inverse = 1.0 / jnp.sqrt(state[2] / state[0] + EPSILON)
     coefs = jnp.concatenate([average[:, None], inverse[:, None], orient], axis=1)

time: 119 us -> 99.4 us (0.84)
  Pallas kernels: 60.5 us -> 46.1 us
  starting transfers between devices: 30.3 us -> 21.6 us
  waiting for transfers between devices: 13.8 us -> 21.6 us
  local copies, waits for them, and re-layouts: 10.7 us -> 5.77 us
    ppermute x10 -> x3, starting transfers between devices: 13.4 us -> 1.94 us  [exchange_all(): lax.ppermute(block, axis, [(i, i ^ step) for i in range(count)])]
    ppermute x0 -> x3, waiting for transfers between devices: none -> 9.03 us  [local(): state = merge(state, lax.ppermute(state, 'tile', swap_pairs))]
    pallas_call x4, Pallas kernels: 40.7 us -> 32.1 us  [correlate(): pl.pallas_call(functools.partial(corr_kernel, dims, rot), out_shape=(jax....]
    ppermute x3, waiting for transfers between devices: 4.9 us -> 10.4 us  [gather_step(): other = lax.ppermute(block, axis, [(i, i ^ step) for i in range(count)])]
    pallas_call x1, Pallas kernels: 9.23 us -> 3.86 us  [slab_x(): pl.pallas_call(functools.partial(slab_x_kernel, dims), out_shape=jax.Shap...]
    ppermute x4, waiting for transfers between devices: 4.6 us -> 0.02 us  [local(): fars.append(lax.ppermute(far, 'rot', far_swap))]
    ppermute x0 -> x3, starting transfers between devices: none -> 2.66 us  [local(): state = merge(state, lax.ppermute(state, 'tile', swap_pairs))]
    ppermute x10 -> x3, waiting for transfers between devices: 4.24 us -> 2.13 us  [exchange_all(): lax.ppermute(block, axis, [(i, i ^ step) for i in range(count)])]
  transfers between devices with their start and end apart: 22 -> 18, of which waited for: 6 -> 7; matrix products, arithmetic and copies ran while one was open for 4% -> 3% of each run, Pallas kernels for 39% -> 35%
where the time goes in v4:
time: 99.4 us; the launch traced here: 99 us
  Pallas kernels  46.1 us (46%)
  starting transfers between devices  21.6 us (22%)
  waiting for transfers between devices  21.6 us (22%)
  local copies, waits for them, and re-layouts  5.77 us (6%)
  other arithmetic  1.92 us (2%)
  between operations  1.01 us (1%)
    pallas_call x4, Pallas kernels, correlate(): pl.pallas_call(functools.partial(corr_kernel, dims, rot), out_shape=(jax....  32.1 us
    ppermute x3, waiting for transfers between devices, gather_step(): other = lax.ppermute(block, axis, [(i, i ^ step) for i in range(count)])  10.4 us
    ppermute x3, waiting for transfers between devices, local(): state = merge(state, lax.ppermute(state, 'tile', swap_pairs))  9.03 us
    pallas_call x2, Pallas kernels, slab_rows(): pl.pallas_call(functools.partial(slab_rows_kernel, dims, row_slices), out...  6.54 us
    ppermute x4, starting transfers between devices, local(): fars.append(lax.ppermute(far, 'rot', far_swap))  5.21 us
    ppermute x1, starting transfers between devices, neighbours(): lax.ppermute(block, axis, forward)  5 us
    ppermute x3, starting transfers between devices, gather_step(): other = lax.ppermute(block, axis, [(i, i ^ step) for i in range(count)])  4.83 us
    unnamed x26, local copies, waits for them, and re-layouts  4.39 us
  transfers between devices with their start and end apart: 18, of which 7 were waited for; matrix products, arithmetic and copies ran while one was open for 3% of the time, Pallas kernels for 35%

profile of v4, /device:TPU:0, one launch (start us, length us, event | category | flops | bytes accessed | tf_op | source)
XLA Modules:
  0.0 99.0 jit_solution(3988669542902596389)
XLA Ops:
  0.6 5.0 %collective-permute-start.3 = (bf16[32,5120]{1,0:T(8,128)(2,1)}, bf16[32,5120]{1,0:T(8,128)(2,1)S(1)}, u32[]{:S(2)}, u32[]{:S(2)}) collective-permute-start(bf16[32,5120]{1,0:T(8,128)(2,1)} %refs_0_.1), channel_id=1, source_target_pairs={{0,4},{4,8},{8,12},{12,16},{16,20},{20,24},{24,28},{1,5},{5,9},{9,... | collective-permute-start | bytes 983048 | tf_op jit(solution)/shard_map/ppermute | solution.py:550
  5.6 1.3 %collective-permute-start.4 = (bf16[32,5120]{1,0:T(8,128)(2,1)}, bf16[32,5120]{1,0:T(8,128)(2,1)S(1)}, u32[]{:S(2)}, u32[]{:S(2)}) collective-permute-start(bf16[32,5120]{1,0:T(8,128)(2,1)} %refs_0_.1), channel_id=1, source_target_pairs={{4,0},{8,4},{12,8},{16,12},{20,16},{24,20},{28,24},{5,1},{9,5},{13... | collective-permute-start | bytes 983048 | tf_op jit(solution)/shard_map/ppermute | solution.py:550
  6.9 1.0 broadcast_in_dim_reshape.3
  7.9 4.7 %collective-permute-start = (bf16[1,24,2304]{2,1,0:T(8,128)(2,1)S(1)}, bf16[1,24,2304]{2,1,0:T(8,128)(2,1)S(1)}, u32[]{:S(2)}, u32[]{:S(2)}) collective-permute-start(bf16[1,24,2304]{2,1,0:T(8,128)(2,1)S(1)} %broadcast_in_dim_reshape.3), channel_id=1, source_target_pairs={{0,16},{4,20},{8,24},{12,28},{16,0},{20,4},{24,8},{28,12},{1,17},{... | collective-permute-start | bytes 331784 | tf_op jit(solution)/shard_map/ppermute | solution.py:523
  12.6 0.9 fusion
  13.6 1.0 %copy-done.1 = bf16[32,5120]{1,0:T(8,128)(2,1)S(1)} copy-done((bf16[32,5120]{1,0:T(8,128)(2,1)S(1)}, bf16[32,5120]{1,0:T(8,128)(2,1)}, u32[]{:S(2)}) %copy-start.1) | copy-done | bytes 327704
  14.6 0.7 copy-done.2
  15.3 0.9 copy-done.5
  16.2 0.8 copy-done.8
  17.0 3.2 %slab_own.1 = (f32[3616,128]{1,0:T(8,128)S(1)}, f32[40,32,128]{2,1,0:T(8,128)S(1)}) custom-call(bf16[32,5120]{1,0:T(8,128)(2,1)S(1)} %copy-done.1, s32[32,80]{1,0:T(8,128)S(1)} %copy-done.2, bf16[128,512]{1,0:T(8,128)(2,1)S(1)} %copy-done.5, bf16[112,240]{1,0:T(8,128)(2,1)S(1)} %copy-done.8), custom_call_target="tpu_custom_call" | custom-call | flops 3200000000 | bytes 1000000 | tf_op jit(solution)/shard_map/slab_own/pallas_call | solution.py:264
  20.2 3.5 %collective-permute-done = bf16[1,24,2304]{2,1,0:T(8,128)(2,1)S(1)} collective-permute-done((bf16[1,24,2304]{2,1,0:T(8,128)(2,1)S(1)}, bf16[1,24,2304]{2,1,0:T(8,128)(2,1)S(1)}, u32[]{:S(2)}, u32[]{:S(2)}) %collective-permute-start) | collective-permute-done | bytes 110624 | tf_op jit(solution)/shard_map/ppermute | solution.py:523
  23.9 3.4 %slab_halo.1.halo_ref = f32[5424,128]{1,0:T(8,128)S(1)} custom-call(bf16[32,5120]{1,0:T(8,128)(2,1)S(1)} %collective-permute-done.3.refs_0_, bf16[32,5120]{1,0:T(8,128)(2,1)S(1)} %collective-permute-done.4.refs_1_, bf16[128,512]{1,0:T(8,128)(2,1)S(1)} %copy-done.5, bf16[112,240]{1,0:T(8,128)(2,1)S(1)} %copy-done.8), custom_call_target="tpu_custom_call" | custom-call | flops 4800000000 | bytes 1000000 | tf_op jit(solution)/shard_map/slab_halo/pallas_call | solution.py:264
  27.2 2.5 %collective-permute-done.1 = bf16[2,24,2304]{2,1,0:T(8,128)(2,1)S(1)} collective-permute-done((bf16[2,24,2304]{2,1,0:T(8,128)(2,1)S(1)}, bf16[2,24,2304]{2,1,0:T(8,128)(2,1)S(1)}, u32[]{:S(2)}, u32[]{:S(2)}) %collective-permute-start.1) | collective-permute-done | bytes 221216 | tf_op jit(solution)/shard_map/ppermute | solution.py:523
  30.0 3.9 %slab_x.1.spec_ref = f32[13,2,80,1024]{3,2,1,0:T(8,128)S(1)} custom-call(f32[3616,128]{1,0:T(8,128)S(1)} %get-tuple-element.37.own_ref, f32[5424,128]{1,0:T(8,128)S(1)} %slab_halo.1.halo_ref, bf16[80,240]{1,0:T(8,128)(2,1)S(1)} %copy-done.10), custom_call_target="tpu_custom_call" | custom-call | flops 5000000000 | bytes 1000000 | tf_op jit(solution)/shard_map/slab_x/pallas_call | solution.py:309
  33.9 4.4 %collective-permute-done.2 = bf16[4,24,2304]{2,1,0:T(8,128)(2,1)S(1)} collective-permute-done((bf16[4,24,2304]{2,1,0:T(8,128)(2,1)S(1)}, bf16[4,24,2304]{2,1,0:T(8,128)(2,1)S(1)}, u32[]{:S(2)}, u32[]{:S(2)}) %collective-permute-start.2) | collective-permute-done | bytes 442400 | tf_op jit(solution)/shard_map/ppermute | solution.py:523
  38.7 0.9 copy-done.3
  39.6 7.9 %correlate.4 = (f32[32,1280]{1,0:T(8,128)S(1)}, f32[32,1280]{1,0:T(8,128)S(1)}, f32[2,32,1280]{2,1,0:T(8,128)S(1)}, f32[8,128]{1,0:T(8,128)S(1)}) custom-call(s32[1]{0:T(128)} %bitcast.place_ref, f32[8,24,2304]{2,1,0:T(8,128)S(1)} %bitcast_convert_fusion.tmpl_ref, f32[40,32,128]{2,1,0:T(8,128)S(1)} %get-tuple-element.36.mask_ref, ...), custom_call_target="tpu_custom_call" | custom-call | flops 15000000512 | bytes 10000000 | tf_op jit(solution)/shard_map/correlate/pallas_call | solution.py:443
  47.6 1.6 %collective-permute-start.5 = (f32[2,32,1280]{2,1,0:T(8,128)S(1)}, f32[2,32,1280]{2,1,0:T(8,128)S(1)}, u32[]{:S(2)}, u32[]{:S(2)}) collective-permute-start(f32[2,32,1280]{2,1,0:T(8,128)S(1)} %get-tuple-element.40), channel_id=1, source_target_pairs={{0,2},{1,3},{2,0},{3,1},{4,6},{5,7},{6,4},{7,5},{8,10},{9,11},{10,... | collective-permute-start | bytes 983048 | tf_op jit(solution)/shard_map/ppermute | solution.py:603
  49.1 8.1 %correlate.5 = (f32[32,1280]{1,0:T(8,128)S(1)}, f32[32,1280]{1,0:T(8,128)S(1)}, f32[2,32,1280]{2,1,0:T(8,128)S(1)}, f32[8,128]{1,0:T(8,128)S(1)}) custom-call(s32[1]{0:T(128)} %bitcast.place_ref, f32[8,24,2304]{2,1,0:T(8,128)S(1)} %bitcast_convert_fusion.tmpl_ref, f32[40,32,128]{2,1,0:T(8,128)S(1)} %get-tuple-element.36.mask_ref, ...), custom_call_target="tpu_custom_call" | custom-call | flops 15000000512 | bytes 10000000 | tf_op jit(solution)/shard_map/correlate/pallas_call | solution.py:443
  57.9 7.9 %correlate.6 = (f32[32,1280]{1,0:T(8,128)S(1)}, f32[32,1280]{1,0:T(8,128)S(1)}, f32[2,32,1280]{2,1,0:T(8,128)S(1)}, f32[8,128]{1,0:T(8,128)S(1)}) custom-call(s32[1]{0:T(128)} %bitcast.place_ref, f32[8,24,2304]{2,1,0:T(8,128)S(1)} %bitcast_convert_fusion.tmpl_ref, f32[40,32,128]{2,1,0:T(8,128)S(1)} %get-tuple-element.36.mask_ref, ...), custom_call_target="tpu_custom_call" | custom-call | flops 15000000512 | bytes 10000000 | tf_op jit(solution)/shard_map/correlate/pallas_call | solution.py:443
  66.5 1.5 %collective-permute-start.8 = (f32[2,32,1280]{2,1,0:T(8,128)S(1)}, f32[2,32,1280]{2,1,0:T(8,128)S(1)}, u32[]{:S(2)}, u32[]{:S(2)}) collective-permute-start(f32[2,32,1280]{2,1,0:T(8,128)S(1)} %get-tuple-element.52), channel_id=1, source_target_pairs={{0,2},{1,3},{2,0},{3,1},{4,6},{5,7},{6,4},{7,5},{8,10},{9,11},{10,... | collective-permute-start | bytes 983048 | tf_op jit(solution)/shard_map/ppermute | solution.py:603
  68.1 8.2 %correlate.7 = (f32[32,1280]{1,0:T(8,128)S(1)}, f32[32,1280]{1,0:T(8,128)S(1)}, f32[2,32,1280]{2,1,0:T(8,128)S(1)}, f32[8,128]{1,0:T(8,128)S(1)}) custom-call(s32[1]{0:T(128)} %bitcast.place_ref, f32[8,24,2304]{2,1,0:T(8,128)S(1)} %bitcast_convert_fusion.tmpl_ref, f32[40,32,128]{2,1,0:T(8,128)S(1)} %get-tuple-element.36.mask_ref, ...), custom_call_target="tpu_custom_call" | custom-call | flops 15000000512 | bytes 10000000 | tf_op jit(solution)/shard_map/correlate/pallas_call | solution.py:443
  76.4 1.5 %collective-permute-start.16 = (f32[2,32,1280]{2,1,0:T(8,128)S(1)}, f32[2,32,1280]{2,1,0:T(8,128)S(1)}, u32[]{:S(2)}, u32[]{:S(2)}) collective-permute-start(f32[2,32,1280]{2,1,0:T(8,128)S(1)} %get-tuple-element.66), channel_id=1, source_target_pairs={{0,2},{1,3},{2,0},{3,1},{4,6},{5,7},{6,4},{7,5},{8,10},{9,11},{10,... | collective-permute-start | bytes 983048 | tf_op jit(solution)/shard_map/ppermute | solution.py:603
  78.2 3.4 %collective-permute-done.10 = f32[3,4]{1,0:T(4,128)S(1)} collective-permute-done((f32[3,4]{1,0:T(4,128)S(1)}, f32[3,4]{1,0:T(4,128)S(1)}, u32[]{:S(2)}, u32[]{:S(2)}) %collective-permute-start.10) | collective-permute-done | bytes 80 | tf_op jit(solution)/shard_map/ppermute | solution.py:613
  81.7 0.7 collective-permute-start.11
  82.4 2.9 %collective-permute-done.11 = f32[3,4]{1,0:T(4,128)S(1)} collective-permute-done((f32[3,4]{1,0:T(4,128)S(1)}, f32[3,4]{1,0:T(4,128)S(1)}, u32[]{:S(2)}, u32[]{:S(2)}) %collective-permute-start.11) | collective-permute-done | bytes 80 | tf_op jit(solution)/shard_map/ppermute | solution.py:613
  85.3 1.7 %collective-permute-start.12 = (f32[3,4]{1,0:T(4,128)S(1)}, f32[3,4]{1,0:T(4,128)S(1)}, u32[]{:S(2)}, u32[]{:S(2)}) collective-permute-start(f32[3,4]{1,0:T(4,128)S(1)} %select_add_fusion.1), channel_id=1, source_target_pairs={{0,16},{4,20},{8,24},{12,28},{16,0},{20,4},{24,8},{28,12},{1,17},{... | collective-permute-start | bytes 152 | tf_op jit(solution)/shard_map/ppermute | solution.py:613
  87.1 2.8 %collective-permute-done.12 = f32[3,4]{1,0:T(4,128)S(1)} collective-permute-done((f32[3,4]{1,0:T(4,128)S(1)}, f32[3,4]{1,0:T(4,128)S(1)}, u32[]{:S(2)}, u32[]{:S(2)}) %collective-permute-start.12) | collective-permute-done | bytes 80 | tf_op jit(solution)/shard_map/ppermute | solution.py:613
  89.9 0.9 pad_maximum_fusion.1
  92.3 0.9 collective-permute-start.15
  93.2 2.1 %collective-permute-done.14 = f32[4,6]{1,0:T(4,128)S(1)} collective-permute-done((f32[4,6]{1,0:T(4,128)S(1)}, f32[4,6]{1,0:T(4,128)S(1)}, u32[]{:S(2)}, u32[]{:S(2)}) %collective-permute-start.14) | collective-permute-done | bytes 128 | tf_op jit(solution)/shard_map/ppermute | solution.py:542
  95.3 3.6 %combine.1 = (f32[32,1280]{1,0:T(8,128)}, f32[32,1280]{1,0:T(8,128)}, f32[4,32,1280]{2,1,0:T(8,128)}) custom-call(s32[1]{0:T(128)} %bitcast.place_ref, f32[16,6]{1,0:T(8,128)S(1)} %bitcast.76, f32[40,32,128]{2,1,0:T(8,128)S(1)} %get-tuple-element.36.mask_ref, f32[32,1280]{1,0:T(8,128)S(1)} %get-tuple-element.57.refs_0_, ...), custom_call_target="tpu_custom_call" | custom-call | tf_op jit(solution)/shard_map/combine/pallas_call | solution.py:507
  (77 shorter events, 4.3 us)
Async XLA Ops:
  0.6 12.0 %copy-start = (f32[4,4096]{1,0:T(4,128)S(1)}, f32[4,4096]{1,0:T(4,128)}, u32[]{:S(2)}) copy-start(f32[4,4096]{1,0:T(4,128)} %param.18) | copy-start | bytes 196612
  0.6 23.2 %collective-permute-start.3 = (bf16[32,5120]{1,0:T(8,128)(2,1)}, bf16[32,5120]{1,0:T(8,128)(2,1)S(1)}, u32[]{:S(2)}, u32[]{:S(2)}) collective-permute-start(bf16[32,5120]{1,0:T(8,128)(2,1)} %refs_0_.1), channel_id=1, source_target_pairs={{0,4},{4,8},{8,12},{12,16},{16,20},{20,24},{24,28},{1,5},{5,9},{9,... | collective-permute-start | bytes 983048 | tf_op jit(solution)/shard_map/ppermute | solution.py:550
  5.6 18.2 %collective-permute-start.4 = (bf16[32,5120]{1,0:T(8,128)(2,1)}, bf16[32,5120]{1,0:T(8,128)(2,1)S(1)}, u32[]{:S(2)}, u32[]{:S(2)}) collective-permute-start(bf16[32,5120]{1,0:T(8,128)(2,1)} %refs_0_.1), channel_id=1, source_target_pairs={{4,0},{8,4},{12,8},{16,12},{20,16},{24,20},{28,24},{5,1},{9,5},{13... | collective-permute-start | bytes 983048 | tf_op jit(solution)/shard_map/ppermute | solution.py:550
  7.9 15.8 %collective-permute-start = (bf16[1,24,2304]{2,1,0:T(8,128)(2,1)S(1)}, bf16[1,24,2304]{2,1,0:T(8,128)(2,1)S(1)}, u32[]{:S(2)}, u32[]{:S(2)}) collective-permute-start(bf16[1,24,2304]{2,1,0:T(8,128)(2,1)S(1)} %broadcast_in_dim_reshape.3), channel_id=1, source_target_pairs={{0,16},{4,20},{8,24},{12,28},{16,0},{20,4},{24,8},{28,12},{1,17},{... | collective-permute-start | bytes 331784 | tf_op jit(solution)/shard_map/ppermute | solution.py:523
  13.6 1.0 %copy-start.1 = (bf16[32,5120]{1,0:T(8,128)(2,1)S(1)}, bf16[32,5120]{1,0:T(8,128)(2,1)}, u32[]{:S(2)}) copy-start(bf16[32,5120]{1,0:T(8,128)(2,1)} %refs_0_.1) | copy-start | bytes 983044
  14.6 0.7 copy-start.2
  15.3 0.9 copy-start.5
  16.2 0.8 copy-start.8
  23.8 6.0 %collective-permute-start.1 = (bf16[2,24,2304]{2,1,0:T(8,128)(2,1)S(1)}, bf16[2,24,2304]{2,1,0:T(8,128)(2,1)S(1)}, u32[]{:S(2)}, u32[]{:S(2)}) collective-permute-start(bf16[2,24,2304]{2,1,0:T(8,128)(2,1)S(1)} %maximum_bitcast_fusion), channel_id=1, source_target_pairs={{0,8},{4,12},{8,0},{12,4},{16,24},{20,28},{24,16},{28,20},{1,9},{5... | collective-permute-start | bytes 663560 | tf_op jit(solution)/shard_map/ppermute | solution.py:523
  27.2 2.8 %copy-start.10 = (bf16[80,240]{1,0:T(8,128)(2,1)S(1)}, bf16[80,240]{1,0:T(8,128)(2,1)}, u32[]{:S(2)}) copy-start(bf16[80,240]{1,0:T(8,128)(2,1)} %constant.47.clone.x_ref) | copy-start | bytes 115204
  29.9 8.4 %collective-permute-start.2 = (bf16[4,24,2304]{2,1,0:T(8,128)(2,1)S(1)}, bf16[4,24,2304]{2,1,0:T(8,128)(2,1)S(1)}, u32[]{:S(2)}, u32[]{:S(2)}) collective-permute-start(bf16[4,24,2304]{2,1,0:T(8,128)(2,1)S(1)} %bitcast.77), channel_id=1, source_target_pairs={{0,4},{4,0},{8,12},{12,8},{16,20},{20,16},{24,28},{28,24},{1,5},{5... | collective-permute-start | bytes 1327112 | tf_op jit(solution)/shard_map/ppermute | solution.py:523
  38.4 1.2 %copy-start.3 = (bf16[8,256,256]{2,1,0:T(8,128)(2,1)S(1)}, bf16[8,256,256]{2,1,0:T(8,128)(2,1)}, u32[]{:S(2)}) copy-start(bf16[8,256,256]{2,1,0:T(8,128)(2,1)} %constant.48.clone.z_ref) | copy-start | bytes 3145732
  38.4 1.2 %copy-start.4 = (bf16[256,256]{1,0:T(8,128)(2,1)S(1)}, bf16[256,256]{1,0:T(8,128)(2,1)}, u32[]{:S(2)}) copy-start(bf16[256,256]{1,0:T(8,128)(2,1)} %constant.54.clone.bz_ref) | copy-start | bytes 393220
  38.4 1.2 %copy-start.6 = (bf16[160,208]{1,0:T(8,128)(2,1)S(1)}, bf16[160,208]{1,0:T(8,128)(2,1)}, u32[]{:S(2)}) copy-start(bf16[160,208]{1,0:T(8,128)(2,1)} %constant.53.clone.by_ref) | copy-start | bytes 199684
  38.4 1.2 %copy-start.7 = (bf16[112,144]{1,0:T(8,128)(2,1)S(1)}, bf16[112,144]{1,0:T(8,128)(2,1)}, u32[]{:S(2)}) copy-start(bf16[112,144]{1,0:T(8,128)(2,1)} %constant.50.clone.y_ref) | copy-start | bytes 96772
  38.4 1.2 %copy-start.9 = (bf16[80,144]{1,0:T(8,128)(2,1)S(1)}, bf16[80,144]{1,0:T(8,128)(2,1)}, u32[]{:S(2)}) copy-start(bf16[80,144]{1,0:T(8,128)(2,1)} %constant.51.clone.x_ref) | copy-start | bytes 69124
  38.4 1.2 %copy-start.11 = (bf16[64,160]{1,0:T(8,128)(2,1)S(1)}, bf16[64,160]{1,0:T(8,128)(2,1)}, u32[]{:S(2)}) copy-start(bf16[64,160]{1,0:T(8,128)(2,1)} %constant.52.clone.bx_ref) | copy-start | bytes 61444
  38.4 1.2 %copy-start.12 = (f32[8,128]{1,0:T(8,128)S(1)}, f32[8,128]{1,0:T(8,128)}, u32[]{:S(2)}) copy-start(f32[8,128]{1,0:T(8,128)} %constant.49.clone.ones_ref) | copy-start | bytes 12292
  47.6 10.3 %collective-permute-start.5 = (f32[2,32,1280]{2,1,0:T(8,128)S(1)}, f32[2,32,1280]{2,1,0:T(8,128)S(1)}, u32[]{:S(2)}, u32[]{:S(2)}) collective-permute-start(f32[2,32,1280]{2,1,0:T(8,128)S(1)} %get-tuple-element.40), channel_id=1, source_target_pairs={{0,2},{1,3},{2,0},{3,1},{4,6},{5,7},{6,4},{7,5},{8,10},{9,11},{10,... | collective-permute-start | bytes 983048 | tf_op jit(solution)/shard_map/ppermute | solution.py:603
  57.3 8.5 %collective-permute-start.6 = (f32[2,32,1280]{2,1,0:T(8,128)S(1)}, f32[2,32,1280]{2,1,0:T(8,128)S(1)}, u32[]{:S(2)}, u32[]{:S(2)}) collective-permute-start(f32[2,32,1280]{2,1,0:T(8,128)S(1)} %get-tuple-element.45), channel_id=1, source_target_pairs={{0,2},{1,3},{2,0},{3,1},{4,6},{5,7},{6,4},{7,5},{8,10},{9,11},{10,... | collective-permute-start | bytes 983048 | tf_op jit(solution)/shard_map/ppermute | solution.py:603
  65.9 10.5 %collective-permute-start.9 = (f32[2,32,1280]{2,1,0:T(8,128)S(1)}, f32[2,32,1280]{2,1,0:T(8,128)S(1)}, u32[]{:S(2)}, u32[]{:S(2)}) collective-permute-start(f32[2,32,1280]{2,1,0:T(8,128)S(1)} %pad_maximum_fusion.4), channel_id=1, source_target_pairs={{0,1},{1,0},{2,3},{3,2},{4,5},{5,4},{6,7},{7,6},{8,9},{9,8},{10,11... | collective-permute-start | bytes 983048 | tf_op jit(solution)/shard_map/ppermute | solution.py:605
  66.0 2.1 %collective-permute-start.7 = (f32[2,32,1280]{2,1,0:T(8,128)S(1)}, f32[2,32,1280]{2,1,0:T(8,128)S(1)}, u32[]{:S(2)}, u32[]{:S(2)}) collective-permute-start(f32[2,32,1280]{2,1,0:T(8,128)S(1)} %pad_maximum_fusion.3), channel_id=1, source_target_pairs={{0,1},{1,0},{2,3},{3,2},{4,5},{5,4},{6,7},{7,6},{8,9},{9,8},{10,11... | collective-permute-start | bytes 983048 | tf_op jit(solution)/shard_map/ppermute | solution.py:605
  66.5 9.7 %collective-permute-start.8 = (f32[2,32,1280]{2,1,0:T(8,128)S(1)}, f32[2,32,1280]{2,1,0:T(8,128)S(1)}, u32[]{:S(2)}, u32[]{:S(2)}) collective-permute-start(f32[2,32,1280]{2,1,0:T(8,128)S(1)} %get-tuple-element.52), channel_id=1, source_target_pairs={{0,2},{1,3},{2,0},{3,1},{4,6},{5,7},{6,4},{7,5},{8,10},{9,11},{10,... | collective-permute-start | bytes 983048 | tf_op jit(solution)/shard_map/ppermute | solution.py:603
  76.4 13.5 %collective-permute-start.16 = (f32[2,32,1280]{2,1,0:T(8,128)S(1)}, f32[2,32,1280]{2,1,0:T(8,128)S(1)}, u32[]{:S(2)}, u32[]{:S(2)}) collective-permute-start(f32[2,32,1280]{2,1,0:T(8,128)S(1)} %get-tuple-element.66), channel_id=1, source_target_pairs={{0,2},{1,3},{2,0},{3,1},{4,6},{5,7},{6,4},{7,5},{8,10},{9,11},{10,... | collective-permute-start | bytes 983048 | tf_op jit(solution)/shard_map/ppermute | solution.py:603
  77.9 3.7 %collective-permute-start.10 = (f32[3,4]{1,0:T(4,128)S(1)}, f32[3,4]{1,0:T(4,128)S(1)}, u32[]{:S(2)}, u32[]{:S(2)}) collective-permute-start(f32[3,4]{1,0:T(4,128)S(1)} %pad_maximum_fusion.6), channel_id=1, source_target_pairs={{0,4},{4,0},{8,12},{12,8},{16,20},{20,16},{24,28},{28,24},{1,5},{5... | collective-permute-start | bytes 152 | tf_op jit(solution)/shard_map/ppermute | solution.py:613
  81.7 3.6 %collective-permute-start.11 = (f32[3,4]{1,0:T(4,128)S(1)}, f32[3,4]{1,0:T(4,128)S(1)}, u32[]{:S(2)}, u32[]{:S(2)}) collective-permute-start(f32[3,4]{1,0:T(4,128)S(1)} %select_add_fusion.2), channel_id=1, source_target_pairs={{0,8},{4,12},{8,0},{12,4},{16,24},{20,28},{24,16},{28,20},{1,9},{5... | collective-permute-start | bytes 152 | tf_op jit(solution)/shard_map/ppermute | solution.py:613
  85.3 4.5 %collective-permute-start.12 = (f32[3,4]{1,0:T(4,128)S(1)}, f32[3,4]{1,0:T(4,128)S(1)}, u32[]{:S(2)}, u32[]{:S(2)}) collective-permute-start(f32[3,4]{1,0:T(4,128)S(1)} %select_add_fusion.1), channel_id=1, source_target_pairs={{0,16},{4,20},{8,24},{12,28},{16,0},{20,4},{24,8},{28,12},{1,17},{... | collective-permute-start | bytes 152 | tf_op jit(solution)/shard_map/ppermute | solution.py:613
  90.8 4.5 %collective-permute-start.17 = (f32[4,32,1280]{2,1,0:T(8,128)}, f32[4,32,1280]{2,1,0:T(8,128)S(1)}, u32[]{:S(2)}, u32[]{:S(2)}) collective-permute-start(f32[4,32,1280]{2,1,0:T(8,128)} %pad_maximum_fusion.1), channel_id=1, source_target_pairs={{0,1},{1,0},{2,3},{3,2},{4,5},{5,4},{6,7},{7,6},{8,9},{9,8},{10,11... | collective-permute-start | bytes 1966088 | tf_op jit(solution)/shard_map/ppermute | solution.py:620
  91.1 2.0 %collective-permute-start.13 = (f32[4,6]{1,0:T(4,128)S(1)}, f32[4,6]{1,0:T(4,128)S(1)}, u32[]{:S(2)}, u32[]{:S(2)}) collective-permute-start(f32[4,6]{1,0:T(4,128)S(1)} %pad_maximum_fusion.7), channel_id=1, source_target_pairs={{0,1},{1,0},{2,3},{3,2},{4,5},{5,4},{6,7},{7,6},{8,9},{9,8},{10,11... | collective-permute-start | bytes 296 | tf_op jit(solution)/shard_map/ppermute | solution.py:542
  91.6 3.6 %collective-permute-start.14 = (f32[4,6]{1,0:T(4,128)S(1)}, f32[4,6]{1,0:T(4,128)S(1)}, u32[]{:S(2)}, u32[]{:S(2)}) collective-permute-start(f32[4,6]{1,0:T(4,128)S(1)} %pad_maximum_fusion.7), channel_id=1, source_target_pairs={{0,2},{1,3},{2,0},{3,1},{4,6},{5,7},{6,4},{7,5},{8,10},{9,11},{10,... | collective-permute-start | bytes 296 | tf_op jit(solution)/shard_map/ppermute | solution.py:542
  92.3 3.0 %collective-permute-start.15 = (f32[4,6]{1,0:T(4,128)S(1)}, f32[4,6]{1,0:T(4,128)S(1)}, u32[]{:S(2)}, u32[]{:S(2)}) collective-permute-start(f32[4,6]{1,0:T(4,128)S(1)} %pad_maximum_fusion.7), channel_id=1, source_target_pairs={{0,3},{1,2},{2,1},{3,0},{4,7},{5,6},{6,5},{7,4},{8,11},{9,10},{10,... | collective-permute-start | bytes 296 | tf_op jit(solution)/shard_map/ppermute | solution.py:542

commit v5 on v4

--- a/solution.py
+++ b/solution.py
@@ -64,18 +64,14 @@
         rows = slice(j * z_cells, (j + 1) * z_cells)
         slab[rows, 2 * j * LANES : (2 * j + 1) * LANES] = high
         slab[rows, (2 * j + 1) * LANES : (2 * j + 2) * LANES] = low
-    tables["slab_z"] = slab
-    tables["slab_y"] = row_table(k_y, np.arange(y_cells), n_y, -1.0, 1.0, True)
+    slab_y = row_table(k_y, np.arange(y_cells), n_y, -1.0, 1.0, True)
+    slab_y = np.pad(slab_y, ((0, 0), (0, slab.shape[1] - slab_y.shape[1])))
+    tables["slab_rows"] = np.concatenate([slab, slab_y], axis=0)
     own = np.arange(HALF, HALF + x_cells)
     halo = np.concatenate([np.arange(HALF), np.arange(HALF + x_cells, n_x)])
     tables["slab_x"] = row_table(k_x, np.concatenate([own, halo]), n_x, -1.0, 1.0, True)
     high, low = two_parts(depth_table(np.arange(TEMPL) - HALF, n_z, 1.0, 1.0))
-    tmpl = np.zeros((8, 2 * LANES, 2 * LANES), ml_dtypes.bfloat16)
-    for j in range(8):
-        start = TEMPL * j - (LANES if j >= 4 else 0)
-        tmpl[j, start : start + TEMPL, :LANES] = high
-        tmpl[j, start : start + TEMPL, LANES:] = low
-    tables["tmpl_z"] = tmpl
+    tables["tmpl_z"] = np.concatenate([high, low], axis=1)
     ones = (high.astype(np.float64) + low.astype(np.float64)).sum(axis=0)
     tables["ones_z"] = np.broadcast_to(ones.astype(np.float32)[None], (8, LANES)).copy()
     tables["tmpl_y"] = row_table(k_y, np.arange(TEMPL) - HALF + mid_y, n_y, 1.0, 1.0, True)
@@ -181,49 +177,37 @@
         turn(t, True)
 
 
-def slab_rows_kernel(dims, row_slices, *refs):
-    parts = len(row_slices)
-    if parts == 1:
-        ins, (rows_ref, mask_ref), scratch = refs[:4], refs[4:6], refs[6:]
-        depth_buf, parts_buf, slab_buf, valid_ref, z_ref, y_ref, sems = scratch
-        slab_refs = [slab_buf]
-        copies = [
-            pltpu.make_async_copy(source, target, sems.at[i])
-            for i, (source, target) in enumerate(zip(ins, (slab_buf, valid_ref, z_ref, y_ref)))
-        ]
-        for copy in copies:
-            copy.start()
-        for copy in copies:
-            copy.wait()
-    else:
-        slab_refs, (z_ref, y_ref, rows_ref, depth_buf, parts_buf) = refs[:parts], refs[parts:]
+def slab_rows_kernel(dims, place_ref, *refs):
+    sources, (table_ref, rows_ref, depth_buf, parts_buf) = refs[:-4], refs[-4:]
     x_cells, y_cells, z_cells = dims
-    count = sum(stop - start for start, stop in row_slices)
+    half = x_cells // 2
+    count = depth_buf.shape[0] // y_cells - 1
     n_y = y_cells + HALF
     pad_y = n_y // 2 + -(n_y // 2) % 8
     many = 4
 
-    if parts == 1:
-        valid = valid_ref[...].astype(F32)
-        low_lane = lax.broadcasted_iota(jnp.int32, (x_cells, LANES), 1) < z_cells
-        for q in range(y_cells // 2):
-            mask_ref[q] = jnp.where(low_lane, valid[:, 2 * q : 2 * q + 1], valid[:, 2 * q + 1 : 2 * q + 2])
+    def read(lanes):
+        if len(sources) == 1:
+            return sources[0][:, lanes].astype(F32)
+        first = (place_ref[0] & 1) == 0
+        mine, other = ([ref[i, :, lanes].astype(F32) for i in range(2)] for ref in sources)
+        low, high = (
+            jnp.concatenate([jnp.where(first, m, o), jnp.where(first, o, m)], axis=0)
+            for m, o in zip(mine, other)
+        )
+        return jnp.concatenate([low[x_cells - HALF :], high[:HALF]], axis=0)
 
     def depth_step(i):
-        top = 0
-        for ref, (start, stop) in zip(slab_refs, row_slices):
-            size = stop - start
-            lanes = [pl.ds(pl.multiple_of((many * i + u) * LANES, LANES), LANES) for u in range(many)]
-            block = jnp.concatenate([ref[:, l].astype(F32)[start:stop] for l in lanes], axis=0)
-            out = jnp.dot(block.astype(BF16), z_ref[...], preferred_element_type=F32)
-            for u in range(many):
-                part = out[u * size : (u + 1) * size]
-                for j in range(2):
-                    store(
-                        depth_buf, (2 * many * i + 2 * u + j) * odd(count) + top,
-                        lane_block(part, 2 * j) + lane_block(part, 2 * j + 1),
-                    )
-            top += size
+        lanes = [pl.ds(pl.multiple_of((many * i + u) * LANES, LANES), LANES) for u in range(many)]
+        block = jnp.concatenate([read(l) for l in lanes], axis=0).astype(BF16)
+        out = jnp.dot(block, table_ref[: 2 * z_cells], preferred_element_type=F32)
+        for u in range(many):
+            part = out[u * count : (u + 1) * count]
+            for j in range(2):
+                store(
+                    depth_buf, (2 * many * i + 2 * u + j) * odd(count),
+                    lane_block(part, 2 * j) + lane_block(part, 2 * j + 1),
+                )
 
     loop(y_cells // (2 * many), depth_step)
 
@@ -232,7 +216,7 @@
         parts_buf[slot] = split_rows(value, True)
 
     def y_step(i, slot):
-        plus, minus = pair_dot(y_ref[...], parts_buf[slot], True)
+        plus, minus = pair_dot(table_ref[2 * z_cells :, : 3 * y_cells], parts_buf[slot], True)
         for u in range(GROUP):
             start = (GROUP * i + u) * odd(2 * pad_y)
             store(rows_ref, start, lane_block(plus, u))
@@ -241,39 +225,29 @@
     pipeline(count // GROUP, [gather_rows, y_step], 2)
 
 
-def slab_rows(blocks, row_slices, valid, dims, tables, name):
+def slab_rows(place, blocks, count, dims, tables, name):
     x_cells, y_cells, z_cells = dims
-    count = sum(stop - start for start, stop in row_slices)
     n_y = y_cells + HALF
     pad_y = n_y // 2 + -(n_y // 2) % 8
     vmem = pl.BlockSpec(memory_space=pltpu.VMEM)
-    out_shape = [jax.ShapeDtypeStruct((count * odd(2 * pad_y), LANES), F32)]
-    scratch = [
-        pltpu.VMEM((y_cells * odd(count), LANES), F32),
-        pltpu.VMEM((2, 3 * y_cells, GROUP * LANES), BF16),
-    ]
-    slab_z, slab_y = tables["slab_z"], tables["slab_y"]
-    source = vmem
-    if valid is not None:
-        source = pl.BlockSpec(memory_space=pltpu.HBM)
-        for array in (blocks[0], valid, slab_z, slab_y):
-            scratch.append(pltpu.VMEM(array.shape, array.dtype))
-        scratch.append(pltpu.SemaphoreType.DMA((4,)))
-        blocks = blocks + [valid]
-        out_shape.append(jax.ShapeDtypeStruct((y_cells // 2, x_cells, LANES), F32))
     return pl.pallas_call(
-        functools.partial(slab_rows_kernel, dims, row_slices),
-        out_shape=tuple(out_shape),
-        in_specs=[source] * (2 + len(blocks)),
-        out_specs=(vmem,) * len(out_shape),
-        scratch_shapes=scratch,
+        functools.partial(slab_rows_kernel, dims),
+        out_shape=jax.ShapeDtypeStruct((count * odd(2 * pad_y), LANES), F32),
+        in_specs=[pl.BlockSpec(memory_space=pltpu.SMEM)] + [vmem] * (1 + len(blocks)),
+        out_specs=vmem,
+        scratch_shapes=[
+            pltpu.VMEM((y_cells * odd(count), LANES), F32),
+            pltpu.VMEM((2, 3 * y_cells, GROUP * LANES), BF16),
+        ],
         compiler_params=pltpu.CompilerParams(vmem_limit_bytes=20 * 1024 * 1024),
         cost_estimate=pl.CostEstimate(flops=count * 10**8, bytes_accessed=10**6, transcendentals=0),
         name=name,
-    )(*blocks, slab_z, slab_y)
-
-
-def slab_x_kernel(dims, own_ref, halo_ref, x_ref, spec_ref, parts_buf):
+    )(place, *blocks, tables["slab_rows"])
+
+
+def slab_x_kernel(
+    dims, own_ref, halo_ref, x_ref, valid_ref, tz_ref, spec_ref, mask_ref, z_ref, parts_buf
+):
     x_cells, y_cells, z_cells = dims
     n_y = y_cells + HALF
     pad_y = n_y // 2 + -(n_y // 2) % 8
@@ -299,8 +273,17 @@
 
     pipeline(n_y // GROUP, [gather_rows, x_step], 2)
 
-
-def slab_x(own, halo, dims, tables):
+    valid = valid_ref[...].astype(F32)
+    low_lane = lax.broadcasted_iota(jnp.int32, (x_cells, LANES), 1) < z_cells
+    for q in range(y_cells // 2):
+        mask_ref[q] = jnp.where(low_lane, valid[:, 2 * q : 2 * q + 1], valid[:, 2 * q + 1 : 2 * q + 2])
+    z_ref[...] = jnp.zeros(z_ref.shape, BF16)
+    for j in range(8):
+        start = TEMPL * j - (LANES if j >= 4 else 0)
+        z_ref[j, start : start + TEMPL, :] = tz_ref[...]
+
+
+def slab_x(own, halo, valid, dims, tables):
     x_cells, y_cells, z_cells = dims
     n_x, n_y = x_cells + TEMPL, y_cells + HALF
     steps = n_y // GROUP
@@ -308,14 +291,18 @@
     shape = (steps, 2, n_x, GROUP * LANES)
     return pl.pallas_call(
         functools.partial(slab_x_kernel, dims),
-        out_shape=jax.ShapeDtypeStruct(shape, F32),
-        in_specs=[vmem] * 3,
-        out_specs=vmem,
+        out_shape=(
+            jax.ShapeDtypeStruct(shape, F32),
+            jax.ShapeDtypeStruct((y_cells // 2, x_cells, LANES), F32),
+            jax.ShapeDtypeStruct((8, 2 * LANES, 2 * LANES), BF16),
+        ),
+        in_specs=[vmem] * 5,
+        out_specs=(vmem,) * 3,
         scratch_shapes=[pltpu.VMEM((2, 3 * n_x, GROUP * LANES), BF16)],
         compiler_params=pltpu.CompilerParams(vmem_limit_bytes=20 * 1024 * 1024),
         cost_estimate=pl.CostEstimate(flops=5 * 10**9, bytes_accessed=10**6, transcendentals=0),
         name="slab_x",
-    )(own, halo, tables["slab_x"])
+    )(own, halo, tables["slab_x"], valid, tables["tmpl_z"])
 
 
 def corr_kernel(
@@ -434,7 +421,7 @@
     stat_ref[...] = jnp.where(row == 0, number_sum, jnp.where(row == 1, total_sum, jnp.sum(square)))
 
 
-def correlate(place, bank, rot, mask, spec, dims, tables):
+def correlate(place, bank, rot, mask, spec, tmpl_z, dims, tables):
     x_cells, y_cells, z_cells = dims
     n_x, n_y = x_cells + TEMPL, y_cells + HALF
     pad_y = n_y // 2 + -(n_y // 2) % 8
@@ -464,7 +451,7 @@
         name="correlate",
     )(
         place, bank, mask, spec,
-        tables["tmpl_z"], tables["ones_z"], tables["tmpl_y"], tables["tmpl_x"],
+        tmpl_z, tables["ones_z"], tables["tmpl_y"], tables["tmpl_x"],
         tables["back_x"], tables["back_y"], tables["back_z"],
     )
 
@@ -568,31 +555,32 @@
     block = block[None]
     steps = gather_steps(tiles)
     block = gather_step(block, "tile", steps[0])
-    low, high = neighbours(tomogram, "tile")
+    half = x_cells // 2
+    piece = lax.dynamic_slice_in_dim(tomogram, (me & 1) * half, half, 0)
+    mine = jnp.stack(neighbours(piece, "tile"))
+    side_swap = [(i, i ^ 1) for i in range(groups)]
+    other = lax.ppermute(mine, "rot", side_swap)
     for step in steps[1:-1]:
         block = gather_step(block, "tile", step)
     one_hot = (rot_index[:, None] == jnp.arange(quats.shape[1], dtype=jnp.int32)[None, :]).astype(F32)
     orient = jnp.einsum("rq,kq->rk", one_hot, quats, precision=lax.Precision.HIGHEST)
     place = me_place = jnp.reshape(me, (1,)).astype(jnp.int32)
-    own, mask = slab_rows([tomogram], [(0, x_cells)], valid, dims, tables, "slab_own")
-    (halo,) = slab_rows(
-        [low, high], [(x_cells - HALF, x_cells), (0, HALF)], None, dims, tables, "slab_halo"
-    )
-    spec = slab_x(own, halo, dims, tables)
+    own = slab_rows(place, [tomogram], x_cells, dims, tables, "slab_own")
+    halo = slab_rows(place, [mine, other], TEMPL, dims, tables, "slab_halo")
+    spec, mask, tmpl_z = slab_x(own, halo, valid, dims, tables)
     block = gather_step(block, "tile", steps[-1])
     if not whole_rows:
         block = jnp.transpose(block, (1, 0, 2)).reshape(rots, 8, TEMPL // 8, row)
         block = jnp.transpose(block, (1, 0, 2, 3))
     bank = block.reshape(8, rots * (TEMPL // 8), row).astype(F32)
     far_swap = [(i, i ^ 2) for i in range(groups)]
-    side_swap = [(i, i ^ 1) for i in range(groups)]
     mines, sides, fars, from_sides, stats = [], [], [], [], []
     for r in range(rots):
         if r >= 2:
             place, fars[r - 2] = lax.optimization_barrier((place, fars[r - 2]))
         if r >= 3:
             place, from_sides[r - 3] = lax.optimization_barrier((place, from_sides[r - 3]))
-        mine, side, far, stat = correlate(place, bank, r, mask, spec, dims, tables)
+        mine, side, far, stat = correlate(place, bank, r, mask, spec, tmpl_z, dims, tables)
         if r >= 1:
             stat, fars[r - 1] = lax.optimization_barrier((stat, fars[r - 1]))
         if r >= 1 and r < rots - 1:
@@ -607,17 +595,19 @@
     state, fars[rots - 2], from_sides[rots - 3] = lax.optimization_barrier(
         (state, fars[rots - 2], from_sides[rots - 3])
     )
+    last = jnp.stack([part for r in range(rots - 2, rots) for part in (sides[r], fars[r][1])])
     step = 1
     while step < tiles:
-        swap_pairs = [(i, i ^ step) for i in range(tiles)]
-        state = merge(state, lax.ppermute(state, "tile", swap_pairs))
+        partner = lax.ppermute(state, "tile", [(i, i ^ step) for i in range(tiles)])
         step *= 2
+        if step == tiles:
+            partner, last = lax.optimization_barrier((partner, last))
+        state = merge(state, partner)
     average = state[1] / state[0]
     inverse = 1.0 / jnp.sqrt(state[2] / state[0] + EPSILON)
     coefs = jnp.concatenate([average[:, None], inverse[:, None], orient], axis=1)
     coefs = exchange_all(coefs, "rot", 1, groups)
-    last = [part for r in range(rots - 2, rots) for part in (sides[r], fars[r][1])]
-    last = lax.ppermute(jnp.stack(last), "rot", side_swap)
+    last = lax.ppermute(last, "rot", side_swap)
     from_sides += [last[:2], last[2:]]
     flat = mines + [f[0] for f in from_sides] + [f[0] for f in fars] + [f[1] for f in from_sides]
     return combine(me_place, coefs.reshape(groups * rots, 6), mask, flat)

time: 99.4 us -> 96.9 us (0.975)
  waiting for transfers between devices: 21.6 us -> 17.9 us
  starting transfers between devices: 21.6 us -> 24.4 us
    ppermute x4 -> x5, starting transfers between devices: 2.66 us -> 5.62 us  [the longest x3 5.54 us: local(): partner = lax.ppermute(state, 'tile', [(i, i ^ step) for i in range(tiles)])]
    ppermute x4 -> x5, waiting for transfers between devices: 9.04 us -> 6.61 us  [the longest x3 6.6 us: local(): partner = lax.ppermute(state, 'tile', [(i, i ^ step) for i in range(tiles)])]
    unnamed x26 -> x28, local copies, waits for them, and re-layouts: 4.39 us -> 2.6 us
    ppermute x3, waiting for transfers between devices: 10.4 us -> 9.1 us  [gather_step(): other = lax.ppermute(block, axis, [(i, i ^ step) for i in range(count)])]
    squeeze x3, local copies, waits for them, and re-layouts: 0.1 us -> 1.26 us  [local(): f[1]]
  transfers between devices with their start and end apart: 18 -> 19, of which waited for: 7 -> 8; matrix products, arithmetic and copies ran while one was open for 3% -> 2% of each run, Pallas kernels for 35% -> 35%
where the time goes in v5:
time: 96.9 us; the launch traced here: 96.6 us
  Pallas kernels  45.8 us (47%)
  starting transfers between devices  24.4 us (25%)
  waiting for transfers between devices  17.9 us (18%)
  local copies, waits for them, and re-layouts  6.09 us (6%)
  other arithmetic  1.12 us (1%)
  between operations  1.09 us (1%)
    pallas_call x4, Pallas kernels, correlate(): pl.pallas_call(functools.partial(corr_kernel, dims, rot), out_shape=(jax....  32.2 us
    ppermute x3, waiting for transfers between devices, gather_step(): other = lax.ppermute(block, axis, [(i, i ^ step) for i in range(count)])  9.1 us
    ppermute x3, waiting for transfers between devices, local(): partner = lax.ppermute(state, 'tile', [(i, i ^ step) for i in range(tiles)])  6.6 us
    pallas_call x2, Pallas kernels, slab_rows(): pl.pallas_call(functools.partial(slab_rows_kernel, dims), out_shape=jax.S...  5.6 us
    ppermute x3, starting transfers between devices, local(): partner = lax.ppermute(state, 'tile', [(i, i ^ step) for i in range(tiles)])  5.54 us
    ppermute x4, starting transfers between devices, local(): fars.append(lax.ppermute(far, 'rot', far_swap))  5.2 us
    ppermute x1, starting transfers between devices, neighbours(): lax.ppermute(block, axis, forward)  4.85 us
    ppermute x3, starting transfers between devices, gather_step(): other = lax.ppermute(block, axis, [(i, i ^ step) for i in range(count)])  4.84 us
  transfers between devices with their start and end apart: 19, of which 8 were waited for; matrix products, arithmetic and copies ran while one was open for 2% of the time, Pallas kernels for 35%

profile of v5, /device:TPU:0, one launch (start us, length us, event | category | flops | bytes accessed | tf_op | source)
XLA Modules:
  0.0 96.6 jit_solution(7065817257033055576)
XLA Ops:
  0.7 1.0 constant_dynamic-slice_fusion
  1.6 4.9 %collective-permute-start.3 = (bf16[16,5120]{1,0:T(8,128)(2,1)S(1)}, bf16[16,5120]{1,0:T(8,128)(2,1)S(1)}, u32[]{:S(2)}, u32[]{:S(2)}) collective-permute-start(bf16[16,5120]{1,0:T(8,128)(2,1)S(1)} %constant_dynamic-slice_fusion), channel_id=1, source_target_pairs={{0,4},{4,8},{8,12},{12,16},{16,20},{20,24},{24,28},{1,5},{5,9},{9,... | collective-permute-start | bytes 491528 | tf_op jit(solution)/shard_map/ppermute | solution.py:537
  6.5 1.3 %collective-permute-start.4 = (bf16[16,5120]{1,0:T(8,128)(2,1)S(1)}, bf16[16,5120]{1,0:T(8,128)(2,1)S(1)}, u32[]{:S(2)}, u32[]{:S(2)}) collective-permute-start(bf16[16,5120]{1,0:T(8,128)(2,1)S(1)} %constant_dynamic-slice_fusion), channel_id=1, source_target_pairs={{4,0},{8,4},{12,8},{16,12},{20,16},{24,20},{28,24},{5,1},{9,5},{13... | collective-permute-start | bytes 491528 | tf_op jit(solution)/shard_map/ppermute | solution.py:537
  7.8 1.0 %broadcast_in_dim_reshape.3 = bf16[1,24,2304]{2,1,0:T(8,128)(2,1)S(1)} reshape(bf16[4,13824]{1,0:T(4,128)(2,1)} %param.15) | data formatting | bytes 221184 | tf_op jit(solution)/shard_map/broadcast_in_dim;reshape | solution.py:555
  8.8 4.7 %collective-permute-start = (bf16[1,24,2304]{2,1,0:T(8,128)(2,1)S(1)}, bf16[1,24,2304]{2,1,0:T(8,128)(2,1)S(1)}, u32[]{:S(2)}, u32[]{:S(2)}) collective-permute-start(bf16[1,24,2304]{2,1,0:T(8,128)(2,1)S(1)} %broadcast_in_dim_reshape.3), channel_id=1, source_target_pairs={{0,16},{4,20},{8,24},{12,28},{16,0},{20,4},{24,8},{28,12},{1,17},{... | collective-permute-start | bytes 331784 | tf_op jit(solution)/shard_map/ppermute | solution.py:510
  13.5 1.0 %copy-done.1 = bf16[32,5120]{1,0:T(8,128)(2,1)S(1)} copy-done((bf16[32,5120]{1,0:T(8,128)(2,1)S(1)}, bf16[32,5120]{1,0:T(8,128)(2,1)}, u32[]{:S(2)}) %copy-start.1) | copy-done | bytes 327704
  14.4 0.9 copy-done.3
  15.4 2.3 %slab_own.1.own_ref = f32[3616,128]{1,0:T(8,128)S(1)} custom-call(s32[1]{0:T(128)} %bitcast.place_ref, bf16[32,5120]{1,0:T(8,128)(2,1)S(1)} %copy-done.1, bf16[240,512]{1,0:T(8,128)(2,1)S(1)} %copy-done.3), custom_call_target="tpu_custom_call" | custom-call | flops 3200000000 | bytes 1000000 | tf_op jit(solution)/shard_map/slab_own/pallas_call | solution.py:233
  17.9 2.8 %collective-permute-done = bf16[1,24,2304]{2,1,0:T(8,128)(2,1)S(1)} collective-permute-done((bf16[1,24,2304]{2,1,0:T(8,128)(2,1)S(1)}, bf16[1,24,2304]{2,1,0:T(8,128)(2,1)S(1)}, u32[]{:S(2)}, u32[]{:S(2)}) %collective-permute-start) | collective-permute-done | bytes 110624 | tf_op jit(solution)/shard_map/ppermute | solution.py:510
  21.1 5.8 %collective-permute-done.1 = bf16[2,24,2304]{2,1,0:T(8,128)(2,1)S(1)} collective-permute-done((bf16[2,24,2304]{2,1,0:T(8,128)(2,1)S(1)}, bf16[2,24,2304]{2,1,0:T(8,128)(2,1)S(1)}, u32[]{:S(2)}, u32[]{:S(2)}) %collective-permute-start.1) | collective-permute-done | bytes 221216 | tf_op jit(solution)/shard_map/ppermute | solution.py:510
  27.1 3.4 %slab_halo.1.halo_ref = f32[5424,128]{1,0:T(8,128)S(1)} custom-call(s32[1]{0:T(128)} %bitcast.place_ref, bf16[2,16,5120]{2,1,0:T(8,128)(2,1)S(1)} %pad_maximum_fusion.3.refs_0_, bf16[2,16,5120]{2,1,0:T(8,128)(2,1)S(1)} %collective-permute-done.5.refs_1_, bf16[240,512]{1,0:T(8,128)(2,1)S(1)} %copy-done.4), custom_call_target="tpu_custom_call" | custom-call | flops 4800000000 | bytes 1000000 | tf_op jit(solution)/shard_map/slab_halo/pallas_call | solution.py:233
  30.5 4.4 %slab_x.1 = (f32[13,2,80,1024]{3,2,1,0:T(8,128)S(1)}, f32[40,32,128]{2,1,0:T(8,128)S(1)}, bf16[8,256,256]{2,1,0:T(8,128)(2,1)S(1)}) custom-call(f32[3616,128]{1,0:T(8,128)S(1)} %slab_own.1.own_ref, f32[5424,128]{1,0:T(8,128)S(1)} %slab_halo.1.halo_ref, bf16[80,240]{1,0:T(8,128)(2,1)S(1)} %copy-done.9, s32[32,80]{1,0:T(8,128)S(1)} %copy-done.2, ...), custom_call_target="tpu_custom_call" | custom-call | flops 5000000000 | bytes 1000000 | tf_op jit(solution)/shard_map/slab_x/pallas_call | solution.py:292
  35.8 0.6 copy-done.5
  36.4 7.9 %correlate.4 = (f32[32,1280]{1,0:T(8,128)S(1)}, f32[32,1280]{1,0:T(8,128)S(1)}, f32[2,32,1280]{2,1,0:T(8,128)S(1)}, f32[8,128]{1,0:T(8,128)S(1)}) custom-call(s32[1]{0:T(128)} %bitcast.place_ref, f32[8,24,2304]{2,1,0:T(8,128)S(1)} %bitcast_convert_fusion.tmpl_ref, f32[40,32,128]{2,1,0:T(8,128)S(1)} %get-tuple-element.39.mask_ref, ...), custom_call_target="tpu_custom_call" | custom-call | flops 15000000512 | bytes 10000000 | tf_op jit(solution)/shard_map/correlate/pallas_call | solution.py:430
  44.4 1.6 %collective-permute-start.6 = (f32[2,32,1280]{2,1,0:T(8,128)S(1)}, f32[2,32,1280]{2,1,0:T(8,128)S(1)}, u32[]{:S(2)}, u32[]{:S(2)}) collective-permute-start(f32[2,32,1280]{2,1,0:T(8,128)S(1)} %get-tuple-element.44), channel_id=1, source_target_pairs={{0,2},{1,3},{2,0},{3,1},{4,6},{5,7},{6,4},{7,5},{8,10},{9,11},{10,... | collective-permute-start | bytes 983048 | tf_op jit(solution)/shard_map/ppermute | solution.py:591
  46.0 8.1 %correlate.5 = (f32[32,1280]{1,0:T(8,128)S(1)}, f32[32,1280]{1,0:T(8,128)S(1)}, f32[2,32,1280]{2,1,0:T(8,128)S(1)}, f32[8,128]{1,0:T(8,128)S(1)}) custom-call(s32[1]{0:T(128)} %bitcast.place_ref, f32[8,24,2304]{2,1,0:T(8,128)S(1)} %bitcast_convert_fusion.tmpl_ref, f32[40,32,128]{2,1,0:T(8,128)S(1)} %get-tuple-element.39.mask_ref, ...), custom_call_target="tpu_custom_call" | custom-call | flops 15000000512 | bytes 10000000 | tf_op jit(solution)/shard_map/correlate/pallas_call | solution.py:430
  54.1 0.6 collective-permute-start.7
  54.7 7.9 %correlate.6 = (f32[32,1280]{1,0:T(8,128)S(1)}, f32[32,1280]{1,0:T(8,128)S(1)}, f32[2,32,1280]{2,1,0:T(8,128)S(1)}, f32[8,128]{1,0:T(8,128)S(1)}) custom-call(s32[1]{0:T(128)} %bitcast.place_ref, f32[8,24,2304]{2,1,0:T(8,128)S(1)} %bitcast_convert_fusion.tmpl_ref, f32[40,32,128]{2,1,0:T(8,128)S(1)} %get-tuple-element.39.mask_ref, ...), custom_call_target="tpu_custom_call" | custom-call | flops 15000000512 | bytes 10000000 | tf_op jit(solution)/shard_map/correlate/pallas_call | solution.py:430
  62.8 0.6 collective-permute-start.8
  63.4 1.5 %collective-permute-start.9 = (f32[2,32,1280]{2,1,0:T(8,128)S(1)}, f32[2,32,1280]{2,1,0:T(8,128)S(1)}, u32[]{:S(2)}, u32[]{:S(2)}) collective-permute-start(f32[2,32,1280]{2,1,0:T(8,128)S(1)} %get-tuple-element.56), channel_id=1, source_target_pairs={{0,2},{1,3},{2,0},{3,1},{4,6},{5,7},{6,4},{7,5},{8,10},{9,11},{10,... | collective-permute-start | bytes 983048 | tf_op jit(solution)/shard_map/ppermute | solution.py:591
  64.9 8.2 %correlate.7 = (f32[32,1280]{1,0:T(8,128)S(1)}, f32[32,1280]{1,0:T(8,128)S(1)}, f32[2,32,1280]{2,1,0:T(8,128)S(1)}, f32[8,128]{1,0:T(8,128)S(1)}) custom-call(s32[1]{0:T(128)} %bitcast.place_ref, f32[8,24,2304]{2,1,0:T(8,128)S(1)} %bitcast_convert_fusion.tmpl_ref, f32[40,32,128]{2,1,0:T(8,128)S(1)} %get-tuple-element.39.mask_ref, ...), custom_call_target="tpu_custom_call" | custom-call | flops 15000000512 | bytes 10000000 | tf_op jit(solution)/shard_map/correlate/pallas_call | solution.py:430
  73.2 1.5 %collective-permute-start.14 = (f32[2,32,1280]{2,1,0:T(8,128)S(1)}, f32[2,32,1280]{2,1,0:T(8,128)S(1)}, u32[]{:S(2)}, u32[]{:S(2)}) collective-permute-start(f32[2,32,1280]{2,1,0:T(8,128)S(1)} %get-tuple-element.64), channel_id=1, source_target_pairs={{0,2},{1,3},{2,0},{3,1},{4,6},{5,7},{6,4},{7,5},{8,10},{9,11},{10,... | collective-permute-start | bytes 983048 | tf_op jit(solution)/shard_map/ppermute | solution.py:591
  74.8 1.5 %collective-permute-start.11 = (f32[3,4]{1,0:T(4,128)S(1)}, f32[3,4]{1,0:T(4,128)S(1)}, u32[]{:S(2)}, u32[]{:S(2)}) collective-permute-start(f32[3,4]{1,0:T(4,128)S(1)} %pad_maximum_fusion.7), channel_id=1, source_target_pairs={{0,4},{4,0},{8,12},{12,8},{16,20},{20,16},{24,28},{28,24},{1,5},{5... | collective-permute-start | bytes 152 | tf_op jit(solution)/shard_map/ppermute | solution.py:601
  76.3 2.0 %collective-permute-done.11 = f32[3,4]{1,0:T(4,128)S(1)} collective-permute-done((f32[3,4]{1,0:T(4,128)S(1)}, f32[3,4]{1,0:T(4,128)S(1)}, u32[]{:S(2)}, u32[]{:S(2)}) %collective-permute-start.11) | collective-permute-done | bytes 80 | tf_op jit(solution)/shard_map/ppermute | solution.py:601
  78.9 3.1 %collective-permute-done.12 = f32[3,4]{1,0:T(4,128)S(1)} collective-permute-done((f32[3,4]{1,0:T(4,128)S(1)}, f32[3,4]{1,0:T(4,128)S(1)}, u32[]{:S(2)}, u32[]{:S(2)}) %collective-permute-start.12) | collective-permute-done | bytes 80 | tf_op jit(solution)/shard_map/ppermute | solution.py:601
  82.1 3.6 %collective-permute-start.13 = (f32[3,4]{1,0:T(4,128)S(1)}, f32[3,4]{1,0:T(4,128)S(1)}, u32[]{:S(2)}, u32[]{:S(2)}) collective-permute-start(f32[3,4]{1,0:T(4,128)S(1)} %select_add_fusion.1), channel_id=1, source_target_pairs={{0,16},{4,20},{8,24},{12,28},{16,0},{20,4},{24,8},{28,12},{1,17},{... | collective-permute-start | bytes 152 | tf_op jit(solution)/shard_map/ppermute | solution.py:601
  85.7 1.5 %collective-permute-done.13 = f32[3,4]{1,0:T(4,128)S(1)} collective-permute-done((f32[3,4]{1,0:T(4,128)S(1)}, f32[3,4]{1,0:T(4,128)S(1)}, u32[]{:S(2)}, u32[]{:S(2)}) %collective-permute-start.13) | collective-permute-done | bytes 80 | tf_op jit(solution)/shard_map/ppermute | solution.py:601
  88.1 0.6 collective-permute-start.16
  88.7 0.9 collective-permute-start.17
  89.6 2.1 %collective-permute-done.16 = f32[4,6]{1,0:T(4,128)S(1)} collective-permute-done((f32[4,6]{1,0:T(4,128)S(1)}, f32[4,6]{1,0:T(4,128)S(1)}, u32[]{:S(2)}, u32[]{:S(2)}) %collective-permute-start.16) | collective-permute-done | bytes 128 | tf_op jit(solution)/shard_map/ppermute | solution.py:529
  91.8 1.2 %slice_bitcast_fusion = (f32[32,1280]{1,0:T(8,128)S(1)}, f32[32,1280]{1,0:T(8,128)S(1)}, f32[32,1280]{1,0:T(8,128)S(1)}, f32[32,1280]{1,0:T(8,128)S(1)}) fusion(f32[4,32,1280]{2,1,0:T(8,128)} %collective-permute-done.18), kind=kLoop, calls=%fused_computation.12 | loop fusion | bytes 1310720 | tf_op jit(solution)/shard_map/squeeze | solution.py:612
  93.0 3.6 %combine.1 = (f32[32,1280]{1,0:T(8,128)}, f32[32,1280]{1,0:T(8,128)}, f32[4,32,1280]{2,1,0:T(8,128)}) custom-call(s32[1]{0:T(128)} %bitcast.place_ref, f32[16,6]{1,0:T(8,128)S(1)} %bitcast.78, f32[40,32,128]{2,1,0:T(8,128)S(1)} %get-tuple-element.39.mask_ref, f32[32,1280]{1,0:T(8,128)S(1)} %get-tuple-element.66.refs_0_, ...), custom_call_target="tpu_custom_call" | custom-call | tf_op jit(solution)/shard_map/combine/pallas_call | solution.py:494
  (83 shorter events, 3.8 us)
Async XLA Ops:
  0.6 17.0 %copy-start = (f32[4,4096]{1,0:T(4,128)S(1)}, f32[4,4096]{1,0:T(4,128)}, u32[]{:S(2)}) copy-start(f32[4,4096]{1,0:T(4,128)} %param.17) | copy-start | bytes 196612
  1.6 19.3 %collective-permute-start.3 = (bf16[16,5120]{1,0:T(8,128)(2,1)S(1)}, bf16[16,5120]{1,0:T(8,128)(2,1)S(1)}, u32[]{:S(2)}, u32[]{:S(2)}) collective-permute-start(bf16[16,5120]{1,0:T(8,128)(2,1)S(1)} %constant_dynamic-slice_fusion), channel_id=1, source_target_pairs={{0,4},{4,8},{8,12},{12,16},{16,20},{20,24},{24,28},{1,5},{5,9},{9,... | collective-permute-start | bytes 491528 | tf_op jit(solution)/shard_map/ppermute | solution.py:537
  6.5 14.5 %collective-permute-start.4 = (bf16[16,5120]{1,0:T(8,128)(2,1)S(1)}, bf16[16,5120]{1,0:T(8,128)(2,1)S(1)}, u32[]{:S(2)}, u32[]{:S(2)}) collective-permute-start(bf16[16,5120]{1,0:T(8,128)(2,1)S(1)} %constant_dynamic-slice_fusion), channel_id=1, source_target_pairs={{4,0},{8,4},{12,8},{16,12},{20,16},{24,20},{28,24},{5,1},{9,5},{13... | collective-permute-start | bytes 491528 | tf_op jit(solution)/shard_map/ppermute | solution.py:537
  8.8 12.0 %collective-permute-start = (bf16[1,24,2304]{2,1,0:T(8,128)(2,1)S(1)}, bf16[1,24,2304]{2,1,0:T(8,128)(2,1)S(1)}, u32[]{:S(2)}, u32[]{:S(2)}) collective-permute-start(bf16[1,24,2304]{2,1,0:T(8,128)(2,1)S(1)} %broadcast_in_dim_reshape.3), channel_id=1, source_target_pairs={{0,16},{4,20},{8,24},{12,28},{16,0},{20,4},{24,8},{28,12},{1,17},{... | collective-permute-start | bytes 331784 | tf_op jit(solution)/shard_map/ppermute | solution.py:510
  13.5 1.0 %copy-start.1 = (bf16[32,5120]{1,0:T(8,128)(2,1)S(1)}, bf16[32,5120]{1,0:T(8,128)(2,1)}, u32[]{:S(2)}) copy-start(bf16[32,5120]{1,0:T(8,128)(2,1)} %refs_0_.1) | copy-start | bytes 983044
  14.4 0.9 copy-start.3
  15.4 2.3 %copy-start.13 = (s32[4]{0:T(128)S(1)}, s32[4]{0:T(128)}, u32[]{:S(2)}) copy-start(s32[4]{0:T(128)} %param.18) | copy-start | bytes 52
  20.8 6.3 %copy-start.4 = (bf16[240,512]{1,0:T(8,128)(2,1)S(1)}, bf16[240,512]{1,0:T(8,128)(2,1)}, u32[]{:S(2)}) copy-start(bf16[240,512]{1,0:T(8,128)(2,1)} %constant.47.clone.refs_1_.refs_2_) | copy-start | bytes 737284
  20.8 6.0 %collective-permute-start.1 = (bf16[2,24,2304]{2,1,0:T(8,128)(2,1)S(1)}, bf16[2,24,2304]{2,1,0:T(8,128)(2,1)S(1)}, u32[]{:S(2)}, u32[]{:S(2)}) collective-permute-start(bf16[2,24,2304]{2,1,0:T(8,128)(2,1)S(1)} %maximum_bitcast_fusion), channel_id=1, source_target_pairs={{0,8},{4,12},{8,0},{12,4},{16,24},{20,28},{24,16},{28,20},{1,9},{5... | collective-permute-start | bytes 663560 | tf_op jit(solution)/shard_map/ppermute | solution.py:510
  21.0 6.1 %collective-permute-start.5 = (bf16[2,16,5120]{2,1,0:T(8,128)(2,1)S(1)}, bf16[2,16,5120]{2,1,0:T(8,128)(2,1)S(1)}, u32[]{:S(2)}, u32[]{:S(2)}) collective-permute-start(bf16[2,16,5120]{2,1,0:T(8,128)(2,1)S(1)} %pad_maximum_fusion.3.refs_0_), channel_id=1, source_target_pairs={{0,1},{1,0},{2,3},{3,2},{4,5},{5,4},{6,7},{7,6},{8,9},{9,8},{10,11... | collective-permute-start | bytes 983048 | tf_op jit(solution)/shard_map/ppermute | solution.py:562
  27.0 3.5 %copy-start.2 = (s32[32,80]{1,0:T(8,128)S(1)}, s32[32,80]{1,0:T(8,128)}, u32[]{:S(2)}) copy-start(s32[32,80]{1,0:T(8,128)} %valid_ref.1) | copy-start | bytes 30724
  27.0 3.5 %copy-start.9 = (bf16[80,240]{1,0:T(8,128)(2,1)S(1)}, bf16[80,240]{1,0:T(8,128)(2,1)}, u32[]{:S(2)}) copy-start(bf16[80,240]{1,0:T(8,128)(2,1)} %constant.48.clone.x_ref) | copy-start | bytes 115204
  27.0 3.5 %copy-start.11 = (bf16[48,256]{1,0:T(8,128)(2,1)S(1)}, bf16[48,256]{1,0:T(8,128)(2,1)}, u32[]{:S(2)}) copy-start(bf16[48,256]{1,0:T(8,128)(2,1)} %constant.49.clone.tz_ref) | copy-start | bytes 73732
  27.0 8.4 %collective-permute-start.2 = (bf16[4,24,2304]{2,1,0:T(8,128)(2,1)S(1)}, bf16[4,24,2304]{2,1,0:T(8,128)(2,1)S(1)}, u32[]{:S(2)}, u32[]{:S(2)}) collective-permute-start(bf16[4,24,2304]{2,1,0:T(8,128)(2,1)S(1)} %bitcast.79), channel_id=1, source_target_pairs={{0,4},{4,0},{8,12},{12,8},{16,20},{20,16},{24,28},{28,24},{1,5},{5... | collective-permute-start | bytes 1327112 | tf_op jit(solution)/shard_map/ppermute | solution.py:510
  35.5 0.9 copy-start.5
  35.5 0.9 copy-start.6
  35.5 0.9 copy-start.7
  35.5 0.9 copy-start.8
  35.5 0.9 copy-start.10
  44.4 10.3 %collective-permute-start.6 = (f32[2,32,1280]{2,1,0:T(8,128)S(1)}, f32[2,32,1280]{2,1,0:T(8,128)S(1)}, u32[]{:S(2)}, u32[]{:S(2)}) collective-permute-start(f32[2,32,1280]{2,1,0:T(8,128)S(1)} %get-tuple-element.44), channel_id=1, source_target_pairs={{0,2},{1,3},{2,0},{3,1},{4,6},{5,7},{6,4},{7,5},{8,10},{9,11},{10,... | collective-permute-start | bytes 983048 | tf_op jit(solution)/shard_map/ppermute | solution.py:591
  54.1 8.5 %collective-permute-start.7 = (f32[2,32,1280]{2,1,0:T(8,128)S(1)}, f32[2,32,1280]{2,1,0:T(8,128)S(1)}, u32[]{:S(2)}, u32[]{:S(2)}) collective-permute-start(f32[2,32,1280]{2,1,0:T(8,128)S(1)} %get-tuple-element.49), channel_id=1, source_target_pairs={{0,2},{1,3},{2,0},{3,1},{4,6},{5,7},{6,4},{7,5},{8,10},{9,11},{10,... | collective-permute-start | bytes 983048 | tf_op jit(solution)/shard_map/ppermute | solution.py:591
  62.7 10.5 %collective-permute-start.10 = (f32[2,32,1280]{2,1,0:T(8,128)S(1)}, f32[2,32,1280]{2,1,0:T(8,128)S(1)}, u32[]{:S(2)}, u32[]{:S(2)}) collective-permute-start(f32[2,32,1280]{2,1,0:T(8,128)S(1)} %pad_maximum_fusion.5), channel_id=1, source_target_pairs={{0,1},{1,0},{2,3},{3,2},{4,5},{5,4},{6,7},{7,6},{8,9},{9,8},{10,11... | collective-permute-start | bytes 983048 | tf_op jit(solution)/shard_map/ppermute | solution.py:593
  62.8 2.1 %collective-permute-start.8 = (f32[2,32,1280]{2,1,0:T(8,128)S(1)}, f32[2,32,1280]{2,1,0:T(8,128)S(1)}, u32[]{:S(2)}, u32[]{:S(2)}) collective-permute-start(f32[2,32,1280]{2,1,0:T(8,128)S(1)} %pad_maximum_fusion.4), channel_id=1, source_target_pairs={{0,1},{1,0},{2,3},{3,2},{4,5},{5,4},{6,7},{7,6},{8,9},{9,8},{10,11... | collective-permute-start | bytes 983048 | tf_op jit(solution)/shard_map/ppermute | solution.py:593
  63.4 9.7 %collective-permute-start.9 = (f32[2,32,1280]{2,1,0:T(8,128)S(1)}, f32[2,32,1280]{2,1,0:T(8,128)S(1)}, u32[]{:S(2)}, u32[]{:S(2)}) collective-permute-start(f32[2,32,1280]{2,1,0:T(8,128)S(1)} %get-tuple-element.56), channel_id=1, source_target_pairs={{0,2},{1,3},{2,0},{3,1},{4,6},{5,7},{6,4},{7,5},{8,10},{9,11},{10,... | collective-permute-start | bytes 983048 | tf_op jit(solution)/shard_map/ppermute | solution.py:591
  73.2 12.4 %collective-permute-start.14 = (f32[2,32,1280]{2,1,0:T(8,128)S(1)}, f32[2,32,1280]{2,1,0:T(8,128)S(1)}, u32[]{:S(2)}, u32[]{:S(2)}) collective-permute-start(f32[2,32,1280]{2,1,0:T(8,128)S(1)} %get-tuple-element.64), channel_id=1, source_target_pairs={{0,2},{1,3},{2,0},{3,1},{4,6},{5,7},{6,4},{7,5},{8,10},{9,11},{10,... | collective-permute-start | bytes 983048 | tf_op jit(solution)/shard_map/ppermute | solution.py:591
  74.8 3.6 %collective-permute-start.11 = (f32[3,4]{1,0:T(4,128)S(1)}, f32[3,4]{1,0:T(4,128)S(1)}, u32[]{:S(2)}, u32[]{:S(2)}) collective-permute-start(f32[3,4]{1,0:T(4,128)S(1)} %pad_maximum_fusion.7), channel_id=1, source_target_pairs={{0,4},{4,0},{8,12},{12,8},{16,20},{20,16},{24,28},{28,24},{1,5},{5... | collective-permute-start | bytes 152 | tf_op jit(solution)/shard_map/ppermute | solution.py:601
  78.4 3.6 %collective-permute-start.12 = (f32[3,4]{1,0:T(4,128)S(1)}, f32[3,4]{1,0:T(4,128)S(1)}, u32[]{:S(2)}, u32[]{:S(2)}) collective-permute-start(f32[3,4]{1,0:T(4,128)S(1)} %select_add_fusion.2), channel_id=1, source_target_pairs={{0,8},{4,12},{8,0},{12,4},{16,24},{20,28},{24,16},{28,20},{1,9},{5... | collective-permute-start | bytes 152 | tf_op jit(solution)/shard_map/ppermute | solution.py:601
  82.1 5.1 %collective-permute-start.13 = (f32[3,4]{1,0:T(4,128)S(1)}, f32[3,4]{1,0:T(4,128)S(1)}, u32[]{:S(2)}, u32[]{:S(2)}) collective-permute-start(f32[3,4]{1,0:T(4,128)S(1)} %select_add_fusion.1), channel_id=1, source_target_pairs={{0,16},{4,20},{8,24},{12,28},{16,0},{20,4},{24,8},{28,12},{1,17},{... | collective-permute-start | bytes 152 | tf_op jit(solution)/shard_map/ppermute | solution.py:601
  87.2 4.5 %collective-permute-start.18 = (f32[4,32,1280]{2,1,0:T(8,128)S(1)}, f32[4,32,1280]{2,1,0:T(8,128)}, u32[]{:S(2)}, u32[]{:S(2)}) collective-permute-start(f32[4,32,1280]{2,1,0:T(8,128)S(1)} %pad_maximum_fusion.1), channel_id=1, source_target_pairs={{0,1},{1,0},{2,3},{3,2},{4,5},{5,4},{6,7},{7,6},{8,9},{9,8},{10,11... | collective-permute-start | bytes 1966088 | tf_op jit(solution)/shard_map/ppermute | solution.py:610
  87.6 2.0 %collective-permute-start.15 = (f32[4,6]{1,0:T(4,128)S(1)}, f32[4,6]{1,0:T(4,128)S(1)}, u32[]{:S(2)}, u32[]{:S(2)}) collective-permute-start(f32[4,6]{1,0:T(4,128)S(1)} %pad_maximum_fusion.8), channel_id=1, source_target_pairs={{0,1},{1,0},{2,3},{3,2},{4,5},{5,4},{6,7},{7,6},{8,9},{9,8},{10,11... | collective-permute-start | bytes 296 | tf_op jit(solution)/shard_map/ppermute | solution.py:529
  88.1 3.6 %collective-permute-start.16 = (f32[4,6]{1,0:T(4,128)S(1)}, f32[4,6]{1,0:T(4,128)S(1)}, u32[]{:S(2)}, u32[]{:S(2)}) collective-permute-start(f32[4,6]{1,0:T(4,128)S(1)} %pad_maximum_fusion.8), channel_id=1, source_target_pairs={{0,2},{1,3},{2,0},{3,1},{4,6},{5,7},{6,4},{7,5},{8,10},{9,11},{10,... | collective-permute-start | bytes 296 | tf_op jit(solution)/shard_map/ppermute | solution.py:529
  88.7 3.0 %collective-permute-start.17 = (f32[4,6]{1,0:T(4,128)S(1)}, f32[4,6]{1,0:T(4,128)S(1)}, u32[]{:S(2)}, u32[]{:S(2)}) collective-permute-start(f32[4,6]{1,0:T(4,128)S(1)} %pad_maximum_fusion.8), channel_id=1, source_target_pairs={{0,3},{1,2},{2,1},{3,0},{4,7},{5,6},{6,5},{7,4},{8,11},{9,10},{10,... | collective-permute-start | bytes 296 | tf_op jit(solution)/shard_map/ppermute | solution.py:529
  (1 other events, 0.9 us)

commit v6 on v5

--- a/solution.py
+++ b/solution.py
@@ -15,6 +15,11 @@
 EPSILON = 1e-06
 LANES = 128
 SPLIT = 64
+BLOCKS = 8
+EACH = TEMPL // BLOCKS
+CHUNKS = TEMPL * TEMPL // LANES
+BLOCK_ROWS = EACH * CHUNKS + -EACH * CHUNKS % 16
+HELD = (0, 4, 2, 6)
 F32 = jnp.float32
 BF16 = jnp.bfloat16
 
@@ -75,7 +80,8 @@
     ones = (high.astype(np.float64) + low.astype(np.float64)).sum(axis=0)
     tables["ones_z"] = np.broadcast_to(ones.astype(np.float32)[None], (8, LANES)).copy()
     tables["tmpl_y"] = row_table(k_y, np.arange(TEMPL) - HALF + mid_y, n_y, 1.0, 1.0, True)
-    tables["tmpl_x"] = row_table(k_x, np.arange(TEMPL) + mid_x, n_x, 1.0, 1.0, True)
+    tmpl_rows = np.arange(TEMPL).reshape(BLOCKS, EACH).T.reshape(-1)
+    tables["tmpl_x"] = row_table(k_x, tmpl_rows + mid_x, n_x, 1.0, 1.0, True)
     tables["back_x"] = row_table(half_odd(x_cells), both_x, n_x, 1.0, 1.0 / n_x, False)
     tables["back_y"] = row_table(half_odd(y_cells), both_y, n_y, 1.0, 1.0 / n_y, False)
     back = depth_table(np.arange(z_cells), n_z, -1.0, 2.0 / n_z).T
@@ -306,18 +312,25 @@
 
 
 def corr_kernel(
-    dims, rot, place_ref, tmpl_ref, mask_ref, spec_ref,
+    dims, rot, entry, place_ref, held_ref, last_ref, mask_ref, spec_ref,
     z_ref, ones_ref, y_ref, x_ref, bx_ref, by_ref, bz_ref,
     mine_ref, side_ref, far_ref, stat_ref,
-    depth_buf, rows_buf, first_buf, second_buf, third_buf, back_buf, vol_buf,
+    bank_buf, depth_buf, rows_buf, first_buf, second_buf, third_buf, back_buf, vol_buf,
 ):
     x_cells, y_cells, z_cells = dims
     n_x, n_y = x_cells + TEMPL, y_cells + HALF
     half_y = n_y // 2
     pad_y = half_y + -half_y % 8
-    each = TEMPL // 8
-    rows = slice(rot * each, (rot + 1) * each)
-    tmpl = jnp.concatenate([tmpl_ref[t, rows, :] for t in range(8)], axis=0)
+    for i, block in enumerate(HELD):
+        for ref, at, tile in ((held_ref, rot, block), (last_ref, entry, block ^ 1)):
+            store(bank_buf, (place_ref[1] ^ tile) * odd(BLOCK_ROWS), ref[at, i].astype(F32))
+    tmpl = jnp.concatenate(
+        [
+            pick(bank_buf, [a * CHUNKS + i for i in range(CHUNKS)], BLOCKS, odd(BLOCK_ROWS))
+            for a in range(EACH)
+        ],
+        axis=0,
+    )
     inv_size = 1.0 / TEMPL**3
     mean = jnp.sum(tmpl) * inv_size
     centred = tmpl - mean
@@ -421,23 +434,24 @@
     stat_ref[...] = jnp.where(row == 0, number_sum, jnp.where(row == 1, total_sum, jnp.sum(square)))
 
 
-def correlate(place, bank, rot, mask, spec, tmpl_z, dims, tables):
+def correlate(place, held, rot, last, entry, mask, spec, tmpl_z, dims, tables):
     x_cells, y_cells, z_cells = dims
     n_x, n_y = x_cells + TEMPL, y_cells + HALF
     pad_y = n_y // 2 + -(n_y // 2) % 8
     width = y_cells * z_cells // 4
     vmem = pl.BlockSpec(memory_space=pltpu.VMEM)
     return pl.pallas_call(
-        functools.partial(corr_kernel, dims, rot),
+        functools.partial(corr_kernel, dims, rot, entry),
         out_shape=(
             jax.ShapeDtypeStruct((x_cells, width), F32),
             jax.ShapeDtypeStruct((x_cells, width), F32),
             jax.ShapeDtypeStruct((2, x_cells, width), F32),
             jax.ShapeDtypeStruct((8, LANES), F32),
         ),
-        in_specs=[pl.BlockSpec(memory_space=pltpu.SMEM)] + [vmem] * 10,
+        in_specs=[pl.BlockSpec(memory_space=pltpu.SMEM)] + [vmem] * 11,
         out_specs=(vmem,) * 4,
         scratch_shapes=[
+            pltpu.VMEM((BLOCKS * odd(BLOCK_ROWS), LANES), F32),
             pltpu.VMEM((TEMPL * odd(TEMPL), LANES), F32),
             pltpu.VMEM((TEMPL * odd(2 * pad_y), LANES), F32),
             pltpu.VMEM((2, 3 * TEMPL, GROUP * LANES), BF16),
@@ -450,14 +464,13 @@
         cost_estimate=pl.CostEstimate(flops=15 * 10**9, bytes_accessed=10**7, transcendentals=0),
         name="correlate",
     )(
-        place, bank, mask, spec,
+        place, held, last, mask, spec,
         tmpl_z, tables["ones_z"], tables["tmpl_y"], tables["tmpl_x"],
         tables["back_x"], tables["back_y"], tables["back_z"],
     )
 
 
-def score_kernel(place_ref, coef_ref, mask_ref, *refs):
-    pieces = refs[: len(refs) - 3]
+def score_kernel(pieces, place_ref, coef_ref, mask_ref, *refs):
     best_ref, evid_ref, mom_ref = refs[len(refs) - 3 :]
 
     blocks = best_ref.shape[1] // LANES
@@ -468,8 +481,9 @@
             rows = slice(top, top + 8)
             mask = mask_ref[place_ref[0] * blocks + i, rows]
             scores = []
-            for k, piece in enumerate(pieces):
-                scores.append((piece[rows, lanes] - coef_ref[k, 0]) * coef_ref[k, 1])
+            for k, (at, entry) in enumerate(pieces):
+                corr = refs[at][rows, lanes] if entry is None else refs[at][entry, rows, lanes]
+                scores.append((corr - coef_ref[k, 0]) * coef_ref[k, 1])
             high = functools.reduce(jnp.maximum, scores)
             total = jnp.zeros_like(high)
             moment = [jnp.zeros_like(high) for _ in range(4)]
@@ -487,30 +501,37 @@
     loop(blocks, step)
 
 
-def combine(place, coefs, mask, pieces):
-    shape = pieces[0].shape
+def combine(place, coefs, mask, arrays, pieces):
+    shape = arrays[0].shape
     vmem = pl.BlockSpec(memory_space=pltpu.VMEM)
     out = jax.ShapeDtypeStruct(shape, F32)
     return pl.pallas_call(
-        score_kernel,
+        functools.partial(score_kernel, pieces),
         out_shape=(out, out, jax.ShapeDtypeStruct((4,) + shape, F32)),
-        in_specs=[pl.BlockSpec(memory_space=pltpu.SMEM)] * 2 + [vmem] * (1 + len(pieces)),
+        in_specs=[pl.BlockSpec(memory_space=pltpu.SMEM)] * 2 + [vmem] * (1 + len(arrays)),
         out_specs=(vmem,) * 3,
         compiler_params=pltpu.CompilerParams(vmem_limit_bytes=16 * 1024 * 1024),
         name="combine",
-    )(place, coefs, mask, *pieces)
-
-
-def gather_steps(count):
-    return [1 << i for i in reversed(range(count.bit_length() - 1))]
-
-
-def gather_step(block, axis, step):
-    count = lax.axis_size(axis)
-    other = lax.ppermute(block, axis, [(i, i ^ step) for i in range(count)])
-    upper = (lax.axis_index(axis) & step) != 0
-    pair = [jnp.where(upper, other, block), jnp.where(upper, block, other)]
-    return jnp.stack(pair, axis=1).reshape((-1,) + block.shape[1:])
+    )(place, coefs, mask, *arrays)
+
+
+def swap_blocks(block, axis, step):
+    return lax.ppermute(block, axis, [(i, i ^ step) for i in range(lax.axis_size(axis))])
+
+
+def general_gather(templates):
+    rots = templates.shape[0]
+    count = lax.axis_size("tile")
+    block = templates[:, None]
+    for step in [1 << i for i in reversed(range(count.bit_length() - 1))]:
+        other = swap_blocks(block, "tile", step)
+        upper = (lax.axis_index("tile") & step) != 0
+        pair = [jnp.where(upper, other, block), jnp.where(upper, block, other)]
+        block = jnp.stack(pair, axis=2).reshape((rots, -1) + block.shape[2:])
+    block = block.reshape(rots, BLOCKS, EACH * CHUNKS, LANES)
+    block = jnp.pad(block, ((0, 0), (0, 0), (0, BLOCK_ROWS - EACH * CHUNKS), (0, 0)))
+    held = jnp.stack([block[:, i] for i in HELD], axis=1)
+    return held, jnp.stack([block[:, i ^ 1] for i in HELD], axis=1)
 
 
 def merge(first, other):
@@ -548,54 +569,53 @@
     me = lax.axis_index("rot")
     rots = templates.shape[0]
 
-    row = TEMPL * TEMPL
-    chunk = templates.shape[1]
-    whole_rows = chunk % row == 0
-    block = templates.reshape(rots * chunk // row, row) if whole_rows else templates
-    block = block[None]
-    steps = gather_steps(tiles)
-    block = gather_step(block, "tile", steps[0])
+    tile = lax.axis_index("tile")
+    by_blocks = tiles == BLOCKS
+    if by_blocks:
+        held = templates.reshape(rots, 1, EACH * CHUNKS, LANES)
+        held = jnp.pad(held, ((0, 0), (0, 0), (0, BLOCK_ROWS - EACH * CHUNKS), (0, 0)))
+        held = jnp.concatenate([held, swap_blocks(held, "tile", 4)], axis=1)
     half = x_cells // 2
     piece = lax.dynamic_slice_in_dim(tomogram, (me & 1) * half, half, 0)
     mine = jnp.stack(neighbours(piece, "tile"))
     side_swap = [(i, i ^ 1) for i in range(groups)]
     other = lax.ppermute(mine, "rot", side_swap)
-    for step in steps[1:-1]:
-        block = gather_step(block, "tile", step)
+    if by_blocks:
+        held = jnp.concatenate([held, swap_blocks(held, "tile", 2)], axis=1)
+    else:
+        held, last = general_gather(templates)
+        tile = jnp.zeros_like(tile)
     one_hot = (rot_index[:, None] == jnp.arange(quats.shape[1], dtype=jnp.int32)[None, :]).astype(F32)
     orient = jnp.einsum("rq,kq->rk", one_hot, quats, precision=lax.Precision.HIGHEST)
-    place = me_place = jnp.reshape(me, (1,)).astype(jnp.int32)
+    place = me_place = jnp.stack([me, tile]).astype(jnp.int32)
     own = slab_rows(place, [tomogram], x_cells, dims, tables, "slab_own")
     halo = slab_rows(place, [mine, other], TEMPL, dims, tables, "slab_halo")
+    if by_blocks:
+        held, halo = lax.optimization_barrier((held, halo))
+        lasts = [swap_blocks(held[:1], "tile", 1), swap_blocks(held[1:], "tile", 1)]
+    else:
+        lasts = [last[:1], last[1:]]
     spec, mask, tmpl_z = slab_x(own, halo, valid, dims, tables)
-    block = gather_step(block, "tile", steps[-1])
-    if not whole_rows:
-        block = jnp.transpose(block, (1, 0, 2)).reshape(rots, 8, TEMPL // 8, row)
-        block = jnp.transpose(block, (1, 0, 2, 3))
-    bank = block.reshape(8, rots * (TEMPL // 8), row).astype(F32)
     far_swap = [(i, i ^ 2) for i in range(groups)]
-    mines, sides, fars, from_sides, stats = [], [], [], [], []
+    mines, sides, fars, stats = [], [], [], []
     for r in range(rots):
         if r >= 2:
             place, fars[r - 2] = lax.optimization_barrier((place, fars[r - 2]))
-        if r >= 3:
-            place, from_sides[r - 3] = lax.optimization_barrier((place, from_sides[r - 3]))
-        mine, side, far, stat = correlate(place, bank, r, mask, spec, tmpl_z, dims, tables)
+        mine, side, far, stat = correlate(
+            place, held, r, lasts[min(r, 1)], max(r - 1, 0), mask, spec, tmpl_z, dims, tables
+        )
         if r >= 1:
             stat, fars[r - 1] = lax.optimization_barrier((stat, fars[r - 1]))
-        if r >= 1 and r < rots - 1:
-            both = jnp.stack([sides[r - 1], fars[r - 1][1]])
         mines.append(mine)
         sides.append(side)
         stats.append(stat[:3, 0])
         fars.append(lax.ppermute(far, "rot", far_swap))
-        if r >= 1 and r < rots - 1:
-            from_sides.append(lax.ppermute(both, "rot", side_swap))
+        if r == rots - 2:
+            early = jnp.stack(sides + [f[1] for f in fars[:-1]])
+            early = lax.ppermute(early, "rot", side_swap)
     state = jnp.stack(stats, axis=1)
-    state, fars[rots - 2], from_sides[rots - 3] = lax.optimization_barrier(
-        (state, fars[rots - 2], from_sides[rots - 3])
-    )
-    last = jnp.stack([part for r in range(rots - 2, rots) for part in (sides[r], fars[r][1])])
+    state, early, fars[rots - 2] = lax.optimization_barrier((state, early, fars[rots - 2]))
+    last = jnp.stack([sides[rots - 1], fars[rots - 2][1], fars[rots - 1][1]])
     step = 1
     while step < tiles:
         partner = lax.ppermute(state, "tile", [(i, i ^ step) for i in range(tiles)])
@@ -608,9 +628,13 @@
     coefs = jnp.concatenate([average[:, None], inverse[:, None], orient], axis=1)
     coefs = exchange_all(coefs, "rot", 1, groups)
     last = lax.ppermute(last, "rot", side_swap)
-    from_sides += [last[:2], last[2:]]
-    flat = mines + [f[0] for f in from_sides] + [f[0] for f in fars] + [f[1] for f in from_sides]
-    return combine(me_place, coefs.reshape(groups * rots, 6), mask, flat)
+    arrays = mines + fars + [early, last]
+    at_far, at_early, at_last = rots, 2 * rots, 2 * rots + 1
+    pieces = [(r, None) for r in range(rots)]
+    pieces += [(at_early, r) for r in range(rots - 1)] + [(at_last, 0)]
+    pieces += [(at_far + r, 0) for r in range(rots)]
+    pieces += [(at_early, rots - 1 + r) for r in range(rots - 2)] + [(at_last, 1), (at_last, 2)]
+    return combine(me_place, coefs.reshape(groups * rots, 6), mask, arrays, pieces)
 
 
 def solution(mesh):

time: 96.9 us -> 107 us (1.10)
  other arithmetic: 1.12 us -> 19.7 us
  Pallas kernels: 45.8 us -> 31.5 us
  waiting for transfers between devices: 17.9 us -> 21.2 us
  starting transfers between devices: 24.4 us -> 26.3 us
    pallas_call x0 -> x2, other arithmetic: none -> 18.2 us  [correlate(): pl.pallas_call(functools.partial(corr_kernel, dims, rot, entry), out_shap...]
    pallas_call x5 -> x3, Pallas kernels: 35.8 us -> 20.4 us  [the longest x2 17 us: correlate(): pl.pallas_call(functools.partial(corr_kernel, dims, rot, entry), out_shap...]
    ppermute x4, waiting for transfers between devices: 0.01 us -> 9.2 us  [local(): fars.append(lax.ppermute(far, 'rot', far_swap))]
    ppermute x5, waiting for transfers between devices: 9.11 us -> 1.06 us  [the longest x4 1.06 us: swap_blocks(): lax.ppermute(block, axis, [(i, i ^ step) for i in range(lax.axis_size(axi...]
    ppermute x5, starting transfers between devices: 5.47 us -> 11.2 us  [the longest x4 11.1 us: swap_blocks(): lax.ppermute(block, axis, [(i, i ^ step) for i in range(lax.axis_size(axi...]
    ppermute x1, waiting for transfers between devices: 0.01 us -> 2.17 us  [neighbours(): lax.ppermute(block, axis, backward)]
    unnamed x28 -> x36, local copies, waits for them, and re-layouts: 2.6 us -> 4.76 us
    ppermute x1, starting transfers between devices: 4.85 us -> 3.4 us  [neighbours(): lax.ppermute(block, axis, forward)]
  transfers between devices with their start and end apart: 19 -> 19, of which waited for: 8 -> 7; matrix products, arithmetic and copies ran while one was open for 2% -> 20% of each run, Pallas kernels for 35% -> 23%
where the time goes in v6:
time: 107 us
  Pallas kernels  31.5 us (29%)
  starting transfers between devices  26.3 us (25%)
  waiting for transfers between devices  21.2 us (20%)
  other arithmetic  19.7 us (18%)
  local copies, waits for them, and re-layouts  7 us (7%)
    pallas_call x2, other arithmetic, correlate(): pl.pallas_call(functools.partial(corr_kernel, dims, rot, entry), out_shap...  18.2 us
    pallas_call x2, Pallas kernels, correlate(): pl.pallas_call(functools.partial(corr_kernel, dims, rot, entry), out_shap...  17 us
    ppermute x4, starting transfers between devices, swap_blocks(): lax.ppermute(block, axis, [(i, i ^ step) for i in range(lax.axis_size(axi...  11.1 us
    ppermute x4, waiting for transfers between devices, local(): fars.append(lax.ppermute(far, 'rot', far_swap))  9.2 us
    pallas_call x2, Pallas kernels, slab_rows(): pl.pallas_call(functools.partial(slab_rows_kernel, dims), out_shape=jax.S...  6.69 us
    ppermute x3, waiting for transfers between devices, local(): partner = lax.ppermute(state, 'tile', [(i, i ^ step) for i in range(tiles)])  6.65 us
    unnamed x36, local copies, waits for them, and re-layouts  4.76 us
    pallas_call x1, Pallas kernels, slab_x(): pl.pallas_call(functools.partial(slab_x_kernel, dims), out_shape=(jax.Sha...  4.38 us
  transfers between devices with their start and end apart: 19, of which 7 were waited for; matrix products, arithmetic and copies ran while one was open for 20% of the time, Pallas kernels for 23%

profile of v6, /device:TPU:0, one launch (start us, length us, event | category | flops | bytes accessed | tf_op | source)
XLA Modules:
  0.0 107.0 jit_solution(17432716789210722287)
XLA Ops:
  0.6 1.0 reshape.63
  1.7 4.1 %collective-permute-start = (bf16[4,1,112,128]{3,2,1,0:T(8,128)(2,1)S(1)}, bf16[4,1,112,128]{3,2,1,0:T(8,128)(2,1)S(1)}, u32[]{:S(2)}, u32[]{:S(2)}) collective-permute-start(bf16[4,1,112,128]{3,2,1,0:T(8,128)(2,1)S(1)} %pad.4), channel_id=1, source_target_pairs={{0,16},{4,20},{8,24},{12,28},{16,0},{20,4},{24,8},{28,12},{1,17},{... | collective-permute-start | bytes 344072 | tf_op jit(solution)/shard_map/ppermute | solution.py:519
  5.8 0.9 constant_dynamic-slice_fusion
  6.7 3.4 %collective-permute-start.2 = (bf16[16,5120]{1,0:T(8,128)(2,1)S(1)}, bf16[16,5120]{1,0:T(8,128)(2,1)S(1)}, u32[]{:S(2)}, u32[]{:S(2)}) collective-permute-start(bf16[16,5120]{1,0:T(8,128)(2,1)S(1)} %constant_dynamic-slice_fusion), channel_id=1, source_target_pairs={{0,4},{4,8},{8,12},{12,16},{16,20},{20,24},{24,28},{1,5},{5,9},{9,... | collective-permute-start | bytes 491528 | tf_op jit(solution)/shard_map/ppermute | solution.py:558
  10.1 1.3 %collective-permute-start.3 = (bf16[16,5120]{1,0:T(8,128)(2,1)S(1)}, bf16[16,5120]{1,0:T(8,128)(2,1)S(1)}, u32[]{:S(2)}, u32[]{:S(2)}) collective-permute-start(bf16[16,5120]{1,0:T(8,128)(2,1)S(1)} %constant_dynamic-slice_fusion), channel_id=1, source_target_pairs={{4,0},{8,4},{12,8},{16,12},{20,16},{24,20},{28,24},{5,1},{9,5},{13... | collective-permute-start | bytes 491528 | tf_op jit(solution)/shard_map/ppermute | solution.py:558
  11.5 3.7 %collective-permute-start.1 = (bf16[4,2,112,128]{3,2,1,0:T(8,128)(2,1)S(1)}, bf16[4,2,112,128]{3,2,1,0:T(8,128)(2,1)S(1)}, u32[]{:S(2)}, u32[]{:S(2)}) collective-permute-start(bf16[4,2,112,128]{3,2,1,0:T(8,128)(2,1)S(1)} %pad_maximum_fusion.3), channel_id=1, source_target_pairs={{0,8},{4,12},{8,0},{12,4},{16,24},{20,28},{24,16},{28,20},{1,9},{5... | collective-permute-start | bytes 688136 | tf_op jit(solution)/shard_map/ppermute | solution.py:519
  15.2 2.2 %collective-permute-done.3 = bf16[16,5120]{1,0:T(8,128)(2,1)S(1)} collective-permute-done((bf16[16,5120]{1,0:T(8,128)(2,1)S(1)}, bf16[16,5120]{1,0:T(8,128)(2,1)S(1)}, u32[]{:S(2)}, u32[]{:S(2)}) %collective-permute-start.3) | collective-permute-done | bytes 163872 | tf_op jit(solution)/shard_map/ppermute | solution.py:558
  17.5 1.0 copy-done.5
  18.5 0.9 copy-done.7
  19.4 2.8 %slab_own.1.own_ref = f32[3616,128]{1,0:T(8,128)S(1)} custom-call(s32[2]{0:T(128)S(1)} %pad_add_fusion.place_ref, bf16[32,5120]{1,0:T(8,128)(2,1)S(1)} %copy-done.5, bf16[240,512]{1,0:T(8,128)(2,1)S(1)} %copy-done.7), custom_call_target="tpu_custom_call" | custom-call | flops 3200000000 | bytes 1000000 | tf_op jit(solution)/shard_map/slab_own/pallas_call | solution.py:239
  22.2 1.0 collective-permute-done.1
  23.4 3.9 %slab_halo.1.halo_ref = f32[5424,128]{1,0:T(8,128)S(1)} custom-call(s32[2]{0:T(128)S(1)} %pad_add_fusion.place_ref, bf16[2,16,5120]{2,1,0:T(8,128)(2,1)S(1)} %pad_maximum_fusion.2.refs_0_, bf16[2,16,5120]{2,1,0:T(8,128)(2,1)S(1)} %collective-permute-done.4.refs_1_, bf16[240,512]{1,0:T(8,128)(2,1)S(1)} %copy-done.7), custom_call_target="tpu_custom_call" | custom-call | flops 4800000000 | bytes 1000000 | tf_op jit(solution)/shard_map/slab_halo/pallas_call | solution.py:239
  27.4 3.2 %collective-permute-start.5 = (bf16[1,4,112,128]{3,2,1,0:T(8,128)(2,1)S(1)}, bf16[1,4,112,128]{3,2,1,0:T(8,128)(2,1)S(1)}, u32[]{:S(2)}, u32[]{:S(2)}) collective-permute-start(bf16[1,4,112,128]{3,2,1,0:T(8,128)(2,1)S(1)} %slice.76), channel_id=1, source_target_pairs={{0,4},{4,0},{8,12},{12,8},{16,20},{20,16},{24,28},{28,24},{1,5},{5... | collective-permute-start | bytes 344072 | tf_op jit(solution)/shard_map/ppermute | solution.py:519
  30.7 4.4 %slab_x.1 = (f32[13,2,80,1024]{3,2,1,0:T(8,128)S(1)}, f32[40,32,128]{2,1,0:T(8,128)S(1)}, bf16[8,256,256]{2,1,0:T(8,128)(2,1)S(1)}) custom-call(f32[3616,128]{1,0:T(8,128)S(1)} %slab_own.1.own_ref, f32[5424,128]{1,0:T(8,128)S(1)} %slab_halo.1.halo_ref, bf16[80,240]{1,0:T(8,128)(2,1)S(1)} %copy-done.12, s32[32,80]{1,0:T(8,128)S(1)} %copy-done.6, ...), custom_call_target="tpu_custom_call" | custom-call | flops 5000000000 | bytes 1000000 | tf_op jit(solution)/shard_map/slab_x/pallas_call | solution.py:298
  35.2 8.5 %correlate.4 = (f32[32,1280]{1,0:T(8,128)S(1)}, f32[32,1280]{1,0:T(8,128)S(1)}, f32[2,32,1280]{2,1,0:T(8,128)S(1)}, f32[8,128]{1,0:T(8,128)S(1)}) custom-call(s32[2]{0:T(128)S(1)} %pad_add_fusion.place_ref, bf16[4,4,112,128]{3,2,1,0:T(8,128)(2,1)S(1)} %pad_maximum_fusion.1.held_ref, bf16[1,4,112,128]{3,2,1,0:T(8,128)(2,1)S(1)} %collective-permute-done.5.last_ref, ...), custom_call_target="tpu_custom_call" | custom-call | flops 15000000512 | bytes 10000000 | tf_op jit(solution)/shard_map/correlate/pallas_call | solution.py:443
  43.7 1.6 %collective-permute-start.7 = (f32[2,32,1280]{2,1,0:T(8,128)S(1)}, f32[2,32,1280]{2,1,0:T(8,128)S(1)}, u32[]{:S(2)}, u32[]{:S(2)}) collective-permute-start(f32[2,32,1280]{2,1,0:T(8,128)S(1)} %get-tuple-element.46), channel_id=1, source_target_pairs={{0,2},{1,3},{2,0},{3,1},{4,6},{5,7},{6,4},{7,5},{8,10},{9,11},{10,... | collective-permute-start | bytes 983048 | tf_op jit(solution)/shard_map/ppermute | solution.py:612
  45.3 9.2 %correlate.7 = (f32[5,32,1280]{2,1,0:T(8,128)S(1)}, f32[8,128]{1,0:T(8,128)S(1)}, f32[2,32,1280]{2,1,0:T(8,128)S(1)}, f32[32,1280]{1,0:T(8,128)}) fusion(f32[5,32,1280]{2,1,0:T(8,128)S(1)} %bitcast_dynamic-update-slice_fusion.2, s32[2]{0:T(128)S(1)} %pad_add_fusion.place_ref, bf16[4,4,112,128]{3,2,1,0:T(8,128)(2,1)S(1)} %pad_maximum_fusion.1.held_ref, ...), kind=kCustom, calls=%fused_computation.5 | custom fusion | flops 15000000512 | bytes 12034560 | tf_op jit(solution)/shard_map/correlate/pallas_call | solution.py:443
  55.0 9.0 %correlate.6 = (f32[5,32,1280]{2,1,0:T(8,128)S(1)}, f32[8,128]{1,0:T(8,128)S(1)}, f32[2,32,1280]{2,1,0:T(8,128)S(1)}, f32[32,1280]{1,0:T(8,128)}) fusion(f32[5,32,1280]{2,1,0:T(8,128)S(1)} %get-tuple-element.84, s32[2]{0:T(128)S(1)} %pad_add_fusion.place_ref, bf16[4,4,112,128]{3,2,1,0:T(8,128)(2,1)S(1)} %pad_maximum_fusion.1.held_ref, ...), kind=kCustom, calls=%fused_computation.4 | custom fusion | flops 15000000512 | bytes 12034560 | tf_op jit(solution)/shard_map/correlate/pallas_call | solution.py:443
  64.0 1.5 %collective-permute-start.9 = (f32[2,32,1280]{2,1,0:T(8,128)S(1)}, f32[2,32,1280]{2,1,0:T(8,128)S(1)}, u32[]{:S(2)}, u32[]{:S(2)}) collective-permute-start(f32[2,32,1280]{2,1,0:T(8,128)S(1)} %get-tuple-element.79), channel_id=1, source_target_pairs={{0,2},{1,3},{2,0},{3,1},{4,6},{5,7},{6,4},{7,5},{8,10},{9,11},{10,... | collective-permute-start | bytes 983048 | tf_op jit(solution)/shard_map/ppermute | solution.py:612
  65.7 8.5 %correlate.5 = (f32[32,1280]{1,0:T(8,128)S(1)}, f32[32,1280]{1,0:T(8,128)S(1)}, f32[2,32,1280]{2,1,0:T(8,128)S(1)}, f32[8,128]{1,0:T(8,128)S(1)}) custom-call(s32[2]{0:T(128)S(1)} %pad_add_fusion.place_ref, bf16[4,4,112,128]{3,2,1,0:T(8,128)(2,1)S(1)} %pad_maximum_fusion.1.held_ref, bf16[3,4,112,128]{3,2,1,0:T(8,128)(2,1)S(1)} %collective-permute-done.6.last_ref, ...), custom_call_target="tpu_custom_call" | custom-call | flops 15000000512 | bytes 10000000 | tf_op jit(solution)/shard_map/correlate/pallas_call | solution.py:443
  75.2 9.2 %collective-permute-done.14.refs_7_ = f32[2,32,1280]{2,1,0:T(8,128)S(1)} collective-permute-done((f32[2,32,1280]{2,1,0:T(8,128)S(1)}, f32[2,32,1280]{2,1,0:T(8,128)S(1)}, u32[]{:S(2)}, u32[]{:S(2)}) %collective-permute-start.14) | collective-permute-done | bytes 327712 | tf_op jit(solution)/shard_map/ppermute | solution.py:612
  84.4 2.0 %collective-permute-start.11 = (f32[3,4]{1,0:T(4,128)S(1)}, f32[3,4]{1,0:T(4,128)S(1)}, u32[]{:S(2)}, u32[]{:S(2)}) collective-permute-start(f32[3,4]{1,0:T(4,128)S(1)} %pad_maximum_fusion.5), channel_id=1, source_target_pairs={{0,4},{4,0},{8,12},{12,8},{16,20},{20,16},{24,28},{28,24},{1,5},{5... | collective-permute-start | bytes 152 | tf_op jit(solution)/shard_map/ppermute | solution.py:621
  86.5 0.8 pad_maximum_fusion
  88.8 3.0 %collective-permute-done.12 = f32[3,4]{1,0:T(4,128)S(1)} collective-permute-done((f32[3,4]{1,0:T(4,128)S(1)}, f32[3,4]{1,0:T(4,128)S(1)}, u32[]{:S(2)}, u32[]{:S(2)}) %collective-permute-start.12) | collective-permute-done | bytes 80 | tf_op jit(solution)/shard_map/ppermute | solution.py:621
  91.8 1.6 %collective-permute-start.13 = (f32[3,4]{1,0:T(4,128)S(1)}, f32[3,4]{1,0:T(4,128)S(1)}, u32[]{:S(2)}, u32[]{:S(2)}) collective-permute-start(f32[3,4]{1,0:T(4,128)S(1)} %select_add_fusion.1), channel_id=1, source_target_pairs={{0,16},{4,20},{8,24},{12,28},{16,0},{20,4},{24,8},{28,12},{1,17},{... | collective-permute-start | bytes 152 | tf_op jit(solution)/shard_map/ppermute | solution.py:621
  93.4 2.9 %collective-permute-done.13 = f32[3,4]{1,0:T(4,128)S(1)} collective-permute-done((f32[3,4]{1,0:T(4,128)S(1)}, f32[3,4]{1,0:T(4,128)S(1)}, u32[]{:S(2)}, u32[]{:S(2)}) %collective-permute-start.13) | collective-permute-done | bytes 80 | tf_op jit(solution)/shard_map/ppermute | solution.py:621
  97.8 0.9 collective-permute-start.17
  98.7 2.1 %collective-permute-done.16 = f32[4,6]{1,0:T(4,128)S(1)} collective-permute-done((f32[4,6]{1,0:T(4,128)S(1)}, f32[4,6]{1,0:T(4,128)S(1)}, u32[]{:S(2)}, u32[]{:S(2)}) %collective-permute-start.16) | collective-permute-done | bytes 128 | tf_op jit(solution)/shard_map/ppermute | solution.py:550
  100.9 0.9 copy-done.1
  101.8 0.9 copy-done.2
  102.7 0.9 copy-done.4
  103.6 3.4 %combine.1 = (f32[32,1280]{1,0:T(8,128)}, f32[32,1280]{1,0:T(8,128)}, f32[4,32,1280]{2,1,0:T(8,128)}) custom-call(s32[2]{0:T(128)S(1)} %pad_add_fusion.place_ref, f32[16,6]{1,0:T(8,128)S(1)} %bitcast.30, f32[40,32,128]{2,1,0:T(8,128)S(1)} %get-tuple-element.41.mask_ref, f32[32,1280]{1,0:T(8,128)S(1)} %get-tuple-element.68.refs_0_, f32[32,1280]{1,0:T(8,128)S(1)} %copy-done.1, ...), custom_call_target="tpu_custom_call" | custom-call | tf_op jit(solution)/shard_map/combine/pallas_call | solution.py:508
  (82 shorter events, 5.1 us)
Async XLA Ops:
  0.6 74.1 %copy-start = (f32[4,4096]{1,0:T(4,128)S(1)}, f32[4,4096]{1,0:T(4,128)}, u32[]{:S(2)}) copy-start(f32[4,4096]{1,0:T(4,128)} %param.17) | copy-start | bytes 196612
  1.7 9.8 %collective-permute-start = (bf16[4,1,112,128]{3,2,1,0:T(8,128)(2,1)S(1)}, bf16[4,1,112,128]{3,2,1,0:T(8,128)(2,1)S(1)}, u32[]{:S(2)}, u32[]{:S(2)}) collective-permute-start(bf16[4,1,112,128]{3,2,1,0:T(8,128)(2,1)S(1)} %pad.4), channel_id=1, source_target_pairs={{0,16},{4,20},{8,24},{12,28},{16,0},{20,4},{24,8},{28,12},{1,17},{... | collective-permute-start | bytes 344072 | tf_op jit(solution)/shard_map/ppermute | solution.py:519
  6.7 8.5 %collective-permute-start.2 = (bf16[16,5120]{1,0:T(8,128)(2,1)S(1)}, bf16[16,5120]{1,0:T(8,128)(2,1)S(1)}, u32[]{:S(2)}, u32[]{:S(2)}) collective-permute-start(bf16[16,5120]{1,0:T(8,128)(2,1)S(1)} %constant_dynamic-slice_fusion), channel_id=1, source_target_pairs={{0,4},{4,8},{8,12},{12,16},{16,20},{20,24},{24,28},{1,5},{5,9},{9,... | collective-permute-start | bytes 491528 | tf_op jit(solution)/shard_map/ppermute | solution.py:558
  10.1 7.3 %collective-permute-start.3 = (bf16[16,5120]{1,0:T(8,128)(2,1)S(1)}, bf16[16,5120]{1,0:T(8,128)(2,1)S(1)}, u32[]{:S(2)}, u32[]{:S(2)}) collective-permute-start(bf16[16,5120]{1,0:T(8,128)(2,1)S(1)} %constant_dynamic-slice_fusion), channel_id=1, source_target_pairs={{4,0},{8,4},{12,8},{16,12},{20,16},{24,20},{28,24},{5,1},{9,5},{13... | collective-permute-start | bytes 491528 | tf_op jit(solution)/shard_map/ppermute | solution.py:558
  11.5 11.8 %collective-permute-start.1 = (bf16[4,2,112,128]{3,2,1,0:T(8,128)(2,1)S(1)}, bf16[4,2,112,128]{3,2,1,0:T(8,128)(2,1)S(1)}, u32[]{:S(2)}, u32[]{:S(2)}) collective-permute-start(bf16[4,2,112,128]{3,2,1,0:T(8,128)(2,1)S(1)} %pad_maximum_fusion.3), channel_id=1, source_target_pairs={{0,8},{4,12},{8,0},{12,4},{16,24},{20,28},{24,16},{28,20},{1,9},{5... | collective-permute-start | bytes 688136 | tf_op jit(solution)/shard_map/ppermute | solution.py:519
  17.4 5.9 %collective-permute-start.4 = (bf16[2,16,5120]{2,1,0:T(8,128)(2,1)S(1)}, bf16[2,16,5120]{2,1,0:T(8,128)(2,1)S(1)}, u32[]{:S(2)}, u32[]{:S(2)}) collective-permute-start(bf16[2,16,5120]{2,1,0:T(8,128)(2,1)S(1)} %pad_maximum_fusion.2.refs_0_), channel_id=1, source_target_pairs={{0,1},{1,0},{2,3},{3,2},{4,5},{5,4},{6,7},{7,6},{8,9},{9,8},{10,11... | collective-permute-start | bytes 983048 | tf_op jit(solution)/shard_map/ppermute | solution.py:582
  17.5 1.0 copy-start.5
  23.3 7.4 %copy-start.6 = (s32[32,80]{1,0:T(8,128)S(1)}, s32[32,80]{1,0:T(8,128)}, u32[]{:S(2)}) copy-start(s32[32,80]{1,0:T(8,128)} %valid_ref.1) | copy-start | bytes 30724
  23.3 7.4 %copy-start.12 = (bf16[80,240]{1,0:T(8,128)(2,1)S(1)}, bf16[80,240]{1,0:T(8,128)(2,1)}, u32[]{:S(2)}) copy-start(bf16[80,240]{1,0:T(8,128)(2,1)} %constant.47.clone.x_ref) | copy-start | bytes 115204
  23.4 7.4 %copy-start.14 = (bf16[48,256]{1,0:T(8,128)(2,1)S(1)}, bf16[48,256]{1,0:T(8,128)(2,1)}, u32[]{:S(2)}) copy-start(bf16[48,256]{1,0:T(8,128)(2,1)} %constant.48.clone.tz_ref) | copy-start | bytes 73732
  27.3 7.8 %copy-start.8 = (bf16[256,256]{1,0:T(8,128)(2,1)S(1)}, bf16[256,256]{1,0:T(8,128)(2,1)}, u32[]{:S(2)}) copy-start(bf16[256,256]{1,0:T(8,128)(2,1)} %constant.54.clone.bz_ref) | copy-start | bytes 393220
  27.3 7.8 %copy-start.9 = (bf16[160,208]{1,0:T(8,128)(2,1)S(1)}, bf16[160,208]{1,0:T(8,128)(2,1)}, u32[]{:S(2)}) copy-start(bf16[160,208]{1,0:T(8,128)(2,1)} %constant.53.clone.by_ref) | copy-start | bytes 199684
  27.4 7.8 %copy-start.10 = (bf16[112,144]{1,0:T(8,128)(2,1)S(1)}, bf16[112,144]{1,0:T(8,128)(2,1)}, u32[]{:S(2)}) copy-start(bf16[112,144]{1,0:T(8,128)(2,1)} %constant.50.clone.y_ref) | copy-start | bytes 96772
  27.4 7.8 %copy-start.11 = (bf16[80,144]{1,0:T(8,128)(2,1)S(1)}, bf16[80,144]{1,0:T(8,128)(2,1)}, u32[]{:S(2)}) copy-start(bf16[80,144]{1,0:T(8,128)(2,1)} %constant.51.clone.x_ref) | copy-start | bytes 69124
  27.4 7.8 %copy-start.13 = (bf16[64,160]{1,0:T(8,128)(2,1)S(1)}, bf16[64,160]{1,0:T(8,128)(2,1)}, u32[]{:S(2)}) copy-start(bf16[64,160]{1,0:T(8,128)(2,1)} %constant.52.clone.bx_ref) | copy-start | bytes 61444
  27.4 7.8 %copy-start.15 = (f32[8,128]{1,0:T(8,128)S(1)}, f32[8,128]{1,0:T(8,128)}, u32[]{:S(2)}) copy-start(f32[8,128]{1,0:T(8,128)} %constant.49.clone.ones_ref) | copy-start | bytes 12292
  27.4 7.7 %collective-permute-start.5 = (bf16[1,4,112,128]{3,2,1,0:T(8,128)(2,1)S(1)}, bf16[1,4,112,128]{3,2,1,0:T(8,128)(2,1)S(1)}, u32[]{:S(2)}, u32[]{:S(2)}) collective-permute-start(bf16[1,4,112,128]{3,2,1,0:T(8,128)(2,1)S(1)} %slice.76), channel_id=1, source_target_pairs={{0,4},{4,0},{8,12},{12,8},{16,20},{20,16},{24,28},{28,24},{1,5},{5... | collective-permute-start | bytes 344072 | tf_op jit(solution)/shard_map/ppermute | solution.py:519
  30.7 14.6 %collective-permute-start.6 = (bf16[3,4,112,128]{3,2,1,0:T(8,128)(2,1)S(1)}, bf16[3,4,112,128]{3,2,1,0:T(8,128)(2,1)S(1)}, u32[]{:S(2)}, u32[]{:S(2)}) collective-permute-start(bf16[3,4,112,128]{3,2,1,0:T(8,128)(2,1)S(1)} %slice.78), channel_id=1, source_target_pairs={{0,4},{4,0},{8,12},{12,8},{16,20},{20,16},{24,28},{28,24},{1,5},{5... | collective-permute-start | bytes 1032200 | tf_op jit(solution)/shard_map/ppermute | solution.py:519
  43.7 11.3 %collective-permute-start.7 = (f32[2,32,1280]{2,1,0:T(8,128)S(1)}, f32[2,32,1280]{2,1,0:T(8,128)S(1)}, u32[]{:S(2)}, u32[]{:S(2)}) collective-permute-start(f32[2,32,1280]{2,1,0:T(8,128)S(1)} %get-tuple-element.46), channel_id=1, source_target_pairs={{0,2},{1,3},{2,0},{3,1},{4,6},{5,7},{6,4},{7,5},{8,10},{9,11},{10,... | collective-permute-start | bytes 983048 | tf_op jit(solution)/shard_map/ppermute | solution.py:612
  54.5 11.1 %collective-permute-start.8 = (f32[2,32,1280]{2,1,0:T(8,128)S(1)}, f32[2,32,1280]{2,1,0:T(8,128)S(1)}, u32[]{:S(2)}, u32[]{:S(2)}) collective-permute-start(f32[2,32,1280]{2,1,0:T(8,128)S(1)} %get-tuple-element.87), channel_id=1, source_target_pairs={{0,2},{1,3},{2,0},{3,1},{4,6},{5,7},{6,4},{7,5},{8,10},{9,11},{10,... | collective-permute-start | bytes 983048 | tf_op jit(solution)/shard_map/ppermute | solution.py:612
  64.0 11.1 %collective-permute-start.9 = (f32[2,32,1280]{2,1,0:T(8,128)S(1)}, f32[2,32,1280]{2,1,0:T(8,128)S(1)}, u32[]{:S(2)}, u32[]{:S(2)}) collective-permute-start(f32[2,32,1280]{2,1,0:T(8,128)S(1)} %get-tuple-element.79), channel_id=1, source_target_pairs={{0,2},{1,3},{2,0},{3,1},{4,6},{5,7},{6,4},{7,5},{8,10},{9,11},{10,... | collective-permute-start | bytes 983048 | tf_op jit(solution)/shard_map/ppermute | solution.py:612
  65.6 9.2 %copy-start.16 = (s32[4]{0:T(128)S(1)}, s32[4]{0:T(128)}, u32[]{:S(2)}) copy-start(s32[4]{0:T(128)} %param.18) | copy-start | bytes 52
  65.6 18.8 %collective-permute-start.10 = (f32[5,32,1280]{2,1,0:T(8,128)S(1)}, f32[5,32,1280]{2,1,0:T(8,128)S(1)}, u32[]{:S(2)}, u32[]{:S(2)}) collective-permute-start(f32[5,32,1280]{2,1,0:T(8,128)S(1)} %slice_dynamic-update-slice_fusion), channel_id=1, source_target_pairs={{0,1},{1,0},{2,3},{3,2},{4,5},{5,4},{6,7},{7,6},{8,9},{9,8},{10,11... | collective-permute-start | bytes 2457608 | tf_op jit(solution)/shard_map/ppermute | solution.py:615
  74.2 19.3 %copy-start.3 = (f32[32,1280]{1,0:T(8,128)}, f32[32,1280]{1,0:T(8,128)S(1)}, u32[]{:S(2)}) copy-start(f32[32,1280]{1,0:T(8,128)S(1)} %get-tuple-element.71.refs_3_) | copy-start | bytes 491524
  74.2 10.2 %collective-permute-start.14 = (f32[2,32,1280]{2,1,0:T(8,128)S(1)}, f32[2,32,1280]{2,1,0:T(8,128)S(1)}, u32[]{:S(2)}, u32[]{:S(2)}) collective-permute-start(f32[2,32,1280]{2,1,0:T(8,128)S(1)} %get-tuple-element.66), channel_id=1, source_target_pairs={{0,2},{1,3},{2,0},{3,1},{4,6},{5,7},{6,4},{7,5},{8,10},{9,11},{10,... | collective-permute-start | bytes 983048 | tf_op jit(solution)/shard_map/ppermute | solution.py:612
  84.4 3.7 %collective-permute-start.11 = (f32[3,4]{1,0:T(4,128)S(1)}, f32[3,4]{1,0:T(4,128)S(1)}, u32[]{:S(2)}, u32[]{:S(2)}) collective-permute-start(f32[3,4]{1,0:T(4,128)S(1)} %pad_maximum_fusion.5), channel_id=1, source_target_pairs={{0,4},{4,0},{8,12},{12,8},{16,20},{20,16},{24,28},{28,24},{1,5},{5... | collective-permute-start | bytes 152 | tf_op jit(solution)/shard_map/ppermute | solution.py:621
  88.2 3.6 %collective-permute-start.12 = (f32[3,4]{1,0:T(4,128)S(1)}, f32[3,4]{1,0:T(4,128)S(1)}, u32[]{:S(2)}, u32[]{:S(2)}) collective-permute-start(f32[3,4]{1,0:T(4,128)S(1)} %select_add_fusion.2), channel_id=1, source_target_pairs={{0,8},{4,12},{8,0},{12,4},{16,24},{20,28},{24,16},{28,20},{1,9},{5... | collective-permute-start | bytes 152 | tf_op jit(solution)/shard_map/ppermute | solution.py:621
  91.8 4.5 %collective-permute-start.13 = (f32[3,4]{1,0:T(4,128)S(1)}, f32[3,4]{1,0:T(4,128)S(1)}, u32[]{:S(2)}, u32[]{:S(2)}) collective-permute-start(f32[3,4]{1,0:T(4,128)S(1)} %select_add_fusion.1), channel_id=1, source_target_pairs={{0,16},{4,20},{8,24},{12,28},{16,0},{20,4},{24,8},{28,12},{1,17},{... | collective-permute-start | bytes 152 | tf_op jit(solution)/shard_map/ppermute | solution.py:621
  96.3 4.5 %collective-permute-start.18 = (f32[3,32,1280]{2,1,0:T(8,128)}, f32[3,32,1280]{2,1,0:T(8,128)S(1)}, u32[]{:S(2)}, u32[]{:S(2)}) collective-permute-start(f32[3,32,1280]{2,1,0:T(8,128)} %pad_maximum_fusion), channel_id=1, source_target_pairs={{0,1},{1,0},{2,3},{3,2},{4,5},{5,4},{6,7},{7,6},{8,9},{9,8},{10,11... | collective-permute-start | bytes 1474568 | tf_op jit(solution)/shard_map/ppermute | solution.py:630
  96.7 2.0 %collective-permute-start.15 = (f32[4,6]{1,0:T(4,128)S(1)}, f32[4,6]{1,0:T(4,128)S(1)}, u32[]{:S(2)}, u32[]{:S(2)}) collective-permute-start(f32[4,6]{1,0:T(4,128)S(1)} %pad_maximum_fusion.6), channel_id=1, source_target_pairs={{0,1},{1,0},{2,3},{3,2},{4,5},{5,4},{6,7},{7,6},{8,9},{9,8},{10,11... | collective-permute-start | bytes 296 | tf_op jit(solution)/shard_map/ppermute | solution.py:550
  97.2 3.6 %collective-permute-start.16 = (f32[4,6]{1,0:T(4,128)S(1)}, f32[4,6]{1,0:T(4,128)S(1)}, u32[]{:S(2)}, u32[]{:S(2)}) collective-permute-start(f32[4,6]{1,0:T(4,128)S(1)} %pad_maximum_fusion.6), channel_id=1, source_target_pairs={{0,2},{1,3},{2,0},{3,1},{4,6},{5,7},{6,4},{7,5},{8,10},{9,11},{10,... | collective-permute-start | bytes 296 | tf_op jit(solution)/shard_map/ppermute | solution.py:550
  97.8 3.0 %collective-permute-start.17 = (f32[4,6]{1,0:T(4,128)S(1)}, f32[4,6]{1,0:T(4,128)S(1)}, u32[]{:S(2)}, u32[]{:S(2)}) collective-permute-start(f32[4,6]{1,0:T(4,128)S(1)} %pad_maximum_fusion.6), channel_id=1, source_target_pairs={{0,3},{1,2},{2,1},{3,0},{4,7},{5,6},{6,5},{7,4},{8,11},{9,10},{10,... | collective-permute-start | bytes 296 | tf_op jit(solution)/shard_map/ppermute | solution.py:550
  (4 other events, 3.7 us)

commit v7 on v6

--- a/solution.py
+++ b/solution.py
@@ -245,7 +245,7 @@
             pltpu.VMEM((y_cells * odd(count), LANES), F32),
             pltpu.VMEM((2, 3 * y_cells, GROUP * LANES), BF16),
         ],
-        compiler_params=pltpu.CompilerParams(vmem_limit_bytes=20 * 1024 * 1024),
+        compiler_params=pltpu.CompilerParams(vmem_limit_bytes=9 * 1024 * 1024),
         cost_estimate=pl.CostEstimate(flops=count * 10**8, bytes_accessed=10**6, transcendentals=0),
         name=name,
     )(place, *blocks, tables["slab_rows"])
@@ -305,7 +305,7 @@
         in_specs=[vmem] * 5,
         out_specs=(vmem,) * 3,
         scratch_shapes=[pltpu.VMEM((2, 3 * n_x, GROUP * LANES), BF16)],
-        compiler_params=pltpu.CompilerParams(vmem_limit_bytes=20 * 1024 * 1024),
+        compiler_params=pltpu.CompilerParams(vmem_limit_bytes=6 * 1024 * 1024),
         cost_estimate=pl.CostEstimate(flops=5 * 10**9, bytes_accessed=10**6, transcendentals=0),
         name="slab_x",
     )(own, halo, tables["slab_x"], valid, tables["tmpl_z"])
@@ -460,7 +460,7 @@
             pltpu.VMEM((n_y * odd(x_cells), LANES), F32),
             pltpu.VMEM((x_cells * odd(y_cells), LANES), F32),
         ],
-        compiler_params=pltpu.CompilerParams(vmem_limit_bytes=24 * 1024 * 1024),
+        compiler_params=pltpu.CompilerParams(vmem_limit_bytes=14 * 1024 * 1024),
         cost_estimate=pl.CostEstimate(flops=15 * 10**9, bytes_accessed=10**7, transcendentals=0),
         name="correlate",
     )(
@@ -510,7 +510,7 @@
         out_shape=(out, out, jax.ShapeDtypeStruct((4,) + shape, F32)),
         in_specs=[pl.BlockSpec(memory_space=pltpu.SMEM)] * 2 + [vmem] * (1 + len(arrays)),
         out_specs=(vmem,) * 3,
-        compiler_params=pltpu.CompilerParams(vmem_limit_bytes=16 * 1024 * 1024),
+        compiler_params=pltpu.CompilerParams(vmem_limit_bytes=4 * 1024 * 1024),
         name="combine",
     )(place, coefs, mask, *arrays)
 
@@ -615,14 +615,16 @@
             early = lax.ppermute(early, "rot", side_swap)
     state = jnp.stack(stats, axis=1)
     state, early, fars[rots - 2] = lax.optimization_barrier((state, early, fars[rots - 2]))
-    last = jnp.stack([sides[rots - 1], fars[rots - 2][1], fars[rots - 1][1]])
     step = 1
     while step < tiles:
         partner = lax.ppermute(state, "tile", [(i, i ^ step) for i in range(tiles)])
-        step *= 2
-        if step == tiles:
+        if step * 4 == tiles:
+            partner, fars[rots - 1] = lax.optimization_barrier((partner, fars[rots - 1]))
+            last = jnp.stack([sides[rots - 1], fars[rots - 2][1], fars[rots - 1][1]])
+        if step * 2 == tiles:
             partner, last = lax.optimization_barrier((partner, last))
         state = merge(state, partner)
+        step *= 2
     average = state[1] / state[0]
     inverse = 1.0 / jnp.sqrt(state[2] / state[0] + EPSILON)
     coefs = jnp.concatenate([average[:, None], inverse[:, None], orient], axis=1)

time: 107 us -> 102 us (0.953)
  starting transfers between devices: 26.3 us -> 20.3 us
  waiting for transfers between devices: 21.2 us -> 22.4 us
    ppermute x4, waiting for transfers between devices: 1.06 us -> 8.24 us  [swap_blocks(): lax.ppermute(block, axis, [(i, i ^ step) for i in range(lax.axis_size(axi...]
    ppermute x4, starting transfers between devices: 11.1 us -> 6.85 us  [swap_blocks(): lax.ppermute(block, axis, [(i, i ^ step) for i in range(lax.axis_size(axi...]
    ppermute x4, waiting for transfers between devices: 9.2 us -> 5.86 us  [local(): fars.append(lax.ppermute(far, 'rot', far_swap))]
    ppermute x3, starting transfers between devices: 4.25 us -> 1.09 us  [local(): partner = lax.ppermute(state, 'tile', [(i, i ^ step) for i in range(tiles)])]
    ppermute x1, waiting for transfers between devices: 2.17 us -> 0.01 us  [neighbours(): lax.ppermute(block, axis, backward)]
    ppermute x1, starting transfers between devices: 3.4 us -> 4.85 us  [neighbours(): lax.ppermute(block, axis, forward)]
    unnamed x36 -> x38, local copies, waits for them, and re-layouts: 4.76 us -> 4.77 us
  transfers between devices with their start and end apart: 19 -> 19, of which waited for: 7 -> 6; matrix products, arithmetic and copies ran while one was open for 20% -> 21% of each run, Pallas kernels for 23% -> 24%
where the time goes in v7:
time: 102 us
  Pallas kernels  31.4 us (31%)
  waiting for transfers between devices  22.4 us (22%)
  starting transfers between devices  20.3 us (20%)
  other arithmetic  19.7 us (19%)
  local copies, waits for them, and re-layouts  7.02 us (7%)
  between operations  1.09 us (1%)
    pallas_call x2, other arithmetic, correlate(): pl.pallas_call(functools.partial(corr_kernel, dims, rot, entry), out_shap...  18.2 us
    pallas_call x2, Pallas kernels, correlate(): pl.pallas_call(functools.partial(corr_kernel, dims, rot, entry), out_shap...  16.9 us
    ppermute x4, waiting for transfers between devices, swap_blocks(): lax.ppermute(block, axis, [(i, i ^ step) for i in range(lax.axis_size(axi...  8.24 us
    ppermute x4, starting transfers between devices, swap_blocks(): lax.ppermute(block, axis, [(i, i ^ step) for i in range(lax.axis_size(axi...  6.85 us
    pallas_call x2, Pallas kernels, slab_rows(): pl.pallas_call(functools.partial(slab_rows_kernel, dims), out_shape=jax.S...  6.67 us
    ppermute x3, waiting for transfers between devices, local(): partner = lax.ppermute(state, 'tile', [(i, i ^ step) for i in range(tiles)])  6.16 us
    ppermute x4, waiting for transfers between devices, local(): fars.append(lax.ppermute(far, 'rot', far_swap))  5.86 us
    ppermute x1, starting transfers between devices, neighbours(): lax.ppermute(block, axis, forward)  4.85 us
  transfers between devices with their start and end apart: 19, of which 6 were waited for; matrix products, arithmetic and copies ran while one was open for 21% of the time, Pallas kernels for 24%

profile of v7, /device:TPU:0, one launch (start us, length us, event | category | flops | bytes accessed | tf_op | source)
XLA Modules:
  0.0 102.1 jit_solution(17961976701133069118)
XLA Ops:
  0.7 1.0 constant_dynamic-slice_fusion
  1.7 4.9 %collective-permute-start.2 = (bf16[16,5120]{1,0:T(8,128)(2,1)S(1)}, bf16[16,5120]{1,0:T(8,128)(2,1)S(1)}, u32[]{:S(2)}, u32[]{:S(2)}) collective-permute-start(bf16[16,5120]{1,0:T(8,128)(2,1)S(1)} %constant_dynamic-slice_fusion), channel_id=1, source_target_pairs={{0,4},{4,8},{8,12},{12,16},{16,20},{20,24},{24,28},{1,5},{5,9},{9,... | collective-permute-start | bytes 491528 | tf_op jit(solution)/shard_map/ppermute | solution.py:558
  6.5 1.3 %collective-permute-start.3 = (bf16[16,5120]{1,0:T(8,128)(2,1)S(1)}, bf16[16,5120]{1,0:T(8,128)(2,1)S(1)}, u32[]{:S(2)}, u32[]{:S(2)}) collective-permute-start(bf16[16,5120]{1,0:T(8,128)(2,1)S(1)} %constant_dynamic-slice_fusion), channel_id=1, source_target_pairs={{4,0},{8,4},{12,8},{16,12},{20,16},{24,20},{28,24},{5,1},{9,5},{13... | collective-permute-start | bytes 491528 | tf_op jit(solution)/shard_map/ppermute | solution.py:558
  7.8 1.0 reshape.63
  8.8 4.7 %collective-permute-start = (bf16[4,1,112,128]{3,2,1,0:T(8,128)(2,1)S(1)}, bf16[4,1,112,128]{3,2,1,0:T(8,128)(2,1)S(1)}, u32[]{:S(2)}, u32[]{:S(2)}) collective-permute-start(bf16[4,1,112,128]{3,2,1,0:T(8,128)(2,1)S(1)} %pad.4), channel_id=1, source_target_pairs={{0,16},{4,20},{8,24},{12,28},{16,0},{20,4},{24,8},{28,12},{1,17},{... | collective-permute-start | bytes 344072 | tf_op jit(solution)/shard_map/ppermute | solution.py:519
  13.6 1.0 copy-done.5
  14.6 0.9 copy-done.7
  15.5 2.8 %slab_own.1.own_ref = f32[3616,128]{1,0:T(8,128)S(1)} custom-call(s32[2]{0:T(128)S(1)} %pad_add_fusion.place_ref, bf16[32,5120]{1,0:T(8,128)(2,1)S(1)} %copy-done.5, bf16[240,512]{1,0:T(8,128)(2,1)S(1)} %copy-done.7), custom_call_target="tpu_custom_call" | custom-call | flops 3200000000 | bytes 1000000 | tf_op jit(solution)/shard_map/slab_own/pallas_call | solution.py:239
  18.4 2.7 %collective-permute-done = bf16[4,1,112,128]{3,2,1,0:T(8,128)(2,1)S(1)} collective-permute-done((bf16[4,1,112,128]{3,2,1,0:T(8,128)(2,1)S(1)}, bf16[4,1,112,128]{3,2,1,0:T(8,128)(2,1)S(1)}, u32[]{:S(2)}, u32[]{:S(2)}) %collective-permute-start) | collective-permute-done | bytes 114720 | tf_op jit(solution)/shard_map/ppermute | solution.py:519
  21.6 5.6 %collective-permute-done.1 = bf16[4,2,112,128]{3,2,1,0:T(8,128)(2,1)S(1)} collective-permute-done((bf16[4,2,112,128]{3,2,1,0:T(8,128)(2,1)S(1)}, bf16[4,2,112,128]{3,2,1,0:T(8,128)(2,1)S(1)}, u32[]{:S(2)}, u32[]{:S(2)}) %collective-permute-start.1) | collective-permute-done | bytes 229408 | tf_op jit(solution)/shard_map/ppermute | solution.py:519
  27.2 3.9 %slab_halo.1.halo_ref = f32[5424,128]{1,0:T(8,128)S(1)} custom-call(s32[2]{0:T(128)S(1)} %pad_add_fusion.place_ref, bf16[2,16,5120]{2,1,0:T(8,128)(2,1)S(1)} %pad_maximum_fusion.2.refs_0_, bf16[2,16,5120]{2,1,0:T(8,128)(2,1)S(1)} %collective-permute-done.4.refs_1_, bf16[240,512]{1,0:T(8,128)(2,1)S(1)} %copy-done.8), custom_call_target="tpu_custom_call" | custom-call | flops 4800000000 | bytes 1000000 | tf_op jit(solution)/shard_map/slab_halo/pallas_call | solution.py:239
  31.3 2.0 %collective-permute-start.6 = (bf16[3,4,112,128]{3,2,1,0:T(8,128)(2,1)S(1)}, bf16[3,4,112,128]{3,2,1,0:T(8,128)(2,1)S(1)}, u32[]{:S(2)}, u32[]{:S(2)}) collective-permute-start(bf16[3,4,112,128]{3,2,1,0:T(8,128)(2,1)S(1)} %slice.78), channel_id=1, source_target_pairs={{0,4},{4,0},{8,12},{12,8},{16,20},{20,16},{24,28},{28,24},{1,5},{5... | collective-permute-start | bytes 1032200 | tf_op jit(solution)/shard_map/ppermute | solution.py:519
  33.3 4.3 %slab_x.1 = (f32[13,2,80,1024]{3,2,1,0:T(8,128)S(1)}, f32[40,32,128]{2,1,0:T(8,128)S(1)}, bf16[8,256,256]{2,1,0:T(8,128)(2,1)S(1)}) custom-call(f32[3616,128]{1,0:T(8,128)S(1)} %slab_own.1.own_ref, f32[5424,128]{1,0:T(8,128)S(1)} %slab_halo.1.halo_ref, bf16[80,240]{1,0:T(8,128)(2,1)S(1)} %copy-done.13, s32[32,80]{1,0:T(8,128)S(1)} %copy-done.6, ...), custom_call_target="tpu_custom_call" | custom-call | flops 5000000000 | bytes 1000000 | tf_op jit(solution)/shard_map/slab_x/pallas_call | solution.py:298
  37.8 8.5 %correlate.4 = (f32[32,1280]{1,0:T(8,128)S(1)}, f32[32,1280]{1,0:T(8,128)S(1)}, f32[2,32,1280]{2,1,0:T(8,128)S(1)}, f32[8,128]{1,0:T(8,128)S(1)}) custom-call(s32[2]{0:T(128)S(1)} %pad_add_fusion.place_ref, bf16[4,4,112,128]{3,2,1,0:T(8,128)(2,1)S(1)} %pad_maximum_fusion.1.held_ref, bf16[1,4,112,128]{3,2,1,0:T(8,128)(2,1)S(1)} %collective-permute-done.5.last_ref, ...), custom_call_target="tpu_custom_call" | custom-call | flops 15000000512 | bytes 10000000 | tf_op jit(solution)/shard_map/correlate/pallas_call | solution.py:443
  46.2 1.6 %collective-permute-start.7 = (f32[2,32,1280]{2,1,0:T(8,128)S(1)}, f32[2,32,1280]{2,1,0:T(8,128)S(1)}, u32[]{:S(2)}, u32[]{:S(2)}) collective-permute-start(f32[2,32,1280]{2,1,0:T(8,128)S(1)} %get-tuple-element.48), channel_id=1, source_target_pairs={{0,2},{1,3},{2,0},{3,1},{4,6},{5,7},{6,4},{7,5},{8,10},{9,11},{10,... | collective-permute-start | bytes 983048 | tf_op jit(solution)/shard_map/ppermute | solution.py:612
  47.9 9.2 %correlate.7 = (f32[5,32,1280]{2,1,0:T(8,128)S(1)}, f32[8,128]{1,0:T(8,128)S(1)}, f32[2,32,1280]{2,1,0:T(8,128)S(1)}, f32[32,1280]{1,0:T(8,128)}) fusion(f32[5,32,1280]{2,1,0:T(8,128)S(1)} %bitcast_dynamic-update-slice_fusion.2, s32[2]{0:T(128)S(1)} %pad_add_fusion.place_ref, bf16[4,4,112,128]{3,2,1,0:T(8,128)(2,1)S(1)} %pad_maximum_fusion.1.held_ref, ...), kind=kCustom, calls=%fused_computation.5 | custom fusion | flops 15000000512 | bytes 12034560 | tf_op jit(solution)/shard_map/correlate/pallas_call | solution.py:443
  57.5 9.0 %correlate.6 = (f32[5,32,1280]{2,1,0:T(8,128)S(1)}, f32[8,128]{1,0:T(8,128)S(1)}, f32[2,32,1280]{2,1,0:T(8,128)S(1)}, f32[32,1280]{1,0:T(8,128)}) fusion(f32[5,32,1280]{2,1,0:T(8,128)S(1)} %get-tuple-element.80, s32[2]{0:T(128)S(1)} %pad_add_fusion.place_ref, bf16[4,4,112,128]{3,2,1,0:T(8,128)(2,1)S(1)} %pad_maximum_fusion.1.held_ref, ...), kind=kCustom, calls=%fused_computation.4 | custom fusion | flops 15000000512 | bytes 12034560 | tf_op jit(solution)/shard_map/correlate/pallas_call | solution.py:443
  66.5 1.5 %collective-permute-start.9 = (f32[2,32,1280]{2,1,0:T(8,128)S(1)}, f32[2,32,1280]{2,1,0:T(8,128)S(1)}, u32[]{:S(2)}, u32[]{:S(2)}) collective-permute-start(f32[2,32,1280]{2,1,0:T(8,128)S(1)} %get-tuple-element.91), channel_id=1, source_target_pairs={{0,2},{1,3},{2,0},{3,1},{4,6},{5,7},{6,4},{7,5},{8,10},{9,11},{10,... | collective-permute-start | bytes 983048 | tf_op jit(solution)/shard_map/ppermute | solution.py:612
  68.2 8.5 %correlate.5 = (f32[32,1280]{1,0:T(8,128)S(1)}, f32[32,1280]{1,0:T(8,128)S(1)}, f32[2,32,1280]{2,1,0:T(8,128)S(1)}, f32[8,128]{1,0:T(8,128)S(1)}) custom-call(s32[2]{0:T(128)S(1)} %pad_add_fusion.place_ref, bf16[4,4,112,128]{3,2,1,0:T(8,128)(2,1)S(1)} %pad_maximum_fusion.1.held_ref, bf16[3,4,112,128]{3,2,1,0:T(8,128)(2,1)S(1)} %collective-permute-done.6.last_ref, ...), custom_call_target="tpu_custom_call" | custom-call | flops 15000000512 | bytes 10000000 | tf_op jit(solution)/shard_map/correlate/pallas_call | solution.py:443
  76.7 0.5 collective-permute-start.13
  77.4 3.5 %collective-permute-done.11 = f32[3,4]{1,0:T(4,128)S(1)} collective-permute-done((f32[3,4]{1,0:T(4,128)S(1)}, f32[3,4]{1,0:T(4,128)S(1)}, u32[]{:S(2)}, u32[]{:S(2)}) %collective-permute-start.11) | collective-permute-done | bytes 80 | tf_op jit(solution)/shard_map/ppermute | solution.py:620
  81.0 5.8 %collective-permute-done.13.refs_7_ = f32[2,32,1280]{2,1,0:T(8,128)S(1)} collective-permute-done((f32[2,32,1280]{2,1,0:T(8,128)S(1)}, f32[2,32,1280]{2,1,0:T(8,128)S(1)}, u32[]{:S(2)}, u32[]{:S(2)}) %collective-permute-start.13) | collective-permute-done | bytes 327712 | tf_op jit(solution)/shard_map/ppermute | solution.py:612
  87.0 1.0 collective-permute-start.14
  88.0 0.8 pad_maximum_fusion
  88.8 2.7 %collective-permute-done.14 = f32[3,4]{1,0:T(4,128)S(1)} collective-permute-done((f32[3,4]{1,0:T(4,128)S(1)}, f32[3,4]{1,0:T(4,128)S(1)}, u32[]{:S(2)}, u32[]{:S(2)}) %collective-permute-start.14) | collective-permute-done | bytes 80 | tf_op jit(solution)/shard_map/ppermute | solution.py:620
  91.8 0.5 collective-permute-start.15
  92.9 1.0 collective-permute-start.17
  93.9 2.1 %collective-permute-done.16 = f32[4,6]{1,0:T(4,128)S(1)} collective-permute-done((f32[4,6]{1,0:T(4,128)S(1)}, f32[4,6]{1,0:T(4,128)S(1)}, u32[]{:S(2)}, u32[]{:S(2)}) %collective-permute-start.16) | collective-permute-done | bytes 128 | tf_op jit(solution)/shard_map/ppermute | solution.py:550
  96.0 0.9 copy-done.1
  96.9 0.9 copy-done.2
  97.8 0.9 copy-done.4
  98.7 3.4 %combine.1 = (f32[32,1280]{1,0:T(8,128)}, f32[32,1280]{1,0:T(8,128)}, f32[4,32,1280]{2,1,0:T(8,128)}) custom-call(s32[2]{0:T(128)S(1)} %pad_add_fusion.place_ref, f32[16,6]{1,0:T(8,128)S(1)} %bitcast.30, f32[40,32,128]{2,1,0:T(8,128)S(1)} %get-tuple-element.43.mask_ref, f32[32,1280]{1,0:T(8,128)S(1)} %get-tuple-element.72.refs_0_, f32[32,1280]{1,0:T(8,128)S(1)} %copy-done.1, ...), custom_call_target="tpu_custom_call" | custom-call | tf_op jit(solution)/shard_map/combine/pallas_call | solution.py:508
  (84 shorter events, 2.7 us)
Async XLA Ops:
  0.6 20.6 %copy-start = (f32[4,4096]{1,0:T(4,128)S(1)}, f32[4,4096]{1,0:T(4,128)}, u32[]{:S(2)}) copy-start(f32[4,4096]{1,0:T(4,128)} %param.17) | copy-start | bytes 196612
  0.6 26.6 %copy-start.8 = (bf16[240,512]{1,0:T(8,128)(2,1)S(1)}, bf16[240,512]{1,0:T(8,128)(2,1)}, u32[]{:S(2)}) copy-start(bf16[240,512]{1,0:T(8,128)(2,1)} %constant.46.clone.refs_2_.refs_1_) | copy-start | bytes 737284
  0.7 20.6 %copy-start.17 = (s32[4]{0:T(128)S(1)}, s32[4]{0:T(128)}, u32[]{:S(2)}) copy-start(s32[4]{0:T(128)} %param.18) | copy-start | bytes 52
  1.7 19.4 %collective-permute-start.2 = (bf16[16,5120]{1,0:T(8,128)(2,1)S(1)}, bf16[16,5120]{1,0:T(8,128)(2,1)S(1)}, u32[]{:S(2)}, u32[]{:S(2)}) collective-permute-start(bf16[16,5120]{1,0:T(8,128)(2,1)S(1)} %constant_dynamic-slice_fusion), channel_id=1, source_target_pairs={{0,4},{4,8},{8,12},{12,16},{16,20},{20,24},{24,28},{1,5},{5,9},{9,... | collective-permute-start | bytes 491528 | tf_op jit(solution)/shard_map/ppermute | solution.py:558
  6.5 14.6 %collective-permute-start.3 = (bf16[16,5120]{1,0:T(8,128)(2,1)S(1)}, bf16[16,5120]{1,0:T(8,128)(2,1)S(1)}, u32[]{:S(2)}, u32[]{:S(2)}) collective-permute-start(bf16[16,5120]{1,0:T(8,128)(2,1)S(1)} %constant_dynamic-slice_fusion), channel_id=1, source_target_pairs={{4,0},{8,4},{12,8},{16,12},{20,16},{24,20},{28,24},{5,1},{9,5},{13... | collective-permute-start | bytes 491528 | tf_op jit(solution)/shard_map/ppermute | solution.py:558
  8.8 12.2 %collective-permute-start = (bf16[4,1,112,128]{3,2,1,0:T(8,128)(2,1)S(1)}, bf16[4,1,112,128]{3,2,1,0:T(8,128)(2,1)S(1)}, u32[]{:S(2)}, u32[]{:S(2)}) collective-permute-start(bf16[4,1,112,128]{3,2,1,0:T(8,128)(2,1)S(1)} %pad.4), channel_id=1, source_target_pairs={{0,16},{4,20},{8,24},{12,28},{16,0},{20,4},{24,8},{28,12},{1,17},{... | collective-permute-start | bytes 344072 | tf_op jit(solution)/shard_map/ppermute | solution.py:519
  21.0 6.1 %collective-permute-start.1 = (bf16[4,2,112,128]{3,2,1,0:T(8,128)(2,1)S(1)}, bf16[4,2,112,128]{3,2,1,0:T(8,128)(2,1)S(1)}, u32[]{:S(2)}, u32[]{:S(2)}) collective-permute-start(bf16[4,2,112,128]{3,2,1,0:T(8,128)(2,1)S(1)} %pad_maximum_fusion.3), channel_id=1, source_target_pairs={{0,8},{4,12},{8,0},{12,4},{16,24},{20,28},{24,16},{28,20},{1,9},{5... | collective-permute-start | bytes 688136 | tf_op jit(solution)/shard_map/ppermute | solution.py:519
  21.2 6.0 %collective-permute-start.4 = (bf16[2,16,5120]{2,1,0:T(8,128)(2,1)S(1)}, bf16[2,16,5120]{2,1,0:T(8,128)(2,1)S(1)}, u32[]{:S(2)}, u32[]{:S(2)}) collective-permute-start(bf16[2,16,5120]{2,1,0:T(8,128)(2,1)S(1)} %pad_maximum_fusion.2.refs_0_), channel_id=1, source_target_pairs={{0,1},{1,0},{2,3},{3,2},{4,5},{5,4},{6,7},{7,6},{8,9},{9,8},{10,11... | collective-permute-start | bytes 983048 | tf_op jit(solution)/shard_map/ppermute | solution.py:582
  27.2 6.2 %copy-start.6 = (s32[32,80]{1,0:T(8,128)S(1)}, s32[32,80]{1,0:T(8,128)}, u32[]{:S(2)}) copy-start(s32[32,80]{1,0:T(8,128)} %valid_ref.1) | copy-start | bytes 30724
  27.2 6.1 %copy-start.13 = (bf16[80,240]{1,0:T(8,128)(2,1)S(1)}, bf16[80,240]{1,0:T(8,128)(2,1)}, u32[]{:S(2)}) copy-start(bf16[80,240]{1,0:T(8,128)(2,1)} %constant.47.clone.x_ref) | copy-start | bytes 115204
  27.2 6.1 %copy-start.15 = (bf16[48,256]{1,0:T(8,128)(2,1)S(1)}, bf16[48,256]{1,0:T(8,128)(2,1)}, u32[]{:S(2)}) copy-start(bf16[48,256]{1,0:T(8,128)(2,1)} %constant.48.clone.tz_ref) | copy-start | bytes 73732
  31.2 6.5 %copy-start.9 = (bf16[256,256]{1,0:T(8,128)(2,1)S(1)}, bf16[256,256]{1,0:T(8,128)(2,1)}, u32[]{:S(2)}) copy-start(bf16[256,256]{1,0:T(8,128)(2,1)} %constant.54.clone.bz_ref) | copy-start | bytes 393220
  31.2 6.5 %copy-start.10 = (bf16[160,208]{1,0:T(8,128)(2,1)S(1)}, bf16[160,208]{1,0:T(8,128)(2,1)}, u32[]{:S(2)}) copy-start(bf16[160,208]{1,0:T(8,128)(2,1)} %constant.53.clone.by_ref) | copy-start | bytes 199684
  31.2 6.5 %copy-start.11 = (bf16[112,144]{1,0:T(8,128)(2,1)S(1)}, bf16[112,144]{1,0:T(8,128)(2,1)}, u32[]{:S(2)}) copy-start(bf16[112,144]{1,0:T(8,128)(2,1)} %constant.50.clone.y_ref) | copy-start | bytes 96772
  31.2 6.5 %copy-start.12 = (bf16[80,144]{1,0:T(8,128)(2,1)S(1)}, bf16[80,144]{1,0:T(8,128)(2,1)}, u32[]{:S(2)}) copy-start(bf16[80,144]{1,0:T(8,128)(2,1)} %constant.51.clone.x_ref) | copy-start | bytes 69124
  31.2 6.5 %copy-start.14 = (bf16[64,160]{1,0:T(8,128)(2,1)S(1)}, bf16[64,160]{1,0:T(8,128)(2,1)}, u32[]{:S(2)}) copy-start(bf16[64,160]{1,0:T(8,128)(2,1)} %constant.52.clone.bx_ref) | copy-start | bytes 61444
  31.2 6.5 %copy-start.16 = (f32[8,128]{1,0:T(8,128)S(1)}, f32[8,128]{1,0:T(8,128)}, u32[]{:S(2)}) copy-start(f32[8,128]{1,0:T(8,128)} %constant.49.clone.ones_ref) | copy-start | bytes 12292
  31.2 6.5 %collective-permute-start.5 = (bf16[1,4,112,128]{3,2,1,0:T(8,128)(2,1)S(1)}, bf16[1,4,112,128]{3,2,1,0:T(8,128)(2,1)S(1)}, u32[]{:S(2)}, u32[]{:S(2)}) collective-permute-start(bf16[1,4,112,128]{3,2,1,0:T(8,128)(2,1)S(1)} %slice.76), channel_id=1, source_target_pairs={{0,4},{4,0},{8,12},{12,8},{16,20},{20,16},{24,28},{28,24},{1,5},{5... | collective-permute-start | bytes 344072 | tf_op jit(solution)/shard_map/ppermute | solution.py:519
  31.3 16.5 %collective-permute-start.6 = (bf16[3,4,112,128]{3,2,1,0:T(8,128)(2,1)S(1)}, bf16[3,4,112,128]{3,2,1,0:T(8,128)(2,1)S(1)}, u32[]{:S(2)}, u32[]{:S(2)}) collective-permute-start(bf16[3,4,112,128]{3,2,1,0:T(8,128)(2,1)S(1)} %slice.78), channel_id=1, source_target_pairs={{0,4},{4,0},{8,12},{12,8},{16,20},{20,16},{24,28},{28,24},{1,5},{5... | collective-permute-start | bytes 1032200 | tf_op jit(solution)/shard_map/ppermute | solution.py:519
  46.2 11.3 %collective-permute-start.7 = (f32[2,32,1280]{2,1,0:T(8,128)S(1)}, f32[2,32,1280]{2,1,0:T(8,128)S(1)}, u32[]{:S(2)}, u32[]{:S(2)}) collective-permute-start(f32[2,32,1280]{2,1,0:T(8,128)S(1)} %get-tuple-element.48), channel_id=1, source_target_pairs={{0,2},{1,3},{2,0},{3,1},{4,6},{5,7},{6,4},{7,5},{8,10},{9,11},{10,... | collective-permute-start | bytes 983048 | tf_op jit(solution)/shard_map/ppermute | solution.py:612
  57.0 11.0 %collective-permute-start.8 = (f32[2,32,1280]{2,1,0:T(8,128)S(1)}, f32[2,32,1280]{2,1,0:T(8,128)S(1)}, u32[]{:S(2)}, u32[]{:S(2)}) collective-permute-start(f32[2,32,1280]{2,1,0:T(8,128)S(1)} %get-tuple-element.83), channel_id=1, source_target_pairs={{0,2},{1,3},{2,0},{3,1},{4,6},{5,7},{6,4},{7,5},{8,10},{9,11},{10,... | collective-permute-start | bytes 983048 | tf_op jit(solution)/shard_map/ppermute | solution.py:612
  66.5 10.7 %collective-permute-start.9 = (f32[2,32,1280]{2,1,0:T(8,128)S(1)}, f32[2,32,1280]{2,1,0:T(8,128)S(1)}, u32[]{:S(2)}, u32[]{:S(2)}) collective-permute-start(f32[2,32,1280]{2,1,0:T(8,128)S(1)} %get-tuple-element.91), channel_id=1, source_target_pairs={{0,2},{1,3},{2,0},{3,1},{4,6},{5,7},{6,4},{7,5},{8,10},{9,11},{10,... | collective-permute-start | bytes 983048 | tf_op jit(solution)/shard_map/ppermute | solution.py:612
  68.1 9.2 %collective-permute-start.10 = (f32[5,32,1280]{2,1,0:T(8,128)S(1)}, f32[5,32,1280]{2,1,0:T(8,128)S(1)}, u32[]{:S(2)}, u32[]{:S(2)}) collective-permute-start(f32[5,32,1280]{2,1,0:T(8,128)S(1)} %slice_dynamic-update-slice_fusion), channel_id=1, source_target_pairs={{0,1},{1,0},{2,3},{3,2},{4,5},{5,4},{6,7},{7,6},{8,9},{9,8},{10,11... | collective-permute-start | bytes 2457608 | tf_op jit(solution)/shard_map/ppermute | solution.py:615
  76.7 12.1 %copy-start.3 = (f32[32,1280]{1,0:T(8,128)}, f32[32,1280]{1,0:T(8,128)S(1)}, u32[]{:S(2)}) copy-start(f32[32,1280]{1,0:T(8,128)S(1)} %get-tuple-element.75.refs_3_) | copy-start | bytes 491524
  76.7 10.2 %collective-permute-start.13 = (f32[2,32,1280]{2,1,0:T(8,128)S(1)}, f32[2,32,1280]{2,1,0:T(8,128)S(1)}, u32[]{:S(2)}, u32[]{:S(2)}) collective-permute-start(f32[2,32,1280]{2,1,0:T(8,128)S(1)} %get-tuple-element.66), channel_id=1, source_target_pairs={{0,2},{1,3},{2,0},{3,1},{4,6},{5,7},{6,4},{7,5},{8,10},{9,11},{10,... | collective-permute-start | bytes 983048 | tf_op jit(solution)/shard_map/ppermute | solution.py:612
  77.3 3.6 %collective-permute-start.11 = (f32[3,4]{1,0:T(4,128)S(1)}, f32[3,4]{1,0:T(4,128)S(1)}, u32[]{:S(2)}, u32[]{:S(2)}) collective-permute-start(f32[3,4]{1,0:T(4,128)S(1)} %pad_maximum_fusion.5), channel_id=1, source_target_pairs={{0,4},{4,0},{8,12},{12,8},{16,20},{20,16},{24,28},{28,24},{1,5},{5... | collective-permute-start | bytes 152 | tf_op jit(solution)/shard_map/ppermute | solution.py:620
  81.0 5.9 %collective-permute-start.12 = (f32[3,4]{1,0:T(4,128)S(1)}, f32[3,4]{1,0:T(4,128)S(1)}, u32[]{:S(2)}, u32[]{:S(2)}) collective-permute-start(f32[3,4]{1,0:T(4,128)S(1)} %select_add_fusion.2), channel_id=1, source_target_pairs={{0,8},{4,12},{8,0},{12,4},{16,24},{20,28},{24,16},{28,20},{1,9},{5... | collective-permute-start | bytes 152 | tf_op jit(solution)/shard_map/ppermute | solution.py:620
  87.0 4.5 %collective-permute-start.14 = (f32[3,4]{1,0:T(4,128)S(1)}, f32[3,4]{1,0:T(4,128)S(1)}, u32[]{:S(2)}, u32[]{:S(2)}) collective-permute-start(f32[3,4]{1,0:T(4,128)S(1)} %select_add_fusion.1), channel_id=1, source_target_pairs={{0,16},{4,20},{8,24},{12,28},{16,0},{20,4},{24,8},{28,12},{1,17},{... | collective-permute-start | bytes 152 | tf_op jit(solution)/shard_map/ppermute | solution.py:620
  91.5 4.5 %collective-permute-start.18 = (f32[3,32,1280]{2,1,0:T(8,128)}, f32[3,32,1280]{2,1,0:T(8,128)S(1)}, u32[]{:S(2)}, u32[]{:S(2)}) collective-permute-start(f32[3,32,1280]{2,1,0:T(8,128)} %pad_maximum_fusion), channel_id=1, source_target_pairs={{0,1},{1,0},{2,3},{3,2},{4,5},{5,4},{6,7},{7,6},{8,9},{9,8},{10,11... | collective-permute-start | bytes 1474568 | tf_op jit(solution)/shard_map/ppermute | solution.py:632
  91.8 2.0 %collective-permute-start.15 = (f32[4,6]{1,0:T(4,128)S(1)}, f32[4,6]{1,0:T(4,128)S(1)}, u32[]{:S(2)}, u32[]{:S(2)}) collective-permute-start(f32[4,6]{1,0:T(4,128)S(1)} %pad_maximum_fusion.6), channel_id=1, source_target_pairs={{0,1},{1,0},{2,3},{3,2},{4,5},{5,4},{6,7},{7,6},{8,9},{9,8},{10,11... | collective-permute-start | bytes 296 | tf_op jit(solution)/shard_map/ppermute | solution.py:550
  92.4 3.6 %collective-permute-start.16 = (f32[4,6]{1,0:T(4,128)S(1)}, f32[4,6]{1,0:T(4,128)S(1)}, u32[]{:S(2)}, u32[]{:S(2)}) collective-permute-start(f32[4,6]{1,0:T(4,128)S(1)} %pad_maximum_fusion.6), channel_id=1, source_target_pairs={{0,2},{1,3},{2,0},{3,1},{4,6},{5,7},{6,4},{7,5},{8,10},{9,11},{10,... | collective-permute-start | bytes 296 | tf_op jit(solution)/shard_map/ppermute | solution.py:550
  92.9 3.0 %collective-permute-start.17 = (f32[4,6]{1,0:T(4,128)S(1)}, f32[4,6]{1,0:T(4,128)S(1)}, u32[]{:S(2)}, u32[]{:S(2)}) collective-permute-start(f32[4,6]{1,0:T(4,128)S(1)} %pad_maximum_fusion.6), channel_id=1, source_target_pairs={{0,3},{1,2},{2,1},{3,0},{4,7},{5,6},{6,5},{7,4},{8,11},{9,10},{10,... | collective-permute-start | bytes 296 | tf_op jit(solution)/shard_map/ppermute | solution.py:550
  (5 other events, 4.7 us)

commit v8 on v7

--- a/solution.py
+++ b/solution.py
@@ -312,7 +312,7 @@
 
 
 def corr_kernel(
-    dims, rot, entry, place_ref, held_ref, last_ref, mask_ref, spec_ref,
+    dims, rot, entry, place_ref, tile_ref, held_ref, last_ref, mask_ref, spec_ref,
     z_ref, ones_ref, y_ref, x_ref, bx_ref, by_ref, bz_ref,
     mine_ref, side_ref, far_ref, stat_ref,
     bank_buf, depth_buf, rows_buf, first_buf, second_buf, third_buf, back_buf, vol_buf,
@@ -323,7 +323,7 @@
     pad_y = half_y + -half_y % 8
     for i, block in enumerate(HELD):
         for ref, at, tile in ((held_ref, rot, block), (last_ref, entry, block ^ 1)):
-            store(bank_buf, (place_ref[1] ^ tile) * odd(BLOCK_ROWS), ref[at, i].astype(F32))
+            store(bank_buf, (tile_ref[0] ^ tile) * odd(BLOCK_ROWS), ref[at, i].astype(F32))
     tmpl = jnp.concatenate(
         [
             pick(bank_buf, [a * CHUNKS + i for i in range(CHUNKS)], BLOCKS, odd(BLOCK_ROWS))
@@ -434,7 +434,7 @@
     stat_ref[...] = jnp.where(row == 0, number_sum, jnp.where(row == 1, total_sum, jnp.sum(square)))
 
 
-def correlate(place, held, rot, last, entry, mask, spec, tmpl_z, dims, tables):
+def correlate(place, tile, held, rot, last, entry, mask, spec, tmpl_z, dims, tables):
     x_cells, y_cells, z_cells = dims
     n_x, n_y = x_cells + TEMPL, y_cells + HALF
     pad_y = n_y // 2 + -(n_y // 2) % 8
@@ -448,7 +448,7 @@
             jax.ShapeDtypeStruct((2, x_cells, width), F32),
             jax.ShapeDtypeStruct((8, LANES), F32),
         ),
-        in_specs=[pl.BlockSpec(memory_space=pltpu.SMEM)] + [vmem] * 11,
+        in_specs=[pl.BlockSpec(memory_space=pltpu.SMEM)] * 2 + [vmem] * 11,
         out_specs=(vmem,) * 4,
         scratch_shapes=[
             pltpu.VMEM((BLOCKS * odd(BLOCK_ROWS), LANES), F32),
@@ -464,7 +464,7 @@
         cost_estimate=pl.CostEstimate(flops=15 * 10**9, bytes_accessed=10**7, transcendentals=0),
         name="correlate",
     )(
-        place, held, last, mask, spec,
+        place, tile, held, last, mask, spec,
         tmpl_z, tables["ones_z"], tables["tmpl_y"], tables["tmpl_x"],
         tables["back_x"], tables["back_y"], tables["back_z"],
     )
@@ -477,26 +477,26 @@
 
     def step(i):
         lanes = pl.ds(pl.multiple_of(i * LANES, LANES), LANES)
-        for top in range(0, best_ref.shape[0], 8):
-            rows = slice(top, top + 8)
-            mask = mask_ref[place_ref[0] * blocks + i, rows]
-            scores = []
-            for k, (at, entry) in enumerate(pieces):
-                corr = refs[at][rows, lanes] if entry is None else refs[at][entry, rows, lanes]
-                scores.append((corr - coef_ref[k, 0]) * coef_ref[k, 1])
-            high = functools.reduce(jnp.maximum, scores)
-            total = jnp.zeros_like(high)
-            moment = [jnp.zeros_like(high) for _ in range(4)]
-            for k, score in enumerate(scores):
-                weight = jnp.exp(score - high)
-                total = total + weight
-                for c in range(4):
-                    moment[c] = moment[c] + weight * coef_ref[k, 2 + c]
-            best_ref[rows, lanes] = mask * high
-            evid_ref[rows, lanes] = mask * (high + jnp.log(total))
-            share = mask / total
+
+        def score(k):
+            at, entry = pieces[k]
+            corr = refs[at][:, lanes] if entry is None else refs[at][entry, :, lanes]
+            return (corr - coef_ref[k, 0]) * coef_ref[k, 1]
+
+        mask = mask_ref[place_ref[0] * blocks + i]
+        high = functools.reduce(jnp.maximum, [score(k) for k in range(len(pieces))])
+        total = jnp.zeros_like(high)
+        moment = [jnp.zeros_like(high) for _ in range(4)]
+        for k in range(len(pieces)):
+            weight = jnp.exp(score(k) - high)
+            total = total + weight
             for c in range(4):
-                mom_ref[c, rows, lanes] = moment[c] * share
+                moment[c] = moment[c] + weight * coef_ref[k, 2 + c]
+        best_ref[:, lanes] = mask * high
+        evid_ref[:, lanes] = mask * (high + jnp.log(total))
+        share = mask / total
+        for c in range(4):
+            mom_ref[c, :, lanes] = moment[c] * share
 
     loop(blocks, step)
 
@@ -574,9 +574,12 @@
     if by_blocks:
         held = templates.reshape(rots, 1, EACH * CHUNKS, LANES)
         held = jnp.pad(held, ((0, 0), (0, 0), (0, BLOCK_ROWS - EACH * CHUNKS), (0, 0)))
+        held, tomogram_after = lax.optimization_barrier((held, tomogram))
         held = jnp.concatenate([held, swap_blocks(held, "tile", 4)], axis=1)
+    else:
+        tomogram_after = tomogram
     half = x_cells // 2
-    piece = lax.dynamic_slice_in_dim(tomogram, (me & 1) * half, half, 0)
+    piece = lax.dynamic_slice_in_dim(tomogram_after, (me & 1) * half, half, 0)
     mine = jnp.stack(neighbours(piece, "tile"))
     side_swap = [(i, i ^ 1) for i in range(groups)]
     other = lax.ppermute(mine, "rot", side_swap)
@@ -587,7 +590,8 @@
         tile = jnp.zeros_like(tile)
     one_hot = (rot_index[:, None] == jnp.arange(quats.shape[1], dtype=jnp.int32)[None, :]).astype(F32)
     orient = jnp.einsum("rq,kq->rk", one_hot, quats, precision=lax.Precision.HIGHEST)
-    place = me_place = jnp.stack([me, tile]).astype(jnp.int32)
+    place = me_place = jnp.reshape(me, (1,)).astype(jnp.int32)
+    tile = jnp.reshape(tile, (1,)).astype(jnp.int32)
     own = slab_rows(place, [tomogram], x_cells, dims, tables, "slab_own")
     halo = slab_rows(place, [mine, other], TEMPL, dims, tables, "slab_halo")
     if by_blocks:
@@ -602,7 +606,7 @@
         if r >= 2:
             place, fars[r - 2] = lax.optimization_barrier((place, fars[r - 2]))
         mine, side, far, stat = correlate(
-            place, held, r, lasts[min(r, 1)], max(r - 1, 0), mask, spec, tmpl_z, dims, tables
+            place, tile, held, r, lasts[min(r, 1)], max(r - 1, 0), mask, spec, tmpl_z, dims, tables
         )
         if r >= 1:
             stat, fars[r - 1] = lax.optimization_barrier((stat, fars[r - 1]))
@@ -611,7 +615,7 @@
         stats.append(stat[:3, 0])
         fars.append(lax.ppermute(far, "rot", far_swap))
         if r == rots - 2:
-            early = jnp.stack(sides + [f[1] for f in fars[:-1]])
+            early = jnp.stack(sides[:-1] + [f[1] for f in fars[:-1]])
             early = lax.ppermute(early, "rot", side_swap)
     state = jnp.stack(stats, axis=1)
     state, early, fars[rots - 2] = lax.optimization_barrier((state, early, fars[rots - 2]))
@@ -619,8 +623,8 @@
     while step < tiles:
         partner = lax.ppermute(state, "tile", [(i, i ^ step) for i in range(tiles)])
         if step * 4 == tiles:
-            partner, fars[rots - 1] = lax.optimization_barrier((partner, fars[rots - 1]))
-            last = jnp.stack([sides[rots - 1], fars[rots - 2][1], fars[rots - 1][1]])
+            late = jnp.where(partner[0, 0] >= 0.0, fars[rots - 1][1], 0.0)
+            last = jnp.stack([sides[rots - 2], sides[rots - 1], fars[rots - 2][1], late])
         if step * 2 == tiles:
             partner, last = lax.optimization_barrier((partner, last))
         state = merge(state, partner)
@@ -633,9 +637,9 @@
     arrays = mines + fars + [early, last]
     at_far, at_early, at_last = rots, 2 * rots, 2 * rots + 1
     pieces = [(r, None) for r in range(rots)]
-    pieces += [(at_early, r) for r in range(rots - 1)] + [(at_last, 0)]
+    pieces += [(at_early, r) for r in range(rots - 2)] + [(at_last, 0), (at_last, 1)]
     pieces += [(at_far + r, 0) for r in range(rots)]
-    pieces += [(at_early, rots - 1 + r) for r in range(rots - 2)] + [(at_last, 1), (at_last, 2)]
+    pieces += [(at_early, rots - 2 + r) for r in range(rots - 2)] + [(at_last, 2), (at_last, 3)]
     return combine(me_place, coefs.reshape(groups * rots, 6), mask, arrays, pieces)
 
 

time: 102 us -> 98.2 us (0.963)
  other arithmetic: 19.7 us -> 1.56 us
  Pallas kernels: 31.4 us -> 44.2 us
  local copies, waits for them, and re-layouts: 7.02 us -> 9.4 us
  waiting for transfers between devices: 22.4 us -> 21 us
    pallas_call x2 -> x0, other arithmetic: 18.2 us -> none  [correlate(): pl.pallas_call(functools.partial(corr_kernel, dims, rot, entry), out_shap...]
    pallas_call x2 -> x4, Pallas kernels: 16.9 us -> 31.1 us  [correlate(): pl.pallas_call(functools.partial(corr_kernel, dims, rot, entry), out_shap...]
    ppermute x4, waiting for transfers between devices: 5.86 us -> 0.94 us  [local(): fars.append(lax.ppermute(far, 'rot', far_swap))]
    ppermute x3, waiting for transfers between devices: 6.16 us -> 8.5 us  [local(): partner = lax.ppermute(state, 'tile', [(i, i ^ step) for i in range(tiles)])]
    unnamed x38 -> x44, local copies, waits for them, and re-layouts: 4.77 us -> 6.68 us
    pallas_call x2, Pallas kernels: 6.67 us -> 5.59 us  [slab_rows(): pl.pallas_call(functools.partial(slab_rows_kernel, dims), out_shape=jax.S...]
  transfers between devices with their start and end apart: 19 -> 19, of which waited for: 6 -> 8; matrix products, arithmetic and copies ran while one was open for 21% -> 3% of each run, Pallas kernels for 24% -> 39%
where the time goes in v8:
time: 98.2 us; the launch traced here: 97.9 us
  Pallas kernels  44.2 us (45%)
  waiting for transfers between devices  21 us (21%)
  starting transfers between devices  19.6 us (20%)
  local copies, waits for them, and re-layouts  9.4 us (10%)
  between operations  1.77 us (2%)
  other arithmetic  1.56 us (2%)
    pallas_call x4, Pallas kernels, correlate(): pl.pallas_call(functools.partial(corr_kernel, dims, rot, entry), out_shap...  31.1 us
    ppermute x4, waiting for transfers between devices, swap_blocks(): lax.ppermute(block, axis, [(i, i ^ step) for i in range(lax.axis_size(axi...  8.58 us
    ppermute x3, waiting for transfers between devices, local(): partner = lax.ppermute(state, 'tile', [(i, i ^ step) for i in range(tiles)])  8.5 us
    ppermute x4, starting transfers between devices, swap_blocks(): lax.ppermute(block, axis, [(i, i ^ step) for i in range(lax.axis_size(axi...  6.85 us
    unnamed x44, local copies, waits for them, and re-layouts  6.68 us
    pallas_call x2, Pallas kernels, slab_rows(): pl.pallas_call(functools.partial(slab_rows_kernel, dims), out_shape=jax.S...  5.59 us
    ppermute x1, starting transfers between devices, neighbours(): lax.ppermute(block, axis, forward)  4.85 us
    pallas_call x1, Pallas kernels, slab_x(): pl.pallas_call(functools.partial(slab_x_kernel, dims), out_shape=(jax.Sha...  4.37 us
  transfers between devices with their start and end apart: 19, of which 8 were waited for; matrix products, arithmetic and copies ran while one was open for 3% of the time, Pallas kernels for 39%

profile of v8, /device:TPU:0, one launch (start us, length us, event | category | flops | bytes accessed | tf_op | source)
XLA Modules:
  0.0 97.9 jit_solution(1062475615453595344)
XLA Ops:
  0.7 1.0 %reshape.73 = bf16[4,1,108,128]{3,2,0,1:T(8,128)(2,1)S(1)} reshape(bf16[4,13824]{1,0:T(4,128)(2,1)} %param.15) | data formatting | bytes 221184 | tf_op jit(solution)/shard_map/reshape | solution.py:575
  1.7 0.9 constant_dynamic-slice_fusion
  2.6 4.9 %collective-permute-start.2 = (bf16[16,5120]{1,0:T(8,128)(2,1)S(1)}, bf16[16,5120]{1,0:T(8,128)(2,1)S(1)}, u32[]{:S(2)}, u32[]{:S(2)}) collective-permute-start(bf16[16,5120]{1,0:T(8,128)(2,1)S(1)} %constant_dynamic-slice_fusion), channel_id=1, source_target_pairs={{0,4},{4,8},{8,12},{12,16},{16,20},{20,24},{24,28},{1,5},{5,9},{9,... | collective-permute-start | bytes 491528 | tf_op jit(solution)/shard_map/ppermute | solution.py:558
  7.5 1.3 %collective-permute-start.3 = (bf16[16,5120]{1,0:T(8,128)(2,1)S(1)}, bf16[16,5120]{1,0:T(8,128)(2,1)S(1)}, u32[]{:S(2)}, u32[]{:S(2)}) collective-permute-start(bf16[16,5120]{1,0:T(8,128)(2,1)S(1)} %constant_dynamic-slice_fusion), channel_id=1, source_target_pairs={{4,0},{8,4},{12,8},{16,12},{20,16},{24,20},{28,24},{5,1},{9,5},{13... | collective-permute-start | bytes 491528 | tf_op jit(solution)/shard_map/ppermute | solution.py:558
  8.8 4.7 %collective-permute-start = (bf16[4,1,112,128]{3,2,1,0:T(8,128)(2,1)S(1)}, bf16[4,1,112,128]{3,2,1,0:T(8,128)(2,1)S(1)}, u32[]{:S(2)}, u32[]{:S(2)}) collective-permute-start(bf16[4,1,112,128]{3,2,1,0:T(8,128)(2,1)S(1)} %pad.4), channel_id=1, source_target_pairs={{0,16},{4,20},{8,24},{12,28},{16,0},{20,4},{24,8},{28,12},{1,17},{... | collective-permute-start | bytes 344072 | tf_op jit(solution)/shard_map/ppermute | solution.py:519
  13.5 1.0 copy-done.7
  14.4 0.9 copy-done.9
  15.4 2.3 %slab_own.1.own_ref = f32[3616,128]{1,0:T(8,128)S(1)} custom-call(s32[1]{0:T(128)} %bitcast.place_ref, bf16[32,5120]{1,0:T(8,128)(2,1)S(1)} %copy-done.7, bf16[240,512]{1,0:T(8,128)(2,1)S(1)} %copy-done.9), custom_call_target="tpu_custom_call" | custom-call | flops 3200000000 | bytes 1000000 | tf_op jit(solution)/shard_map/slab_own/pallas_call | solution.py:239
  17.7 1.3 %copy-done.19 = f32[3616,128]{1,0:T(8,128)} copy-done((f32[3616,128]{1,0:T(8,128)}, f32[3616,128]{1,0:T(8,128)S(1)}, u32[]{:S(2)}) %copy-start.19) | copy-done | bytes 1851416
  18.9 3.0 %collective-permute-done = bf16[4,1,112,128]{3,2,1,0:T(8,128)(2,1)S(1)} collective-permute-done((bf16[4,1,112,128]{3,2,1,0:T(8,128)(2,1)S(1)}, bf16[4,1,112,128]{3,2,1,0:T(8,128)(2,1)S(1)}, u32[]{:S(2)}, u32[]{:S(2)}) %collective-permute-start) | collective-permute-done | bytes 114720 | tf_op jit(solution)/shard_map/ppermute | solution.py:519
  22.5 5.6 %collective-permute-done.1 = bf16[4,2,112,128]{3,2,1,0:T(8,128)(2,1)S(1)} collective-permute-done((bf16[4,2,112,128]{3,2,1,0:T(8,128)(2,1)S(1)}, bf16[4,2,112,128]{3,2,1,0:T(8,128)(2,1)S(1)}, u32[]{:S(2)}, u32[]{:S(2)}) %collective-permute-start.1) | collective-permute-done | bytes 229408 | tf_op jit(solution)/shard_map/ppermute | solution.py:519
  28.2 3.3 %slab_halo.1.halo_ref = f32[5424,128]{1,0:T(8,128)S(1)} custom-call(s32[1]{0:T(128)} %bitcast.place_ref, bf16[2,16,5120]{2,1,0:T(8,128)(2,1)S(1)} %pad_maximum_fusion.3.refs_0_, bf16[2,16,5120]{2,1,0:T(8,128)(2,1)S(1)} %collective-permute-done.4.refs_1_, bf16[240,512]{1,0:T(8,128)(2,1)S(1)} %copy-done.10), custom_call_target="tpu_custom_call" | custom-call | flops 4800000000 | bytes 1000000 | tf_op jit(solution)/shard_map/slab_halo/pallas_call | solution.py:239
  31.7 2.0 %collective-permute-start.6 = (bf16[3,4,112,128]{3,2,1,0:T(8,128)(2,1)S(1)}, bf16[3,4,112,128]{3,2,1,0:T(8,128)(2,1)S(1)}, u32[]{:S(2)}, u32[]{:S(2)}) collective-permute-start(bf16[3,4,112,128]{3,2,1,0:T(8,128)(2,1)S(1)} %slice.81), channel_id=1, source_target_pairs={{0,4},{4,0},{8,12},{12,8},{16,20},{20,16},{24,28},{28,24},{1,5},{5... | collective-permute-start | bytes 1032200 | tf_op jit(solution)/shard_map/ppermute | solution.py:519
  33.8 4.4 %slab_x.1 = (f32[13,2,80,1024]{3,2,1,0:T(8,128)S(1)}, f32[40,32,128]{2,1,0:T(8,128)S(1)}, bf16[8,256,256]{2,1,0:T(8,128)(2,1)S(1)}) custom-call(f32[3616,128]{1,0:T(8,128)S(1)} %copy-done.20, f32[5424,128]{1,0:T(8,128)S(1)} %slab_halo.1.halo_ref, bf16[80,240]{1,0:T(8,128)(2,1)S(1)} %copy-done.15, s32[32,80]{1,0:T(8,128)S(1)} %copy-done.8, ...), custom_call_target="tpu_custom_call" | custom-call | flops 5000000000 | bytes 1000000 | tf_op jit(solution)/shard_map/slab_x/pallas_call | solution.py:298
  38.2 7.7 %correlate.4 = (f32[32,1280]{1,0:T(8,128)S(1)}, f32[32,1280]{1,0:T(8,128)S(1)}, f32[2,32,1280]{2,1,0:T(8,128)S(1)}, f32[8,128]{1,0:T(8,128)S(1)}) custom-call(s32[1]{0:T(128)} %bitcast.place_ref, s32[1]{0:T(128)} %bitcast.1.tile_ref, bf16[4,4,112,128]{3,2,1,0:T(8,128)(2,1)S(1)} %pad_maximum_fusion.2.held_ref, ...), custom_call_target="tpu_custom_call" | custom-call | flops 15000000512 | bytes 10000000 | tf_op jit(solution)/shard_map/correlate/pallas_call | solution.py:443
  45.9 1.6 %collective-permute-start.7 = (f32[2,32,1280]{2,1,0:T(8,128)S(1)}, f32[2,32,1280]{2,1,0:T(8,128)S(1)}, u32[]{:S(2)}, u32[]{:S(2)}) collective-permute-start(f32[2,32,1280]{2,1,0:T(8,128)S(1)} %get-tuple-element.50), channel_id=1, source_target_pairs={{0,2},{1,3},{2,0},{3,1},{4,6},{5,7},{6,4},{7,5},{8,10},{9,11},{10,... | collective-permute-start | bytes 983048 | tf_op jit(solution)/shard_map/ppermute | solution.py:616
  47.5 7.9 %correlate.5 = (f32[32,1280]{1,0:T(8,128)S(1)}, f32[32,1280]{1,0:T(8,128)S(1)}, f32[2,32,1280]{2,1,0:T(8,128)S(1)}, f32[8,128]{1,0:T(8,128)S(1)}) custom-call(s32[1]{0:T(128)} %bitcast.place_ref, s32[1]{0:T(128)} %bitcast.1.tile_ref, bf16[4,4,112,128]{3,2,1,0:T(8,128)(2,1)S(1)} %pad_maximum_fusion.2.held_ref, ...), custom_call_target="tpu_custom_call" | custom-call | flops 15000000512 | bytes 10000000 | tf_op jit(solution)/shard_map/correlate/pallas_call | solution.py:443
  56.7 7.7 %correlate.6 = (f32[32,1280]{1,0:T(8,128)S(1)}, f32[32,1280]{1,0:T(8,128)S(1)}, f32[2,32,1280]{2,1,0:T(8,128)S(1)}, f32[8,128]{1,0:T(8,128)S(1)}) custom-call(s32[1]{0:T(128)} %bitcast.place_ref, s32[1]{0:T(128)} %bitcast.1.tile_ref, bf16[4,4,112,128]{3,2,1,0:T(8,128)(2,1)S(1)} %pad_maximum_fusion.2.held_ref, ...), custom_call_target="tpu_custom_call" | custom-call | flops 15000000512 | bytes 10000000 | tf_op jit(solution)/shard_map/correlate/pallas_call | solution.py:443
  64.4 1.6 %collective-permute-start.9 = (f32[2,32,1280]{2,1,0:T(8,128)S(1)}, f32[2,32,1280]{2,1,0:T(8,128)S(1)}, u32[]{:S(2)}, u32[]{:S(2)}) collective-permute-start(f32[2,32,1280]{2,1,0:T(8,128)S(1)} %get-tuple-element.60), channel_id=1, source_target_pairs={{0,2},{1,3},{2,0},{3,1},{4,6},{5,7},{6,4},{7,5},{8,10},{9,11},{10,... | collective-permute-start | bytes 983048 | tf_op jit(solution)/shard_map/ppermute | solution.py:616
  66.2 7.7 %correlate.7 = (f32[32,1280]{1,0:T(8,128)S(1)}, f32[32,1280]{1,0:T(8,128)S(1)}, f32[2,32,1280]{2,1,0:T(8,128)S(1)}, f32[8,128]{1,0:T(8,128)S(1)}) custom-call(s32[1]{0:T(128)} %bitcast.place_ref, s32[1]{0:T(128)} %bitcast.1.tile_ref, bf16[4,4,112,128]{3,2,1,0:T(8,128)(2,1)S(1)} %pad_maximum_fusion.2.held_ref, ...), custom_call_target="tpu_custom_call" | custom-call | flops 15000000512 | bytes 10000000 | tf_op jit(solution)/shard_map/correlate/pallas_call | solution.py:443
  74.8 3.5 %collective-permute-done.11 = f32[3,4]{1,0:T(4,128)S(1)} collective-permute-done((f32[3,4]{1,0:T(4,128)S(1)}, f32[3,4]{1,0:T(4,128)S(1)}, u32[]{:S(2)}, u32[]{:S(2)}) %collective-permute-start.11) | collective-permute-done | bytes 80 | tf_op jit(solution)/shard_map/ppermute | solution.py:624
  78.4 3.6 %collective-permute-done.12 = f32[3,4]{1,0:T(4,128)S(1)} collective-permute-done((f32[3,4]{1,0:T(4,128)S(1)}, f32[3,4]{1,0:T(4,128)S(1)}, u32[]{:S(2)}, u32[]{:S(2)}) %collective-permute-start.12) | collective-permute-done | bytes 80 | tf_op jit(solution)/shard_map/ppermute | solution.py:624
  83.2 0.9 collective-permute-done.14.refs_7_
  84.2 0.9 pad_maximum_fusion.1
  85.1 1.5 %collective-permute-done.13 = f32[3,4]{1,0:T(4,128)S(1)} collective-permute-done((f32[3,4]{1,0:T(4,128)S(1)}, f32[3,4]{1,0:T(4,128)S(1)}, u32[]{:S(2)}, u32[]{:S(2)}) %collective-permute-start.13) | collective-permute-done | bytes 80 | tf_op jit(solution)/shard_map/ppermute | solution.py:624
  87.4 1.5 %collective-permute-start.16 = (f32[4,6]{1,0:T(4,128)S(1)}, f32[4,6]{1,0:T(4,128)S(1)}, u32[]{:S(2)}, u32[]{:S(2)}) collective-permute-start(f32[4,6]{1,0:T(4,128)S(1)} %pad_maximum_fusion.7), channel_id=1, source_target_pairs={{0,2},{1,3},{2,0},{3,1},{4,6},{5,7},{6,4},{7,5},{8,10},{9,11},{10,... | collective-permute-start | bytes 296 | tf_op jit(solution)/shard_map/ppermute | solution.py:550
  89.0 2.0 %collective-permute-done.16 = f32[4,6]{1,0:T(4,128)S(1)} collective-permute-done((f32[4,6]{1,0:T(4,128)S(1)}, f32[4,6]{1,0:T(4,128)S(1)}, u32[]{:S(2)}, u32[]{:S(2)}) %collective-permute-start.16) | collective-permute-done | bytes 128 | tf_op jit(solution)/shard_map/ppermute | solution.py:550
  91.0 1.0 collective-permute-done.17
  92.0 0.9 copy-done.2
  92.9 0.9 copy-done.4
  93.8 0.9 copy-done.6
  94.7 3.1 %combine.1 = (f32[32,1280]{1,0:T(8,128)}, f32[32,1280]{1,0:T(8,128)}, f32[4,32,1280]{2,1,0:T(8,128)}) custom-call(s32[1]{0:T(128)} %bitcast.place_ref, f32[16,6]{1,0:T(8,128)S(1)} %bitcast.31, f32[40,32,128]{2,1,0:T(8,128)S(1)} %get-tuple-element.45.mask_ref, f32[32,1280]{1,0:T(8,128)S(1)} %get-tuple-element.72.refs_0_, f32[32,1280]{1,0:T(8,128)S(1)} %copy-done.2, ...), custom_call_target="tpu_custom_call" | custom-call | tf_op jit(solution)/shard_map/combine/pallas_call | solution.py:508
  (92 shorter events, 4.6 us)
Async XLA Ops:
  0.6 21.6 %copy-start = (f32[4,4096]{1,0:T(4,128)S(1)}, f32[4,4096]{1,0:T(4,128)}, u32[]{:S(2)}) copy-start(f32[4,4096]{1,0:T(4,128)} %param.17) | copy-start | bytes 196612
  2.6 19.4 %collective-permute-start.2 = (bf16[16,5120]{1,0:T(8,128)(2,1)S(1)}, bf16[16,5120]{1,0:T(8,128)(2,1)S(1)}, u32[]{:S(2)}, u32[]{:S(2)}) collective-permute-start(bf16[16,5120]{1,0:T(8,128)(2,1)S(1)} %constant_dynamic-slice_fusion), channel_id=1, source_target_pairs={{0,4},{4,8},{8,12},{12,16},{16,20},{20,24},{24,28},{1,5},{5,9},{9,... | collective-permute-start | bytes 491528 | tf_op jit(solution)/shard_map/ppermute | solution.py:558
  7.5 14.6 %collective-permute-start.3 = (bf16[16,5120]{1,0:T(8,128)(2,1)S(1)}, bf16[16,5120]{1,0:T(8,128)(2,1)S(1)}, u32[]{:S(2)}, u32[]{:S(2)}) collective-permute-start(bf16[16,5120]{1,0:T(8,128)(2,1)S(1)} %constant_dynamic-slice_fusion), channel_id=1, source_target_pairs={{4,0},{8,4},{12,8},{16,12},{20,16},{24,20},{28,24},{5,1},{9,5},{13... | collective-permute-start | bytes 491528 | tf_op jit(solution)/shard_map/ppermute | solution.py:558
  8.8 13.2 %collective-permute-start = (bf16[4,1,112,128]{3,2,1,0:T(8,128)(2,1)S(1)}, bf16[4,1,112,128]{3,2,1,0:T(8,128)(2,1)S(1)}, u32[]{:S(2)}, u32[]{:S(2)}) collective-permute-start(bf16[4,1,112,128]{3,2,1,0:T(8,128)(2,1)S(1)} %pad.4), channel_id=1, source_target_pairs={{0,16},{4,20},{8,24},{12,28},{16,0},{20,4},{24,8},{28,12},{1,17},{... | collective-permute-start | bytes 344072 | tf_op jit(solution)/shard_map/ppermute | solution.py:519
  15.4 6.8 %copy-start.21 = (s32[4]{0:T(128)S(1)}, s32[4]{0:T(128)}, u32[]{:S(2)}) copy-start(s32[4]{0:T(128)} %param.18) | copy-start | bytes 52
  15.4 12.8 %copy-start.10 = (bf16[240,512]{1,0:T(8,128)(2,1)S(1)}, bf16[240,512]{1,0:T(8,128)(2,1)}, u32[]{:S(2)}) copy-start(bf16[240,512]{1,0:T(8,128)(2,1)} %constant.48.clone.refs_2_.refs_1_) | copy-start | bytes 737284
  22.0 6.1 %collective-permute-start.1 = (bf16[4,2,112,128]{3,2,1,0:T(8,128)(2,1)S(1)}, bf16[4,2,112,128]{3,2,1,0:T(8,128)(2,1)S(1)}, u32[]{:S(2)}, u32[]{:S(2)}) collective-permute-start(bf16[4,2,112,128]{3,2,1,0:T(8,128)(2,1)S(1)} %pad_maximum_fusion.4), channel_id=1, source_target_pairs={{0,8},{4,12},{8,0},{12,4},{16,24},{20,28},{24,16},{28,20},{1,9},{5... | collective-permute-start | bytes 688136 | tf_op jit(solution)/shard_map/ppermute | solution.py:519
  22.1 6.0 %collective-permute-start.4 = (bf16[2,16,5120]{2,1,0:T(8,128)(2,1)S(1)}, bf16[2,16,5120]{2,1,0:T(8,128)(2,1)S(1)}, u32[]{:S(2)}, u32[]{:S(2)}) collective-permute-start(bf16[2,16,5120]{2,1,0:T(8,128)(2,1)S(1)} %pad_maximum_fusion.3.refs_0_), channel_id=1, source_target_pairs={{0,1},{1,0},{2,3},{3,2},{4,5},{5,4},{6,7},{7,6},{8,9},{9,8},{10,11... | collective-permute-start | bytes 983048 | tf_op jit(solution)/shard_map/ppermute | solution.py:585
  28.1 5.6 %copy-start.8 = (s32[32,80]{1,0:T(8,128)S(1)}, s32[32,80]{1,0:T(8,128)}, u32[]{:S(2)}) copy-start(s32[32,80]{1,0:T(8,128)} %valid_ref.1) | copy-start | bytes 30724
  28.1 5.6 %copy-start.15 = (bf16[80,240]{1,0:T(8,128)(2,1)S(1)}, bf16[80,240]{1,0:T(8,128)(2,1)}, u32[]{:S(2)}) copy-start(bf16[80,240]{1,0:T(8,128)(2,1)} %constant.49.clone.x_ref) | copy-start | bytes 115204
  28.1 5.6 %copy-start.17 = (bf16[48,256]{1,0:T(8,128)(2,1)S(1)}, bf16[48,256]{1,0:T(8,128)(2,1)}, u32[]{:S(2)}) copy-start(bf16[48,256]{1,0:T(8,128)(2,1)} %constant.50.clone.tz_ref) | copy-start | bytes 73732
  31.6 6.6 %copy-start.11 = (bf16[256,256]{1,0:T(8,128)(2,1)S(1)}, bf16[256,256]{1,0:T(8,128)(2,1)}, u32[]{:S(2)}) copy-start(bf16[256,256]{1,0:T(8,128)(2,1)} %constant.56.clone.bz_ref) | copy-start | bytes 393220
  31.6 6.6 %copy-start.12 = (bf16[160,208]{1,0:T(8,128)(2,1)S(1)}, bf16[160,208]{1,0:T(8,128)(2,1)}, u32[]{:S(2)}) copy-start(bf16[160,208]{1,0:T(8,128)(2,1)} %constant.55.clone.by_ref) | copy-start | bytes 199684
  31.6 6.6 %copy-start.13 = (bf16[112,144]{1,0:T(8,128)(2,1)S(1)}, bf16[112,144]{1,0:T(8,128)(2,1)}, u32[]{:S(2)}) copy-start(bf16[112,144]{1,0:T(8,128)(2,1)} %constant.52.clone.y_ref) | copy-start | bytes 96772
  31.6 6.6 %copy-start.14 = (bf16[80,144]{1,0:T(8,128)(2,1)S(1)}, bf16[80,144]{1,0:T(8,128)(2,1)}, u32[]{:S(2)}) copy-start(bf16[80,144]{1,0:T(8,128)(2,1)} %constant.53.clone.x_ref) | copy-start | bytes 69124
  31.6 6.6 %copy-start.16 = (bf16[64,160]{1,0:T(8,128)(2,1)S(1)}, bf16[64,160]{1,0:T(8,128)(2,1)}, u32[]{:S(2)}) copy-start(bf16[64,160]{1,0:T(8,128)(2,1)} %constant.54.clone.bx_ref) | copy-start | bytes 61444
  31.6 6.6 %copy-start.18 = (f32[8,128]{1,0:T(8,128)S(1)}, f32[8,128]{1,0:T(8,128)}, u32[]{:S(2)}) copy-start(f32[8,128]{1,0:T(8,128)} %constant.51.clone.ones_ref) | copy-start | bytes 12292
  31.6 6.5 %collective-permute-start.5 = (bf16[1,4,112,128]{3,2,1,0:T(8,128)(2,1)S(1)}, bf16[1,4,112,128]{3,2,1,0:T(8,128)(2,1)S(1)}, u32[]{:S(2)}, u32[]{:S(2)}) collective-permute-start(bf16[1,4,112,128]{3,2,1,0:T(8,128)(2,1)S(1)} %slice.79), channel_id=1, source_target_pairs={{0,4},{4,0},{8,12},{12,8},{16,20},{20,16},{24,28},{28,24},{1,5},{5... | collective-permute-start | bytes 344072 | tf_op jit(solution)/shard_map/ppermute | solution.py:519
  31.7 15.8 %collective-permute-start.6 = (bf16[3,4,112,128]{3,2,1,0:T(8,128)(2,1)S(1)}, bf16[3,4,112,128]{3,2,1,0:T(8,128)(2,1)S(1)}, u32[]{:S(2)}, u32[]{:S(2)}) collective-permute-start(bf16[3,4,112,128]{3,2,1,0:T(8,128)(2,1)S(1)} %slice.81), channel_id=1, source_target_pairs={{0,4},{4,0},{8,12},{12,8},{16,20},{20,16},{24,28},{28,24},{1,5},{5... | collective-permute-start | bytes 1032200 | tf_op jit(solution)/shard_map/ppermute | solution.py:519
  45.9 10.7 %collective-permute-start.7 = (f32[2,32,1280]{2,1,0:T(8,128)S(1)}, f32[2,32,1280]{2,1,0:T(8,128)S(1)}, u32[]{:S(2)}, u32[]{:S(2)}) collective-permute-start(f32[2,32,1280]{2,1,0:T(8,128)S(1)} %get-tuple-element.50), channel_id=1, source_target_pairs={{0,2},{1,3},{2,0},{3,1},{4,6},{5,7},{6,4},{7,5},{8,10},{9,11},{10,... | collective-permute-start | bytes 983048 | tf_op jit(solution)/shard_map/ppermute | solution.py:616
  56.1 9.9 %collective-permute-start.8 = (f32[2,32,1280]{2,1,0:T(8,128)S(1)}, f32[2,32,1280]{2,1,0:T(8,128)S(1)}, u32[]{:S(2)}, u32[]{:S(2)}) collective-permute-start(f32[2,32,1280]{2,1,0:T(8,128)S(1)} %get-tuple-element.55), channel_id=1, source_target_pairs={{0,2},{1,3},{2,0},{3,1},{4,6},{5,7},{6,4},{7,5},{8,10},{9,11},{10,... | collective-permute-start | bytes 983048 | tf_op jit(solution)/shard_map/ppermute | solution.py:616
  64.4 10.2 %collective-permute-start.9 = (f32[2,32,1280]{2,1,0:T(8,128)S(1)}, f32[2,32,1280]{2,1,0:T(8,128)S(1)}, u32[]{:S(2)}, u32[]{:S(2)}) collective-permute-start(f32[2,32,1280]{2,1,0:T(8,128)S(1)} %get-tuple-element.60), channel_id=1, source_target_pairs={{0,2},{1,3},{2,0},{3,1},{4,6},{5,7},{6,4},{7,5},{8,10},{9,11},{10,... | collective-permute-start | bytes 983048 | tf_op jit(solution)/shard_map/ppermute | solution.py:616
  66.1 8.6 %collective-permute-start.10 = (f32[4,32,1280]{2,1,0:T(8,128)S(1)}, f32[4,32,1280]{2,1,0:T(8,128)S(1)}, u32[]{:S(2)}, u32[]{:S(2)}) collective-permute-start(f32[4,32,1280]{2,1,0:T(8,128)S(1)} %pad_maximum_fusion), channel_id=1, source_target_pairs={{0,1},{1,0},{2,3},{3,2},{4,5},{5,4},{6,7},{7,6},{8,9},{9,8},{10,11... | collective-permute-start | bytes 1966088 | tf_op jit(solution)/shard_map/ppermute | solution.py:619
  74.0 11.1 %copy-start.5 = (f32[32,1280]{1,0:T(8,128)}, f32[32,1280]{1,0:T(8,128)S(1)}, u32[]{:S(2)}) copy-start(f32[32,1280]{1,0:T(8,128)S(1)} %get-tuple-element.75.refs_3_) | copy-start | bytes 491524
  74.0 10.2 %collective-permute-start.14 = (f32[2,32,1280]{2,1,0:T(8,128)S(1)}, f32[2,32,1280]{2,1,0:T(8,128)S(1)}, u32[]{:S(2)}, u32[]{:S(2)}) collective-permute-start(f32[2,32,1280]{2,1,0:T(8,128)S(1)} %get-tuple-element.70), channel_id=1, source_target_pairs={{0,2},{1,3},{2,0},{3,1},{4,6},{5,7},{6,4},{7,5},{8,10},{9,11},{10,... | collective-permute-start | bytes 983048 | tf_op jit(solution)/shard_map/ppermute | solution.py:616
  74.7 3.6 %collective-permute-start.11 = (f32[3,4]{1,0:T(4,128)S(1)}, f32[3,4]{1,0:T(4,128)S(1)}, u32[]{:S(2)}, u32[]{:S(2)}) collective-permute-start(f32[3,4]{1,0:T(4,128)S(1)} %pad_maximum_fusion.6), channel_id=1, source_target_pairs={{0,4},{4,0},{8,12},{12,8},{16,20},{20,16},{24,28},{28,24},{1,5},{5... | collective-permute-start | bytes 152 | tf_op jit(solution)/shard_map/ppermute | solution.py:624
  78.4 3.6 %collective-permute-start.12 = (f32[3,4]{1,0:T(4,128)S(1)}, f32[3,4]{1,0:T(4,128)S(1)}, u32[]{:S(2)}, u32[]{:S(2)}) collective-permute-start(f32[3,4]{1,0:T(4,128)S(1)} %select_add_fusion.2), channel_id=1, source_target_pairs={{0,8},{4,12},{8,0},{12,4},{16,24},{20,28},{24,16},{28,20},{1,9},{5... | collective-permute-start | bytes 152 | tf_op jit(solution)/shard_map/ppermute | solution.py:624
  82.1 4.5 %collective-permute-start.13 = (f32[3,4]{1,0:T(4,128)S(1)}, f32[3,4]{1,0:T(4,128)S(1)}, u32[]{:S(2)}, u32[]{:S(2)}) collective-permute-start(f32[3,4]{1,0:T(4,128)S(1)} %select_add_fusion.1), channel_id=1, source_target_pairs={{0,16},{4,20},{8,24},{12,28},{16,0},{20,4},{24,8},{28,12},{1,17},{... | collective-permute-start | bytes 152 | tf_op jit(solution)/shard_map/ppermute | solution.py:624
  86.5 5.4 %collective-permute-start.18 = (f32[4,32,1280]{2,1,0:T(8,128)}, f32[4,32,1280]{2,1,0:T(8,128)S(1)}, u32[]{:S(2)}, u32[]{:S(2)}) collective-permute-start(f32[4,32,1280]{2,1,0:T(8,128)} %pad_maximum_fusion.1), channel_id=1, source_target_pairs={{0,1},{1,0},{2,3},{3,2},{4,5},{5,4},{6,7},{7,6},{8,9},{9,8},{10,11... | collective-permute-start | bytes 1966088 | tf_op jit(solution)/shard_map/ppermute | solution.py:636
  86.9 2.1 %collective-permute-start.15 = (f32[4,6]{1,0:T(4,128)S(1)}, f32[4,6]{1,0:T(4,128)S(1)}, u32[]{:S(2)}, u32[]{:S(2)}) collective-permute-start(f32[4,6]{1,0:T(4,128)S(1)} %pad_maximum_fusion.7), channel_id=1, source_target_pairs={{0,1},{1,0},{2,3},{3,2},{4,5},{5,4},{6,7},{7,6},{8,9},{9,8},{10,11... | collective-permute-start | bytes 296 | tf_op jit(solution)/shard_map/ppermute | solution.py:550
  87.4 3.6 %collective-permute-start.16 = (f32[4,6]{1,0:T(4,128)S(1)}, f32[4,6]{1,0:T(4,128)S(1)}, u32[]{:S(2)}, u32[]{:S(2)}) collective-permute-start(f32[4,6]{1,0:T(4,128)S(1)} %pad_maximum_fusion.7), channel_id=1, source_target_pairs={{0,2},{1,3},{2,0},{3,1},{4,6},{5,7},{6,4},{7,5},{8,10},{9,11},{10,... | collective-permute-start | bytes 296 | tf_op jit(solution)/shard_map/ppermute | solution.py:550
  89.0 3.0 %collective-permute-start.17 = (f32[4,6]{1,0:T(4,128)S(1)}, f32[4,6]{1,0:T(4,128)S(1)}, u32[]{:S(2)}, u32[]{:S(2)}) collective-permute-start(f32[4,6]{1,0:T(4,128)S(1)} %pad_maximum_fusion.7), channel_id=1, source_target_pairs={{0,3},{1,2},{2,1},{3,0},{4,7},{5,6},{6,5},{7,4},{8,11},{9,10},{10,... | collective-permute-start | bytes 296 | tf_op jit(solution)/shard_map/ppermute | solution.py:550
  (9 other events, 13.9 us)

commit v9 on v8

--- a/solution.py
+++ b/solution.py
@@ -245,7 +245,7 @@
             pltpu.VMEM((y_cells * odd(count), LANES), F32),
             pltpu.VMEM((2, 3 * y_cells, GROUP * LANES), BF16),
         ],
-        compiler_params=pltpu.CompilerParams(vmem_limit_bytes=9 * 1024 * 1024),
+        compiler_params=pltpu.CompilerParams(vmem_limit_bytes=20 * 1024 * 1024),
         cost_estimate=pl.CostEstimate(flops=count * 10**8, bytes_accessed=10**6, transcendentals=0),
         name=name,
     )(place, *blocks, tables["slab_rows"])
@@ -305,7 +305,7 @@
         in_specs=[vmem] * 5,
         out_specs=(vmem,) * 3,
         scratch_shapes=[pltpu.VMEM((2, 3 * n_x, GROUP * LANES), BF16)],
-        compiler_params=pltpu.CompilerParams(vmem_limit_bytes=6 * 1024 * 1024),
+        compiler_params=pltpu.CompilerParams(vmem_limit_bytes=20 * 1024 * 1024),
         cost_estimate=pl.CostEstimate(flops=5 * 10**9, bytes_accessed=10**6, transcendentals=0),
         name="slab_x",
     )(own, halo, tables["slab_x"], valid, tables["tmpl_z"])
@@ -460,7 +460,7 @@
             pltpu.VMEM((n_y * odd(x_cells), LANES), F32),
             pltpu.VMEM((x_cells * odd(y_cells), LANES), F32),
         ],
-        compiler_params=pltpu.CompilerParams(vmem_limit_bytes=14 * 1024 * 1024),
+        compiler_params=pltpu.CompilerParams(vmem_limit_bytes=24 * 1024 * 1024),
         cost_estimate=pl.CostEstimate(flops=15 * 10**9, bytes_accessed=10**7, transcendentals=0),
         name="correlate",
     )(
@@ -510,7 +510,7 @@
         out_shape=(out, out, jax.ShapeDtypeStruct((4,) + shape, F32)),
         in_specs=[pl.BlockSpec(memory_space=pltpu.SMEM)] * 2 + [vmem] * (1 + len(arrays)),
         out_specs=(vmem,) * 3,
-        compiler_params=pltpu.CompilerParams(vmem_limit_bytes=4 * 1024 * 1024),
+        compiler_params=pltpu.CompilerParams(vmem_limit_bytes=16 * 1024 * 1024),
         name="combine",
     )(place, coefs, mask, *arrays)
 
@@ -574,12 +574,12 @@
     if by_blocks:
         held = templates.reshape(rots, 1, EACH * CHUNKS, LANES)
         held = jnp.pad(held, ((0, 0), (0, 0), (0, BLOCK_ROWS - EACH * CHUNKS), (0, 0)))
-        held, tomogram_after = lax.optimization_barrier((held, tomogram))
-        held = jnp.concatenate([held, swap_blocks(held, "tile", 4)], axis=1)
-    else:
-        tomogram_after = tomogram
+        first = swap_blocks(held, "tile", 4)
+        held = jnp.concatenate([held, first], axis=1)
     half = x_cells // 2
-    piece = lax.dynamic_slice_in_dim(tomogram_after, (me & 1) * half, half, 0)
+    piece = lax.dynamic_slice_in_dim(tomogram, (me & 1) * half, half, 0)
+    if by_blocks:
+        piece = jnp.where(first[0, 0, 0, 0].astype(F32) < 100.0, piece, jnp.zeros_like(piece))
     mine = jnp.stack(neighbours(piece, "tile"))
     side_swap = [(i, i ^ 1) for i in range(groups)]
     other = lax.ppermute(mine, "rot", side_swap)
@@ -595,7 +595,6 @@
     own = slab_rows(place, [tomogram], x_cells, dims, tables, "slab_own")
     halo = slab_rows(place, [mine, other], TEMPL, dims, tables, "slab_halo")
     if by_blocks:
-        held, halo = lax.optimization_barrier((held, halo))
         lasts = [swap_blocks(held[:1], "tile", 1), swap_blocks(held[1:], "tile", 1)]
     else:
         lasts = [last[:1], last[1:]]

time: 98.2 us -> 99.9 us (1.017)
  starting transfers between devices: 19.6 us -> 24.1 us
  waiting for transfers between devices: 21 us -> 17.9 us
    ppermute x4, waiting for transfers between devices: 8.58 us -> 5.5 us  [swap_blocks(): lax.ppermute(block, axis, [(i, i ^ step) for i in range(lax.axis_size(axi...]
    ppermute x3, starting transfers between devices: 0.13 us -> 3.19 us  [local(): partner = lax.ppermute(state, 'tile', [(i, i ^ step) for i in range(tiles)])]
    ppermute x4, starting transfers between devices: 6.85 us -> 9.7 us  [swap_blocks(): lax.ppermute(block, axis, [(i, i ^ step) for i in range(lax.axis_size(axi...]
    ppermute x1, waiting for transfers between devices: 0.01 us -> 2.35 us  [neighbours(): lax.ppermute(block, axis, backward)]
    ppermute x3, waiting for transfers between devices: 8.5 us -> 7.07 us  [local(): partner = lax.ppermute(state, 'tile', [(i, i ^ step) for i in range(tiles)])]
    ppermute x1, starting transfers between devices: 4.85 us -> 3.45 us  [neighbours(): lax.ppermute(block, axis, forward)]
    unnamed x44 -> x46, local copies, waits for them, and re-layouts: 6.68 us -> 6.69 us
  transfers between devices with their start and end apart: 19 -> 19, of which waited for: 8 -> 7; matrix products, arithmetic and copies ran while one was open for 3% -> 3% of each run, Pallas kernels for 39% -> 41%
where the time goes in v9:
time: 99.9 us; the launch traced here: 99.6 us
  Pallas kernels  44.3 us (44%)
  starting transfers between devices  24.1 us (24%)
  waiting for transfers between devices  17.9 us (18%)
  local copies, waits for them, and re-layouts  8.99 us (9%)
  between operations  2.45 us (2%)
  other arithmetic  1.6 us (2%)
    pallas_call x4, Pallas kernels, correlate(): pl.pallas_call(functools.partial(corr_kernel, dims, rot, entry), out_shap...  31.2 us
    ppermute x4, starting transfers between devices, swap_blocks(): lax.ppermute(block, axis, [(i, i ^ step) for i in range(lax.axis_size(axi...  9.7 us
    ppermute x3, waiting for transfers between devices, local(): partner = lax.ppermute(state, 'tile', [(i, i ^ step) for i in range(tiles)])  7.07 us
    unnamed x46, local copies, waits for them, and re-layouts  6.69 us
    pallas_call x2, Pallas kernels, slab_rows(): pl.pallas_call(functools.partial(slab_rows_kernel, dims), out_shape=jax.S...  5.61 us
    ppermute x4, waiting for transfers between devices, swap_blocks(): lax.ppermute(block, axis, [(i, i ^ step) for i in range(lax.axis_size(axi...  5.5 us
    pallas_call x1, Pallas kernels, slab_x(): pl.pallas_call(functools.partial(slab_x_kernel, dims), out_shape=(jax.Sha...  4.38 us
    ppermute x4, starting transfers between devices, local(): fars.append(lax.ppermute(far, 'rot', far_swap))  4.27 us
  transfers between devices with their start and end apart: 19, of which 7 were waited for; matrix products, arithmetic and copies ran while one was open for 3% of the time, Pallas kernels for 41%

profile of v9, /device:TPU:0, one launch (start us, length us, event | category | flops | bytes accessed | tf_op | source)
XLA Modules:
  0.0 99.6 jit_solution(3935998353222024723)
XLA Ops:
  0.6 1.0 %reshape.76 = bf16[4,1,108,128]{3,2,0,1:T(8,128)(2,1)S(1)} reshape(bf16[4,13824]{1,0:T(4,128)(2,1)} %param.15) | data formatting | bytes 221184 | tf_op jit(solution)/shard_map/reshape | solution.py:575
  1.7 4.1 %collective-permute-start = (bf16[4,1,112,128]{3,2,1,0:T(8,128)(2,1)S(1)}, bf16[4,1,112,128]{3,2,1,0:T(8,128)(2,1)S(1)}, u32[]{:S(2)}, u32[]{:S(2)}) collective-permute-start(bf16[4,1,112,128]{3,2,1,0:T(8,128)(2,1)S(1)} %pad.4), channel_id=1, source_target_pairs={{0,16},{4,20},{8,24},{12,28},{16,0},{20,4},{24,8},{28,12},{1,17},{... | collective-permute-start | bytes 344072 | tf_op jit(solution)/shard_map/ppermute | solution.py:519
  5.8 1.0 copy-done.7
  6.7 0.9 copy-done.10
  7.7 2.3 %slab_own.1.own_ref = f32[3616,128]{1,0:T(8,128)S(1)} custom-call(s32[1]{0:T(128)} %bitcast.place_ref, bf16[32,5120]{1,0:T(8,128)(2,1)S(1)} %copy-done.7, bf16[240,512]{1,0:T(8,128)(2,1)S(1)} %copy-done.10), custom_call_target="tpu_custom_call" | custom-call | flops 3200000000 | bytes 1000000 | tf_op jit(solution)/shard_map/slab_own/pallas_call | solution.py:239
  10.0 1.3 %copy-done.20 = f32[3616,128]{1,0:T(8,128)} copy-done((f32[3616,128]{1,0:T(8,128)}, f32[3616,128]{1,0:T(8,128)S(1)}, u32[]{:S(2)}) %copy-start.20) | copy-done | bytes 1851416
  12.6 3.5 %collective-permute-start.3 = (bf16[16,5120]{1,0:T(8,128)(2,1)S(1)}, bf16[16,5120]{1,0:T(8,128)(2,1)S(1)}, u32[]{:S(2)}, u32[]{:S(2)}) collective-permute-start(bf16[16,5120]{1,0:T(8,128)(2,1)S(1)} %dynamic-slice_select_fusion), channel_id=1, source_target_pairs={{0,4},{4,8},{8,12},{12,16},{16,20},{20,24},{24,28},{1,5},{5,9},{9,... | collective-permute-start | bytes 491528 | tf_op jit(solution)/shard_map/ppermute | solution.py:558
  16.1 1.3 %collective-permute-start.4 = (bf16[16,5120]{1,0:T(8,128)(2,1)S(1)}, bf16[16,5120]{1,0:T(8,128)(2,1)S(1)}, u32[]{:S(2)}, u32[]{:S(2)}) collective-permute-start(bf16[16,5120]{1,0:T(8,128)(2,1)S(1)} %dynamic-slice_select_fusion), channel_id=1, source_target_pairs={{4,0},{8,4},{12,8},{16,12},{20,16},{24,20},{28,24},{5,1},{9,5},{13... | collective-permute-start | bytes 491528 | tf_op jit(solution)/shard_map/ppermute | solution.py:558
  17.4 3.5 %collective-permute-start.1 = (bf16[4,2,112,128]{3,2,1,0:T(8,128)(2,1)S(1)}, bf16[4,2,112,128]{3,2,1,0:T(8,128)(2,1)S(1)}, u32[]{:S(2)}, u32[]{:S(2)}) collective-permute-start(bf16[4,2,112,128]{3,2,1,0:T(8,128)(2,1)S(1)} %pad_maximum_fusion.4), channel_id=1, source_target_pairs={{0,8},{4,12},{8,0},{12,4},{16,24},{20,28},{24,16},{28,20},{1,9},{5... | collective-permute-start | bytes 688136 | tf_op jit(solution)/shard_map/ppermute | solution.py:519
  20.9 2.3 %collective-permute-done.4 = bf16[16,5120]{1,0:T(8,128)(2,1)S(1)} collective-permute-done((bf16[16,5120]{1,0:T(8,128)(2,1)S(1)}, bf16[16,5120]{1,0:T(8,128)(2,1)S(1)}, u32[]{:S(2)}, u32[]{:S(2)}) %collective-permute-start.4) | collective-permute-done | bytes 163872 | tf_op jit(solution)/shard_map/ppermute | solution.py:558
  23.7 5.4 %collective-permute-done.1 = bf16[4,2,112,128]{3,2,1,0:T(8,128)(2,1)S(1)} collective-permute-done((bf16[4,2,112,128]{3,2,1,0:T(8,128)(2,1)S(1)}, bf16[4,2,112,128]{3,2,1,0:T(8,128)(2,1)S(1)}, u32[]{:S(2)}, u32[]{:S(2)}) %collective-permute-start.1) | collective-permute-done | bytes 229408 | tf_op jit(solution)/shard_map/ppermute | solution.py:519
  29.3 2.0 %collective-permute-start.6 = (bf16[3,4,112,128]{3,2,1,0:T(8,128)(2,1)S(1)}, bf16[3,4,112,128]{3,2,1,0:T(8,128)(2,1)S(1)}, u32[]{:S(2)}, u32[]{:S(2)}) collective-permute-start(bf16[3,4,112,128]{3,2,1,0:T(8,128)(2,1)S(1)} %slice.111), channel_id=1, source_target_pairs={{0,4},{4,0},{8,12},{12,8},{16,20},{20,16},{24,28},{28,24},{1,5},{5... | collective-permute-start | bytes 1032200 | tf_op jit(solution)/shard_map/ppermute | solution.py:519
  31.3 3.4 %slab_halo.1.halo_ref = f32[5424,128]{1,0:T(8,128)S(1)} custom-call(s32[1]{0:T(128)} %bitcast.place_ref, bf16[2,16,5120]{2,1,0:T(8,128)(2,1)S(1)} %pad_maximum_fusion.3.refs_0_, bf16[2,16,5120]{2,1,0:T(8,128)(2,1)S(1)} %collective-permute-done.5.refs_1_, bf16[240,512]{1,0:T(8,128)(2,1)S(1)} %copy-done.11), custom_call_target="tpu_custom_call" | custom-call | flops 4800000000 | bytes 1000000 | tf_op jit(solution)/shard_map/slab_halo/pallas_call | solution.py:239
  34.8 4.4 %slab_x.1 = (f32[13,2,80,1024]{3,2,1,0:T(8,128)S(1)}, f32[40,32,128]{2,1,0:T(8,128)S(1)}, bf16[8,256,256]{2,1,0:T(8,128)(2,1)S(1)}) custom-call(f32[3616,128]{1,0:T(8,128)S(1)} %copy-done.21, f32[5424,128]{1,0:T(8,128)S(1)} %slab_halo.1.halo_ref, bf16[80,240]{1,0:T(8,128)(2,1)S(1)} %copy-done.16, s32[32,80]{1,0:T(8,128)S(1)} %copy-done.9, ...), custom_call_target="tpu_custom_call" | custom-call | flops 5000000000 | bytes 1000000 | tf_op jit(solution)/shard_map/slab_x/pallas_call | solution.py:298
  39.2 7.7 %correlate.4 = (f32[32,1280]{1,0:T(8,128)S(1)}, f32[32,1280]{1,0:T(8,128)S(1)}, f32[2,32,1280]{2,1,0:T(8,128)S(1)}, f32[8,128]{1,0:T(8,128)S(1)}) custom-call(s32[1]{0:T(128)} %bitcast.place_ref, s32[1]{0:T(128)} %bitcast.1.tile_ref, bf16[4,4,112,128]{3,2,1,0:T(8,128)(2,1)S(1)} %pad_maximum_fusion.2.held_ref, ...), custom_call_target="tpu_custom_call" | custom-call | flops 15000000512 | bytes 10000000 | tf_op jit(solution)/shard_map/correlate/pallas_call | solution.py:443
  47.0 1.6 %collective-permute-start.7 = (f32[2,32,1280]{2,1,0:T(8,128)S(1)}, f32[2,32,1280]{2,1,0:T(8,128)S(1)}, u32[]{:S(2)}, u32[]{:S(2)}) collective-permute-start(f32[2,32,1280]{2,1,0:T(8,128)S(1)} %get-tuple-element.42), channel_id=1, source_target_pairs={{0,2},{1,3},{2,0},{3,1},{4,6},{5,7},{6,4},{7,5},{8,10},{9,11},{10,... | collective-permute-start | bytes 983048 | tf_op jit(solution)/shard_map/ppermute | solution.py:615
  48.6 7.8 %correlate.5 = (f32[32,1280]{1,0:T(8,128)S(1)}, f32[32,1280]{1,0:T(8,128)S(1)}, f32[2,32,1280]{2,1,0:T(8,128)S(1)}, f32[8,128]{1,0:T(8,128)S(1)}) custom-call(s32[1]{0:T(128)} %bitcast.place_ref, s32[1]{0:T(128)} %bitcast.1.tile_ref, bf16[4,4,112,128]{3,2,1,0:T(8,128)(2,1)S(1)} %pad_maximum_fusion.2.held_ref, ...), custom_call_target="tpu_custom_call" | custom-call | flops 15000000512 | bytes 10000000 | tf_op jit(solution)/shard_map/correlate/pallas_call | solution.py:443
  56.4 0.7 copy-done.1
  57.5 7.9 %correlate.6 = (f32[32,1280]{1,0:T(8,128)S(1)}, f32[32,1280]{1,0:T(8,128)S(1)}, f32[2,32,1280]{2,1,0:T(8,128)S(1)}, f32[8,128]{1,0:T(8,128)S(1)}) custom-call(s32[1]{0:T(128)} %bitcast.place_ref, s32[1]{0:T(128)} %bitcast.1.tile_ref, bf16[4,4,112,128]{3,2,1,0:T(8,128)(2,1)S(1)} %pad_maximum_fusion.2.held_ref, ...), custom_call_target="tpu_custom_call" | custom-call | flops 15000000512 | bytes 10000000 | tf_op jit(solution)/shard_map/correlate/pallas_call | solution.py:443
  65.5 1.6 %collective-permute-start.9 = (f32[2,32,1280]{2,1,0:T(8,128)S(1)}, f32[2,32,1280]{2,1,0:T(8,128)S(1)}, u32[]{:S(2)}, u32[]{:S(2)}) collective-permute-start(f32[2,32,1280]{2,1,0:T(8,128)S(1)} %get-tuple-element.52), channel_id=1, source_target_pairs={{0,2},{1,3},{2,0},{3,1},{4,6},{5,7},{6,4},{7,5},{8,10},{9,11},{10,... | collective-permute-start | bytes 983048 | tf_op jit(solution)/shard_map/ppermute | solution.py:615
  67.2 7.8 %correlate.7 = (f32[32,1280]{1,0:T(8,128)S(1)}, f32[32,1280]{1,0:T(8,128)S(1)}, f32[2,32,1280]{2,1,0:T(8,128)S(1)}, f32[8,128]{1,0:T(8,128)S(1)}) custom-call(s32[1]{0:T(128)} %bitcast.place_ref, s32[1]{0:T(128)} %bitcast.1.tile_ref, bf16[4,4,112,128]{3,2,1,0:T(8,128)(2,1)S(1)} %pad_maximum_fusion.2.held_ref, ...), custom_call_target="tpu_custom_call" | custom-call | flops 15000000512 | bytes 10000000 | tf_op jit(solution)/shard_map/correlate/pallas_call | solution.py:443
  75.8 3.5 %collective-permute-done.11 = f32[3,4]{1,0:T(4,128)S(1)} collective-permute-done((f32[3,4]{1,0:T(4,128)S(1)}, f32[3,4]{1,0:T(4,128)S(1)}, u32[]{:S(2)}, u32[]{:S(2)}) %collective-permute-start.11) | collective-permute-done | bytes 80 | tf_op jit(solution)/shard_map/ppermute | solution.py:623
  79.4 3.6 %collective-permute-done.12 = f32[3,4]{1,0:T(4,128)S(1)} collective-permute-done((f32[3,4]{1,0:T(4,128)S(1)}, f32[3,4]{1,0:T(4,128)S(1)}, u32[]{:S(2)}, u32[]{:S(2)}) %collective-permute-start.12) | collective-permute-done | bytes 80 | tf_op jit(solution)/shard_map/ppermute | solution.py:623
  83.1 3.1 %collective-permute-start.13 = (f32[3,4]{1,0:T(4,128)S(1)}, f32[3,4]{1,0:T(4,128)S(1)}, u32[]{:S(2)}, u32[]{:S(2)}) collective-permute-start(f32[3,4]{1,0:T(4,128)S(1)} %select_add_fusion.1), channel_id=1, source_target_pairs={{0,16},{4,20},{8,24},{12,28},{16,0},{20,4},{24,8},{28,12},{1,17},{... | collective-permute-start | bytes 152 | tf_op jit(solution)/shard_map/ppermute | solution.py:623
  87.3 0.9 pad_maximum_fusion.1
  89.1 1.5 %collective-permute-start.16 = (f32[4,6]{1,0:T(4,128)S(1)}, f32[4,6]{1,0:T(4,128)S(1)}, u32[]{:S(2)}, u32[]{:S(2)}) collective-permute-start(f32[4,6]{1,0:T(4,128)S(1)} %pad_maximum_fusion.7), channel_id=1, source_target_pairs={{0,2},{1,3},{2,0},{3,1},{4,6},{5,7},{6,4},{7,5},{8,10},{9,11},{10,... | collective-permute-start | bytes 296 | tf_op jit(solution)/shard_map/ppermute | solution.py:550
  90.7 2.0 %collective-permute-done.16 = f32[4,6]{1,0:T(4,128)S(1)} collective-permute-done((f32[4,6]{1,0:T(4,128)S(1)}, f32[4,6]{1,0:T(4,128)S(1)}, u32[]{:S(2)}, u32[]{:S(2)}) %collective-permute-start.16) | collective-permute-done | bytes 128 | tf_op jit(solution)/shard_map/ppermute | solution.py:550
  92.7 1.0 %collective-permute-done.17 = f32[4,6]{1,0:T(4,128)S(1)} collective-permute-done((f32[4,6]{1,0:T(4,128)S(1)}, f32[4,6]{1,0:T(4,128)S(1)}, u32[]{:S(2)}, u32[]{:S(2)}) %collective-permute-start.17) | collective-permute-done | bytes 128 | tf_op jit(solution)/shard_map/ppermute | solution.py:550
  93.7 0.9 copy-done.2
  94.6 0.9 copy-done.4
  95.6 0.9 copy-done.6
  96.5 3.1 %combine.1 = (f32[32,1280]{1,0:T(8,128)}, f32[32,1280]{1,0:T(8,128)}, f32[4,32,1280]{2,1,0:T(8,128)}) custom-call(s32[1]{0:T(128)} %bitcast.place_ref, f32[16,6]{1,0:T(8,128)S(1)} %bitcast.32, f32[40,32,128]{2,1,0:T(8,128)S(1)} %get-tuple-element.37.mask_ref, f32[32,1280]{1,0:T(8,128)S(1)} %get-tuple-element.64.refs_0_, f32[32,1280]{1,0:T(8,128)S(1)} %copy-done.2, ...), custom_call_target="tpu_custom_call" | custom-call | tf_op jit(solution)/shard_map/combine/pallas_call | solution.py:508
  (95 shorter events, 4.5 us)
Async XLA Ops:
  0.6 22.8 %copy-start = (f32[4,4096]{1,0:T(4,128)S(1)}, f32[4,4096]{1,0:T(4,128)}, u32[]{:S(2)}) copy-start(f32[4,4096]{1,0:T(4,128)} %param.17) | copy-start | bytes 196612
  1.7 9.7 %collective-permute-start = (bf16[4,1,112,128]{3,2,1,0:T(8,128)(2,1)S(1)}, bf16[4,1,112,128]{3,2,1,0:T(8,128)(2,1)S(1)}, u32[]{:S(2)}, u32[]{:S(2)}) collective-permute-start(bf16[4,1,112,128]{3,2,1,0:T(8,128)(2,1)S(1)} %pad.4), channel_id=1, source_target_pairs={{0,16},{4,20},{8,24},{12,28},{16,0},{20,4},{24,8},{28,12},{1,17},{... | collective-permute-start | bytes 344072 | tf_op jit(solution)/shard_map/ppermute | solution.py:519
  7.7 4.9 %copy-start.8 = (bf16[32,5120]{1,0:T(8,128)(2,1)S(1)}, bf16[32,5120]{1,0:T(8,128)(2,1)}, u32[]{:S(2)}) copy-start(bf16[32,5120]{1,0:T(8,128)(2,1)} %refs_0_.1) | copy-start | bytes 983044
  7.7 15.7 %copy-start.22 = (s32[4]{0:T(128)S(1)}, s32[4]{0:T(128)}, u32[]{:S(2)}) copy-start(s32[4]{0:T(128)} %param.18) | copy-start | bytes 52
  11.3 20.1 %copy-start.11 = (bf16[240,512]{1,0:T(8,128)(2,1)S(1)}, bf16[240,512]{1,0:T(8,128)(2,1)}, u32[]{:S(2)}) copy-start(bf16[240,512]{1,0:T(8,128)(2,1)} %constant.52.clone.refs_1_.refs_2_) | copy-start | bytes 737284
  12.6 8.3 %collective-permute-start.3 = (bf16[16,5120]{1,0:T(8,128)(2,1)S(1)}, bf16[16,5120]{1,0:T(8,128)(2,1)S(1)}, u32[]{:S(2)}, u32[]{:S(2)}) collective-permute-start(bf16[16,5120]{1,0:T(8,128)(2,1)S(1)} %dynamic-slice_select_fusion), channel_id=1, source_target_pairs={{0,4},{4,8},{8,12},{12,16},{16,20},{20,24},{24,28},{1,5},{5,9},{9,... | collective-permute-start | bytes 491528 | tf_op jit(solution)/shard_map/ppermute | solution.py:558
  16.1 7.2 %collective-permute-start.4 = (bf16[16,5120]{1,0:T(8,128)(2,1)S(1)}, bf16[16,5120]{1,0:T(8,128)(2,1)S(1)}, u32[]{:S(2)}, u32[]{:S(2)}) collective-permute-start(bf16[16,5120]{1,0:T(8,128)(2,1)S(1)} %dynamic-slice_select_fusion), channel_id=1, source_target_pairs={{4,0},{8,4},{12,8},{16,12},{20,16},{24,20},{28,24},{5,1},{9,5},{13... | collective-permute-start | bytes 491528 | tf_op jit(solution)/shard_map/ppermute | solution.py:558
  17.4 11.6 %collective-permute-start.1 = (bf16[4,2,112,128]{3,2,1,0:T(8,128)(2,1)S(1)}, bf16[4,2,112,128]{3,2,1,0:T(8,128)(2,1)S(1)}, u32[]{:S(2)}, u32[]{:S(2)}) collective-permute-start(bf16[4,2,112,128]{3,2,1,0:T(8,128)(2,1)S(1)} %pad_maximum_fusion.4), channel_id=1, source_target_pairs={{0,8},{4,12},{8,0},{12,4},{16,24},{20,28},{24,16},{28,20},{1,9},{5... | collective-permute-start | bytes 688136 | tf_op jit(solution)/shard_map/ppermute | solution.py:519
  23.3 8.0 %collective-permute-start.5 = (bf16[2,16,5120]{2,1,0:T(8,128)(2,1)S(1)}, bf16[2,16,5120]{2,1,0:T(8,128)(2,1)S(1)}, u32[]{:S(2)}, u32[]{:S(2)}) collective-permute-start(bf16[2,16,5120]{2,1,0:T(8,128)(2,1)S(1)} %pad_maximum_fusion.3.refs_0_), channel_id=1, source_target_pairs={{0,1},{1,0},{2,3},{3,2},{4,5},{5,4},{6,7},{7,6},{8,9},{9,8},{10,11... | collective-permute-start | bytes 983048 | tf_op jit(solution)/shard_map/ppermute | solution.py:585
  29.2 5.5 %copy-start.9 = (s32[32,80]{1,0:T(8,128)S(1)}, s32[32,80]{1,0:T(8,128)}, u32[]{:S(2)}) copy-start(s32[32,80]{1,0:T(8,128)} %valid_ref.1) | copy-start | bytes 30724
  29.2 5.5 %copy-start.16 = (bf16[80,240]{1,0:T(8,128)(2,1)S(1)}, bf16[80,240]{1,0:T(8,128)(2,1)}, u32[]{:S(2)}) copy-start(bf16[80,240]{1,0:T(8,128)(2,1)} %constant.53.clone.x_ref) | copy-start | bytes 115204
  29.2 5.5 %copy-start.18 = (bf16[48,256]{1,0:T(8,128)(2,1)S(1)}, bf16[48,256]{1,0:T(8,128)(2,1)}, u32[]{:S(2)}) copy-start(bf16[48,256]{1,0:T(8,128)(2,1)} %constant.54.clone.tz_ref) | copy-start | bytes 73732
  29.2 5.5 %copy-start.21 = (f32[3616,128]{1,0:T(8,128)S(1)}, f32[3616,128]{1,0:T(8,128)}, u32[]{:S(2)}) copy-start(f32[3616,128]{1,0:T(8,128)} %copy-done.20) | copy-start | bytes 5554180
  29.2 10.0 %collective-permute-start.2 = (bf16[1,4,112,128]{3,2,1,0:T(8,128)(2,1)S(1)}, bf16[1,4,112,128]{3,2,1,0:T(8,128)(2,1)S(1)}, u32[]{:S(2)}, u32[]{:S(2)}) collective-permute-start(bf16[1,4,112,128]{3,2,1,0:T(8,128)(2,1)S(1)} %slice.109), channel_id=1, source_target_pairs={{0,4},{4,0},{8,12},{12,8},{16,20},{20,16},{24,28},{28,24},{1,5},{5... | collective-permute-start | bytes 344072 | tf_op jit(solution)/shard_map/ppermute | solution.py:519
  29.3 19.3 %collective-permute-start.6 = (bf16[3,4,112,128]{3,2,1,0:T(8,128)(2,1)S(1)}, bf16[3,4,112,128]{3,2,1,0:T(8,128)(2,1)S(1)}, u32[]{:S(2)}, u32[]{:S(2)}) collective-permute-start(bf16[3,4,112,128]{3,2,1,0:T(8,128)(2,1)S(1)} %slice.111), channel_id=1, source_target_pairs={{0,4},{4,0},{8,12},{12,8},{16,20},{20,16},{24,28},{28,24},{1,5},{5... | collective-permute-start | bytes 1032200 | tf_op jit(solution)/shard_map/ppermute | solution.py:519
  34.7 4.5 %copy-start.12 = (bf16[256,256]{1,0:T(8,128)(2,1)S(1)}, bf16[256,256]{1,0:T(8,128)(2,1)}, u32[]{:S(2)}) copy-start(bf16[256,256]{1,0:T(8,128)(2,1)} %constant.60.clone.bz_ref) | copy-start | bytes 393220
  34.7 4.5 %copy-start.13 = (bf16[160,208]{1,0:T(8,128)(2,1)S(1)}, bf16[160,208]{1,0:T(8,128)(2,1)}, u32[]{:S(2)}) copy-start(bf16[160,208]{1,0:T(8,128)(2,1)} %constant.59.clone.by_ref) | copy-start | bytes 199684
  34.7 4.5 %copy-start.14 = (bf16[112,144]{1,0:T(8,128)(2,1)S(1)}, bf16[112,144]{1,0:T(8,128)(2,1)}, u32[]{:S(2)}) copy-start(bf16[112,144]{1,0:T(8,128)(2,1)} %constant.56.clone.y_ref) | copy-start | bytes 96772
  34.7 4.5 %copy-start.15 = (bf16[80,144]{1,0:T(8,128)(2,1)S(1)}, bf16[80,144]{1,0:T(8,128)(2,1)}, u32[]{:S(2)}) copy-start(bf16[80,144]{1,0:T(8,128)(2,1)} %constant.57.clone.x_ref) | copy-start | bytes 69124
  47.0 10.5 %collective-permute-start.7 = (f32[2,32,1280]{2,1,0:T(8,128)S(1)}, f32[2,32,1280]{2,1,0:T(8,128)S(1)}, u32[]{:S(2)}, u32[]{:S(2)}) collective-permute-start(f32[2,32,1280]{2,1,0:T(8,128)S(1)} %get-tuple-element.42), channel_id=1, source_target_pairs={{0,2},{1,3},{2,0},{3,1},{4,6},{5,7},{6,4},{7,5},{8,10},{9,11},{10,... | collective-permute-start | bytes 983048 | tf_op jit(solution)/shard_map/ppermute | solution.py:615
  57.0 10.0 %collective-permute-start.8 = (f32[2,32,1280]{2,1,0:T(8,128)S(1)}, f32[2,32,1280]{2,1,0:T(8,128)S(1)}, u32[]{:S(2)}, u32[]{:S(2)}) collective-permute-start(f32[2,32,1280]{2,1,0:T(8,128)S(1)} %get-tuple-element.47), channel_id=1, source_target_pairs={{0,2},{1,3},{2,0},{3,1},{4,6},{5,7},{6,4},{7,5},{8,10},{9,11},{10,... | collective-permute-start | bytes 983048 | tf_op jit(solution)/shard_map/ppermute | solution.py:615
  65.5 10.1 %collective-permute-start.9 = (f32[2,32,1280]{2,1,0:T(8,128)S(1)}, f32[2,32,1280]{2,1,0:T(8,128)S(1)}, u32[]{:S(2)}, u32[]{:S(2)}) collective-permute-start(f32[2,32,1280]{2,1,0:T(8,128)S(1)} %get-tuple-element.52), channel_id=1, source_target_pairs={{0,2},{1,3},{2,0},{3,1},{4,6},{5,7},{6,4},{7,5},{8,10},{9,11},{10,... | collective-permute-start | bytes 983048 | tf_op jit(solution)/shard_map/ppermute | solution.py:615
  67.1 8.6 %collective-permute-start.10 = (f32[4,32,1280]{2,1,0:T(8,128)S(1)}, f32[4,32,1280]{2,1,0:T(8,128)S(1)}, u32[]{:S(2)}, u32[]{:S(2)}) collective-permute-start(f32[4,32,1280]{2,1,0:T(8,128)S(1)} %pad_maximum_fusion), channel_id=1, source_target_pairs={{0,1},{1,0},{2,3},{3,2},{4,5},{5,4},{6,7},{7,6},{8,9},{9,8},{10,11... | collective-permute-start | bytes 1966088 | tf_op jit(solution)/shard_map/ppermute | solution.py:618
  75.0 13.2 %copy-start.5 = (f32[32,1280]{1,0:T(8,128)}, f32[32,1280]{1,0:T(8,128)S(1)}, u32[]{:S(2)}) copy-start(f32[32,1280]{1,0:T(8,128)S(1)} %get-tuple-element.67.refs_3_) | copy-start | bytes 491524
  75.0 12.3 %collective-permute-start.14 = (f32[2,32,1280]{2,1,0:T(8,128)S(1)}, f32[2,32,1280]{2,1,0:T(8,128)S(1)}, u32[]{:S(2)}, u32[]{:S(2)}) collective-permute-start(f32[2,32,1280]{2,1,0:T(8,128)S(1)} %get-tuple-element.62), channel_id=1, source_target_pairs={{0,2},{1,3},{2,0},{3,1},{4,6},{5,7},{6,4},{7,5},{8,10},{9,11},{10,... | collective-permute-start | bytes 983048 | tf_op jit(solution)/shard_map/ppermute | solution.py:615
  75.7 3.6 %collective-permute-start.11 = (f32[3,4]{1,0:T(4,128)S(1)}, f32[3,4]{1,0:T(4,128)S(1)}, u32[]{:S(2)}, u32[]{:S(2)}) collective-permute-start(f32[3,4]{1,0:T(4,128)S(1)} %pad_maximum_fusion.6), channel_id=1, source_target_pairs={{0,4},{4,0},{8,12},{12,8},{16,20},{20,16},{24,28},{28,24},{1,5},{5... | collective-permute-start | bytes 152 | tf_op jit(solution)/shard_map/ppermute | solution.py:623
  79.4 3.6 %collective-permute-start.12 = (f32[3,4]{1,0:T(4,128)S(1)}, f32[3,4]{1,0:T(4,128)S(1)}, u32[]{:S(2)}, u32[]{:S(2)}) collective-permute-start(f32[3,4]{1,0:T(4,128)S(1)} %select_add_fusion.2), channel_id=1, source_target_pairs={{0,8},{4,12},{8,0},{12,4},{16,24},{20,28},{24,16},{28,20},{1,9},{5... | collective-permute-start | bytes 152 | tf_op jit(solution)/shard_map/ppermute | solution.py:623
  83.1 5.2 %collective-permute-start.13 = (f32[3,4]{1,0:T(4,128)S(1)}, f32[3,4]{1,0:T(4,128)S(1)}, u32[]{:S(2)}, u32[]{:S(2)}) collective-permute-start(f32[3,4]{1,0:T(4,128)S(1)} %select_add_fusion.1), channel_id=1, source_target_pairs={{0,16},{4,20},{8,24},{12,28},{16,0},{20,4},{24,8},{28,12},{1,17},{... | collective-permute-start | bytes 152 | tf_op jit(solution)/shard_map/ppermute | solution.py:623
  88.2 5.5 %collective-permute-start.18 = (f32[4,32,1280]{2,1,0:T(8,128)}, f32[4,32,1280]{2,1,0:T(8,128)S(1)}, u32[]{:S(2)}, u32[]{:S(2)}) collective-permute-start(f32[4,32,1280]{2,1,0:T(8,128)} %pad_maximum_fusion.1), channel_id=1, source_target_pairs={{0,1},{1,0},{2,3},{3,2},{4,5},{5,4},{6,7},{7,6},{8,9},{9,8},{10,11... | collective-permute-start | bytes 1966088 | tf_op jit(solution)/shard_map/ppermute | solution.py:635
  88.6 2.1 %collective-permute-start.15 = (f32[4,6]{1,0:T(4,128)S(1)}, f32[4,6]{1,0:T(4,128)S(1)}, u32[]{:S(2)}, u32[]{:S(2)}) collective-permute-start(f32[4,6]{1,0:T(4,128)S(1)} %pad_maximum_fusion.7), channel_id=1, source_target_pairs={{0,1},{1,0},{2,3},{3,2},{4,5},{5,4},{6,7},{7,6},{8,9},{9,8},{10,11... | collective-permute-start | bytes 296 | tf_op jit(solution)/shard_map/ppermute | solution.py:550
  89.1 3.6 %collective-permute-start.16 = (f32[4,6]{1,0:T(4,128)S(1)}, f32[4,6]{1,0:T(4,128)S(1)}, u32[]{:S(2)}, u32[]{:S(2)}) collective-permute-start(f32[4,6]{1,0:T(4,128)S(1)} %pad_maximum_fusion.7), channel_id=1, source_target_pairs={{0,2},{1,3},{2,0},{3,1},{4,6},{5,7},{6,4},{7,5},{8,10},{9,11},{10,... | collective-permute-start | bytes 296 | tf_op jit(solution)/shard_map/ppermute | solution.py:550
  90.7 3.0 %collective-permute-start.17 = (f32[4,6]{1,0:T(4,128)S(1)}, f32[4,6]{1,0:T(4,128)S(1)}, u32[]{:S(2)}, u32[]{:S(2)}) collective-permute-start(f32[4,6]{1,0:T(4,128)S(1)} %pad_maximum_fusion.7), channel_id=1, source_target_pairs={{0,3},{1,2},{2,1},{3,0},{4,7},{5,6},{6,5},{7,4},{8,11},{9,10},{10,... | collective-permute-start | bytes 296 | tf_op jit(solution)/shard_map/ppermute | solution.py:550
  (10 other events, 17.2 us)

commit v10 on v8

--- a/solution.py
+++ b/solution.py
@@ -362,7 +362,7 @@
             store(rows_buf, start, lane_block(plus, u))
             store(rows_buf, start + pad_y, lane_block(minus, u))
 
-    pipeline(TEMPL // GROUP, [gather_a, y_step], 2)
+    pipeline(TEMPL // GROUP, [gather_a, y_step], 3)
 
     def gather_ky(i, slot):
         firsts = [GROUP // 2 * i + u // 2 + u % 2 * pad_y for u in range(GROUP)]
@@ -381,7 +381,7 @@
             store(back_buf, start, lane_block(plus, u))
             store(back_buf, start + x_cells // 2, lane_block(minus, u))
 
-    pipeline(n_y // GROUP, [gather_ky, multiply, back_x], 2)
+    pipeline(n_y // GROUP, [gather_ky, multiply, back_x], 4)
 
     def gather_x(i, slot):
         value = pick(back_buf, [GROUP * i + u for u in range(GROUP)], n_y, odd(x_cells))
@@ -454,13 +454,13 @@
             pltpu.VMEM((BLOCKS * odd(BLOCK_ROWS), LANES), F32),
             pltpu.VMEM((TEMPL * odd(TEMPL), LANES), F32),
             pltpu.VMEM((TEMPL * odd(2 * pad_y), LANES), F32),
-            pltpu.VMEM((2, 3 * TEMPL, GROUP * LANES), BF16),
-            pltpu.VMEM((2, 2 * n_x, GROUP * LANES), BF16),
+            pltpu.VMEM((4, 3 * TEMPL, GROUP * LANES), BF16),
+            pltpu.VMEM((4, 2 * n_x, GROUP * LANES), BF16),
             pltpu.VMEM((2, 2 * n_y, GROUP * LANES), BF16),
             pltpu.VMEM((n_y * odd(x_cells), LANES), F32),
             pltpu.VMEM((x_cells * odd(y_cells), LANES), F32),
         ],
-        compiler_params=pltpu.CompilerParams(vmem_limit_bytes=14 * 1024 * 1024),
+        compiler_params=pltpu.CompilerParams(vmem_limit_bytes=16 * 1024 * 1024),
         cost_estimate=pl.CostEstimate(flops=15 * 10**9, bytes_accessed=10**7, transcendentals=0),
         name="correlate",
     )(
@@ -470,9 +470,14 @@
     )
 
 
-def score_kernel(pieces, place_ref, coef_ref, mask_ref, *refs):
-    best_ref, evid_ref, mom_ref = refs[len(refs) - 3 :]
-
+def score_kernel(pieces, own, place_ref, coef_ref, mask_ref, *refs):
+    refs, (best_ref, evid_ref, mom_ref, own_buf, sems) = list(refs[:-5]), refs[-5:]
+    copies = [pltpu.make_async_copy(refs[i], own_buf.at[i], sems.at[i]) for i in range(own)]
+    for copy in copies:
+        copy.start()
+    for copy in copies:
+        copy.wait()
+    refs[:own] = [own_buf.at[i] for i in range(own)]
     blocks = best_ref.shape[1] // LANES
 
     def step(i):
@@ -501,15 +506,17 @@
     loop(blocks, step)
 
 
-def combine(place, coefs, mask, arrays, pieces):
+def combine(place, coefs, mask, arrays, pieces, own):
     shape = arrays[0].shape
     vmem = pl.BlockSpec(memory_space=pltpu.VMEM)
     out = jax.ShapeDtypeStruct(shape, F32)
     return pl.pallas_call(
-        functools.partial(score_kernel, pieces),
+        functools.partial(score_kernel, pieces, own),
         out_shape=(out, out, jax.ShapeDtypeStruct((4,) + shape, F32)),
-        in_specs=[pl.BlockSpec(memory_space=pltpu.SMEM)] * 2 + [vmem] * (1 + len(arrays)),
+        in_specs=[pl.BlockSpec(memory_space=pltpu.SMEM)] * 2
+        + [vmem] + [pl.BlockSpec(memory_space=pl.ANY)] * own + [vmem] * (len(arrays) - own),
         out_specs=(vmem,) * 3,
+        scratch_shapes=[pltpu.VMEM((own,) + shape, F32), pltpu.SemaphoreType.DMA((own,))],
         compiler_params=pltpu.CompilerParams(vmem_limit_bytes=4 * 1024 * 1024),
         name="combine",
     )(place, coefs, mask, *arrays)
@@ -584,7 +591,7 @@
     side_swap = [(i, i ^ 1) for i in range(groups)]
     other = lax.ppermute(mine, "rot", side_swap)
     if by_blocks:
-        held = jnp.concatenate([held, swap_blocks(held, "tile", 2)], axis=1)
+        second = swap_blocks(held, "tile", 2)
     else:
         held, last = general_gather(templates)
         tile = jnp.zeros_like(tile)
@@ -595,7 +602,8 @@
     own = slab_rows(place, [tomogram], x_cells, dims, tables, "slab_own")
     halo = slab_rows(place, [mine, other], TEMPL, dims, tables, "slab_halo")
     if by_blocks:
-        held, halo = lax.optimization_barrier((held, halo))
+        second = jnp.where(halo[0, 0] < 1e9, second, jnp.zeros_like(second))
+        held = jnp.concatenate([held, second], axis=1)
         lasts = [swap_blocks(held[:1], "tile", 1), swap_blocks(held[1:], "tile", 1)]
     else:
         lasts = [last[:1], last[1:]]
@@ -640,7 +648,7 @@
     pieces += [(at_early, r) for r in range(rots - 2)] + [(at_last, 0), (at_last, 1)]
     pieces += [(at_far + r, 0) for r in range(rots)]
     pieces += [(at_early, rots - 2 + r) for r in range(rots - 2)] + [(at_last, 2), (at_last, 3)]
-    return combine(me_place, coefs.reshape(groups * rots, 6), mask, arrays, pieces)
+    return combine(me_place, coefs.reshape(groups * rots, 6), mask, arrays, pieces, rots)
 
 
 def solution(mesh):

time: 98.2 us -> 89.6 us (0.912)
  waiting for transfers between devices: 21 us -> 14 us
  Pallas kernels: 44.2 us -> 38.3 us
  starting transfers between devices: 19.6 us -> 22.6 us
    pallas_call x4, Pallas kernels: 31.1 us -> 24.2 us  [correlate(): pl.pallas_call(functools.partial(corr_kernel, dims, rot, entry), out_shap...]
    ppermute x4, waiting for transfers between devices: 8.58 us -> 4.06 us  [swap_blocks(): lax.ppermute(block, axis, [(i, i ^ step) for i in range(lax.axis_size(axi...]
    ppermute x3, waiting for transfers between devices: 8.5 us -> 5.27 us  [local(): partner = lax.ppermute(state, 'tile', [(i, i ^ step) for i in range(tiles)])]
    ppermute x3, starting transfers between devices: 0.13 us -> 3.29 us  [local(): partner = lax.ppermute(state, 'tile', [(i, i ^ step) for i in range(tiles)])]
  transfers between devices with their start and end apart: 19 -> 19, of which waited for: 8 -> 11; matrix products, arithmetic and copies ran while one was open for 3% -> 3% of each run, Pallas kernels for 39% -> 38%
where the time goes in v10:
time: 89.6 us; the launch traced here: 89.3 us
  Pallas kernels  38.3 us (43%)
  starting transfers between devices  22.6 us (25%)
  waiting for transfers between devices  14 us (16%)
  local copies, waits for them, and re-layouts  9.91 us (11%)
  between operations  2.57 us (3%)
  other arithmetic  1.58 us (2%)
    pallas_call x4, Pallas kernels, correlate(): pl.pallas_call(functools.partial(corr_kernel, dims, rot, entry), out_shap...  24.2 us
    ppermute x4, starting transfers between devices, swap_blocks(): lax.ppermute(block, axis, [(i, i ^ step) for i in range(lax.axis_size(axi...  6.86 us
    unnamed x44, local copies, waits for them, and re-layouts  6.68 us
    pallas_call x2, Pallas kernels, slab_rows(): pl.pallas_call(functools.partial(slab_rows_kernel, dims), out_shape=jax.S...  5.58 us
    ppermute x3, waiting for transfers between devices, local(): partner = lax.ppermute(state, 'tile', [(i, i ^ step) for i in range(tiles)])  5.27 us
    ppermute x1, starting transfers between devices, neighbours(): lax.ppermute(block, axis, forward)  4.85 us
    pallas_call x1, Pallas kernels, slab_x(): pl.pallas_call(functools.partial(slab_x_kernel, dims), out_shape=(jax.Sha...  4.52 us
    ppermute x4, waiting for transfers between devices, swap_blocks(): lax.ppermute(block, axis, [(i, i ^ step) for i in range(lax.axis_size(axi...  4.06 us
  transfers between devices with their start and end apart: 19, of which 11 were waited for; matrix products, arithmetic and copies ran while one was open for 3% of the time, Pallas kernels for 38%

profile of v10, /device:TPU:0, one launch (start us, length us, event | category | flops | bytes accessed | tf_op | source)
XLA Modules:
  0.0 89.3 jit_solution(87700023928944472)
XLA Ops:
  0.7 1.0 %reshape.75 = bf16[4,1,108,128]{3,2,0,1:T(8,128)(2,1)S(1)} reshape(bf16[4,13824]{1,0:T(4,128)(2,1)} %param.15) | data formatting | bytes 221184 | tf_op jit(solution)/shard_map/reshape | solution.py:582
  1.7 0.9 %constant_dynamic-slice_fusion = bf16[16,5120]{1,0:T(8,128)(2,1)S(1)} fusion(bf16[32,5120]{1,0:T(8,128)(2,1)} %refs_0_.1, s32[]{:T(128)S(6)} %select_n.30), kind=kLoop, calls=%fused_computation.24 | loop fusion | bytes 327684 | tf_op jit(solution)/shard_map/dynamic_slice | solution.py:589
  2.6 4.9 %collective-permute-start.1 = (bf16[16,5120]{1,0:T(8,128)(2,1)S(1)}, bf16[16,5120]{1,0:T(8,128)(2,1)S(1)}, u32[]{:S(2)}, u32[]{:S(2)}) collective-permute-start(bf16[16,5120]{1,0:T(8,128)(2,1)S(1)} %constant_dynamic-slice_fusion), channel_id=1, source_target_pairs={{0,4},{4,8},{8,12},{12,16},{16,20},{20,24},{24,28},{1,5},{5,9},{9,... | collective-permute-start | bytes 491528 | tf_op jit(solution)/shard_map/ppermute | solution.py:565
  7.5 1.3 %collective-permute-start.2 = (bf16[16,5120]{1,0:T(8,128)(2,1)S(1)}, bf16[16,5120]{1,0:T(8,128)(2,1)S(1)}, u32[]{:S(2)}, u32[]{:S(2)}) collective-permute-start(bf16[16,5120]{1,0:T(8,128)(2,1)S(1)} %constant_dynamic-slice_fusion), channel_id=1, source_target_pairs={{4,0},{8,4},{12,8},{16,12},{20,16},{24,20},{28,24},{5,1},{9,5},{13... | collective-permute-start | bytes 491528 | tf_op jit(solution)/shard_map/ppermute | solution.py:565
  8.8 4.7 %collective-permute-start = (bf16[4,1,112,128]{3,2,1,0:T(8,128)(2,1)S(1)}, bf16[4,1,112,128]{3,2,1,0:T(8,128)(2,1)S(1)}, u32[]{:S(2)}, u32[]{:S(2)}) collective-permute-start(bf16[4,1,112,128]{3,2,1,0:T(8,128)(2,1)S(1)} %pad.4), channel_id=1, source_target_pairs={{0,16},{4,20},{8,24},{12,28},{16,0},{20,4},{24,8},{28,12},{1,17},{... | collective-permute-start | bytes 344072 | tf_op jit(solution)/shard_map/ppermute | solution.py:526
  13.5 1.0 %copy-done.7 = bf16[32,5120]{1,0:T(8,128)(2,1)S(1)} copy-done((bf16[32,5120]{1,0:T(8,128)(2,1)S(1)}, bf16[32,5120]{1,0:T(8,128)(2,1)}, u32[]{:S(2)}) %copy-start.7) | copy-done | bytes 327704
  14.4 0.9 %copy-done.9 = bf16[240,512]{1,0:T(8,128)(2,1)S(1)} copy-done((bf16[240,512]{1,0:T(8,128)(2,1)S(1)}, bf16[240,512]{1,0:T(8,128)(2,1)}, u32[]{:S(2)}) %copy-start.9) | copy-done | bytes 245784
  15.4 2.3 %slab_own.1.own_ref = f32[3616,128]{1,0:T(8,128)S(1)} custom-call(s32[1]{0:T(128)} %bitcast.place_ref, bf16[32,5120]{1,0:T(8,128)(2,1)S(1)} %copy-done.7, bf16[240,512]{1,0:T(8,128)(2,1)S(1)} %copy-done.9), custom_call_target="tpu_custom_call" | custom-call | flops 3200000000 | bytes 1000000 | tf_op jit(solution)/shard_map/slab_own/pallas_call | solution.py:239
  17.7 1.3 %copy-done.19 = f32[3616,128]{1,0:T(8,128)} copy-done((f32[3616,128]{1,0:T(8,128)}, f32[3616,128]{1,0:T(8,128)S(1)}, u32[]{:S(2)}) %copy-start.19) | copy-done | bytes 1851416
  19.4 2.6 %collective-permute-done = bf16[4,1,112,128]{3,2,1,0:T(8,128)(2,1)S(1)} collective-permute-done((bf16[4,1,112,128]{3,2,1,0:T(8,128)(2,1)S(1)}, bf16[4,1,112,128]{3,2,1,0:T(8,128)(2,1)S(1)}, u32[]{:S(2)}, u32[]{:S(2)}) %collective-permute-start) | collective-permute-done | bytes 114720 | tf_op jit(solution)/shard_map/ppermute | solution.py:526
  22.1 3.3 %slab_halo.1.halo_ref = f32[5424,128]{1,0:T(8,128)S(1)} custom-call(s32[1]{0:T(128)} %bitcast.place_ref, bf16[2,16,5120]{2,1,0:T(8,128)(2,1)S(1)} %pad_maximum_fusion.3.refs_0_, bf16[2,16,5120]{2,1,0:T(8,128)(2,1)S(1)} %collective-permute-done.3.refs_1_, bf16[240,512]{1,0:T(8,128)(2,1)S(1)} %copy-done.10), custom_call_target="tpu_custom_call" | custom-call | flops 4800000000 | bytes 1000000 | tf_op jit(solution)/shard_map/slab_halo/pallas_call | solution.py:239
  26.6 1.5 %collective-permute-done.4 = bf16[4,2,112,128]{3,2,1,0:T(8,128)(2,1)S(1)} collective-permute-done((bf16[4,2,112,128]{3,2,1,0:T(8,128)(2,1)S(1)}, bf16[4,2,112,128]{3,2,1,0:T(8,128)(2,1)S(1)}, u32[]{:S(2)}, u32[]{:S(2)}) %collective-permute-start.4) | collective-permute-done | bytes 229408 | tf_op jit(solution)/shard_map/ppermute | solution.py:526
  28.3 1.6 %collective-permute-start.5 = (bf16[1,4,112,128]{3,2,1,0:T(8,128)(2,1)S(1)}, bf16[1,4,112,128]{3,2,1,0:T(8,128)(2,1)S(1)}, u32[]{:S(2)}, u32[]{:S(2)}) collective-permute-start(bf16[1,4,112,128]{3,2,1,0:T(8,128)(2,1)S(1)} %slice.110), channel_id=1, source_target_pairs={{0,4},{4,0},{8,12},{12,8},{16,20},{20,16},{24,28},{28,24},{1,5},{5... | collective-permute-start | bytes 344072 | tf_op jit(solution)/shard_map/ppermute | solution.py:526
  30.4 4.5 %slab_x.1 = (f32[13,2,80,1024]{3,2,1,0:T(8,128)S(1)}, f32[40,32,128]{2,1,0:T(8,128)S(1)}, bf16[8,256,256]{2,1,0:T(8,128)(2,1)S(1)}) custom-call(f32[3616,128]{1,0:T(8,128)S(1)} %copy-done.20, f32[5424,128]{1,0:T(8,128)S(1)} %slab_halo.1.halo_ref, bf16[80,240]{1,0:T(8,128)(2,1)S(1)} %copy-done.15, s32[32,80]{1,0:T(8,128)S(1)} %copy-done.8, ...), custom_call_target="tpu_custom_call" | custom-call | flops 5000000000 | bytes 1000000 | tf_op jit(solution)/shard_map/slab_x/pallas_call | solution.py:298
  35.0 6.0 %correlate.4 = (f32[32,1280]{1,0:T(8,128)S(1)}, f32[32,1280]{1,0:T(8,128)S(1)}, f32[2,32,1280]{2,1,0:T(8,128)S(1)}, f32[8,128]{1,0:T(8,128)S(1)}) custom-call(s32[1]{0:T(128)} %bitcast.place_ref, s32[1]{0:T(128)} %bitcast.1.tile_ref, bf16[4,4,112,128]{3,2,1,0:T(8,128)(2,1)S(1)} %pad_maximum_fusion.2.held_ref, ...), custom_call_target="tpu_custom_call" | custom-call | flops 15000000512 | bytes 10000000 | tf_op jit(solution)/shard_map/correlate/pallas_call | solution.py:443
  41.0 1.6 %collective-permute-start.7 = (f32[2,32,1280]{2,1,0:T(8,128)S(1)}, f32[2,32,1280]{2,1,0:T(8,128)S(1)}, u32[]{:S(2)}, u32[]{:S(2)}) collective-permute-start(f32[2,32,1280]{2,1,0:T(8,128)S(1)} %get-tuple-element.46), channel_id=1, source_target_pairs={{0,2},{1,3},{2,0},{3,1},{4,6},{5,7},{6,4},{7,5},{8,10},{9,11},{10,... | collective-permute-start | bytes 983048 | tf_op jit(solution)/shard_map/ppermute | solution.py:624
  42.6 6.0 %correlate.5 = (f32[32,1280]{1,0:T(8,128)S(1)}, f32[32,1280]{1,0:T(8,128)S(1)}, f32[2,32,1280]{2,1,0:T(8,128)S(1)}, f32[8,128]{1,0:T(8,128)S(1)}) custom-call(s32[1]{0:T(128)} %bitcast.place_ref, s32[1]{0:T(128)} %bitcast.1.tile_ref, bf16[4,4,112,128]{3,2,1,0:T(8,128)(2,1)S(1)} %pad_maximum_fusion.2.held_ref, ...), custom_call_target="tpu_custom_call" | custom-call | flops 15000000512 | bytes 10000000 | tf_op jit(solution)/shard_map/correlate/pallas_call | solution.py:443
  49.9 6.2 %correlate.6 = (f32[32,1280]{1,0:T(8,128)S(1)}, f32[32,1280]{1,0:T(8,128)S(1)}, f32[2,32,1280]{2,1,0:T(8,128)S(1)}, f32[8,128]{1,0:T(8,128)S(1)}) custom-call(s32[1]{0:T(128)} %bitcast.place_ref, s32[1]{0:T(128)} %bitcast.1.tile_ref, bf16[4,4,112,128]{3,2,1,0:T(8,128)(2,1)S(1)} %pad_maximum_fusion.2.held_ref, ...), custom_call_target="tpu_custom_call" | custom-call | flops 15000000512 | bytes 10000000 | tf_op jit(solution)/shard_map/correlate/pallas_call | solution.py:443
  56.1 1.6 %collective-permute-start.9 = (f32[2,32,1280]{2,1,0:T(8,128)S(1)}, f32[2,32,1280]{2,1,0:T(8,128)S(1)}, u32[]{:S(2)}, u32[]{:S(2)}) collective-permute-start(f32[2,32,1280]{2,1,0:T(8,128)S(1)} %get-tuple-element.56), channel_id=1, source_target_pairs={{0,2},{1,3},{2,0},{3,1},{4,6},{5,7},{6,4},{7,5},{8,10},{9,11},{10,... | collective-permute-start | bytes 983048 | tf_op jit(solution)/shard_map/ppermute | solution.py:624
  58.3 6.0 %correlate.7 = (f32[32,1280]{1,0:T(8,128)S(1)}, f32[32,1280]{1,0:T(8,128)S(1)}, f32[2,32,1280]{2,1,0:T(8,128)S(1)}, f32[8,128]{1,0:T(8,128)S(1)}) custom-call(s32[1]{0:T(128)} %bitcast.place_ref, s32[1]{0:T(128)} %bitcast.1.tile_ref, bf16[4,4,112,128]{3,2,1,0:T(8,128)(2,1)S(1)} %pad_maximum_fusion.2.held_ref, ...), custom_call_target="tpu_custom_call" | custom-call | flops 15000000512 | bytes 10000000 | tf_op jit(solution)/shard_map/correlate/pallas_call | solution.py:443
  64.9 1.7 %collective-permute-start.11 = (f32[3,4]{1,0:T(4,128)S(1)}, f32[3,4]{1,0:T(4,128)S(1)}, u32[]{:S(2)}, u32[]{:S(2)}) collective-permute-start(f32[3,4]{1,0:T(4,128)S(1)} %pad_maximum_fusion.6), channel_id=1, source_target_pairs={{0,4},{4,0},{8,12},{12,8},{16,20},{20,16},{24,28},{28,24},{1,5},{5... | collective-permute-start | bytes 152 | tf_op jit(solution)/shard_map/ppermute | solution.py:632
  66.6 1.9 %collective-permute-done.11 = f32[3,4]{1,0:T(4,128)S(1)} collective-permute-done((f32[3,4]{1,0:T(4,128)S(1)}, f32[3,4]{1,0:T(4,128)S(1)}, u32[]{:S(2)}, u32[]{:S(2)}) %collective-permute-start.11) | collective-permute-done | bytes 80 | tf_op jit(solution)/shard_map/ppermute | solution.py:632
  68.6 1.5 %collective-permute-start.12 = (f32[3,4]{1,0:T(4,128)S(1)}, f32[3,4]{1,0:T(4,128)S(1)}, u32[]{:S(2)}, u32[]{:S(2)}) collective-permute-start(f32[3,4]{1,0:T(4,128)S(1)} %select_add_fusion.2), channel_id=1, source_target_pairs={{0,8},{4,12},{8,0},{12,4},{16,24},{20,28},{24,16},{28,20},{1,9},{5... | collective-permute-start | bytes 152 | tf_op jit(solution)/shard_map/ppermute | solution.py:632
  70.1 2.1 %collective-permute-done.12 = f32[3,4]{1,0:T(4,128)S(1)} collective-permute-done((f32[3,4]{1,0:T(4,128)S(1)}, f32[3,4]{1,0:T(4,128)S(1)}, u32[]{:S(2)}, u32[]{:S(2)}) %collective-permute-start.12) | collective-permute-done | bytes 80 | tf_op jit(solution)/shard_map/ppermute | solution.py:632
  73.5 1.0 %collective-permute-done.14.refs_7_ = f32[2,32,1280]{2,1,0:T(8,128)S(1)} collective-permute-done((f32[2,32,1280]{2,1,0:T(8,128)S(1)}, f32[2,32,1280]{2,1,0:T(8,128)S(1)}, u32[]{:S(2)}, u32[]{:S(2)}) %collective-permute-start.14) | collective-permute-done | bytes 327712 | tf_op jit(solution)/shard_map/ppermute | solution.py:624
  75.4 1.3 %collective-permute-done.13 = f32[3,4]{1,0:T(4,128)S(1)} collective-permute-done((f32[3,4]{1,0:T(4,128)S(1)}, f32[3,4]{1,0:T(4,128)S(1)}, u32[]{:S(2)}, u32[]{:S(2)}) %collective-permute-start.13) | collective-permute-done | bytes 80 | tf_op jit(solution)/shard_map/ppermute | solution.py:632
  77.6 1.6 %collective-permute-start.16 = (f32[4,6]{1,0:T(4,128)S(1)}, f32[4,6]{1,0:T(4,128)S(1)}, u32[]{:S(2)}, u32[]{:S(2)}) collective-permute-start(f32[4,6]{1,0:T(4,128)S(1)} %pad_maximum_fusion.7), channel_id=1, source_target_pairs={{0,2},{1,3},{2,0},{3,1},{4,6},{5,7},{6,4},{7,5},{8,10},{9,11},{10,... | collective-permute-start | bytes 296 | tf_op jit(solution)/shard_map/ppermute | solution.py:557
  79.3 1.9 %collective-permute-done.16 = f32[4,6]{1,0:T(4,128)S(1)} collective-permute-done((f32[4,6]{1,0:T(4,128)S(1)}, f32[4,6]{1,0:T(4,128)S(1)}, u32[]{:S(2)}, u32[]{:S(2)}) %collective-permute-start.16) | collective-permute-done | bytes 128 | tf_op jit(solution)/shard_map/ppermute | solution.py:557
  81.2 1.1 %collective-permute-done.17 = f32[4,6]{1,0:T(4,128)S(1)} collective-permute-done((f32[4,6]{1,0:T(4,128)S(1)}, f32[4,6]{1,0:T(4,128)S(1)}, u32[]{:S(2)}, u32[]{:S(2)}) %collective-permute-start.17) | collective-permute-done | bytes 128 | tf_op jit(solution)/shard_map/ppermute | solution.py:557
  83.3 0.9 %copy-done.4 = f32[32,1280]{1,0:T(8,128)S(1)} copy-done((f32[32,1280]{1,0:T(8,128)S(1)}, f32[32,1280]{1,0:T(8,128)}, u32[]{:S(2)}) %copy-start.4) | copy-done | bytes 163864
  84.2 0.9 %copy-done.6 = f32[32,1280]{1,0:T(8,128)S(1)} copy-done((f32[32,1280]{1,0:T(8,128)S(1)}, f32[32,1280]{1,0:T(8,128)}, u32[]{:S(2)}) %copy-start.6) | copy-done | bytes 163864
  85.1 4.0 %combine.1 = (f32[32,1280]{1,0:T(8,128)}, f32[32,1280]{1,0:T(8,128)}, f32[4,32,1280]{2,1,0:T(8,128)}) custom-call(s32[1]{0:T(128)} %bitcast.place_ref, f32[16,6]{1,0:T(8,128)S(1)} %bitcast.32, f32[40,32,128]{2,1,0:T(8,128)S(1)} %get-tuple-element.41.mask_ref, f32[32,1280]{1,0:T(8,128)S(1)} %get-tuple-element.68.refs_0_, f32[32,1280]{1,0:T(8,128)S(1)} %copy-done.2, ...), custom_call_target="tpu_custom_call" | custom-call | tf_op jit(solution)/shard_map/combine/pallas_call | solution.py:513
  (94 shorter events, 7.7 us)
Async XLA Ops:
  0.6 18.4 %copy-start = (f32[4,4096]{1,0:T(4,128)S(1)}, f32[4,4096]{1,0:T(4,128)}, u32[]{:S(2)}) copy-start(f32[4,4096]{1,0:T(4,128)} %param.17) | copy-start | bytes 196612
  2.6 16.3 %collective-permute-start.1 = (bf16[16,5120]{1,0:T(8,128)(2,1)S(1)}, bf16[16,5120]{1,0:T(8,128)(2,1)S(1)}, u32[]{:S(2)}, u32[]{:S(2)}) collective-permute-start(bf16[16,5120]{1,0:T(8,128)(2,1)S(1)} %constant_dynamic-slice_fusion), channel_id=1, source_target_pairs={{0,4},{4,8},{8,12},{12,16},{16,20},{20,24},{24,28},{1,5},{5,9},{9,... | collective-permute-start | bytes 491528 | tf_op jit(solution)/shard_map/ppermute | solution.py:565
  7.5 11.5 %collective-permute-start.2 = (bf16[16,5120]{1,0:T(8,128)(2,1)S(1)}, bf16[16,5120]{1,0:T(8,128)(2,1)S(1)}, u32[]{:S(2)}, u32[]{:S(2)}) collective-permute-start(bf16[16,5120]{1,0:T(8,128)(2,1)S(1)} %constant_dynamic-slice_fusion), channel_id=1, source_target_pairs={{4,0},{8,4},{12,8},{16,12},{20,16},{24,20},{28,24},{5,1},{9,5},{13... | collective-permute-start | bytes 491528 | tf_op jit(solution)/shard_map/ppermute | solution.py:565
  8.8 13.2 %collective-permute-start = (bf16[4,1,112,128]{3,2,1,0:T(8,128)(2,1)S(1)}, bf16[4,1,112,128]{3,2,1,0:T(8,128)(2,1)S(1)}, u32[]{:S(2)}, u32[]{:S(2)}) collective-permute-start(bf16[4,1,112,128]{3,2,1,0:T(8,128)(2,1)S(1)} %pad.4), channel_id=1, source_target_pairs={{0,16},{4,20},{8,24},{12,28},{16,0},{20,4},{24,8},{28,12},{1,17},{... | collective-permute-start | bytes 344072 | tf_op jit(solution)/shard_map/ppermute | solution.py:526
  15.4 6.7 %copy-start.10 = (bf16[240,512]{1,0:T(8,128)(2,1)S(1)}, bf16[240,512]{1,0:T(8,128)(2,1)}, u32[]{:S(2)}) copy-start(bf16[240,512]{1,0:T(8,128)(2,1)} %constant.52.clone.refs_2_.refs_1_) | copy-start | bytes 737284
  19.0 3.1 %collective-permute-start.3 = (bf16[2,16,5120]{2,1,0:T(8,128)(2,1)S(1)}, bf16[2,16,5120]{2,1,0:T(8,128)(2,1)S(1)}, u32[]{:S(2)}, u32[]{:S(2)}) collective-permute-start(bf16[2,16,5120]{2,1,0:T(8,128)(2,1)S(1)} %pad_maximum_fusion.3.refs_0_), channel_id=1, source_target_pairs={{0,1},{1,0},{2,3},{3,2},{4,5},{5,4},{6,7},{7,6},{8,9},{9,8},{10,11... | collective-permute-start | bytes 983048 | tf_op jit(solution)/shard_map/ppermute | solution.py:592
  22.0 8.4 %copy-start.8 = (s32[32,80]{1,0:T(8,128)S(1)}, s32[32,80]{1,0:T(8,128)}, u32[]{:S(2)}) copy-start(s32[32,80]{1,0:T(8,128)} %valid_ref.1) | copy-start | bytes 30724
  22.0 8.4 %copy-start.15 = (bf16[80,240]{1,0:T(8,128)(2,1)S(1)}, bf16[80,240]{1,0:T(8,128)(2,1)}, u32[]{:S(2)}) copy-start(bf16[80,240]{1,0:T(8,128)(2,1)} %constant.53.clone.x_ref) | copy-start | bytes 115204
  22.0 8.4 %copy-start.17 = (bf16[48,256]{1,0:T(8,128)(2,1)S(1)}, bf16[48,256]{1,0:T(8,128)(2,1)}, u32[]{:S(2)}) copy-start(bf16[48,256]{1,0:T(8,128)(2,1)} %constant.54.clone.tz_ref) | copy-start | bytes 73732
  22.0 8.4 %copy-start.20 = (f32[3616,128]{1,0:T(8,128)S(1)}, f32[3616,128]{1,0:T(8,128)}, u32[]{:S(2)}) copy-start(f32[3616,128]{1,0:T(8,128)} %copy-done.19) | copy-start | bytes 5554180
  22.0 6.1 %collective-permute-start.4 = (bf16[4,2,112,128]{3,2,1,0:T(8,128)(2,1)S(1)}, bf16[4,2,112,128]{3,2,1,0:T(8,128)(2,1)S(1)}, u32[]{:S(2)}, u32[]{:S(2)}) collective-permute-start(bf16[4,2,112,128]{3,2,1,0:T(8,128)(2,1)S(1)} %pad_maximum_fusion.4), channel_id=1, source_target_pairs={{0,8},{4,12},{8,0},{12,4},{16,24},{20,28},{24,16},{28,20},{1,9},{5... | collective-permute-start | bytes 688136 | tf_op jit(solution)/shard_map/ppermute | solution.py:526
  28.2 6.7 %copy-start.11 = (bf16[256,256]{1,0:T(8,128)(2,1)S(1)}, bf16[256,256]{1,0:T(8,128)(2,1)}, u32[]{:S(2)}) copy-start(bf16[256,256]{1,0:T(8,128)(2,1)} %constant.60.clone.bz_ref) | copy-start | bytes 393220
  28.2 6.7 %copy-start.12 = (bf16[160,208]{1,0:T(8,128)(2,1)S(1)}, bf16[160,208]{1,0:T(8,128)(2,1)}, u32[]{:S(2)}) copy-start(bf16[160,208]{1,0:T(8,128)(2,1)} %constant.59.clone.by_ref) | copy-start | bytes 199684
  28.2 6.7 %copy-start.13 = (bf16[112,144]{1,0:T(8,128)(2,1)S(1)}, bf16[112,144]{1,0:T(8,128)(2,1)}, u32[]{:S(2)}) copy-start(bf16[112,144]{1,0:T(8,128)(2,1)} %constant.56.clone.y_ref) | copy-start | bytes 96772
  28.3 6.7 %copy-start.14 = (bf16[80,144]{1,0:T(8,128)(2,1)S(1)}, bf16[80,144]{1,0:T(8,128)(2,1)}, u32[]{:S(2)}) copy-start(bf16[80,144]{1,0:T(8,128)(2,1)} %constant.57.clone.x_ref) | copy-start | bytes 69124
  28.3 6.7 %copy-start.16 = (bf16[64,160]{1,0:T(8,128)(2,1)S(1)}, bf16[64,160]{1,0:T(8,128)(2,1)}, u32[]{:S(2)}) copy-start(bf16[64,160]{1,0:T(8,128)(2,1)} %constant.58.clone.bx_ref) | copy-start | bytes 61444
  28.3 6.7 %copy-start.18 = (f32[8,128]{1,0:T(8,128)S(1)}, f32[8,128]{1,0:T(8,128)}, u32[]{:S(2)}) copy-start(f32[8,128]{1,0:T(8,128)} %constant.55.clone.ones_ref) | copy-start | bytes 12292
  28.3 6.6 %collective-permute-start.5 = (bf16[1,4,112,128]{3,2,1,0:T(8,128)(2,1)S(1)}, bf16[1,4,112,128]{3,2,1,0:T(8,128)(2,1)S(1)}, u32[]{:S(2)}, u32[]{:S(2)}) collective-permute-start(bf16[1,4,112,128]{3,2,1,0:T(8,128)(2,1)S(1)} %slice.110), channel_id=1, source_target_pairs={{0,4},{4,0},{8,12},{12,8},{16,20},{20,16},{24,28},{28,24},{1,5},{5... | collective-permute-start | bytes 344072 | tf_op jit(solution)/shard_map/ppermute | solution.py:526
  29.9 12.7 %collective-permute-start.6 = (bf16[3,4,112,128]{3,2,1,0:T(8,128)(2,1)S(1)}, bf16[3,4,112,128]{3,2,1,0:T(8,128)(2,1)S(1)}, u32[]{:S(2)}, u32[]{:S(2)}) collective-permute-start(bf16[3,4,112,128]{3,2,1,0:T(8,128)(2,1)S(1)} %slice.111), channel_id=1, source_target_pairs={{0,4},{4,0},{8,12},{12,8},{16,20},{20,16},{24,28},{28,24},{1,5},{5... | collective-permute-start | bytes 1032200 | tf_op jit(solution)/shard_map/ppermute | solution.py:526
  41.0 8.9 %collective-permute-start.7 = (f32[2,32,1280]{2,1,0:T(8,128)S(1)}, f32[2,32,1280]{2,1,0:T(8,128)S(1)}, u32[]{:S(2)}, u32[]{:S(2)}) collective-permute-start(f32[2,32,1280]{2,1,0:T(8,128)S(1)} %get-tuple-element.46), channel_id=1, source_target_pairs={{0,2},{1,3},{2,0},{3,1},{4,6},{5,7},{6,4},{7,5},{8,10},{9,11},{10,... | collective-permute-start | bytes 983048 | tf_op jit(solution)/shard_map/ppermute | solution.py:624
  49.2 8.9 %collective-permute-start.8 = (f32[2,32,1280]{2,1,0:T(8,128)S(1)}, f32[2,32,1280]{2,1,0:T(8,128)S(1)}, u32[]{:S(2)}, u32[]{:S(2)}) collective-permute-start(f32[2,32,1280]{2,1,0:T(8,128)S(1)} %get-tuple-element.51), channel_id=1, source_target_pairs={{0,2},{1,3},{2,0},{3,1},{4,6},{5,7},{6,4},{7,5},{8,10},{9,11},{10,... | collective-permute-start | bytes 983048 | tf_op jit(solution)/shard_map/ppermute | solution.py:624
  56.1 8.7 %collective-permute-start.9 = (f32[2,32,1280]{2,1,0:T(8,128)S(1)}, f32[2,32,1280]{2,1,0:T(8,128)S(1)}, u32[]{:S(2)}, u32[]{:S(2)}) collective-permute-start(f32[2,32,1280]{2,1,0:T(8,128)S(1)} %get-tuple-element.56), channel_id=1, source_target_pairs={{0,2},{1,3},{2,0},{3,1},{4,6},{5,7},{6,4},{7,5},{8,10},{9,11},{10,... | collective-permute-start | bytes 983048 | tf_op jit(solution)/shard_map/ppermute | solution.py:624
  58.2 6.6 %collective-permute-start.10 = (f32[4,32,1280]{2,1,0:T(8,128)S(1)}, f32[4,32,1280]{2,1,0:T(8,128)S(1)}, u32[]{:S(2)}, u32[]{:S(2)}) collective-permute-start(f32[4,32,1280]{2,1,0:T(8,128)S(1)} %pad_maximum_fusion), channel_id=1, source_target_pairs={{0,1},{1,0},{2,3},{3,2},{4,5},{5,4},{6,7},{7,6},{8,9},{9,8},{10,11... | collective-permute-start | bytes 1966088 | tf_op jit(solution)/shard_map/ppermute | solution.py:627
  64.3 11.1 %copy-start.5 = (f32[32,1280]{1,0:T(8,128)}, f32[32,1280]{1,0:T(8,128)S(1)}, u32[]{:S(2)}) copy-start(f32[32,1280]{1,0:T(8,128)S(1)} %get-tuple-element.71.refs_3_) | copy-start | bytes 491524
  64.3 10.2 %collective-permute-start.14 = (f32[2,32,1280]{2,1,0:T(8,128)S(1)}, f32[2,32,1280]{2,1,0:T(8,128)S(1)}, u32[]{:S(2)}, u32[]{:S(2)}) collective-permute-start(f32[2,32,1280]{2,1,0:T(8,128)S(1)} %get-tuple-element.66), channel_id=1, source_target_pairs={{0,2},{1,3},{2,0},{3,1},{4,6},{5,7},{6,4},{7,5},{8,10},{9,11},{10,... | collective-permute-start | bytes 983048 | tf_op jit(solution)/shard_map/ppermute | solution.py:624
  64.9 3.6 %collective-permute-start.11 = (f32[3,4]{1,0:T(4,128)S(1)}, f32[3,4]{1,0:T(4,128)S(1)}, u32[]{:S(2)}, u32[]{:S(2)}) collective-permute-start(f32[3,4]{1,0:T(4,128)S(1)} %pad_maximum_fusion.6), channel_id=1, source_target_pairs={{0,4},{4,0},{8,12},{12,8},{16,20},{20,16},{24,28},{28,24},{1,5},{5... | collective-permute-start | bytes 152 | tf_op jit(solution)/shard_map/ppermute | solution.py:632
  68.6 3.6 %collective-permute-start.12 = (f32[3,4]{1,0:T(4,128)S(1)}, f32[3,4]{1,0:T(4,128)S(1)}, u32[]{:S(2)}, u32[]{:S(2)}) collective-permute-start(f32[3,4]{1,0:T(4,128)S(1)} %select_add_fusion.2), channel_id=1, source_target_pairs={{0,8},{4,12},{8,0},{12,4},{16,24},{20,28},{24,16},{28,20},{1,9},{5... | collective-permute-start | bytes 152 | tf_op jit(solution)/shard_map/ppermute | solution.py:632
  72.2 4.5 %collective-permute-start.13 = (f32[3,4]{1,0:T(4,128)S(1)}, f32[3,4]{1,0:T(4,128)S(1)}, u32[]{:S(2)}, u32[]{:S(2)}) collective-permute-start(f32[3,4]{1,0:T(4,128)S(1)} %select_add_fusion.1), channel_id=1, source_target_pairs={{0,16},{4,20},{8,24},{12,28},{16,0},{20,4},{24,8},{28,12},{1,17},{... | collective-permute-start | bytes 152 | tf_op jit(solution)/shard_map/ppermute | solution.py:632
  76.7 5.6 %collective-permute-start.18 = (f32[4,32,1280]{2,1,0:T(8,128)}, f32[4,32,1280]{2,1,0:T(8,128)S(1)}, u32[]{:S(2)}, u32[]{:S(2)}) collective-permute-start(f32[4,32,1280]{2,1,0:T(8,128)} %pad_maximum_fusion.1), channel_id=1, source_target_pairs={{0,1},{1,0},{2,3},{3,2},{4,5},{5,4},{6,7},{7,6},{8,9},{9,8},{10,11... | collective-permute-start | bytes 1966088 | tf_op jit(solution)/shard_map/ppermute | solution.py:644
  77.1 2.2 %collective-permute-start.15 = (f32[4,6]{1,0:T(4,128)S(1)}, f32[4,6]{1,0:T(4,128)S(1)}, u32[]{:S(2)}, u32[]{:S(2)}) collective-permute-start(f32[4,6]{1,0:T(4,128)S(1)} %pad_maximum_fusion.7), channel_id=1, source_target_pairs={{0,1},{1,0},{2,3},{3,2},{4,5},{5,4},{6,7},{7,6},{8,9},{9,8},{10,11... | collective-permute-start | bytes 296 | tf_op jit(solution)/shard_map/ppermute | solution.py:557
  77.6 3.6 %collective-permute-start.16 = (f32[4,6]{1,0:T(4,128)S(1)}, f32[4,6]{1,0:T(4,128)S(1)}, u32[]{:S(2)}, u32[]{:S(2)}) collective-permute-start(f32[4,6]{1,0:T(4,128)S(1)} %pad_maximum_fusion.7), channel_id=1, source_target_pairs={{0,2},{1,3},{2,0},{3,1},{4,6},{5,7},{6,4},{7,5},{8,10},{9,11},{10,... | collective-permute-start | bytes 296 | tf_op jit(solution)/shard_map/ppermute | solution.py:557
  79.3 3.0 %collective-permute-start.17 = (f32[4,6]{1,0:T(4,128)S(1)}, f32[4,6]{1,0:T(4,128)S(1)}, u32[]{:S(2)}, u32[]{:S(2)}) collective-permute-start(f32[4,6]{1,0:T(4,128)S(1)} %pad_maximum_fusion.7), channel_id=1, source_target_pairs={{0,3},{1,2},{2,1},{3,0},{4,7},{5,6},{6,5},{7,4},{8,11},{9,10},{10,... | collective-permute-start | bytes 296 | tf_op jit(solution)/shard_map/ppermute | solution.py:557
  (9 other events, 12.4 us)

commit v11 on v8

--- a/solution.py
+++ b/solution.py
@@ -184,8 +184,13 @@
 
 
 def slab_rows_kernel(dims, place_ref, *refs):
-    sources, (table_ref, rows_ref, depth_buf, parts_buf) = refs[:-4], refs[-4:]
+    *sources, table_ref, rows_ref, depth_buf, parts_buf = refs
     x_cells, y_cells, z_cells = dims
+    base = 0
+    if len(sources) > 1:
+        own_ref, *sources = sources
+        base = own_ref.shape[0]
+        rows_ref[:base, :] = own_ref[...]
     half = x_cells // 2
     count = depth_buf.shape[0] // y_cells - 1
     n_y = y_cells + HALF
@@ -224,35 +229,35 @@
     def y_step(i, slot):
         plus, minus = pair_dot(table_ref[2 * z_cells :, : 3 * y_cells], parts_buf[slot], True)
         for u in range(GROUP):
-            start = (GROUP * i + u) * odd(2 * pad_y)
+            start = base + (GROUP * i + u) * odd(2 * pad_y)
             store(rows_ref, start, lane_block(plus, u))
             store(rows_ref, start + pad_y, lane_block(minus, u))
 
-    pipeline(count // GROUP, [gather_rows, y_step], 2)
-
-
-def slab_rows(place, blocks, count, dims, tables, name):
+    pipeline(count // GROUP, [gather_rows, y_step], 3)
+
+
+def slab_rows(place, blocks, count, passed, dims, tables, name):
     x_cells, y_cells, z_cells = dims
     n_y = y_cells + HALF
     pad_y = n_y // 2 + -(n_y // 2) % 8
     vmem = pl.BlockSpec(memory_space=pltpu.VMEM)
     return pl.pallas_call(
         functools.partial(slab_rows_kernel, dims),
-        out_shape=jax.ShapeDtypeStruct((count * odd(2 * pad_y), LANES), F32),
+        out_shape=jax.ShapeDtypeStruct(((passed + count) * odd(2 * pad_y), LANES), F32),
         in_specs=[pl.BlockSpec(memory_space=pltpu.SMEM)] + [vmem] * (1 + len(blocks)),
         out_specs=vmem,
         scratch_shapes=[
             pltpu.VMEM((y_cells * odd(count), LANES), F32),
-            pltpu.VMEM((2, 3 * y_cells, GROUP * LANES), BF16),
+            pltpu.VMEM((3, 3 * y_cells, GROUP * LANES), BF16),
         ],
-        compiler_params=pltpu.CompilerParams(vmem_limit_bytes=9 * 1024 * 1024),
+        compiler_params=pltpu.CompilerParams(vmem_limit_bytes=12 * 1024 * 1024),
         cost_estimate=pl.CostEstimate(flops=count * 10**8, bytes_accessed=10**6, transcendentals=0),
         name=name,
     )(place, *blocks, tables["slab_rows"])
 
 
 def slab_x_kernel(
-    dims, own_ref, halo_ref, x_ref, valid_ref, tz_ref, spec_ref, mask_ref, z_ref, parts_buf
+    dims, rows_ref, x_ref, valid_ref, tz_ref, spec_ref, mask_ref, z_ref, parts_buf
 ):
     x_cells, y_cells, z_cells = dims
     n_y = y_cells + HALF
@@ -260,13 +265,7 @@
 
     def gather_rows(i, slot):
         firsts = [GROUP // 2 * i + u // 2 + u % 2 * pad_y for u in range(GROUP)]
-        value = jnp.concatenate(
-            [
-                pick(own_ref, firsts, x_cells, odd(2 * pad_y)),
-                pick(halo_ref, firsts, TEMPL, odd(2 * pad_y)),
-            ],
-            axis=0,
-        )
+        value = pick(rows_ref, firsts, x_cells + TEMPL, odd(2 * pad_y))
         parts_buf[slot] = split_rows(value, True)
 
     def x_step(i, slot):
@@ -277,7 +276,7 @@
         spec_ref[i, 0] = jnp.where(real_lane, spec, turned)
         spec_ref[i, 1] = jnp.where(real_lane, -turned, spec)
 
-    pipeline(n_y // GROUP, [gather_rows, x_step], 2)
+    pipeline(n_y // GROUP, [gather_rows, x_step], 4)
 
     valid = valid_ref[...].astype(F32)
     low_lane = lax.broadcasted_iota(jnp.int32, (x_cells, LANES), 1) < z_cells
@@ -289,7 +288,7 @@
         z_ref[j, start : start + TEMPL, :] = tz_ref[...]
 
 
-def slab_x(own, halo, valid, dims, tables):
+def slab_x(rows, valid, dims, tables):
     x_cells, y_cells, z_cells = dims
     n_x, n_y = x_cells + TEMPL, y_cells + HALF
     steps = n_y // GROUP
@@ -302,21 +301,25 @@
             jax.ShapeDtypeStruct((y_cells // 2, x_cells, LANES), F32),
             jax.ShapeDtypeStruct((8, 2 * LANES, 2 * LANES), BF16),
         ),
-        in_specs=[vmem] * 5,
+        in_specs=[vmem] * 4,
         out_specs=(vmem,) * 3,
-        scratch_shapes=[pltpu.VMEM((2, 3 * n_x, GROUP * LANES), BF16)],
-        compiler_params=pltpu.CompilerParams(vmem_limit_bytes=6 * 1024 * 1024),
+        scratch_shapes=[pltpu.VMEM((4, 3 * n_x, GROUP * LANES), BF16)],
+        compiler_params=pltpu.CompilerParams(vmem_limit_bytes=9 * 1024 * 1024),
         cost_estimate=pl.CostEstimate(flops=5 * 10**9, bytes_accessed=10**6, transcendentals=0),
         name="slab_x",
-    )(own, halo, tables["slab_x"], valid, tables["tmpl_z"])
+    )(rows, tables["slab_x"], valid, tables["tmpl_z"])
 
 
 def corr_kernel(
-    dims, rot, entry, place_ref, tile_ref, held_ref, last_ref, mask_ref, spec_ref,
-    z_ref, ones_ref, y_ref, x_ref, bx_ref, by_ref, bz_ref,
-    mine_ref, side_ref, far_ref, stat_ref,
-    bank_buf, depth_buf, rows_buf, first_buf, second_buf, third_buf, back_buf, vol_buf,
+    dims, rot, entry, place_ref, tile_ref, *refs
 ):
+    if rot > 0:
+        before_ref, *refs = refs
+    held_ref, last_ref, mask_ref, spec_ref, z_ref, ones_ref, y_ref, x_ref, bx_ref, by_ref, bz_ref, *refs = refs
+    mines_ref, side_ref, far_ref, stat_ref, *refs = refs
+    bank_buf, depth_buf, rows_buf, first_buf, second_buf, third_buf, back_buf, vol_buf = refs
+    if rot > 0:
+        mines_ref[:rot] = before_ref[...]
     x_cells, y_cells, z_cells = dims
     n_x, n_y = x_cells + TEMPL, y_cells + HALF
     half_y = n_y // 2
@@ -362,7 +365,7 @@
             store(rows_buf, start, lane_block(plus, u))
             store(rows_buf, start + pad_y, lane_block(minus, u))
 
-    pipeline(TEMPL // GROUP, [gather_a, y_step], 2)
+    pipeline(TEMPL // GROUP, [gather_a, y_step], 6)
 
     def gather_ky(i, slot):
         firsts = [GROUP // 2 * i + u // 2 + u % 2 * pad_y for u in range(GROUP)]
@@ -381,7 +384,7 @@
             store(back_buf, start, lane_block(plus, u))
             store(back_buf, start + x_cells // 2, lane_block(minus, u))
 
-    pipeline(n_y // GROUP, [gather_ky, multiply, back_x], 2)
+    pipeline(n_y // GROUP, [gather_ky, multiply, back_x], 4)
 
     def gather_x(i, slot):
         value = pick(back_buf, [GROUP * i + u for u in range(GROUP)], n_y, odd(x_cells))
@@ -395,13 +398,13 @@
             store(vol_buf, x * odd(y_cells), lane_block(plus, u))
             store(vol_buf, x * odd(y_cells) + y_cells // 2, lane_block(minus, u))
 
-    pipeline(x_cells // GROUP, [gather_x, back_y], 2)
+    pipeline(x_cells // GROUP, [gather_x, back_y], 4)
 
     share = y_cells // 8
     me = place_ref[0]
     total = jnp.zeros((x_cells, LANES), F32)
     number = jnp.zeros((x_cells, LANES), F32)
-    targets = [mine_ref, side_ref, far_ref.at[0], far_ref.at[1]]
+    targets = [mines_ref.at[rot], side_ref, far_ref.at[0], far_ref.at[1]]
     for p, target in enumerate(targets):
         first = (me ^ p) * share
         values = []
@@ -434,45 +437,45 @@
     stat_ref[...] = jnp.where(row == 0, number_sum, jnp.where(row == 1, total_sum, jnp.sum(square)))
 
 
-def correlate(place, tile, held, rot, last, entry, mask, spec, tmpl_z, dims, tables):
+def correlate(mines, place, tile, held, rot, last, entry, mask, spec, tmpl_z, dims, tables):
     x_cells, y_cells, z_cells = dims
     n_x, n_y = x_cells + TEMPL, y_cells + HALF
     pad_y = n_y // 2 + -(n_y // 2) % 8
     width = y_cells * z_cells // 4
+    before = [] if mines is None else [mines]
     vmem = pl.BlockSpec(memory_space=pltpu.VMEM)
     return pl.pallas_call(
         functools.partial(corr_kernel, dims, rot, entry),
         out_shape=(
-            jax.ShapeDtypeStruct((x_cells, width), F32),
+            jax.ShapeDtypeStruct((rot + 1, x_cells, width), F32),
             jax.ShapeDtypeStruct((x_cells, width), F32),
             jax.ShapeDtypeStruct((2, x_cells, width), F32),
             jax.ShapeDtypeStruct((8, LANES), F32),
         ),
-        in_specs=[pl.BlockSpec(memory_space=pltpu.SMEM)] * 2 + [vmem] * 11,
+        in_specs=[pl.BlockSpec(memory_space=pltpu.SMEM)] * 2 + [vmem] * (11 + len(before)),
         out_specs=(vmem,) * 4,
         scratch_shapes=[
             pltpu.VMEM((BLOCKS * odd(BLOCK_ROWS), LANES), F32),
             pltpu.VMEM((TEMPL * odd(TEMPL), LANES), F32),
             pltpu.VMEM((TEMPL * odd(2 * pad_y), LANES), F32),
-            pltpu.VMEM((2, 3 * TEMPL, GROUP * LANES), BF16),
-            pltpu.VMEM((2, 2 * n_x, GROUP * LANES), BF16),
-            pltpu.VMEM((2, 2 * n_y, GROUP * LANES), BF16),
+            pltpu.VMEM((6, 3 * TEMPL, GROUP * LANES), BF16),
+            pltpu.VMEM((4, 2 * n_x, GROUP * LANES), BF16),
+            pltpu.VMEM((4, 2 * n_y, GROUP * LANES), BF16),
             pltpu.VMEM((n_y * odd(x_cells), LANES), F32),
             pltpu.VMEM((x_cells * odd(y_cells), LANES), F32),
         ],
-        compiler_params=pltpu.CompilerParams(vmem_limit_bytes=14 * 1024 * 1024),
+        compiler_params=pltpu.CompilerParams(vmem_limit_bytes=20 * 1024 * 1024),
         cost_estimate=pl.CostEstimate(flops=15 * 10**9, bytes_accessed=10**7, transcendentals=0),
         name="correlate",
     )(
-        place, tile, held, last, mask, spec,
+        place, tile, *before, held, last, mask, spec,
         tmpl_z, tables["ones_z"], tables["tmpl_y"], tables["tmpl_x"],
         tables["back_x"], tables["back_y"], tables["back_z"],
     )
 
 
 def score_kernel(pieces, place_ref, coef_ref, mask_ref, *refs):
-    best_ref, evid_ref, mom_ref = refs[len(refs) - 3 :]
-
+    best_ref, evid_ref, mom_ref = refs[-3:]
     blocks = best_ref.shape[1] // LANES
 
     def step(i):
@@ -480,8 +483,7 @@
 
         def score(k):
             at, entry = pieces[k]
-            corr = refs[at][:, lanes] if entry is None else refs[at][entry, :, lanes]
-            return (corr - coef_ref[k, 0]) * coef_ref[k, 1]
+            return (refs[at][entry, :, lanes] - coef_ref[k, 0]) * coef_ref[k, 1]
 
         mask = mask_ref[place_ref[0] * blocks + i]
         high = functools.reduce(jnp.maximum, [score(k) for k in range(len(pieces))])
@@ -502,7 +504,7 @@
 
 
 def combine(place, coefs, mask, arrays, pieces):
-    shape = arrays[0].shape
+    shape = arrays[0].shape[1:]
     vmem = pl.BlockSpec(memory_space=pltpu.VMEM)
     out = jax.ShapeDtypeStruct(shape, F32)
     return pl.pallas_call(
@@ -584,7 +586,7 @@
     side_swap = [(i, i ^ 1) for i in range(groups)]
     other = lax.ppermute(mine, "rot", side_swap)
     if by_blocks:
-        held = jnp.concatenate([held, swap_blocks(held, "tile", 2)], axis=1)
+        second = swap_blocks(held, "tile", 2)
     else:
         held, last = general_gather(templates)
         tile = jnp.zeros_like(tile)
@@ -592,25 +594,25 @@
     orient = jnp.einsum("rq,kq->rk", one_hot, quats, precision=lax.Precision.HIGHEST)
     place = me_place = jnp.reshape(me, (1,)).astype(jnp.int32)
     tile = jnp.reshape(tile, (1,)).astype(jnp.int32)
-    own = slab_rows(place, [tomogram], x_cells, dims, tables, "slab_own")
-    halo = slab_rows(place, [mine, other], TEMPL, dims, tables, "slab_halo")
+    own = slab_rows(place, [tomogram], x_cells, 0, dims, tables, "slab_own")
+    rows = slab_rows(place, [own, mine, other], TEMPL, x_cells, dims, tables, "slab_halo")
     if by_blocks:
-        held, halo = lax.optimization_barrier((held, halo))
+        second = jnp.where(rows[0, 0] < 1e9, second, jnp.zeros_like(second))
+        held = jnp.concatenate([held, second], axis=1)
         lasts = [swap_blocks(held[:1], "tile", 1), swap_blocks(held[1:], "tile", 1)]
     else:
         lasts = [last[:1], last[1:]]
-    spec, mask, tmpl_z = slab_x(own, halo, valid, dims, tables)
+    spec, mask, tmpl_z = slab_x(rows, valid, dims, tables)
     far_swap = [(i, i ^ 2) for i in range(groups)]
-    mines, sides, fars, stats = [], [], [], []
+    mines, sides, fars, stats = None, [], [], []
     for r in range(rots):
         if r >= 2:
             place, fars[r - 2] = lax.optimization_barrier((place, fars[r - 2]))
-        mine, side, far, stat = correlate(
-            place, tile, held, r, lasts[min(r, 1)], max(r - 1, 0), mask, spec, tmpl_z, dims, tables
+        mines, side, far, stat = correlate(
+            mines, place, tile, held, r, lasts[min(r, 1)], max(r - 1, 0), mask, spec, tmpl_z, dims, tables
         )
         if r >= 1:
             stat, fars[r - 1] = lax.optimization_barrier((stat, fars[r - 1]))
-        mines.append(mine)
         sides.append(side)
         stats.append(stat[:3, 0])
         fars.append(lax.ppermute(far, "rot", far_swap))
@@ -634,9 +636,9 @@
     coefs = jnp.concatenate([average[:, None], inverse[:, None], orient], axis=1)
     coefs = exchange_all(coefs, "rot", 1, groups)
     last = lax.ppermute(last, "rot", side_swap)
-    arrays = mines + fars + [early, last]
-    at_far, at_early, at_last = rots, 2 * rots, 2 * rots + 1
-    pieces = [(r, None) for r in range(rots)]
+    arrays = [mines] + fars + [early, last]
+    at_far, at_early, at_last = 1, 1 + rots, 2 + rots
+    pieces = [(0, r) for r in range(rots)]
     pieces += [(at_early, r) for r in range(rots - 2)] + [(at_last, 0), (at_last, 1)]
     pieces += [(at_far + r, 0) for r in range(rots)]
     pieces += [(at_early, rots - 2 + r) for r in range(rots - 2)] + [(at_last, 2), (at_last, 3)]

time: 98.2 us -> 85.8 us (0.87)
  Pallas kernels: 44.2 us -> 36.7 us
  waiting for transfers between devices: 21 us -> 16 us
  local copies, waits for them, and re-layouts: 9.4 us -> 5.23 us
  starting transfers between devices: 19.6 us -> 23.4 us
    pallas_call x4, Pallas kernels: 31.1 us -> 24.3 us  [correlate(): pl.pallas_call(functools.partial(corr_kernel, dims, rot, entry), out_shap...]
    unnamed x44 -> x28, local copies, waits for them, and re-layouts: 6.68 us -> 1.99 us
    ppermute x3, waiting for transfers between devices: 8.5 us -> 4.97 us  [local(): partner = lax.ppermute(state, 'tile', [(i, i ^ step) for i in range(tiles)])]
    ppermute x3, starting transfers between devices: 0.13 us -> 3.19 us  [local(): partner = lax.ppermute(state, 'tile', [(i, i ^ step) for i in range(tiles)])]
    ppermute x4, waiting for transfers between devices: 8.58 us -> 5.88 us  [swap_blocks(): lax.ppermute(block, axis, [(i, i ^ step) for i in range(lax.axis_size(axi...]
    ppermute x4, waiting for transfers between devices: 0.94 us -> 2.1 us  [local(): fars.append(lax.ppermute(far, 'rot', far_swap))]
  transfers between devices with their start and end apart: 19 -> 19, of which waited for: 8 -> 9; matrix products, arithmetic and copies ran while one was open for 3% -> 4% of each run, Pallas kernels for 39% -> 39%
where the time goes in v11:
time: 85.8 us; the launch traced here: 85.5 us
  Pallas kernels  36.7 us (43%)
  starting transfers between devices  23.4 us (27%)
  waiting for transfers between devices  16 us (19%)
  local copies, waits for them, and re-layouts  5.23 us (6%)
  between operations  2.36 us (3%)
  other arithmetic  1.58 us (2%)
    pallas_call x4, Pallas kernels, correlate(): pl.pallas_call(functools.partial(corr_kernel, dims, rot, entry), out_shap...  24.3 us
    ppermute x4, starting transfers between devices, swap_blocks(): lax.ppermute(block, axis, [(i, i ^ step) for i in range(lax.axis_size(axi...  6.86 us
    ppermute x4, waiting for transfers between devices, swap_blocks(): lax.ppermute(block, axis, [(i, i ^ step) for i in range(lax.axis_size(axi...  5.88 us
    pallas_call x2, Pallas kernels, slab_rows(): pl.pallas_call(functools.partial(slab_rows_kernel, dims), out_shape=jax.S...  5.04 us
    ppermute x3, waiting for transfers between devices, local(): partner = lax.ppermute(state, 'tile', [(i, i ^ step) for i in range(tiles)])  4.97 us
    ppermute x1, starting transfers between devices, neighbours(): lax.ppermute(block, axis, forward)  4.85 us
    ppermute x4, starting transfers between devices, local(): fars.append(lax.ppermute(far, 'rot', far_swap))  4.51 us
    pallas_call x1, Pallas kernels, slab_x(): pl.pallas_call(functools.partial(slab_x_kernel, dims), out_shape=(jax.Sha...  3.84 us
  transfers between devices with their start and end apart: 19, of which 9 were waited for; matrix products, arithmetic and copies ran while one was open for 4% of the time, Pallas kernels for 39%

profile of v11, /device:TPU:0, one launch (start us, length us, event | category | flops | bytes accessed | tf_op | source)
XLA Modules:
  0.0 85.5 jit_solution(9702054375305714329)
XLA Ops:
  0.7 1.0 %reshape.75 = bf16[4,1,108,128]{3,2,0,1:T(8,128)(2,1)S(1)} reshape(bf16[4,13824]{1,0:T(4,128)(2,1)} %param.15) | data formatting | bytes 221184 | tf_op jit(solution)/shard_map/reshape | solution.py:577
  1.7 0.9 %constant_dynamic-slice_fusion = bf16[16,5120]{1,0:T(8,128)(2,1)S(1)} fusion(bf16[32,5120]{1,0:T(8,128)(2,1)} %refs_0_.1, s32[]{:T(128)S(6)} %select_n.30), kind=kLoop, calls=%fused_computation.24 | loop fusion | bytes 327684 | tf_op jit(solution)/shard_map/dynamic_slice | solution.py:584
  2.6 4.9 %collective-permute-start.1 = (bf16[16,5120]{1,0:T(8,128)(2,1)S(1)}, bf16[16,5120]{1,0:T(8,128)(2,1)S(1)}, u32[]{:S(2)}, u32[]{:S(2)}) collective-permute-start(bf16[16,5120]{1,0:T(8,128)(2,1)S(1)} %constant_dynamic-slice_fusion), channel_id=1, source_target_pairs={{0,4},{4,8},{8,12},{12,16},{16,20},{20,24},{24,28},{1,5},{5,9},{9,... | collective-permute-start | bytes 491528 | tf_op jit(solution)/shard_map/ppermute | solution.py:560
  7.5 1.3 %collective-permute-start.2 = (bf16[16,5120]{1,0:T(8,128)(2,1)S(1)}, bf16[16,5120]{1,0:T(8,128)(2,1)S(1)}, u32[]{:S(2)}, u32[]{:S(2)}) collective-permute-start(bf16[16,5120]{1,0:T(8,128)(2,1)S(1)} %constant_dynamic-slice_fusion), channel_id=1, source_target_pairs={{4,0},{8,4},{12,8},{16,12},{20,16},{24,20},{28,24},{5,1},{9,5},{13... | collective-permute-start | bytes 491528 | tf_op jit(solution)/shard_map/ppermute | solution.py:560
  8.8 4.7 %collective-permute-start = (bf16[4,1,112,128]{3,2,1,0:T(8,128)(2,1)S(1)}, bf16[4,1,112,128]{3,2,1,0:T(8,128)(2,1)S(1)}, u32[]{:S(2)}, u32[]{:S(2)}) collective-permute-start(bf16[4,1,112,128]{3,2,1,0:T(8,128)(2,1)S(1)} %pad.4), channel_id=1, source_target_pairs={{0,16},{4,20},{8,24},{12,28},{16,0},{20,4},{24,8},{28,12},{1,17},{... | collective-permute-start | bytes 344072 | tf_op jit(solution)/shard_map/ppermute | solution.py:521
  13.5 1.0 %copy-done.1 = bf16[32,5120]{1,0:T(8,128)(2,1)S(1)} copy-done((bf16[32,5120]{1,0:T(8,128)(2,1)S(1)}, bf16[32,5120]{1,0:T(8,128)(2,1)}, u32[]{:S(2)}) %copy-start.1) | copy-done | bytes 327704
  14.4 0.9 %copy-done.3 = bf16[240,512]{1,0:T(8,128)(2,1)S(1)} copy-done((bf16[240,512]{1,0:T(8,128)(2,1)S(1)}, bf16[240,512]{1,0:T(8,128)(2,1)}, u32[]{:S(2)}) %copy-start.3) | copy-done | bytes 245784
  15.4 2.3 %slab_own.1.refs_0_ = f32[3616,128]{1,0:T(8,128)S(1)} custom-call(s32[1]{0:T(128)} %bitcast.place_ref, bf16[32,5120]{1,0:T(8,128)(2,1)S(1)} %copy-done.1, bf16[240,512]{1,0:T(8,128)(2,1)S(1)} %copy-done.3), custom_call_target="tpu_custom_call" | custom-call | flops 3200000000 | bytes 1000000 | tf_op jit(solution)/shard_map/slab_own/pallas_call | solution.py:244
  18.1 3.8 %collective-permute-done = bf16[4,1,112,128]{3,2,1,0:T(8,128)(2,1)S(1)} collective-permute-done((bf16[4,1,112,128]{3,2,1,0:T(8,128)(2,1)S(1)}, bf16[4,1,112,128]{3,2,1,0:T(8,128)(2,1)S(1)}, u32[]{:S(2)}, u32[]{:S(2)}) %collective-permute-start) | collective-permute-done | bytes 114720 | tf_op jit(solution)/shard_map/ppermute | solution.py:521
  22.1 2.8 %slab_halo.1.rows_ref = f32[9040,128]{1,0:T(8,128)S(1)} custom-call(s32[1]{0:T(128)} %bitcast.place_ref, f32[3616,128]{1,0:T(8,128)S(1)} %slab_own.1.refs_0_, bf16[2,16,5120]{2,1,0:T(8,128)(2,1)S(1)} %pad_maximum_fusion.3.refs_1_, bf16[2,16,5120]{2,1,0:T(8,128)(2,1)S(1)} %collective-permute-done.3.refs_2_, bf16[240,512]{1,0:T(8,128)(2,1)S(1)} %copy-done.4), custom_call_target="tpu_custom_call" | custom-call | flops 4800000000 | bytes 1000000 | tf_op jit(solution)/shard_map/slab_halo/pallas_call | solution.py:244
  26.1 2.0 %collective-permute-done.4 = bf16[4,2,112,128]{3,2,1,0:T(8,128)(2,1)S(1)} collective-permute-done((bf16[4,2,112,128]{3,2,1,0:T(8,128)(2,1)S(1)}, bf16[4,2,112,128]{3,2,1,0:T(8,128)(2,1)S(1)}, u32[]{:S(2)}, u32[]{:S(2)}) %collective-permute-start.4) | collective-permute-done | bytes 229408 | tf_op jit(solution)/shard_map/ppermute | solution.py:521
  28.3 1.6 %collective-permute-start.5 = (bf16[1,4,112,128]{3,2,1,0:T(8,128)(2,1)S(1)}, bf16[1,4,112,128]{3,2,1,0:T(8,128)(2,1)S(1)}, u32[]{:S(2)}, u32[]{:S(2)}) collective-permute-start(bf16[1,4,112,128]{3,2,1,0:T(8,128)(2,1)S(1)} %slice.110), channel_id=1, source_target_pairs={{0,4},{4,0},{8,12},{12,8},{16,20},{20,16},{24,28},{28,24},{1,5},{5... | collective-permute-start | bytes 344072 | tf_op jit(solution)/shard_map/ppermute | solution.py:521
  30.4 3.8 %slab_x.1 = (f32[13,2,80,1024]{3,2,1,0:T(8,128)S(1)}, f32[40,32,128]{2,1,0:T(8,128)S(1)}, bf16[8,256,256]{2,1,0:T(8,128)(2,1)S(1)}) custom-call(f32[9040,128]{1,0:T(8,128)S(1)} %slab_halo.1.rows_ref, bf16[80,240]{1,0:T(8,128)(2,1)S(1)} %copy-done.9, s32[32,80]{1,0:T(8,128)S(1)} %copy-done.2, bf16[48,256]{1,0:T(8,128)(2,1)S(1)} %copy-done.11), custom_call_target="tpu_custom_call" | custom-call | flops 5000000000 | bytes 1000000 | tf_op jit(solution)/shard_map/slab_x/pallas_call | solution.py:297
  34.3 6.0 %correlate.4 = (f32[1,32,1280]{2,1,0:T(8,128)S(1)}, f32[32,1280]{1,0:T(8,128)S(1)}, f32[2,32,1280]{2,1,0:T(8,128)S(1)}, f32[8,128]{1,0:T(8,128)S(1)}) custom-call(s32[1]{0:T(128)} %bitcast.place_ref, s32[1]{0:T(128)} %bitcast.1.tile_ref, bf16[4,4,112,128]{3,2,1,0:T(8,128)(2,1)S(1)} %pad_maximum_fusion.2.refs_0_.refs_1_, ...), custom_call_target="tpu_custom_call" | custom-call | flops 15000000512 | bytes 10000000 | tf_op jit(solution)/shard_map/correlate/pallas_call | solution.py:447
  40.3 1.6 %collective-permute-start.7 = (f32[2,32,1280]{2,1,0:T(8,128)S(1)}, f32[2,32,1280]{2,1,0:T(8,128)S(1)}, u32[]{:S(2)}, u32[]{:S(2)}) collective-permute-start(f32[2,32,1280]{2,1,0:T(8,128)S(1)} %get-tuple-element.47), channel_id=1, source_target_pairs={{0,2},{1,3},{2,0},{3,1},{4,6},{5,7},{6,4},{7,5},{8,10},{9,11},{10,... | collective-permute-start | bytes 983048 | tf_op jit(solution)/shard_map/ppermute | solution.py:618
  41.9 6.0 %correlate.5 = (f32[2,32,1280]{2,1,0:T(8,128)S(1)}, f32[32,1280]{1,0:T(8,128)S(1)}, f32[2,32,1280]{2,1,0:T(8,128)S(1)}, f32[8,128]{1,0:T(8,128)S(1)}) custom-call(s32[1]{0:T(128)} %bitcast.place_ref, s32[1]{0:T(128)} %bitcast.1.tile_ref, f32[1,32,1280]{2,1,0:T(8,128)S(1)} %get-tuple-element.45.refs_0_, ...), custom_call_target="tpu_custom_call" | custom-call | flops 15000000512 | bytes 10000000 | tf_op jit(solution)/shard_map/correlate/pallas_call | solution.py:447
  47.9 0.6 collective-permute-start.8
  48.5 0.7 collective-permute-done.7.refs_1_
  49.2 6.2 %correlate.6 = (f32[3,32,1280]{2,1,0:T(8,128)S(1)}, f32[32,1280]{1,0:T(8,128)S(1)}, f32[2,32,1280]{2,1,0:T(8,128)S(1)}, f32[8,128]{1,0:T(8,128)S(1)}) custom-call(s32[1]{0:T(128)} %bitcast.place_ref, s32[1]{0:T(128)} %bitcast.1.tile_ref, f32[2,32,1280]{2,1,0:T(8,128)S(1)} %get-tuple-element.51.refs_0_, ...), custom_call_target="tpu_custom_call" | custom-call | flops 15000000512 | bytes 10000000 | tf_op jit(solution)/shard_map/correlate/pallas_call | solution.py:447
  55.4 2.2 %collective-permute-start.9 = (f32[2,32,1280]{2,1,0:T(8,128)S(1)}, f32[2,32,1280]{2,1,0:T(8,128)S(1)}, u32[]{:S(2)}, u32[]{:S(2)}) collective-permute-start(f32[2,32,1280]{2,1,0:T(8,128)S(1)} %get-tuple-element.59), channel_id=1, source_target_pairs={{0,2},{1,3},{2,0},{3,1},{4,6},{5,7},{6,4},{7,5},{8,10},{9,11},{10,... | collective-permute-start | bytes 983048 | tf_op jit(solution)/shard_map/ppermute | solution.py:618
  57.8 6.0 %correlate.7 = (f32[4,32,1280]{2,1,0:T(8,128)S(1)}, f32[32,1280]{1,0:T(8,128)S(1)}, f32[2,32,1280]{2,1,0:T(8,128)S(1)}, f32[8,128]{1,0:T(8,128)S(1)}) custom-call(s32[1]{0:T(128)} %bitcast.place_ref, s32[1]{0:T(128)} %bitcast.1.tile_ref, f32[3,32,1280]{2,1,0:T(8,128)S(1)} %get-tuple-element.57.refs_0_, ...), custom_call_target="tpu_custom_call" | custom-call | flops 15000000512 | bytes 10000000 | tf_op jit(solution)/shard_map/correlate/pallas_call | solution.py:447
  64.1 1.6 %collective-permute-start.11 = (f32[3,4]{1,0:T(4,128)S(1)}, f32[3,4]{1,0:T(4,128)S(1)}, u32[]{:S(2)}, u32[]{:S(2)}) collective-permute-start(f32[3,4]{1,0:T(4,128)S(1)} %pad_maximum_fusion.6), channel_id=1, source_target_pairs={{0,4},{4,0},{8,12},{12,8},{16,20},{20,16},{24,28},{28,24},{1,5},{5... | collective-permute-start | bytes 152 | tf_op jit(solution)/shard_map/ppermute | solution.py:626
  65.7 1.9 %collective-permute-done.11 = f32[3,4]{1,0:T(4,128)S(1)} collective-permute-done((f32[3,4]{1,0:T(4,128)S(1)}, f32[3,4]{1,0:T(4,128)S(1)}, u32[]{:S(2)}, u32[]{:S(2)}) %collective-permute-start.11) | collective-permute-done | bytes 80 | tf_op jit(solution)/shard_map/ppermute | solution.py:626
  67.8 1.5 %collective-permute-start.12 = (f32[3,4]{1,0:T(4,128)S(1)}, f32[3,4]{1,0:T(4,128)S(1)}, u32[]{:S(2)}, u32[]{:S(2)}) collective-permute-start(f32[3,4]{1,0:T(4,128)S(1)} %select_add_fusion.2), channel_id=1, source_target_pairs={{0,8},{4,12},{8,0},{12,4},{16,24},{20,28},{24,16},{28,20},{1,9},{5... | collective-permute-start | bytes 152 | tf_op jit(solution)/shard_map/ppermute | solution.py:626
  69.3 2.1 %collective-permute-done.12 = f32[3,4]{1,0:T(4,128)S(1)} collective-permute-done((f32[3,4]{1,0:T(4,128)S(1)}, f32[3,4]{1,0:T(4,128)S(1)}, u32[]{:S(2)}, u32[]{:S(2)}) %collective-permute-start.12) | collective-permute-done | bytes 80 | tf_op jit(solution)/shard_map/ppermute | solution.py:626
  72.7 1.4 %collective-permute-done.14.refs_4_ = f32[2,32,1280]{2,1,0:T(8,128)S(1)} collective-permute-done((f32[2,32,1280]{2,1,0:T(8,128)S(1)}, f32[2,32,1280]{2,1,0:T(8,128)S(1)}, u32[]{:S(2)}, u32[]{:S(2)}) %collective-permute-start.14) | collective-permute-done | bytes 327712 | tf_op jit(solution)/shard_map/ppermute | solution.py:618
  74.1 0.9 %pad_maximum_fusion.1 = f32[4,32,1280]{2,1,0:T(8,128)} fusion(f32[1,32,1280]{2,1,0:T(8,128)S(1)} %slice_select_fusion, f32[1,32,1280]{2,1,0:T(8,128)S(1)} %slice.99, f32[1,32,1280]{2,1,0:T(8,128)S(1)} %bitcast.29, f32[1,32,1280]{2,1,0:T(8,128)S(1)} %bitcast.28), kind=kLoop, calls=%fused_computation.1 | loop fusion | flops 491520 | bytes 1310720 | tf_op jit(solution)/shard_map/stack | solution.py:629
  75.0 0.9 %collective-permute-done.13 = f32[3,4]{1,0:T(4,128)S(1)} collective-permute-done((f32[3,4]{1,0:T(4,128)S(1)}, f32[3,4]{1,0:T(4,128)S(1)}, u32[]{:S(2)}, u32[]{:S(2)}) %collective-permute-start.13) | collective-permute-done | bytes 80 | tf_op jit(solution)/shard_map/ppermute | solution.py:626
  76.8 2.0 %collective-permute-start.16 = (f32[4,6]{1,0:T(4,128)S(1)}, f32[4,6]{1,0:T(4,128)S(1)}, u32[]{:S(2)}, u32[]{:S(2)}) collective-permute-start(f32[4,6]{1,0:T(4,128)S(1)} %pad_maximum_fusion.7), channel_id=1, source_target_pairs={{0,2},{1,3},{2,0},{3,1},{4,6},{5,7},{6,4},{7,5},{8,10},{9,11},{10,... | collective-permute-start | bytes 296 | tf_op jit(solution)/shard_map/ppermute | solution.py:552
  78.9 1.5 %collective-permute-done.16 = f32[4,6]{1,0:T(4,128)S(1)} collective-permute-done((f32[4,6]{1,0:T(4,128)S(1)}, f32[4,6]{1,0:T(4,128)S(1)}, u32[]{:S(2)}, u32[]{:S(2)}) %collective-permute-start.16) | collective-permute-done | bytes 128 | tf_op jit(solution)/shard_map/ppermute | solution.py:552
  80.4 1.5 %collective-permute-done.17 = f32[4,6]{1,0:T(4,128)S(1)} collective-permute-done((f32[4,6]{1,0:T(4,128)S(1)}, f32[4,6]{1,0:T(4,128)S(1)}, u32[]{:S(2)}, u32[]{:S(2)}) %collective-permute-start.17) | collective-permute-done | bytes 128 | tf_op jit(solution)/shard_map/ppermute | solution.py:552
  81.9 3.6 %combine.1 = (f32[32,1280]{1,0:T(8,128)}, f32[32,1280]{1,0:T(8,128)}, f32[4,32,1280]{2,1,0:T(8,128)}) custom-call(s32[1]{0:T(128)} %bitcast.place_ref, f32[16,6]{1,0:T(8,128)S(1)} %bitcast.32, f32[40,32,128]{2,1,0:T(8,128)S(1)} %get-tuple-element.41.refs_2_.refs_3_.mask_ref, f32[4,32,1280]{2,1,0:T(8,128)S(1)} %get-tuple-element.71.refs_0_, ...), custom_call_target="tpu_custom_call" | custom-call | tf_op jit(solution)/shard_map/combine/pallas_call | solution.py:510
  (78 shorter events, 3.8 us)
Async XLA Ops:
  0.6 17.2 %copy-start = (f32[4,4096]{1,0:T(4,128)S(1)}, f32[4,4096]{1,0:T(4,128)}, u32[]{:S(2)}) copy-start(f32[4,4096]{1,0:T(4,128)} %param.17) | copy-start | bytes 196612
  2.6 15.0 %collective-permute-start.1 = (bf16[16,5120]{1,0:T(8,128)(2,1)S(1)}, bf16[16,5120]{1,0:T(8,128)(2,1)S(1)}, u32[]{:S(2)}, u32[]{:S(2)}) collective-permute-start(bf16[16,5120]{1,0:T(8,128)(2,1)S(1)} %constant_dynamic-slice_fusion), channel_id=1, source_target_pairs={{0,4},{4,8},{8,12},{12,16},{16,20},{20,24},{24,28},{1,5},{5,9},{9,... | collective-permute-start | bytes 491528 | tf_op jit(solution)/shard_map/ppermute | solution.py:560
  7.5 10.2 %collective-permute-start.2 = (bf16[16,5120]{1,0:T(8,128)(2,1)S(1)}, bf16[16,5120]{1,0:T(8,128)(2,1)S(1)}, u32[]{:S(2)}, u32[]{:S(2)}) collective-permute-start(bf16[16,5120]{1,0:T(8,128)(2,1)S(1)} %constant_dynamic-slice_fusion), channel_id=1, source_target_pairs={{4,0},{8,4},{12,8},{16,12},{20,16},{24,20},{28,24},{5,1},{9,5},{13... | collective-permute-start | bytes 491528 | tf_op jit(solution)/shard_map/ppermute | solution.py:560
  8.8 13.2 %collective-permute-start = (bf16[4,1,112,128]{3,2,1,0:T(8,128)(2,1)S(1)}, bf16[4,1,112,128]{3,2,1,0:T(8,128)(2,1)S(1)}, u32[]{:S(2)}, u32[]{:S(2)}) collective-permute-start(bf16[4,1,112,128]{3,2,1,0:T(8,128)(2,1)S(1)} %pad.4), channel_id=1, source_target_pairs={{0,16},{4,20},{8,24},{12,28},{16,0},{20,4},{24,8},{28,12},{1,17},{... | collective-permute-start | bytes 344072 | tf_op jit(solution)/shard_map/ppermute | solution.py:521
  13.5 1.0 %copy-start.1 = (bf16[32,5120]{1,0:T(8,128)(2,1)S(1)}, bf16[32,5120]{1,0:T(8,128)(2,1)}, u32[]{:S(2)}) copy-start(bf16[32,5120]{1,0:T(8,128)(2,1)} %refs_0_.1) | copy-start | bytes 983044
  15.4 2.4 %copy-start.13 = (s32[4]{0:T(128)S(1)}, s32[4]{0:T(128)}, u32[]{:S(2)}) copy-start(s32[4]{0:T(128)} %param.18) | copy-start | bytes 52
  15.4 6.7 %copy-start.4 = (bf16[240,512]{1,0:T(8,128)(2,1)S(1)}, bf16[240,512]{1,0:T(8,128)(2,1)}, u32[]{:S(2)}) copy-start(bf16[240,512]{1,0:T(8,128)(2,1)} %constant.52.clone.refs_1_.refs_3_) | copy-start | bytes 737284
  17.7 4.4 %collective-permute-start.3 = (bf16[2,16,5120]{2,1,0:T(8,128)(2,1)S(1)}, bf16[2,16,5120]{2,1,0:T(8,128)(2,1)S(1)}, u32[]{:S(2)}, u32[]{:S(2)}) collective-permute-start(bf16[2,16,5120]{2,1,0:T(8,128)(2,1)S(1)} %pad_maximum_fusion.3.refs_1_), channel_id=1, source_target_pairs={{0,1},{1,0},{2,3},{3,2},{4,5},{5,4},{6,7},{7,6},{8,9},{9,8},{10,11... | collective-permute-start | bytes 983048 | tf_op jit(solution)/shard_map/ppermute | solution.py:587
  22.0 8.4 %copy-start.2 = (s32[32,80]{1,0:T(8,128)S(1)}, s32[32,80]{1,0:T(8,128)}, u32[]{:S(2)}) copy-start(s32[32,80]{1,0:T(8,128)} %valid_ref.1) | copy-start | bytes 30724
  22.0 8.4 %copy-start.9 = (bf16[80,240]{1,0:T(8,128)(2,1)S(1)}, bf16[80,240]{1,0:T(8,128)(2,1)}, u32[]{:S(2)}) copy-start(bf16[80,240]{1,0:T(8,128)(2,1)} %constant.53.clone.x_ref) | copy-start | bytes 115204
  22.0 8.4 %copy-start.11 = (bf16[48,256]{1,0:T(8,128)(2,1)S(1)}, bf16[48,256]{1,0:T(8,128)(2,1)}, u32[]{:S(2)}) copy-start(bf16[48,256]{1,0:T(8,128)(2,1)} %constant.54.clone.tz_ref) | copy-start | bytes 73732
  22.0 6.1 %collective-permute-start.4 = (bf16[4,2,112,128]{3,2,1,0:T(8,128)(2,1)S(1)}, bf16[4,2,112,128]{3,2,1,0:T(8,128)(2,1)S(1)}, u32[]{:S(2)}, u32[]{:S(2)}) collective-permute-start(bf16[4,2,112,128]{3,2,1,0:T(8,128)(2,1)S(1)} %pad_maximum_fusion.4), channel_id=1, source_target_pairs={{0,8},{4,12},{8,0},{12,4},{16,24},{20,28},{24,16},{28,20},{1,9},{5... | collective-permute-start | bytes 688136 | tf_op jit(solution)/shard_map/ppermute | solution.py:521
  28.2 6.0 %copy-start.5 = (bf16[256,256]{1,0:T(8,128)(2,1)S(1)}, bf16[256,256]{1,0:T(8,128)(2,1)}, u32[]{:S(2)}) copy-start(bf16[256,256]{1,0:T(8,128)(2,1)} %constant.60.clone.refs_10_.refs_11_) | copy-start | bytes 393220
  28.2 6.0 %copy-start.6 = (bf16[160,208]{1,0:T(8,128)(2,1)S(1)}, bf16[160,208]{1,0:T(8,128)(2,1)}, u32[]{:S(2)}) copy-start(bf16[160,208]{1,0:T(8,128)(2,1)} %constant.59.clone.refs_9_.refs_10_) | copy-start | bytes 199684
  28.2 6.0 %copy-start.7 = (bf16[112,144]{1,0:T(8,128)(2,1)S(1)}, bf16[112,144]{1,0:T(8,128)(2,1)}, u32[]{:S(2)}) copy-start(bf16[112,144]{1,0:T(8,128)(2,1)} %constant.56.clone.refs_6_.refs_7_) | copy-start | bytes 96772
  28.3 6.0 %copy-start.8 = (bf16[80,144]{1,0:T(8,128)(2,1)S(1)}, bf16[80,144]{1,0:T(8,128)(2,1)}, u32[]{:S(2)}) copy-start(bf16[80,144]{1,0:T(8,128)(2,1)} %constant.57.clone.refs_7_.refs_8_) | copy-start | bytes 69124
  28.3 6.0 %copy-start.10 = (bf16[64,160]{1,0:T(8,128)(2,1)S(1)}, bf16[64,160]{1,0:T(8,128)(2,1)}, u32[]{:S(2)}) copy-start(bf16[64,160]{1,0:T(8,128)(2,1)} %constant.58.clone.refs_8_.refs_9_) | copy-start | bytes 61444
  28.3 6.0 %copy-start.12 = (f32[8,128]{1,0:T(8,128)S(1)}, f32[8,128]{1,0:T(8,128)}, u32[]{:S(2)}) copy-start(f32[8,128]{1,0:T(8,128)} %constant.55.clone.refs_5_.refs_6_) | copy-start | bytes 12292
  28.3 6.0 %collective-permute-start.5 = (bf16[1,4,112,128]{3,2,1,0:T(8,128)(2,1)S(1)}, bf16[1,4,112,128]{3,2,1,0:T(8,128)(2,1)S(1)}, u32[]{:S(2)}, u32[]{:S(2)}) collective-permute-start(bf16[1,4,112,128]{3,2,1,0:T(8,128)(2,1)S(1)} %slice.110), channel_id=1, source_target_pairs={{0,4},{4,0},{8,12},{12,8},{16,20},{20,16},{24,28},{28,24},{1,5},{5... | collective-permute-start | bytes 344072 | tf_op jit(solution)/shard_map/ppermute | solution.py:521
  29.9 12.1 %collective-permute-start.6 = (bf16[3,4,112,128]{3,2,1,0:T(8,128)(2,1)S(1)}, bf16[3,4,112,128]{3,2,1,0:T(8,128)(2,1)S(1)}, u32[]{:S(2)}, u32[]{:S(2)}) collective-permute-start(bf16[3,4,112,128]{3,2,1,0:T(8,128)(2,1)S(1)} %slice.111), channel_id=1, source_target_pairs={{0,4},{4,0},{8,12},{12,8},{16,20},{20,16},{24,28},{28,24},{1,5},{5... | collective-permute-start | bytes 1032200 | tf_op jit(solution)/shard_map/ppermute | solution.py:521
  40.3 8.9 %collective-permute-start.7 = (f32[2,32,1280]{2,1,0:T(8,128)S(1)}, f32[2,32,1280]{2,1,0:T(8,128)S(1)}, u32[]{:S(2)}, u32[]{:S(2)}) collective-permute-start(f32[2,32,1280]{2,1,0:T(8,128)S(1)} %get-tuple-element.47), channel_id=1, source_target_pairs={{0,2},{1,3},{2,0},{3,1},{4,6},{5,7},{6,4},{7,5},{8,10},{9,11},{10,... | collective-permute-start | bytes 983048 | tf_op jit(solution)/shard_map/ppermute | solution.py:618
  47.9 9.8 %collective-permute-start.8 = (f32[2,32,1280]{2,1,0:T(8,128)S(1)}, f32[2,32,1280]{2,1,0:T(8,128)S(1)}, u32[]{:S(2)}, u32[]{:S(2)}) collective-permute-start(f32[2,32,1280]{2,1,0:T(8,128)S(1)} %get-tuple-element.53), channel_id=1, source_target_pairs={{0,2},{1,3},{2,0},{3,1},{4,6},{5,7},{6,4},{7,5},{8,10},{9,11},{10,... | collective-permute-start | bytes 983048 | tf_op jit(solution)/shard_map/ppermute | solution.py:618
  55.4 8.6 %collective-permute-start.9 = (f32[2,32,1280]{2,1,0:T(8,128)S(1)}, f32[2,32,1280]{2,1,0:T(8,128)S(1)}, u32[]{:S(2)}, u32[]{:S(2)}) collective-permute-start(f32[2,32,1280]{2,1,0:T(8,128)S(1)} %get-tuple-element.59), channel_id=1, source_target_pairs={{0,2},{1,3},{2,0},{3,1},{4,6},{5,7},{6,4},{7,5},{8,10},{9,11},{10,... | collective-permute-start | bytes 983048 | tf_op jit(solution)/shard_map/ppermute | solution.py:618
  57.8 6.3 %collective-permute-start.10 = (f32[4,32,1280]{2,1,0:T(8,128)S(1)}, f32[4,32,1280]{2,1,0:T(8,128)S(1)}, u32[]{:S(2)}, u32[]{:S(2)}) collective-permute-start(f32[4,32,1280]{2,1,0:T(8,128)S(1)} %pad_maximum_fusion), channel_id=1, source_target_pairs={{0,1},{1,0},{2,3},{3,2},{4,5},{5,4},{6,7},{7,6},{8,9},{9,8},{10,11... | collective-permute-start | bytes 1966088 | tf_op jit(solution)/shard_map/ppermute | solution.py:621
  63.9 10.2 %collective-permute-start.14 = (f32[2,32,1280]{2,1,0:T(8,128)S(1)}, f32[2,32,1280]{2,1,0:T(8,128)S(1)}, u32[]{:S(2)}, u32[]{:S(2)}) collective-permute-start(f32[2,32,1280]{2,1,0:T(8,128)S(1)} %get-tuple-element.69), channel_id=1, source_target_pairs={{0,2},{1,3},{2,0},{3,1},{4,6},{5,7},{6,4},{7,5},{8,10},{9,11},{10,... | collective-permute-start | bytes 983048 | tf_op jit(solution)/shard_map/ppermute | solution.py:618
  64.1 3.6 %collective-permute-start.11 = (f32[3,4]{1,0:T(4,128)S(1)}, f32[3,4]{1,0:T(4,128)S(1)}, u32[]{:S(2)}, u32[]{:S(2)}) collective-permute-start(f32[3,4]{1,0:T(4,128)S(1)} %pad_maximum_fusion.6), channel_id=1, source_target_pairs={{0,4},{4,0},{8,12},{12,8},{16,20},{20,16},{24,28},{28,24},{1,5},{5... | collective-permute-start | bytes 152 | tf_op jit(solution)/shard_map/ppermute | solution.py:626
  67.8 3.6 %collective-permute-start.12 = (f32[3,4]{1,0:T(4,128)S(1)}, f32[3,4]{1,0:T(4,128)S(1)}, u32[]{:S(2)}, u32[]{:S(2)}) collective-permute-start(f32[3,4]{1,0:T(4,128)S(1)} %select_add_fusion.2), channel_id=1, source_target_pairs={{0,8},{4,12},{8,0},{12,4},{16,24},{20,28},{24,16},{28,20},{1,9},{5... | collective-permute-start | bytes 152 | tf_op jit(solution)/shard_map/ppermute | solution.py:626
  71.4 4.5 %collective-permute-start.13 = (f32[3,4]{1,0:T(4,128)S(1)}, f32[3,4]{1,0:T(4,128)S(1)}, u32[]{:S(2)}, u32[]{:S(2)}) collective-permute-start(f32[3,4]{1,0:T(4,128)S(1)} %select_add_fusion.1), channel_id=1, source_target_pairs={{0,16},{4,20},{8,24},{12,28},{16,0},{20,4},{24,8},{28,12},{1,17},{... | collective-permute-start | bytes 152 | tf_op jit(solution)/shard_map/ppermute | solution.py:626
  75.9 6.0 %collective-permute-start.18 = (f32[4,32,1280]{2,1,0:T(8,128)}, f32[4,32,1280]{2,1,0:T(8,128)}, u32[]{:S(2)}, u32[]{:S(2)}) collective-permute-start(f32[4,32,1280]{2,1,0:T(8,128)} %pad_maximum_fusion.1), channel_id=1, source_target_pairs={{0,1},{1,0},{2,3},{3,2},{4,5},{5,4},{6,7},{7,6},{8,9},{9,8},{10,11... | collective-permute-start | bytes 1966088 | tf_op jit(solution)/shard_map/ppermute | solution.py:638
  76.3 2.6 %collective-permute-start.15 = (f32[4,6]{1,0:T(4,128)S(1)}, f32[4,6]{1,0:T(4,128)S(1)}, u32[]{:S(2)}, u32[]{:S(2)}) collective-permute-start(f32[4,6]{1,0:T(4,128)S(1)} %pad_maximum_fusion.7), channel_id=1, source_target_pairs={{0,1},{1,0},{2,3},{3,2},{4,5},{5,4},{6,7},{7,6},{8,9},{9,8},{10,11... | collective-permute-start | bytes 296 | tf_op jit(solution)/shard_map/ppermute | solution.py:552
  76.8 3.6 %collective-permute-start.16 = (f32[4,6]{1,0:T(4,128)S(1)}, f32[4,6]{1,0:T(4,128)S(1)}, u32[]{:S(2)}, u32[]{:S(2)}) collective-permute-start(f32[4,6]{1,0:T(4,128)S(1)} %pad_maximum_fusion.7), channel_id=1, source_target_pairs={{0,2},{1,3},{2,0},{3,1},{4,6},{5,7},{6,4},{7,5},{8,10},{9,11},{10,... | collective-permute-start | bytes 296 | tf_op jit(solution)/shard_map/ppermute | solution.py:552
  78.9 3.0 %collective-permute-start.17 = (f32[4,6]{1,0:T(4,128)S(1)}, f32[4,6]{1,0:T(4,128)S(1)}, u32[]{:S(2)}, u32[]{:S(2)}) collective-permute-start(f32[4,6]{1,0:T(4,128)S(1)} %pad_maximum_fusion.7), channel_id=1, source_target_pairs={{0,3},{1,2},{2,1},{3,0},{4,7},{5,6},{6,5},{7,4},{8,11},{9,10},{10,... | collective-permute-start | bytes 296 | tf_op jit(solution)/shard_map/ppermute | solution.py:552
  (1 other events, 0.9 us)

commit v12 on v11

--- a/solution.py
+++ b/solution.py
@@ -500,7 +500,11 @@
         for c in range(4):
             mom_ref[c, :, lanes] = moment[c] * share
 
-    loop(blocks, step)
+    def two_steps(i):
+        step(2 * i)
+        step(2 * i + 1)
+
+    loop(blocks // 2, two_steps)
 
 
 def combine(place, coefs, mask, arrays, pieces):
@@ -515,6 +519,25 @@
         compiler_params=pltpu.CompilerParams(vmem_limit_bytes=4 * 1024 * 1024),
         name="combine",
     )(place, coefs, mask, *arrays)
+
+
+def pack_kernel(after_ref, *refs):
+    *sources, out_ref = refs
+    for i, source in enumerate(sources):
+        out_ref[i] = source[...] if len(source.shape) == 2 else source[1]
+
+
+def pack(after, sides, fars):
+    vmem = pl.BlockSpec(memory_space=pltpu.VMEM)
+    count = len(sides) + len(fars)
+    return pl.pallas_call(
+        pack_kernel,
+        out_shape=jax.ShapeDtypeStruct((count,) + sides[0].shape, F32),
+        in_specs=[pl.BlockSpec(memory_space=pl.ANY)] + [vmem] * count,
+        out_specs=vmem,
+        compiler_params=pltpu.CompilerParams(vmem_limit_bytes=8 * 1024 * 1024),
+        name="pack",
+    )(after, *sides, *fars)
 
 
 def swap_blocks(block, axis, step):
@@ -574,14 +597,12 @@
     tile = lax.axis_index("tile")
     by_blocks = tiles == BLOCKS
     if by_blocks:
-        held = templates.reshape(rots, 1, EACH * CHUNKS, LANES)
+        first = swap_blocks(templates, "tile", 4)
+        held = [part.reshape(rots, 1, EACH * CHUNKS, LANES) for part in (templates, first)]
+        held = jnp.concatenate(held, axis=1)
         held = jnp.pad(held, ((0, 0), (0, 0), (0, BLOCK_ROWS - EACH * CHUNKS), (0, 0)))
-        held, tomogram_after = lax.optimization_barrier((held, tomogram))
-        held = jnp.concatenate([held, swap_blocks(held, "tile", 4)], axis=1)
-    else:
-        tomogram_after = tomogram
     half = x_cells // 2
-    piece = lax.dynamic_slice_in_dim(tomogram_after, (me & 1) * half, half, 0)
+    piece = lax.dynamic_slice_in_dim(tomogram, (me & 1) * half, half, 0)
     mine = jnp.stack(neighbours(piece, "tile"))
     side_swap = [(i, i ^ 1) for i in range(groups)]
     other = lax.ppermute(mine, "rot", side_swap)
@@ -616,17 +637,13 @@
         sides.append(side)
         stats.append(stat[:3, 0])
         fars.append(lax.ppermute(far, "rot", far_swap))
-        if r == rots - 2:
-            early = jnp.stack(sides[:-1] + [f[1] for f in fars[:-1]])
-            early = lax.ppermute(early, "rot", side_swap)
     state = jnp.stack(stats, axis=1)
-    state, early, fars[rots - 2] = lax.optimization_barrier((state, early, fars[rots - 2]))
+    state, fars[rots - 2] = lax.optimization_barrier((state, fars[rots - 2]))
     step = 1
     while step < tiles:
         partner = lax.ppermute(state, "tile", [(i, i ^ step) for i in range(tiles)])
         if step * 4 == tiles:
-            late = jnp.where(partner[0, 0] >= 0.0, fars[rots - 1][1], 0.0)
-            last = jnp.stack([sides[rots - 2], sides[rots - 1], fars[rots - 2][1], late])
+            last = pack(partner, sides, fars)
         if step * 2 == tiles:
             partner, last = lax.optimization_barrier((partner, last))
         state = merge(state, partner)
@@ -636,12 +653,11 @@
     coefs = jnp.concatenate([average[:, None], inverse[:, None], orient], axis=1)
     coefs = exchange_all(coefs, "rot", 1, groups)
     last = lax.ppermute(last, "rot", side_swap)
-    arrays = [mines] + fars + [early, last]
-    at_far, at_early, at_last = 1, 1 + rots, 2 + rots
+    arrays = [mines] + fars + [last]
     pieces = [(0, r) for r in range(rots)]
-    pieces += [(at_early, r) for r in range(rots - 2)] + [(at_last, 0), (at_last, 1)]
-    pieces += [(at_far + r, 0) for r in range(rots)]
-    pieces += [(at_early, rots - 2 + r) for r in range(rots - 2)] + [(at_last, 2), (at_last, 3)]
+    pieces += [(1 + rots, r) for r in range(rots)]
+    pieces += [(1 + r, 0) for r in range(rots)]
+    pieces += [(1 + rots, rots + r) for r in range(rots)]
     return combine(me_place, coefs.reshape(groups * rots, 6), mask, arrays, pieces)
 
 

time: 85.8 us -> 89.3 us (1.041)
  starting transfers between devices: 23.4 us -> 29.9 us
  waiting for transfers between devices: 16 us -> 13.3 us
  Pallas kernels: 36.7 us -> 38.2 us
    ppermute x3, starting transfers between devices: 3.19 us -> 7.78 us  [local(): partner = lax.ppermute(state, 'tile', [(i, i ^ step) for i in range(tiles)])]
    ppermute x4, waiting for transfers between devices: 5.88 us -> 2.31 us  [swap_blocks(): lax.ppermute(block, axis, [(i, i ^ step) for i in range(lax.axis_size(axi...]
    ppermute x1, waiting for transfers between devices: 0.01 us -> 2.74 us  [neighbours(): lax.ppermute(block, axis, forward)]
    ppermute x4, starting transfers between devices: 6.86 us -> 8.66 us  [swap_blocks(): lax.ppermute(block, axis, [(i, i ^ step) for i in range(lax.axis_size(axi...]
    ppermute x4, waiting for transfers between devices: 2.1 us -> 0.93 us  [local(): fars.append(lax.ppermute(far, 'rot', far_swap))]
    pallas_call x0 -> x1, Pallas kernels: none -> 1.16 us  [pack(): pl.pallas_call(pack_kernel, out_shape=jax.ShapeDtypeStruct((count,) + sid...]
    unnamed x28 -> x34, local copies, waits for them, and re-layouts: 1.99 us -> 3.08 us
    another operation x2 -> x0, other arithmetic: 0.94 us -> none  [the longest x1 0.89 us: local(): jnp.stack([sides[rots - 2], sides[rots - 1], fars[rots - 2][1], late])]
  transfers between devices with their start and end apart: 19 -> 18, of which waited for: 9 -> 8; matrix products, arithmetic and copies ran while one was open for 4% -> 2% of each run, Pallas kernels for 39% -> 39%
where the time goes in v12:
time: 89.3 us; the launch traced here: 89 us
  Pallas kernels  38.2 us (43%)
  starting transfers between devices  29.9 us (33%)
  waiting for transfers between devices  13.3 us (15%)
  local copies, waits for them, and re-layouts  4.9 us (5%)
  between operations  1.68 us (2%)
    pallas_call x4, Pallas kernels, correlate(): pl.pallas_call(functools.partial(corr_kernel, dims, rot, entry), out_shap...  25.1 us
    ppermute x4, starting transfers between devices, swap_blocks(): lax.ppermute(block, axis, [(i, i ^ step) for i in range(lax.axis_size(axi...  8.66 us
    ppermute x3, starting transfers between devices, local(): partner = lax.ppermute(state, 'tile', [(i, i ^ step) for i in range(tiles)])  7.78 us
    ppermute x1, starting transfers between devices, neighbours(): lax.ppermute(block, axis, forward)  5.48 us
    pallas_call x2, Pallas kernels, slab_rows(): pl.pallas_call(functools.partial(slab_rows_kernel, dims), out_shape=jax.S...  5.04 us
    ppermute x3, waiting for transfers between devices, local(): partner = lax.ppermute(state, 'tile', [(i, i ^ step) for i in range(tiles)])  4.35 us
    ppermute x4, starting transfers between devices, local(): fars.append(lax.ppermute(far, 'rot', far_swap))  4.34 us
    pallas_call x1, Pallas kernels, slab_x(): pl.pallas_call(functools.partial(slab_x_kernel, dims), out_shape=(jax.Sha...  3.87 us
  transfers between devices with their start and end apart: 18, of which 8 were waited for; matrix products, arithmetic and copies ran while one was open for 2% of the time, Pallas kernels for 39%

profile of v12, /device:TPU:0, one launch (start us, length us, event | category | flops | bytes accessed | tf_op | source)
XLA Modules:
  0.0 89.0 jit_solution(18068084263810396176)
XLA Ops:
  0.7 1.0 %constant_dynamic-slice_fusion = bf16[16,5120]{1,0:T(8,128)(2,1)S(1)} fusion(bf16[32,5120]{1,0:T(8,128)(2,1)} %refs_0_.1, s32[]{:T(128)S(6)} %select_n.21), kind=kLoop, calls=%fused_computation.30 | loop fusion | bytes 327684 | tf_op jit(solution)/shard_map/dynamic_slice | solution.py:605
  1.6 1.3 %collective-permute-start.2 = (bf16[16,5120]{1,0:T(8,128)(2,1)S(1)}, bf16[16,5120]{1,0:T(8,128)(2,1)S(1)}, u32[]{:S(2)}, u32[]{:S(2)}) collective-permute-start(bf16[16,5120]{1,0:T(8,128)(2,1)S(1)} %constant_dynamic-slice_fusion), channel_id=1, source_target_pairs={{4,0},{8,4},{12,8},{16,12},{20,16},{24,20},{28,24},{5,1},{9,5},{13... | collective-permute-start | bytes 491528 | tf_op jit(solution)/shard_map/ppermute | solution.py:583
  2.9 5.5 %collective-permute-start.1 = (bf16[16,5120]{1,0:T(8,128)(2,1)S(1)}, bf16[16,5120]{1,0:T(8,128)(2,1)S(1)}, u32[]{:S(2)}, u32[]{:S(2)}) collective-permute-start(bf16[16,5120]{1,0:T(8,128)(2,1)S(1)} %constant_dynamic-slice_fusion), channel_id=1, source_target_pairs={{0,4},{4,8},{8,12},{12,16},{16,20},{20,24},{24,28},{1,5},{5,9},{9,... | collective-permute-start | bytes 491528 | tf_op jit(solution)/shard_map/ppermute | solution.py:583
  8.4 3.2 %collective-permute-start = (bf16[4,13824]{1,0:T(4,128)(2,1)}, bf16[4,13824]{1,0:T(4,128)(2,1)S(1)}, u32[]{:S(2)}, u32[]{:S(2)}) collective-permute-start(bf16[4,13824]{1,0:T(4,128)(2,1)} %param.15), channel_id=1, source_target_pairs={{0,16},{4,20},{8,24},{12,28},{16,0},{20,4},{24,8},{28,12},{1,17},{... | collective-permute-start | bytes 331784 | tf_op jit(solution)/shard_map/ppermute | solution.py:544
  11.6 2.7 %collective-permute-done.1 = bf16[16,5120]{1,0:T(8,128)(2,1)S(1)} collective-permute-done((bf16[16,5120]{1,0:T(8,128)(2,1)S(1)}, bf16[16,5120]{1,0:T(8,128)(2,1)S(1)}, u32[]{:S(2)}, u32[]{:S(2)}) %collective-permute-start.1) | collective-permute-done | bytes 163872 | tf_op jit(solution)/shard_map/ppermute | solution.py:583
  14.4 1.0 %copy-done.3 = bf16[32,5120]{1,0:T(8,128)(2,1)S(1)} copy-done((bf16[32,5120]{1,0:T(8,128)(2,1)S(1)}, bf16[32,5120]{1,0:T(8,128)(2,1)}, u32[]{:S(2)}) %copy-start.3) | copy-done | bytes 327704
  15.4 0.9 %copy-done.5 = bf16[240,512]{1,0:T(8,128)(2,1)S(1)} copy-done((bf16[240,512]{1,0:T(8,128)(2,1)S(1)}, bf16[240,512]{1,0:T(8,128)(2,1)}, u32[]{:S(2)}) %copy-start.5) | copy-done | bytes 245784
  16.4 2.3 %slab_own.1.refs_0_ = f32[3616,128]{1,0:T(8,128)S(1)} custom-call(s32[1]{0:T(128)} %bitcast.place_ref, bf16[32,5120]{1,0:T(8,128)(2,1)S(1)} %copy-done.3, bf16[240,512]{1,0:T(8,128)(2,1)S(1)} %copy-done.5), custom_call_target="tpu_custom_call" | custom-call | flops 3200000000 | bytes 1000000 | tf_op jit(solution)/shard_map/slab_own/pallas_call | solution.py:244
  18.9 3.0 %collective-permute-start.4 = (bf16[4,2,112,128]{3,2,1,0:T(8,128)(2,1)S(1)}, bf16[4,2,112,128]{3,2,1,0:T(8,128)(2,1)S(1)}, u32[]{:S(2)}, u32[]{:S(2)}) collective-permute-start(bf16[4,2,112,128]{3,2,1,0:T(8,128)(2,1)S(1)} %fusion.3), channel_id=1, source_target_pairs={{0,8},{4,12},{8,0},{12,4},{16,24},{20,28},{24,16},{28,20},{1,9},{5... | collective-permute-start | bytes 688136 | tf_op jit(solution)/shard_map/ppermute | solution.py:544
  21.9 2.8 %slab_halo.1.rows_ref = f32[9040,128]{1,0:T(8,128)S(1)} custom-call(s32[1]{0:T(128)} %bitcast.place_ref, f32[3616,128]{1,0:T(8,128)S(1)} %slab_own.1.refs_0_, bf16[2,16,5120]{2,1,0:T(8,128)(2,1)S(1)} %pad_maximum_fusion.1.refs_1_, bf16[2,16,5120]{2,1,0:T(8,128)(2,1)S(1)} %collective-permute-done.3.refs_2_, bf16[240,512]{1,0:T(8,128)(2,1)S(1)} %copy-done.6), custom_call_target="tpu_custom_call" | custom-call | flops 4800000000 | bytes 1000000 | tf_op jit(solution)/shard_map/slab_halo/pallas_call | solution.py:244
  25.9 2.3 %collective-permute-done.4 = bf16[4,2,112,128]{3,2,1,0:T(8,128)(2,1)S(1)} collective-permute-done((bf16[4,2,112,128]{3,2,1,0:T(8,128)(2,1)S(1)}, bf16[4,2,112,128]{3,2,1,0:T(8,128)(2,1)S(1)}, u32[]{:S(2)}, u32[]{:S(2)}) %collective-permute-start.4) | collective-permute-done | bytes 229408 | tf_op jit(solution)/shard_map/ppermute | solution.py:544
  28.3 2.4 %collective-permute-start.5 = (bf16[1,4,112,128]{3,2,1,0:T(8,128)(2,1)S(1)}, bf16[1,4,112,128]{3,2,1,0:T(8,128)(2,1)S(1)}, u32[]{:S(2)}, u32[]{:S(2)}) collective-permute-start(bf16[1,4,112,128]{3,2,1,0:T(8,128)(2,1)S(1)} %fusion.4), channel_id=1, source_target_pairs={{0,4},{4,0},{8,12},{12,8},{16,20},{20,16},{24,28},{28,24},{1,5},{5... | collective-permute-start | bytes 344072 | tf_op jit(solution)/shard_map/ppermute | solution.py:544
  30.8 3.9 %slab_x.1 = (f32[13,2,80,1024]{3,2,1,0:T(8,128)S(1)}, f32[40,32,128]{2,1,0:T(8,128)S(1)}, bf16[8,256,256]{2,1,0:T(8,128)(2,1)S(1)}) custom-call(f32[9040,128]{1,0:T(8,128)S(1)} %slab_halo.1.rows_ref, bf16[80,240]{1,0:T(8,128)(2,1)S(1)} %copy-done.11, s32[32,80]{1,0:T(8,128)S(1)} %copy-done.4, bf16[48,256]{1,0:T(8,128)(2,1)S(1)} %copy-done.13), custom_call_target="tpu_custom_call" | custom-call | flops 5000000000 | bytes 1000000 | tf_op jit(solution)/shard_map/slab_x/pallas_call | solution.py:297
  34.8 6.2 %correlate.4 = (f32[1,32,1280]{2,1,0:T(8,128)S(1)}, f32[32,1280]{1,0:T(8,128)S(1)}, f32[2,32,1280]{2,1,0:T(8,128)S(1)}, f32[8,128]{1,0:T(8,128)S(1)}) custom-call(s32[1]{0:T(128)} %bitcast.place_ref, s32[1]{0:T(128)} %bitcast.1.tile_ref, bf16[4,4,112,128]{3,2,1,0:T(8,128)(2,1)S(1)} %pad_maximum_fusion.refs_0_.refs_1_, ...), custom_call_target="tpu_custom_call" | custom-call | flops 15000000512 | bytes 10000000 | tf_op jit(solution)/shard_map/correlate/pallas_call | solution.py:447
  41.0 1.6 %collective-permute-start.7 = (f32[2,32,1280]{2,1,0:T(8,128)S(1)}, f32[2,32,1280]{2,1,0:T(8,128)S(1)}, u32[]{:S(2)}, u32[]{:S(2)}) collective-permute-start(f32[2,32,1280]{2,1,0:T(8,128)S(1)} %get-tuple-element.42), channel_id=1, source_target_pairs={{0,2},{1,3},{2,0},{3,1},{4,6},{5,7},{6,4},{7,5},{8,10},{9,11},{10,... | collective-permute-start | bytes 983048 | tf_op jit(solution)/shard_map/ppermute | solution.py:639
  42.6 6.2 %correlate.5 = (f32[2,32,1280]{2,1,0:T(8,128)S(1)}, f32[32,1280]{1,0:T(8,128)S(1)}, f32[2,32,1280]{2,1,0:T(8,128)S(1)}, f32[8,128]{1,0:T(8,128)S(1)}) custom-call(s32[1]{0:T(128)} %bitcast.place_ref, s32[1]{0:T(128)} %bitcast.1.tile_ref, f32[1,32,1280]{2,1,0:T(8,128)S(1)} %get-tuple-element.40.refs_0_, ...), custom_call_target="tpu_custom_call" | custom-call | flops 15000000512 | bytes 10000000 | tf_op jit(solution)/shard_map/correlate/pallas_call | solution.py:447
  48.8 0.6 collective-permute-start.8
  49.4 0.9 %collective-permute-done.7.refs_4_.refs_1_ = f32[2,32,1280]{2,1,0:T(8,128)S(1)} collective-permute-done((f32[2,32,1280]{2,1,0:T(8,128)S(1)}, f32[2,32,1280]{2,1,0:T(8,128)S(1)}, u32[]{:S(2)}, u32[]{:S(2)}) %collective-permute-start.7) | collective-permute-done | bytes 327712 | tf_op jit(solution)/shard_map/ppermute | solution.py:639
  50.3 6.4 %correlate.6 = (f32[3,32,1280]{2,1,0:T(8,128)S(1)}, f32[32,1280]{1,0:T(8,128)S(1)}, f32[2,32,1280]{2,1,0:T(8,128)S(1)}, f32[8,128]{1,0:T(8,128)S(1)}) custom-call(s32[1]{0:T(128)} %bitcast.place_ref, s32[1]{0:T(128)} %bitcast.1.tile_ref, f32[2,32,1280]{2,1,0:T(8,128)S(1)} %get-tuple-element.46.refs_0_, ...), custom_call_target="tpu_custom_call" | custom-call | flops 15000000512 | bytes 10000000 | tf_op jit(solution)/shard_map/correlate/pallas_call | solution.py:447
  56.8 2.1 %collective-permute-start.9 = (f32[2,32,1280]{2,1,0:T(8,128)S(1)}, f32[2,32,1280]{2,1,0:T(8,128)S(1)}, u32[]{:S(2)}, u32[]{:S(2)}) collective-permute-start(f32[2,32,1280]{2,1,0:T(8,128)S(1)} %get-tuple-element.54), channel_id=1, source_target_pairs={{0,2},{1,3},{2,0},{3,1},{4,6},{5,7},{6,4},{7,5},{8,10},{9,11},{10,... | collective-permute-start | bytes 983048 | tf_op jit(solution)/shard_map/ppermute | solution.py:639
  58.9 6.2 %correlate.7 = (f32[4,32,1280]{2,1,0:T(8,128)S(1)}, f32[32,1280]{1,0:T(8,128)S(1)}, f32[2,32,1280]{2,1,0:T(8,128)S(1)}, f32[8,128]{1,0:T(8,128)S(1)}) custom-call(s32[1]{0:T(128)} %bitcast.place_ref, s32[1]{0:T(128)} %bitcast.1.tile_ref, f32[3,32,1280]{2,1,0:T(8,128)S(1)} %get-tuple-element.52.refs_0_, ...), custom_call_target="tpu_custom_call" | custom-call | flops 15000000512 | bytes 10000000 | tf_op jit(solution)/shard_map/correlate/pallas_call | solution.py:447
  65.3 1.7 %collective-permute-start.10 = (f32[3,4]{1,0:T(4,128)S(1)}, f32[3,4]{1,0:T(4,128)S(1)}, u32[]{:S(2)}, u32[]{:S(2)}) collective-permute-start(f32[3,4]{1,0:T(4,128)S(1)} %pad_maximum_fusion.3), channel_id=1, source_target_pairs={{0,4},{4,0},{8,12},{12,8},{16,20},{20,16},{24,28},{28,24},{1,5},{5... | collective-permute-start | bytes 152 | tf_op jit(solution)/shard_map/ppermute | solution.py:644
  67.0 1.9 %collective-permute-done.10 = f32[3,4]{1,0:T(4,128)S(1)} collective-permute-done((f32[3,4]{1,0:T(4,128)S(1)}, f32[3,4]{1,0:T(4,128)S(1)}, u32[]{:S(2)}, u32[]{:S(2)}) %collective-permute-start.10) | collective-permute-done | bytes 80 | tf_op jit(solution)/shard_map/ppermute | solution.py:644
  69.0 1.5 %collective-permute-start.11 = (f32[3,4]{1,0:T(4,128)S(1)}, f32[3,4]{1,0:T(4,128)S(1)}, u32[]{:S(2)}, u32[]{:S(2)}) collective-permute-start(f32[3,4]{1,0:T(4,128)S(1)} %select_add_fusion.2), channel_id=1, source_target_pairs={{0,8},{4,12},{8,0},{12,4},{16,24},{20,28},{24,16},{28,20},{1,9},{5... | collective-permute-start | bytes 152 | tf_op jit(solution)/shard_map/ppermute | solution.py:644
  70.6 2.0 %collective-permute-done.11.after_ref = f32[3,4]{1,0:T(4,128)S(1)} collective-permute-done((f32[3,4]{1,0:T(4,128)S(1)}, f32[3,4]{1,0:T(4,128)S(1)}, u32[]{:S(2)}, u32[]{:S(2)}) %collective-permute-start.11) | collective-permute-done | bytes 80 | tf_op jit(solution)/shard_map/ppermute | solution.py:644
  72.7 4.6 %collective-permute-start.12 = (f32[3,4]{1,0:T(4,128)S(1)}, f32[3,4]{1,0:T(4,128)S(1)}, u32[]{:S(2)}, u32[]{:S(2)}) collective-permute-start(f32[3,4]{1,0:T(4,128)S(1)} %select_add_fusion.1), channel_id=1, source_target_pairs={{0,16},{4,20},{8,24},{12,28},{16,0},{20,4},{24,8},{28,12},{1,17},{... | collective-permute-start | bytes 152 | tf_op jit(solution)/shard_map/ppermute | solution.py:644
  77.2 1.2 %pack.1 = f32[8,32,1280]{2,1,0:T(8,128)} custom-call(f32[3,4]{1,0:T(4,128)S(1)} %collective-permute-done.11.after_ref, f32[32,1280]{1,0:T(8,128)S(1)} %get-tuple-element.58.refs_0_, f32[32,1280]{1,0:T(8,128)S(1)} %get-tuple-element.59.refs_1_, f32[32,1280]{1,0:T(8,128)S(1)} %get-tuple-element.60.refs_2_, f32[32,1280]{1,0:T(8,128)S(1)} %get-tuple-element.61.refs_3_, ...), custom_call_target="tpu_custom_call" | custom-call | tf_op jit(solution)/shard_map/pack/pallas_call | solution.py:533
  79.5 2.0 %collective-permute-start.15 = (f32[4,6]{1,0:T(4,128)S(1)}, f32[4,6]{1,0:T(4,128)S(1)}, u32[]{:S(2)}, u32[]{:S(2)}) collective-permute-start(f32[4,6]{1,0:T(4,128)S(1)} %pad_maximum_fusion.4), channel_id=1, source_target_pairs={{0,2},{1,3},{2,0},{3,1},{4,6},{5,7},{6,4},{7,5},{8,10},{9,11},{10,... | collective-permute-start | bytes 296 | tf_op jit(solution)/shard_map/ppermute | solution.py:575
  81.8 1.3 %collective-permute-done.15 = f32[4,6]{1,0:T(4,128)S(1)} collective-permute-done((f32[4,6]{1,0:T(4,128)S(1)}, f32[4,6]{1,0:T(4,128)S(1)}, u32[]{:S(2)}, u32[]{:S(2)}) %collective-permute-start.15) | collective-permute-done | bytes 128 | tf_op jit(solution)/shard_map/ppermute | solution.py:575
  83.1 1.7 %collective-permute-done.16 = f32[4,6]{1,0:T(4,128)S(1)} collective-permute-done((f32[4,6]{1,0:T(4,128)S(1)}, f32[4,6]{1,0:T(4,128)S(1)}, u32[]{:S(2)}, u32[]{:S(2)}) %collective-permute-start.16) | collective-permute-done | bytes 128 | tf_op jit(solution)/shard_map/ppermute | solution.py:575
  84.8 1.1 %copy-done.2 = f32[4,32,1280]{2,1,0:T(8,128)S(1)} copy-done((f32[4,32,1280]{2,1,0:T(8,128)S(1)}, f32[4,32,1280]{2,1,0:T(8,128)}, u32[]{:S(2)}) %copy-start.2) | copy-done | bytes 655384
  85.9 3.1 %combine.1 = (f32[32,1280]{1,0:T(8,128)}, f32[32,1280]{1,0:T(8,128)}, f32[4,32,1280]{2,1,0:T(8,128)}) custom-call(s32[1]{0:T(128)} %bitcast.place_ref, f32[16,6]{1,0:T(8,128)S(1)} %bitcast.24, f32[40,32,128]{2,1,0:T(8,128)S(1)} %get-tuple-element.36.refs_2_.refs_3_.mask_ref, f32[4,32,1280]{2,1,0:T(8,128)S(1)} %copy-done.2, ...), custom_call_target="tpu_custom_call" | custom-call | tf_op jit(solution)/shard_map/combine/pallas_call | solution.py:514
  (76 shorter events, 2.9 us)
Async XLA Ops:
  0.6 78.2 %copy-start = (f32[4,4096]{1,0:T(4,128)S(1)}, f32[4,4096]{1,0:T(4,128)}, u32[]{:S(2)}) copy-start(f32[4,4096]{1,0:T(4,128)} %param.17) | copy-start | bytes 196612
  1.6 10.0 %collective-permute-start.2 = (bf16[16,5120]{1,0:T(8,128)(2,1)S(1)}, bf16[16,5120]{1,0:T(8,128)(2,1)S(1)}, u32[]{:S(2)}, u32[]{:S(2)}) collective-permute-start(bf16[16,5120]{1,0:T(8,128)(2,1)S(1)} %constant_dynamic-slice_fusion), channel_id=1, source_target_pairs={{4,0},{8,4},{12,8},{16,12},{20,16},{24,20},{28,24},{5,1},{9,5},{13... | collective-permute-start | bytes 491528 | tf_op jit(solution)/shard_map/ppermute | solution.py:583
  2.9 11.4 %collective-permute-start.1 = (bf16[16,5120]{1,0:T(8,128)(2,1)S(1)}, bf16[16,5120]{1,0:T(8,128)(2,1)S(1)}, u32[]{:S(2)}, u32[]{:S(2)}) collective-permute-start(bf16[16,5120]{1,0:T(8,128)(2,1)S(1)} %constant_dynamic-slice_fusion), channel_id=1, source_target_pairs={{0,4},{4,8},{8,12},{12,16},{16,20},{20,24},{24,28},{1,5},{5,9},{9,... | collective-permute-start | bytes 491528 | tf_op jit(solution)/shard_map/ppermute | solution.py:583
  8.4 10.3 %collective-permute-start = (bf16[4,13824]{1,0:T(4,128)(2,1)}, bf16[4,13824]{1,0:T(4,128)(2,1)S(1)}, u32[]{:S(2)}, u32[]{:S(2)}) collective-permute-start(bf16[4,13824]{1,0:T(4,128)(2,1)} %param.15), channel_id=1, source_target_pairs={{0,16},{4,20},{8,24},{12,28},{16,0},{20,4},{24,8},{28,12},{1,17},{... | collective-permute-start | bytes 331784 | tf_op jit(solution)/shard_map/ppermute | solution.py:544
  14.4 7.6 %collective-permute-start.3 = (bf16[2,16,5120]{2,1,0:T(8,128)(2,1)S(1)}, bf16[2,16,5120]{2,1,0:T(8,128)(2,1)S(1)}, u32[]{:S(2)}, u32[]{:S(2)}) collective-permute-start(bf16[2,16,5120]{2,1,0:T(8,128)(2,1)S(1)} %pad_maximum_fusion.1.refs_1_), channel_id=1, source_target_pairs={{0,1},{1,0},{2,3},{3,2},{4,5},{5,4},{6,7},{7,6},{8,9},{9,8},{10,11... | collective-permute-start | bytes 983048 | tf_op jit(solution)/shard_map/ppermute | solution.py:608
  16.4 2.3 %copy-start.15 = (bf16[4,13824]{1,0:T(4,128)(2,1)S(1)}, bf16[4,13824]{1,0:T(4,128)(2,1)}, u32[]{:S(2)}) copy-start(bf16[4,13824]{1,0:T(4,128)(2,1)} %param.15) | copy-start | bytes 331780
  16.4 5.6 %copy-start.6 = (bf16[240,512]{1,0:T(8,128)(2,1)S(1)}, bf16[240,512]{1,0:T(8,128)(2,1)}, u32[]{:S(2)}) copy-start(bf16[240,512]{1,0:T(8,128)(2,1)} %constant.50.clone.refs_1_.refs_3_) | copy-start | bytes 737284
  18.9 11.9 %copy-start.4 = (s32[32,80]{1,0:T(8,128)S(1)}, s32[32,80]{1,0:T(8,128)}, u32[]{:S(2)}) copy-start(s32[32,80]{1,0:T(8,128)} %valid_ref.1) | copy-start | bytes 30724
  18.9 11.9 %copy-start.11 = (bf16[80,240]{1,0:T(8,128)(2,1)S(1)}, bf16[80,240]{1,0:T(8,128)(2,1)}, u32[]{:S(2)}) copy-start(bf16[80,240]{1,0:T(8,128)(2,1)} %constant.51.clone.x_ref) | copy-start | bytes 115204
  18.9 11.9 %copy-start.13 = (bf16[48,256]{1,0:T(8,128)(2,1)S(1)}, bf16[48,256]{1,0:T(8,128)(2,1)}, u32[]{:S(2)}) copy-start(bf16[48,256]{1,0:T(8,128)(2,1)} %constant.52.clone.tz_ref) | copy-start | bytes 73732
  18.9 9.3 %collective-permute-start.4 = (bf16[4,2,112,128]{3,2,1,0:T(8,128)(2,1)S(1)}, bf16[4,2,112,128]{3,2,1,0:T(8,128)(2,1)S(1)}, u32[]{:S(2)}, u32[]{:S(2)}) collective-permute-start(bf16[4,2,112,128]{3,2,1,0:T(8,128)(2,1)S(1)} %fusion.3), channel_id=1, source_target_pairs={{0,8},{4,12},{8,0},{12,4},{16,24},{20,28},{24,16},{28,20},{1,9},{5... | collective-permute-start | bytes 688136 | tf_op jit(solution)/shard_map/ppermute | solution.py:544
  28.2 6.5 %copy-start.7 = (bf16[256,256]{1,0:T(8,128)(2,1)S(1)}, bf16[256,256]{1,0:T(8,128)(2,1)}, u32[]{:S(2)}) copy-start(bf16[256,256]{1,0:T(8,128)(2,1)} %constant.58.clone.refs_10_.refs_11_) | copy-start | bytes 393220
  28.3 6.5 %copy-start.8 = (bf16[160,208]{1,0:T(8,128)(2,1)S(1)}, bf16[160,208]{1,0:T(8,128)(2,1)}, u32[]{:S(2)}) copy-start(bf16[160,208]{1,0:T(8,128)(2,1)} %constant.57.clone.refs_9_.refs_10_) | copy-start | bytes 199684
  28.3 6.5 %copy-start.9 = (bf16[112,144]{1,0:T(8,128)(2,1)S(1)}, bf16[112,144]{1,0:T(8,128)(2,1)}, u32[]{:S(2)}) copy-start(bf16[112,144]{1,0:T(8,128)(2,1)} %constant.54.clone.refs_6_.refs_7_) | copy-start | bytes 96772
  28.3 6.5 %copy-start.10 = (bf16[80,144]{1,0:T(8,128)(2,1)S(1)}, bf16[80,144]{1,0:T(8,128)(2,1)}, u32[]{:S(2)}) copy-start(bf16[80,144]{1,0:T(8,128)(2,1)} %constant.55.clone.refs_7_.refs_8_) | copy-start | bytes 69124
  28.3 6.5 %copy-start.12 = (bf16[64,160]{1,0:T(8,128)(2,1)S(1)}, bf16[64,160]{1,0:T(8,128)(2,1)}, u32[]{:S(2)}) copy-start(bf16[64,160]{1,0:T(8,128)(2,1)} %constant.56.clone.refs_8_.refs_9_) | copy-start | bytes 61444
  28.3 6.5 %copy-start.14 = (f32[8,128]{1,0:T(8,128)S(1)}, f32[8,128]{1,0:T(8,128)}, u32[]{:S(2)}) copy-start(f32[8,128]{1,0:T(8,128)} %constant.53.clone.refs_5_.refs_6_) | copy-start | bytes 12292
  28.3 6.4 %collective-permute-start.5 = (bf16[1,4,112,128]{3,2,1,0:T(8,128)(2,1)S(1)}, bf16[1,4,112,128]{3,2,1,0:T(8,128)(2,1)S(1)}, u32[]{:S(2)}, u32[]{:S(2)}) collective-permute-start(bf16[1,4,112,128]{3,2,1,0:T(8,128)(2,1)S(1)} %fusion.4), channel_id=1, source_target_pairs={{0,4},{4,0},{8,12},{12,8},{16,20},{20,16},{24,28},{28,24},{1,5},{5... | collective-permute-start | bytes 344072 | tf_op jit(solution)/shard_map/ppermute | solution.py:544
  30.7 11.9 %collective-permute-start.6 = (bf16[3,4,112,128]{3,2,1,0:T(8,128)(2,1)S(1)}, bf16[3,4,112,128]{3,2,1,0:T(8,128)(2,1)S(1)}, u32[]{:S(2)}, u32[]{:S(2)}) collective-permute-start(bf16[3,4,112,128]{3,2,1,0:T(8,128)(2,1)S(1)} %fusion.2), channel_id=1, source_target_pairs={{0,4},{4,0},{8,12},{12,8},{16,20},{20,16},{24,28},{28,24},{1,5},{5... | collective-permute-start | bytes 1032200 | tf_op jit(solution)/shard_map/ppermute | solution.py:544
  41.0 9.3 %collective-permute-start.7 = (f32[2,32,1280]{2,1,0:T(8,128)S(1)}, f32[2,32,1280]{2,1,0:T(8,128)S(1)}, u32[]{:S(2)}, u32[]{:S(2)}) collective-permute-start(f32[2,32,1280]{2,1,0:T(8,128)S(1)} %get-tuple-element.42), channel_id=1, source_target_pairs={{0,2},{1,3},{2,0},{3,1},{4,6},{5,7},{6,4},{7,5},{8,10},{9,11},{10,... | collective-permute-start | bytes 983048 | tf_op jit(solution)/shard_map/ppermute | solution.py:639
  48.8 10.0 %collective-permute-start.8 = (f32[2,32,1280]{2,1,0:T(8,128)S(1)}, f32[2,32,1280]{2,1,0:T(8,128)S(1)}, u32[]{:S(2)}, u32[]{:S(2)}) collective-permute-start(f32[2,32,1280]{2,1,0:T(8,128)S(1)} %get-tuple-element.48), channel_id=1, source_target_pairs={{0,2},{1,3},{2,0},{3,1},{4,6},{5,7},{6,4},{7,5},{8,10},{9,11},{10,... | collective-permute-start | bytes 983048 | tf_op jit(solution)/shard_map/ppermute | solution.py:639
  56.8 8.5 %collective-permute-start.9 = (f32[2,32,1280]{2,1,0:T(8,128)S(1)}, f32[2,32,1280]{2,1,0:T(8,128)S(1)}, u32[]{:S(2)}, u32[]{:S(2)}) collective-permute-start(f32[2,32,1280]{2,1,0:T(8,128)S(1)} %get-tuple-element.54), channel_id=1, source_target_pairs={{0,2},{1,3},{2,0},{3,1},{4,6},{5,7},{6,4},{7,5},{8,10},{9,11},{10,... | collective-permute-start | bytes 983048 | tf_op jit(solution)/shard_map/ppermute | solution.py:639
  65.1 13.3 %copy-start.1 = (f32[4,32,1280]{2,1,0:T(8,128)}, f32[4,32,1280]{2,1,0:T(8,128)S(1)}, u32[]{:S(2)}) copy-start(f32[4,32,1280]{2,1,0:T(8,128)S(1)} %get-tuple-element.67.refs_0_) | copy-start | bytes 1966084
  65.1 13.7 %copy-start.16 = (s32[4]{0:T(128)S(1)}, s32[4]{0:T(128)}, u32[]{:S(2)}) copy-start(s32[4]{0:T(128)} %param.18) | copy-start | bytes 52
  65.1 12.1 %collective-permute-start.13 = (f32[2,32,1280]{2,1,0:T(8,128)S(1)}, f32[2,32,1280]{2,1,0:T(8,128)S(1)}, u32[]{:S(2)}, u32[]{:S(2)}) collective-permute-start(f32[2,32,1280]{2,1,0:T(8,128)S(1)} %get-tuple-element.65), channel_id=1, source_target_pairs={{0,2},{1,3},{2,0},{3,1},{4,6},{5,7},{6,4},{7,5},{8,10},{9,11},{10,... | collective-permute-start | bytes 983048 | tf_op jit(solution)/shard_map/ppermute | solution.py:639
  65.3 3.6 %collective-permute-start.10 = (f32[3,4]{1,0:T(4,128)S(1)}, f32[3,4]{1,0:T(4,128)S(1)}, u32[]{:S(2)}, u32[]{:S(2)}) collective-permute-start(f32[3,4]{1,0:T(4,128)S(1)} %pad_maximum_fusion.3), channel_id=1, source_target_pairs={{0,4},{4,0},{8,12},{12,8},{16,20},{20,16},{24,28},{28,24},{1,5},{5... | collective-permute-start | bytes 152 | tf_op jit(solution)/shard_map/ppermute | solution.py:644
  69.0 3.6 %collective-permute-start.11 = (f32[3,4]{1,0:T(4,128)S(1)}, f32[3,4]{1,0:T(4,128)S(1)}, u32[]{:S(2)}, u32[]{:S(2)}) collective-permute-start(f32[3,4]{1,0:T(4,128)S(1)} %select_add_fusion.2), channel_id=1, source_target_pairs={{0,8},{4,12},{8,0},{12,4},{16,24},{20,28},{24,16},{28,20},{1,9},{5... | collective-permute-start | bytes 152 | tf_op jit(solution)/shard_map/ppermute | solution.py:644
  72.7 6.1 %collective-permute-start.12 = (f32[3,4]{1,0:T(4,128)S(1)}, f32[3,4]{1,0:T(4,128)S(1)}, u32[]{:S(2)}, u32[]{:S(2)}) collective-permute-start(f32[3,4]{1,0:T(4,128)S(1)} %select_add_fusion.1), channel_id=1, source_target_pairs={{0,16},{4,20},{8,24},{12,28},{16,0},{20,4},{24,8},{28,12},{1,17},{... | collective-permute-start | bytes 152 | tf_op jit(solution)/shard_map/ppermute | solution.py:644
  78.8 6.0 %collective-permute-start.17 = (f32[8,32,1280]{2,1,0:T(8,128)}, f32[8,32,1280]{2,1,0:T(8,128)S(1)}, u32[]{:S(2)}, u32[]{:S(2)}) collective-permute-start(f32[8,32,1280]{2,1,0:T(8,128)} %pack.1), channel_id=1, source_target_pairs={{0,1},{1,0},{2,3},{3,2},{4,5},{5,4},{6,7},{7,6},{8,9},{9,8},{10,11... | collective-permute-start | bytes 3932168 | tf_op jit(solution)/shard_map/ppermute | solution.py:655
  79.5 3.6 %collective-permute-start.15 = (f32[4,6]{1,0:T(4,128)S(1)}, f32[4,6]{1,0:T(4,128)S(1)}, u32[]{:S(2)}, u32[]{:S(2)}) collective-permute-start(f32[4,6]{1,0:T(4,128)S(1)} %pad_maximum_fusion.4), channel_id=1, source_target_pairs={{0,2},{1,3},{2,0},{3,1},{4,6},{5,7},{6,4},{7,5},{8,10},{9,11},{10,... | collective-permute-start | bytes 296 | tf_op jit(solution)/shard_map/ppermute | solution.py:575
  81.5 1.6 %collective-permute-start.14 = (f32[4,6]{1,0:T(4,128)S(1)}, f32[4,6]{1,0:T(4,128)S(1)}, u32[]{:S(2)}, u32[]{:S(2)}) collective-permute-start(f32[4,6]{1,0:T(4,128)S(1)} %pad_maximum_fusion.4), channel_id=1, source_target_pairs={{0,1},{1,0},{2,3},{3,2},{4,5},{5,4},{6,7},{7,6},{8,9},{9,8},{10,11... | collective-permute-start | bytes 296 | tf_op jit(solution)/shard_map/ppermute | solution.py:575
  81.8 3.0 %collective-permute-start.16 = (f32[4,6]{1,0:T(4,128)S(1)}, f32[4,6]{1,0:T(4,128)S(1)}, u32[]{:S(2)}, u32[]{:S(2)}) collective-permute-start(f32[4,6]{1,0:T(4,128)S(1)} %pad_maximum_fusion.4), channel_id=1, source_target_pairs={{0,3},{1,2},{2,1},{3,0},{4,7},{5,6},{6,5},{7,4},{8,11},{9,10},{10,... | collective-permute-start | bytes 296 | tf_op jit(solution)/shard_map/ppermute | solution.py:575
  (3 other events, 3.0 us)

commit v13 on v11

--- a/solution.py
+++ b/solution.py
@@ -220,7 +220,11 @@
                     lane_block(part, 2 * j) + lane_block(part, 2 * j + 1),
                 )
 
-    loop(y_cells // (2 * many), depth_step)
+    def two_depth_steps(i):
+        depth_step(2 * i)
+        depth_step(2 * i + 1)
+
+    loop(y_cells // (4 * many), two_depth_steps)
 
     def gather_rows(i, slot):
         value = pick(depth_buf, [GROUP * i + u for u in range(GROUP)], y_cells, odd(count))
@@ -500,7 +504,11 @@
         for c in range(4):
             mom_ref[c, :, lanes] = moment[c] * share
 
-    loop(blocks, step)
+    def two_steps(i):
+        step(2 * i)
+        step(2 * i + 1)
+
+    loop(blocks // 2, two_steps)
 
 
 def combine(place, coefs, mask, arrays, pieces):

time: 85.8 us -> 85.8 us (level)
  Pallas kernels: 36.7 us -> 35.3 us
  waiting for transfers between devices: 16 us -> 17.3 us
    pallas_call x2, Pallas kernels: 5.04 us -> 3.67 us  [slab_rows(): pl.pallas_call(functools.partial(slab_rows_kernel, dims), out_shape=jax.S...]
    ppermute x4, waiting for transfers between devices: 5.88 us -> 7.24 us  [swap_blocks(): lax.ppermute(block, axis, [(i, i ^ step) for i in range(lax.axis_size(axi...]
  transfers between devices with their start and end apart: 19 -> 19, of which waited for: 9 -> 9; matrix products, arithmetic and copies ran while one was open for 4% -> 4% of each run, Pallas kernels for 39% -> 37%
where the time goes in v13:
time: 85.8 us; the launch traced here: 85.4 us
  Pallas kernels  35.3 us (41%)
  starting transfers between devices  23.4 us (27%)
  waiting for transfers between devices  17.3 us (20%)
  local copies, waits for them, and re-layouts  5.23 us (6%)
  between operations  2.36 us (3%)
  other arithmetic  1.58 us (2%)
    pallas_call x4, Pallas kernels, correlate(): pl.pallas_call(functools.partial(corr_kernel, dims, rot, entry), out_shap...  24.3 us
    ppermute x4, waiting for transfers between devices, swap_blocks(): lax.ppermute(block, axis, [(i, i ^ step) for i in range(lax.axis_size(axi...  7.24 us
    ppermute x4, starting transfers between devices, swap_blocks(): lax.ppermute(block, axis, [(i, i ^ step) for i in range(lax.axis_size(axi...  6.86 us
    ppermute x3, waiting for transfers between devices, local(): partner = lax.ppermute(state, 'tile', [(i, i ^ step) for i in range(tiles)])  4.97 us
    ppermute x1, starting transfers between devices, neighbours(): lax.ppermute(block, axis, forward)  4.85 us
    ppermute x4, starting transfers between devices, local(): fars.append(lax.ppermute(far, 'rot', far_swap))  4.51 us
    pallas_call x1, Pallas kernels, slab_x(): pl.pallas_call(functools.partial(slab_x_kernel, dims), out_shape=(jax.Sha...  3.84 us
    pallas_call x2, Pallas kernels, slab_rows(): pl.pallas_call(functools.partial(slab_rows_kernel, dims), out_shape=jax.S...  3.67 us
  transfers between devices with their start and end apart: 19, of which 9 were waited for; matrix products, arithmetic and copies ran while one was open for 4% of the time, Pallas kernels for 37%

profile of v13, /device:TPU:0, one launch (start us, length us, event | category | flops | bytes accessed | tf_op | source)
XLA Modules:
  0.0 85.4 jit_solution(14284890155779227767)
XLA Ops:
  0.7 1.0 %reshape.75 = bf16[4,1,108,128]{3,2,0,1:T(8,128)(2,1)S(1)} reshape(bf16[4,13824]{1,0:T(4,128)(2,1)} %param.15) | data formatting | bytes 221184 | tf_op jit(solution)/shard_map/reshape | solution.py:585
  1.7 0.9 %constant_dynamic-slice_fusion = bf16[16,5120]{1,0:T(8,128)(2,1)S(1)} fusion(bf16[32,5120]{1,0:T(8,128)(2,1)} %refs_0_.1, s32[]{:T(128)S(6)} %select_n.30), kind=kLoop, calls=%fused_computation.24 | loop fusion | bytes 327684 | tf_op jit(solution)/shard_map/dynamic_slice | solution.py:592
  2.6 4.9 %collective-permute-start.1 = (bf16[16,5120]{1,0:T(8,128)(2,1)S(1)}, bf16[16,5120]{1,0:T(8,128)(2,1)S(1)}, u32[]{:S(2)}, u32[]{:S(2)}) collective-permute-start(bf16[16,5120]{1,0:T(8,128)(2,1)S(1)} %constant_dynamic-slice_fusion), channel_id=1, source_target_pairs={{0,4},{4,8},{8,12},{12,16},{16,20},{20,24},{24,28},{1,5},{5,9},{9,... | collective-permute-start | bytes 491528 | tf_op jit(solution)/shard_map/ppermute | solution.py:568
  7.5 1.3 %collective-permute-start.2 = (bf16[16,5120]{1,0:T(8,128)(2,1)S(1)}, bf16[16,5120]{1,0:T(8,128)(2,1)S(1)}, u32[]{:S(2)}, u32[]{:S(2)}) collective-permute-start(bf16[16,5120]{1,0:T(8,128)(2,1)S(1)} %constant_dynamic-slice_fusion), channel_id=1, source_target_pairs={{4,0},{8,4},{12,8},{16,12},{20,16},{24,20},{28,24},{5,1},{9,5},{13... | collective-permute-start | bytes 491528 | tf_op jit(solution)/shard_map/ppermute | solution.py:568
  8.8 4.7 %collective-permute-start = (bf16[4,1,112,128]{3,2,1,0:T(8,128)(2,1)S(1)}, bf16[4,1,112,128]{3,2,1,0:T(8,128)(2,1)S(1)}, u32[]{:S(2)}, u32[]{:S(2)}) collective-permute-start(bf16[4,1,112,128]{3,2,1,0:T(8,128)(2,1)S(1)} %pad.4), channel_id=1, source_target_pairs={{0,16},{4,20},{8,24},{12,28},{16,0},{20,4},{24,8},{28,12},{1,17},{... | collective-permute-start | bytes 344072 | tf_op jit(solution)/shard_map/ppermute | solution.py:529
  13.5 1.0 %copy-done.1 = bf16[32,5120]{1,0:T(8,128)(2,1)S(1)} copy-done((bf16[32,5120]{1,0:T(8,128)(2,1)S(1)}, bf16[32,5120]{1,0:T(8,128)(2,1)}, u32[]{:S(2)}) %copy-start.1) | copy-done | bytes 327704
  14.4 0.9 %copy-done.3 = bf16[240,512]{1,0:T(8,128)(2,1)S(1)} copy-done((bf16[240,512]{1,0:T(8,128)(2,1)S(1)}, bf16[240,512]{1,0:T(8,128)(2,1)}, u32[]{:S(2)}) %copy-start.3) | copy-done | bytes 245784
  15.4 1.6 %slab_own.1.refs_0_ = f32[3616,128]{1,0:T(8,128)S(1)} custom-call(s32[1]{0:T(128)} %bitcast.place_ref, bf16[32,5120]{1,0:T(8,128)(2,1)S(1)} %copy-done.1, bf16[240,512]{1,0:T(8,128)(2,1)S(1)} %copy-done.3), custom_call_target="tpu_custom_call" | custom-call | flops 3200000000 | bytes 1000000 | tf_op jit(solution)/shard_map/slab_own/pallas_call | solution.py:248
  17.4 4.5 %collective-permute-done = bf16[4,1,112,128]{3,2,1,0:T(8,128)(2,1)S(1)} collective-permute-done((bf16[4,1,112,128]{3,2,1,0:T(8,128)(2,1)S(1)}, bf16[4,1,112,128]{3,2,1,0:T(8,128)(2,1)S(1)}, u32[]{:S(2)}, u32[]{:S(2)}) %collective-permute-start) | collective-permute-done | bytes 114720 | tf_op jit(solution)/shard_map/ppermute | solution.py:529
  22.1 2.1 %slab_halo.1.rows_ref = f32[9040,128]{1,0:T(8,128)S(1)} custom-call(s32[1]{0:T(128)} %bitcast.place_ref, f32[3616,128]{1,0:T(8,128)S(1)} %slab_own.1.refs_0_, bf16[2,16,5120]{2,1,0:T(8,128)(2,1)S(1)} %pad_maximum_fusion.3.refs_1_, bf16[2,16,5120]{2,1,0:T(8,128)(2,1)S(1)} %collective-permute-done.3.refs_2_, bf16[240,512]{1,0:T(8,128)(2,1)S(1)} %copy-done.4), custom_call_target="tpu_custom_call" | custom-call | flops 4800000000 | bytes 1000000 | tf_op jit(solution)/shard_map/slab_halo/pallas_call | solution.py:248
  25.4 2.7 %collective-permute-done.4 = bf16[4,2,112,128]{3,2,1,0:T(8,128)(2,1)S(1)} collective-permute-done((bf16[4,2,112,128]{3,2,1,0:T(8,128)(2,1)S(1)}, bf16[4,2,112,128]{3,2,1,0:T(8,128)(2,1)S(1)}, u32[]{:S(2)}, u32[]{:S(2)}) %collective-permute-start.4) | collective-permute-done | bytes 229408 | tf_op jit(solution)/shard_map/ppermute | solution.py:529
  28.3 1.6 %collective-permute-start.5 = (bf16[1,4,112,128]{3,2,1,0:T(8,128)(2,1)S(1)}, bf16[1,4,112,128]{3,2,1,0:T(8,128)(2,1)S(1)}, u32[]{:S(2)}, u32[]{:S(2)}) collective-permute-start(bf16[1,4,112,128]{3,2,1,0:T(8,128)(2,1)S(1)} %slice.110), channel_id=1, source_target_pairs={{0,4},{4,0},{8,12},{12,8},{16,20},{20,16},{24,28},{28,24},{1,5},{5... | collective-permute-start | bytes 344072 | tf_op jit(solution)/shard_map/ppermute | solution.py:529
  30.4 3.8 %slab_x.1 = (f32[13,2,80,1024]{3,2,1,0:T(8,128)S(1)}, f32[40,32,128]{2,1,0:T(8,128)S(1)}, bf16[8,256,256]{2,1,0:T(8,128)(2,1)S(1)}) custom-call(f32[9040,128]{1,0:T(8,128)S(1)} %slab_halo.1.rows_ref, bf16[80,240]{1,0:T(8,128)(2,1)S(1)} %copy-done.9, s32[32,80]{1,0:T(8,128)S(1)} %copy-done.2, bf16[48,256]{1,0:T(8,128)(2,1)S(1)} %copy-done.11), custom_call_target="tpu_custom_call" | custom-call | flops 5000000000 | bytes 1000000 | tf_op jit(solution)/shard_map/slab_x/pallas_call | solution.py:301
  34.3 6.0 %correlate.4 = (f32[1,32,1280]{2,1,0:T(8,128)S(1)}, f32[32,1280]{1,0:T(8,128)S(1)}, f32[2,32,1280]{2,1,0:T(8,128)S(1)}, f32[8,128]{1,0:T(8,128)S(1)}) custom-call(s32[1]{0:T(128)} %bitcast.place_ref, s32[1]{0:T(128)} %bitcast.1.tile_ref, bf16[4,4,112,128]{3,2,1,0:T(8,128)(2,1)S(1)} %pad_maximum_fusion.2.refs_0_.refs_1_, ...), custom_call_target="tpu_custom_call" | custom-call | flops 15000000512 | bytes 10000000 | tf_op jit(solution)/shard_map/correlate/pallas_call | solution.py:451
  40.3 1.6 %collective-permute-start.7 = (f32[2,32,1280]{2,1,0:T(8,128)S(1)}, f32[2,32,1280]{2,1,0:T(8,128)S(1)}, u32[]{:S(2)}, u32[]{:S(2)}) collective-permute-start(f32[2,32,1280]{2,1,0:T(8,128)S(1)} %get-tuple-element.47), channel_id=1, source_target_pairs={{0,2},{1,3},{2,0},{3,1},{4,6},{5,7},{6,4},{7,5},{8,10},{9,11},{10,... | collective-permute-start | bytes 983048 | tf_op jit(solution)/shard_map/ppermute | solution.py:626
  41.9 6.0 %correlate.5 = (f32[2,32,1280]{2,1,0:T(8,128)S(1)}, f32[32,1280]{1,0:T(8,128)S(1)}, f32[2,32,1280]{2,1,0:T(8,128)S(1)}, f32[8,128]{1,0:T(8,128)S(1)}) custom-call(s32[1]{0:T(128)} %bitcast.place_ref, s32[1]{0:T(128)} %bitcast.1.tile_ref, f32[1,32,1280]{2,1,0:T(8,128)S(1)} %get-tuple-element.45.refs_0_, ...), custom_call_target="tpu_custom_call" | custom-call | flops 15000000512 | bytes 10000000 | tf_op jit(solution)/shard_map/correlate/pallas_call | solution.py:451
  47.9 0.6 collective-permute-start.8
  48.5 0.7 collective-permute-done.7.refs_1_
  49.2 6.2 %correlate.6 = (f32[3,32,1280]{2,1,0:T(8,128)S(1)}, f32[32,1280]{1,0:T(8,128)S(1)}, f32[2,32,1280]{2,1,0:T(8,128)S(1)}, f32[8,128]{1,0:T(8,128)S(1)}) custom-call(s32[1]{0:T(128)} %bitcast.place_ref, s32[1]{0:T(128)} %bitcast.1.tile_ref, f32[2,32,1280]{2,1,0:T(8,128)S(1)} %get-tuple-element.51.refs_0_, ...), custom_call_target="tpu_custom_call" | custom-call | flops 15000000512 | bytes 10000000 | tf_op jit(solution)/shard_map/correlate/pallas_call | solution.py:451
  55.4 2.2 %collective-permute-start.9 = (f32[2,32,1280]{2,1,0:T(8,128)S(1)}, f32[2,32,1280]{2,1,0:T(8,128)S(1)}, u32[]{:S(2)}, u32[]{:S(2)}) collective-permute-start(f32[2,32,1280]{2,1,0:T(8,128)S(1)} %get-tuple-element.59), channel_id=1, source_target_pairs={{0,2},{1,3},{2,0},{3,1},{4,6},{5,7},{6,4},{7,5},{8,10},{9,11},{10,... | collective-permute-start | bytes 983048 | tf_op jit(solution)/shard_map/ppermute | solution.py:626
  57.8 6.0 %correlate.7 = (f32[4,32,1280]{2,1,0:T(8,128)S(1)}, f32[32,1280]{1,0:T(8,128)S(1)}, f32[2,32,1280]{2,1,0:T(8,128)S(1)}, f32[8,128]{1,0:T(8,128)S(1)}) custom-call(s32[1]{0:T(128)} %bitcast.place_ref, s32[1]{0:T(128)} %bitcast.1.tile_ref, f32[3,32,1280]{2,1,0:T(8,128)S(1)} %get-tuple-element.57.refs_0_, ...), custom_call_target="tpu_custom_call" | custom-call | flops 15000000512 | bytes 10000000 | tf_op jit(solution)/shard_map/correlate/pallas_call | solution.py:451
  64.1 1.6 %collective-permute-start.11 = (f32[3,4]{1,0:T(4,128)S(1)}, f32[3,4]{1,0:T(4,128)S(1)}, u32[]{:S(2)}, u32[]{:S(2)}) collective-permute-start(f32[3,4]{1,0:T(4,128)S(1)} %pad_maximum_fusion.6), channel_id=1, source_target_pairs={{0,4},{4,0},{8,12},{12,8},{16,20},{20,16},{24,28},{28,24},{1,5},{5... | collective-permute-start | bytes 152 | tf_op jit(solution)/shard_map/ppermute | solution.py:634
  65.7 1.9 %collective-permute-done.11 = f32[3,4]{1,0:T(4,128)S(1)} collective-permute-done((f32[3,4]{1,0:T(4,128)S(1)}, f32[3,4]{1,0:T(4,128)S(1)}, u32[]{:S(2)}, u32[]{:S(2)}) %collective-permute-start.11) | collective-permute-done | bytes 80 | tf_op jit(solution)/shard_map/ppermute | solution.py:634
  67.8 1.5 %collective-permute-start.12 = (f32[3,4]{1,0:T(4,128)S(1)}, f32[3,4]{1,0:T(4,128)S(1)}, u32[]{:S(2)}, u32[]{:S(2)}) collective-permute-start(f32[3,4]{1,0:T(4,128)S(1)} %select_add_fusion.2), channel_id=1, source_target_pairs={{0,8},{4,12},{8,0},{12,4},{16,24},{20,28},{24,16},{28,20},{1,9},{5... | collective-permute-start | bytes 152 | tf_op jit(solution)/shard_map/ppermute | solution.py:634
  69.3 2.1 %collective-permute-done.12 = f32[3,4]{1,0:T(4,128)S(1)} collective-permute-done((f32[3,4]{1,0:T(4,128)S(1)}, f32[3,4]{1,0:T(4,128)S(1)}, u32[]{:S(2)}, u32[]{:S(2)}) %collective-permute-start.12) | collective-permute-done | bytes 80 | tf_op jit(solution)/shard_map/ppermute | solution.py:634
  72.7 1.4 %collective-permute-done.14.refs_4_ = f32[2,32,1280]{2,1,0:T(8,128)S(1)} collective-permute-done((f32[2,32,1280]{2,1,0:T(8,128)S(1)}, f32[2,32,1280]{2,1,0:T(8,128)S(1)}, u32[]{:S(2)}, u32[]{:S(2)}) %collective-permute-start.14) | collective-permute-done | bytes 327712 | tf_op jit(solution)/shard_map/ppermute | solution.py:626
  74.1 0.9 %pad_maximum_fusion.1 = f32[4,32,1280]{2,1,0:T(8,128)} fusion(f32[1,32,1280]{2,1,0:T(8,128)S(1)} %slice_select_fusion, f32[1,32,1280]{2,1,0:T(8,128)S(1)} %slice.99, f32[1,32,1280]{2,1,0:T(8,128)S(1)} %bitcast.29, f32[1,32,1280]{2,1,0:T(8,128)S(1)} %bitcast.28), kind=kLoop, calls=%fused_computation.1 | loop fusion | flops 491520 | bytes 1310720 | tf_op jit(solution)/shard_map/stack | solution.py:637
  75.0 0.9 %collective-permute-done.13 = f32[3,4]{1,0:T(4,128)S(1)} collective-permute-done((f32[3,4]{1,0:T(4,128)S(1)}, f32[3,4]{1,0:T(4,128)S(1)}, u32[]{:S(2)}, u32[]{:S(2)}) %collective-permute-start.13) | collective-permute-done | bytes 80 | tf_op jit(solution)/shard_map/ppermute | solution.py:634
  76.8 2.0 %collective-permute-start.16 = (f32[4,6]{1,0:T(4,128)S(1)}, f32[4,6]{1,0:T(4,128)S(1)}, u32[]{:S(2)}, u32[]{:S(2)}) collective-permute-start(f32[4,6]{1,0:T(4,128)S(1)} %pad_maximum_fusion.7), channel_id=1, source_target_pairs={{0,2},{1,3},{2,0},{3,1},{4,6},{5,7},{6,4},{7,5},{8,10},{9,11},{10,... | collective-permute-start | bytes 296 | tf_op jit(solution)/shard_map/ppermute | solution.py:560
  78.9 1.5 %collective-permute-done.16 = f32[4,6]{1,0:T(4,128)S(1)} collective-permute-done((f32[4,6]{1,0:T(4,128)S(1)}, f32[4,6]{1,0:T(4,128)S(1)}, u32[]{:S(2)}, u32[]{:S(2)}) %collective-permute-start.16) | collective-permute-done | bytes 128 | tf_op jit(solution)/shard_map/ppermute | solution.py:560
  80.4 1.5 %collective-permute-done.17 = f32[4,6]{1,0:T(4,128)S(1)} collective-permute-done((f32[4,6]{1,0:T(4,128)S(1)}, f32[4,6]{1,0:T(4,128)S(1)}, u32[]{:S(2)}, u32[]{:S(2)}) %collective-permute-start.17) | collective-permute-done | bytes 128 | tf_op jit(solution)/shard_map/ppermute | solution.py:560
  81.9 3.5 %combine.1 = (f32[32,1280]{1,0:T(8,128)}, f32[32,1280]{1,0:T(8,128)}, f32[4,32,1280]{2,1,0:T(8,128)}) custom-call(s32[1]{0:T(128)} %bitcast.place_ref, f32[16,6]{1,0:T(8,128)S(1)} %bitcast.32, f32[40,32,128]{2,1,0:T(8,128)S(1)} %get-tuple-element.41.refs_2_.refs_3_.mask_ref, f32[4,32,1280]{2,1,0:T(8,128)S(1)} %get-tuple-element.71.refs_0_, ...), custom_call_target="tpu_custom_call" | custom-call | tf_op jit(solution)/shard_map/combine/pallas_call | solution.py:518
  (78 shorter events, 3.8 us)
Async XLA Ops:
  0.6 16.5 %copy-start = (f32[4,4096]{1,0:T(4,128)S(1)}, f32[4,4096]{1,0:T(4,128)}, u32[]{:S(2)}) copy-start(f32[4,4096]{1,0:T(4,128)} %param.17) | copy-start | bytes 196612
  2.6 14.4 %collective-permute-start.1 = (bf16[16,5120]{1,0:T(8,128)(2,1)S(1)}, bf16[16,5120]{1,0:T(8,128)(2,1)S(1)}, u32[]{:S(2)}, u32[]{:S(2)}) collective-permute-start(bf16[16,5120]{1,0:T(8,128)(2,1)S(1)} %constant_dynamic-slice_fusion), channel_id=1, source_target_pairs={{0,4},{4,8},{8,12},{12,16},{16,20},{20,24},{24,28},{1,5},{5,9},{9,... | collective-permute-start | bytes 491528 | tf_op jit(solution)/shard_map/ppermute | solution.py:568
  7.5 9.5 %collective-permute-start.2 = (bf16[16,5120]{1,0:T(8,128)(2,1)S(1)}, bf16[16,5120]{1,0:T(8,128)(2,1)S(1)}, u32[]{:S(2)}, u32[]{:S(2)}) collective-permute-start(bf16[16,5120]{1,0:T(8,128)(2,1)S(1)} %constant_dynamic-slice_fusion), channel_id=1, source_target_pairs={{4,0},{8,4},{12,8},{16,12},{20,16},{24,20},{28,24},{5,1},{9,5},{13... | collective-permute-start | bytes 491528 | tf_op jit(solution)/shard_map/ppermute | solution.py:568
  8.8 13.2 %collective-permute-start = (bf16[4,1,112,128]{3,2,1,0:T(8,128)(2,1)S(1)}, bf16[4,1,112,128]{3,2,1,0:T(8,128)(2,1)S(1)}, u32[]{:S(2)}, u32[]{:S(2)}) collective-permute-start(bf16[4,1,112,128]{3,2,1,0:T(8,128)(2,1)S(1)} %pad.4), channel_id=1, source_target_pairs={{0,16},{4,20},{8,24},{12,28},{16,0},{20,4},{24,8},{28,12},{1,17},{... | collective-permute-start | bytes 344072 | tf_op jit(solution)/shard_map/ppermute | solution.py:529
  13.5 1.0 %copy-start.1 = (bf16[32,5120]{1,0:T(8,128)(2,1)S(1)}, bf16[32,5120]{1,0:T(8,128)(2,1)}, u32[]{:S(2)}) copy-start(bf16[32,5120]{1,0:T(8,128)(2,1)} %refs_0_.1) | copy-start | bytes 983044
  15.4 1.8 %copy-start.13 = (s32[4]{0:T(128)S(1)}, s32[4]{0:T(128)}, u32[]{:S(2)}) copy-start(s32[4]{0:T(128)} %param.18) | copy-start | bytes 52
  15.4 6.7 %copy-start.4 = (bf16[240,512]{1,0:T(8,128)(2,1)S(1)}, bf16[240,512]{1,0:T(8,128)(2,1)}, u32[]{:S(2)}) copy-start(bf16[240,512]{1,0:T(8,128)(2,1)} %constant.52.clone.refs_1_.refs_3_) | copy-start | bytes 737284
  17.1 5.0 %collective-permute-start.3 = (bf16[2,16,5120]{2,1,0:T(8,128)(2,1)S(1)}, bf16[2,16,5120]{2,1,0:T(8,128)(2,1)S(1)}, u32[]{:S(2)}, u32[]{:S(2)}) collective-permute-start(bf16[2,16,5120]{2,1,0:T(8,128)(2,1)S(1)} %pad_maximum_fusion.3.refs_1_), channel_id=1, source_target_pairs={{0,1},{1,0},{2,3},{3,2},{4,5},{5,4},{6,7},{7,6},{8,9},{9,8},{10,11... | collective-permute-start | bytes 983048 | tf_op jit(solution)/shard_map/ppermute | solution.py:595
  22.0 8.4 %copy-start.2 = (s32[32,80]{1,0:T(8,128)S(1)}, s32[32,80]{1,0:T(8,128)}, u32[]{:S(2)}) copy-start(s32[32,80]{1,0:T(8,128)} %valid_ref.1) | copy-start | bytes 30724
  22.0 8.4 %copy-start.9 = (bf16[80,240]{1,0:T(8,128)(2,1)S(1)}, bf16[80,240]{1,0:T(8,128)(2,1)}, u32[]{:S(2)}) copy-start(bf16[80,240]{1,0:T(8,128)(2,1)} %constant.53.clone.x_ref) | copy-start | bytes 115204
  22.0 8.4 %copy-start.11 = (bf16[48,256]{1,0:T(8,128)(2,1)S(1)}, bf16[48,256]{1,0:T(8,128)(2,1)}, u32[]{:S(2)}) copy-start(bf16[48,256]{1,0:T(8,128)(2,1)} %constant.54.clone.tz_ref) | copy-start | bytes 73732
  22.0 6.1 %collective-permute-start.4 = (bf16[4,2,112,128]{3,2,1,0:T(8,128)(2,1)S(1)}, bf16[4,2,112,128]{3,2,1,0:T(8,128)(2,1)S(1)}, u32[]{:S(2)}, u32[]{:S(2)}) collective-permute-start(bf16[4,2,112,128]{3,2,1,0:T(8,128)(2,1)S(1)} %pad_maximum_fusion.4), channel_id=1, source_target_pairs={{0,8},{4,12},{8,0},{12,4},{16,24},{20,28},{24,16},{28,20},{1,9},{5... | collective-permute-start | bytes 688136 | tf_op jit(solution)/shard_map/ppermute | solution.py:529
  28.2 6.0 %copy-start.5 = (bf16[256,256]{1,0:T(8,128)(2,1)S(1)}, bf16[256,256]{1,0:T(8,128)(2,1)}, u32[]{:S(2)}) copy-start(bf16[256,256]{1,0:T(8,128)(2,1)} %constant.60.clone.refs_10_.refs_11_) | copy-start | bytes 393220
  28.2 6.0 %copy-start.6 = (bf16[160,208]{1,0:T(8,128)(2,1)S(1)}, bf16[160,208]{1,0:T(8,128)(2,1)}, u32[]{:S(2)}) copy-start(bf16[160,208]{1,0:T(8,128)(2,1)} %constant.59.clone.refs_9_.refs_10_) | copy-start | bytes 199684
  28.2 6.0 %copy-start.7 = (bf16[112,144]{1,0:T(8,128)(2,1)S(1)}, bf16[112,144]{1,0:T(8,128)(2,1)}, u32[]{:S(2)}) copy-start(bf16[112,144]{1,0:T(8,128)(2,1)} %constant.56.clone.refs_6_.refs_7_) | copy-start | bytes 96772
  28.3 6.0 %copy-start.8 = (bf16[80,144]{1,0:T(8,128)(2,1)S(1)}, bf16[80,144]{1,0:T(8,128)(2,1)}, u32[]{:S(2)}) copy-start(bf16[80,144]{1,0:T(8,128)(2,1)} %constant.57.clone.refs_7_.refs_8_) | copy-start | bytes 69124
  28.3 6.0 %copy-start.10 = (bf16[64,160]{1,0:T(8,128)(2,1)S(1)}, bf16[64,160]{1,0:T(8,128)(2,1)}, u32[]{:S(2)}) copy-start(bf16[64,160]{1,0:T(8,128)(2,1)} %constant.58.clone.refs_8_.refs_9_) | copy-start | bytes 61444
  28.3 6.0 %copy-start.12 = (f32[8,128]{1,0:T(8,128)S(1)}, f32[8,128]{1,0:T(8,128)}, u32[]{:S(2)}) copy-start(f32[8,128]{1,0:T(8,128)} %constant.55.clone.refs_5_.refs_6_) | copy-start | bytes 12292
  28.3 6.0 %collective-permute-start.5 = (bf16[1,4,112,128]{3,2,1,0:T(8,128)(2,1)S(1)}, bf16[1,4,112,128]{3,2,1,0:T(8,128)(2,1)S(1)}, u32[]{:S(2)}, u32[]{:S(2)}) collective-permute-start(bf16[1,4,112,128]{3,2,1,0:T(8,128)(2,1)S(1)} %slice.110), channel_id=1, source_target_pairs={{0,4},{4,0},{8,12},{12,8},{16,20},{20,16},{24,28},{28,24},{1,5},{5... | collective-permute-start | bytes 344072 | tf_op jit(solution)/shard_map/ppermute | solution.py:529
  29.9 12.1 %collective-permute-start.6 = (bf16[3,4,112,128]{3,2,1,0:T(8,128)(2,1)S(1)}, bf16[3,4,112,128]{3,2,1,0:T(8,128)(2,1)S(1)}, u32[]{:S(2)}, u32[]{:S(2)}) collective-permute-start(bf16[3,4,112,128]{3,2,1,0:T(8,128)(2,1)S(1)} %slice.111), channel_id=1, source_target_pairs={{0,4},{4,0},{8,12},{12,8},{16,20},{20,16},{24,28},{28,24},{1,5},{5... | collective-permute-start | bytes 1032200 | tf_op jit(solution)/shard_map/ppermute | solution.py:529
  40.3 8.9 %collective-permute-start.7 = (f32[2,32,1280]{2,1,0:T(8,128)S(1)}, f32[2,32,1280]{2,1,0:T(8,128)S(1)}, u32[]{:S(2)}, u32[]{:S(2)}) collective-permute-start(f32[2,32,1280]{2,1,0:T(8,128)S(1)} %get-tuple-element.47), channel_id=1, source_target_pairs={{0,2},{1,3},{2,0},{3,1},{4,6},{5,7},{6,4},{7,5},{8,10},{9,11},{10,... | collective-permute-start | bytes 983048 | tf_op jit(solution)/shard_map/ppermute | solution.py:626
  47.9 9.8 %collective-permute-start.8 = (f32[2,32,1280]{2,1,0:T(8,128)S(1)}, f32[2,32,1280]{2,1,0:T(8,128)S(1)}, u32[]{:S(2)}, u32[]{:S(2)}) collective-permute-start(f32[2,32,1280]{2,1,0:T(8,128)S(1)} %get-tuple-element.53), channel_id=1, source_target_pairs={{0,2},{1,3},{2,0},{3,1},{4,6},{5,7},{6,4},{7,5},{8,10},{9,11},{10,... | collective-permute-start | bytes 983048 | tf_op jit(solution)/shard_map/ppermute | solution.py:626
  55.4 8.6 %collective-permute-start.9 = (f32[2,32,1280]{2,1,0:T(8,128)S(1)}, f32[2,32,1280]{2,1,0:T(8,128)S(1)}, u32[]{:S(2)}, u32[]{:S(2)}) collective-permute-start(f32[2,32,1280]{2,1,0:T(8,128)S(1)} %get-tuple-element.59), channel_id=1, source_target_pairs={{0,2},{1,3},{2,0},{3,1},{4,6},{5,7},{6,4},{7,5},{8,10},{9,11},{10,... | collective-permute-start | bytes 983048 | tf_op jit(solution)/shard_map/ppermute | solution.py:626
  57.8 6.3 %collective-permute-start.10 = (f32[4,32,1280]{2,1,0:T(8,128)S(1)}, f32[4,32,1280]{2,1,0:T(8,128)S(1)}, u32[]{:S(2)}, u32[]{:S(2)}) collective-permute-start(f32[4,32,1280]{2,1,0:T(8,128)S(1)} %pad_maximum_fusion), channel_id=1, source_target_pairs={{0,1},{1,0},{2,3},{3,2},{4,5},{5,4},{6,7},{7,6},{8,9},{9,8},{10,11... | collective-permute-start | bytes 1966088 | tf_op jit(solution)/shard_map/ppermute | solution.py:629
  63.9 10.2 %collective-permute-start.14 = (f32[2,32,1280]{2,1,0:T(8,128)S(1)}, f32[2,32,1280]{2,1,0:T(8,128)S(1)}, u32[]{:S(2)}, u32[]{:S(2)}) collective-permute-start(f32[2,32,1280]{2,1,0:T(8,128)S(1)} %get-tuple-element.69), channel_id=1, source_target_pairs={{0,2},{1,3},{2,0},{3,1},{4,6},{5,7},{6,4},{7,5},{8,10},{9,11},{10,... | collective-permute-start | bytes 983048 | tf_op jit(solution)/shard_map/ppermute | solution.py:626
  64.1 3.6 %collective-permute-start.11 = (f32[3,4]{1,0:T(4,128)S(1)}, f32[3,4]{1,0:T(4,128)S(1)}, u32[]{:S(2)}, u32[]{:S(2)}) collective-permute-start(f32[3,4]{1,0:T(4,128)S(1)} %pad_maximum_fusion.6), channel_id=1, source_target_pairs={{0,4},{4,0},{8,12},{12,8},{16,20},{20,16},{24,28},{28,24},{1,5},{5... | collective-permute-start | bytes 152 | tf_op jit(solution)/shard_map/ppermute | solution.py:634
  67.8 3.6 %collective-permute-start.12 = (f32[3,4]{1,0:T(4,128)S(1)}, f32[3,4]{1,0:T(4,128)S(1)}, u32[]{:S(2)}, u32[]{:S(2)}) collective-permute-start(f32[3,4]{1,0:T(4,128)S(1)} %select_add_fusion.2), channel_id=1, source_target_pairs={{0,8},{4,12},{8,0},{12,4},{16,24},{20,28},{24,16},{28,20},{1,9},{5... | collective-permute-start | bytes 152 | tf_op jit(solution)/shard_map/ppermute | solution.py:634
  71.4 4.5 %collective-permute-start.13 = (f32[3,4]{1,0:T(4,128)S(1)}, f32[3,4]{1,0:T(4,128)S(1)}, u32[]{:S(2)}, u32[]{:S(2)}) collective-permute-start(f32[3,4]{1,0:T(4,128)S(1)} %select_add_fusion.1), channel_id=1, source_target_pairs={{0,16},{4,20},{8,24},{12,28},{16,0},{20,4},{24,8},{28,12},{1,17},{... | collective-permute-start | bytes 152 | tf_op jit(solution)/shard_map/ppermute | solution.py:634
  75.9 6.0 %collective-permute-start.18 = (f32[4,32,1280]{2,1,0:T(8,128)}, f32[4,32,1280]{2,1,0:T(8,128)}, u32[]{:S(2)}, u32[]{:S(2)}) collective-permute-start(f32[4,32,1280]{2,1,0:T(8,128)} %pad_maximum_fusion.1), channel_id=1, source_target_pairs={{0,1},{1,0},{2,3},{3,2},{4,5},{5,4},{6,7},{7,6},{8,9},{9,8},{10,11... | collective-permute-start | bytes 1966088 | tf_op jit(solution)/shard_map/ppermute | solution.py:646
  76.3 2.6 %collective-permute-start.15 = (f32[4,6]{1,0:T(4,128)S(1)}, f32[4,6]{1,0:T(4,128)S(1)}, u32[]{:S(2)}, u32[]{:S(2)}) collective-permute-start(f32[4,6]{1,0:T(4,128)S(1)} %pad_maximum_fusion.7), channel_id=1, source_target_pairs={{0,1},{1,0},{2,3},{3,2},{4,5},{5,4},{6,7},{7,6},{8,9},{9,8},{10,11... | collective-permute-start | bytes 296 | tf_op jit(solution)/shard_map/ppermute | solution.py:560
  76.8 3.6 %collective-permute-start.16 = (f32[4,6]{1,0:T(4,128)S(1)}, f32[4,6]{1,0:T(4,128)S(1)}, u32[]{:S(2)}, u32[]{:S(2)}) collective-permute-start(f32[4,6]{1,0:T(4,128)S(1)} %pad_maximum_fusion.7), channel_id=1, source_target_pairs={{0,2},{1,3},{2,0},{3,1},{4,6},{5,7},{6,4},{7,5},{8,10},{9,11},{10,... | collective-permute-start | bytes 296 | tf_op jit(solution)/shard_map/ppermute | solution.py:560
  78.9 3.0 %collective-permute-start.17 = (f32[4,6]{1,0:T(4,128)S(1)}, f32[4,6]{1,0:T(4,128)S(1)}, u32[]{:S(2)}, u32[]{:S(2)}) collective-permute-start(f32[4,6]{1,0:T(4,128)S(1)} %pad_maximum_fusion.7), channel_id=1, source_target_pairs={{0,3},{1,2},{2,1},{3,0},{4,7},{5,6},{6,5},{7,4},{8,11},{9,10},{10,... | collective-permute-start | bytes 296 | tf_op jit(solution)/shard_map/ppermute | solution.py:560
  (1 other events, 0.9 us)

commit v14 on v13

--- a/solution.py
+++ b/solution.py
@@ -523,6 +523,25 @@
         compiler_params=pltpu.CompilerParams(vmem_limit_bytes=4 * 1024 * 1024),
         name="combine",
     )(place, coefs, mask, *arrays)
+
+
+def pack_kernel(after_ref, *refs):
+    *sources, out_ref = refs
+    for i, source in enumerate(sources):
+        out_ref[i] = source[...] if len(source.shape) == 2 else source[1]
+
+
+def pack(after, sides, fars):
+    vmem = pl.BlockSpec(memory_space=pltpu.VMEM)
+    count = len(sides) + len(fars)
+    return pl.pallas_call(
+        pack_kernel,
+        out_shape=jax.ShapeDtypeStruct((count,) + sides[0].shape, F32),
+        in_specs=[pl.BlockSpec(memory_space=pl.ANY)] + [vmem] * count,
+        out_specs=vmem,
+        compiler_params=pltpu.CompilerParams(vmem_limit_bytes=8 * 1024 * 1024),
+        name="pack",
+    )(after, *sides, *fars)
 
 
 def swap_blocks(block, axis, step):
@@ -633,8 +652,7 @@
     while step < tiles:
         partner = lax.ppermute(state, "tile", [(i, i ^ step) for i in range(tiles)])
         if step * 4 == tiles:
-            late = jnp.where(partner[0, 0] >= 0.0, fars[rots - 1][1], 0.0)
-            last = jnp.stack([sides[rots - 2], sides[rots - 1], fars[rots - 2][1], late])
+            last = pack(partner, sides[rots - 2 :], fars[rots - 2 :])
         if step * 2 == tiles:
             partner, last = lax.optimization_barrier((partner, last))
         state = merge(state, partner)

time: 85.8 us -> 86.8 us (1.012)
  waiting for transfers between devices: 17.3 us -> 19.2 us
  other arithmetic: 1.58 us -> 0.67 us
    ppermute x4, waiting for transfers between devices: 2.1 us -> 3.2 us  [local(): fars.append(lax.ppermute(far, 'rot', far_swap))]
    unnamed x28 -> x32, local copies, waits for them, and re-layouts: 1.99 us -> 3.08 us
    another operation x1 -> x0, other arithmetic: 0.89 us -> none  [local(): jnp.stack([sides[rots - 2], sides[rots - 1], fars[rots - 2][1], late])]
  transfers between devices with their start and end apart: 19 -> 19, of which waited for: 9 -> 9; matrix products, arithmetic and copies ran while one was open for 4% -> 2% of each run, Pallas kernels for 37% -> 37%
where the time goes in v14:
time: 86.8 us; the launch traced here: 86.5 us
  Pallas kernels  35.3 us (41%)
  starting transfers between devices  23.5 us (27%)
  waiting for transfers between devices  19.2 us (22%)
  local copies, waits for them, and re-layouts  5.79 us (7%)
  between operations  1.72 us (2%)
    pallas_call x4, Pallas kernels, correlate(): pl.pallas_call(functools.partial(corr_kernel, dims, rot, entry), out_shap...  24.2 us
    ppermute x4, waiting for transfers between devices, swap_blocks(): lax.ppermute(block, axis, [(i, i ^ step) for i in range(lax.axis_size(axi...  7.24 us
    ppermute x4, starting transfers between devices, swap_blocks(): lax.ppermute(block, axis, [(i, i ^ step) for i in range(lax.axis_size(axi...  6.86 us
    ppermute x3, waiting for transfers between devices, local(): partner = lax.ppermute(state, 'tile', [(i, i ^ step) for i in range(tiles)])  5.79 us
    ppermute x1, starting transfers between devices, neighbours(): lax.ppermute(block, axis, forward)  4.85 us
    ppermute x4, starting transfers between devices, local(): fars.append(lax.ppermute(far, 'rot', far_swap))  4.49 us
    pallas_call x1, Pallas kernels, slab_x(): pl.pallas_call(functools.partial(slab_x_kernel, dims), out_shape=(jax.Sha...  3.87 us
    pallas_call x2, Pallas kernels, slab_rows(): pl.pallas_call(functools.partial(slab_rows_kernel, dims), out_shape=jax.S...  3.67 us
  transfers between devices with their start and end apart: 19, of which 9 were waited for; matrix products, arithmetic and copies ran while one was open for 2% of the time, Pallas kernels for 37%

profile of v14, /device:TPU:0, one launch (start us, length us, event | category | flops | bytes accessed | tf_op | source)
XLA Modules:
  0.0 86.5 jit_solution(10335426472093637600)
XLA Ops:
  0.7 1.0 %reshape.73 = bf16[4,1,108,128]{3,2,0,1:T(8,128)(2,1)S(1)} reshape(bf16[4,13824]{1,0:T(4,128)(2,1)} %param.15) | data formatting | bytes 221184 | tf_op jit(solution)/shard_map/reshape | solution.py:604
  1.7 0.9 %constant_dynamic-slice_fusion = bf16[16,5120]{1,0:T(8,128)(2,1)S(1)} fusion(bf16[32,5120]{1,0:T(8,128)(2,1)} %refs_0_.1, s32[]{:T(128)S(6)} %select_n.21), kind=kLoop, calls=%fused_computation.22 | loop fusion | bytes 327684 | tf_op jit(solution)/shard_map/dynamic_slice | solution.py:611
  2.6 4.9 %collective-permute-start.1 = (bf16[16,5120]{1,0:T(8,128)(2,1)S(1)}, bf16[16,5120]{1,0:T(8,128)(2,1)S(1)}, u32[]{:S(2)}, u32[]{:S(2)}) collective-permute-start(bf16[16,5120]{1,0:T(8,128)(2,1)S(1)} %constant_dynamic-slice_fusion), channel_id=1, source_target_pairs={{0,4},{4,8},{8,12},{12,16},{16,20},{20,24},{24,28},{1,5},{5,9},{9,... | collective-permute-start | bytes 491528 | tf_op jit(solution)/shard_map/ppermute | solution.py:587
  7.5 1.3 %collective-permute-start.2 = (bf16[16,5120]{1,0:T(8,128)(2,1)S(1)}, bf16[16,5120]{1,0:T(8,128)(2,1)S(1)}, u32[]{:S(2)}, u32[]{:S(2)}) collective-permute-start(bf16[16,5120]{1,0:T(8,128)(2,1)S(1)} %constant_dynamic-slice_fusion), channel_id=1, source_target_pairs={{4,0},{8,4},{12,8},{16,12},{20,16},{24,20},{28,24},{5,1},{9,5},{13... | collective-permute-start | bytes 491528 | tf_op jit(solution)/shard_map/ppermute | solution.py:587
  8.8 4.7 %collective-permute-start = (bf16[4,1,112,128]{3,2,1,0:T(8,128)(2,1)S(1)}, bf16[4,1,112,128]{3,2,1,0:T(8,128)(2,1)S(1)}, u32[]{:S(2)}, u32[]{:S(2)}) collective-permute-start(bf16[4,1,112,128]{3,2,1,0:T(8,128)(2,1)S(1)} %pad.4), channel_id=1, source_target_pairs={{0,16},{4,20},{8,24},{12,28},{16,0},{20,4},{24,8},{28,12},{1,17},{... | collective-permute-start | bytes 344072 | tf_op jit(solution)/shard_map/ppermute | solution.py:548
  13.5 1.0 %copy-done.3 = bf16[32,5120]{1,0:T(8,128)(2,1)S(1)} copy-done((bf16[32,5120]{1,0:T(8,128)(2,1)S(1)}, bf16[32,5120]{1,0:T(8,128)(2,1)}, u32[]{:S(2)}) %copy-start.3) | copy-done | bytes 327704
  14.4 0.9 %copy-done.5 = bf16[240,512]{1,0:T(8,128)(2,1)S(1)} copy-done((bf16[240,512]{1,0:T(8,128)(2,1)S(1)}, bf16[240,512]{1,0:T(8,128)(2,1)}, u32[]{:S(2)}) %copy-start.5) | copy-done | bytes 245784
  15.4 1.6 %slab_own.1.refs_0_ = f32[3616,128]{1,0:T(8,128)S(1)} custom-call(s32[1]{0:T(128)} %bitcast.place_ref, bf16[32,5120]{1,0:T(8,128)(2,1)S(1)} %copy-done.3, bf16[240,512]{1,0:T(8,128)(2,1)S(1)} %copy-done.5), custom_call_target="tpu_custom_call" | custom-call | flops 3200000000 | bytes 1000000 | tf_op jit(solution)/shard_map/slab_own/pallas_call | solution.py:248
  17.4 4.5 %collective-permute-done = bf16[4,1,112,128]{3,2,1,0:T(8,128)(2,1)S(1)} collective-permute-done((bf16[4,1,112,128]{3,2,1,0:T(8,128)(2,1)S(1)}, bf16[4,1,112,128]{3,2,1,0:T(8,128)(2,1)S(1)}, u32[]{:S(2)}, u32[]{:S(2)}) %collective-permute-start) | collective-permute-done | bytes 114720 | tf_op jit(solution)/shard_map/ppermute | solution.py:548
  22.1 2.1 %slab_halo.1.rows_ref = f32[9040,128]{1,0:T(8,128)S(1)} custom-call(s32[1]{0:T(128)} %bitcast.place_ref, f32[3616,128]{1,0:T(8,128)S(1)} %slab_own.1.refs_0_, bf16[2,16,5120]{2,1,0:T(8,128)(2,1)S(1)} %pad_maximum_fusion.2.refs_1_, bf16[2,16,5120]{2,1,0:T(8,128)(2,1)S(1)} %collective-permute-done.3.refs_2_, bf16[240,512]{1,0:T(8,128)(2,1)S(1)} %copy-done.6), custom_call_target="tpu_custom_call" | custom-call | flops 4800000000 | bytes 1000000 | tf_op jit(solution)/shard_map/slab_halo/pallas_call | solution.py:248
  25.4 2.7 %collective-permute-done.4 = bf16[4,2,112,128]{3,2,1,0:T(8,128)(2,1)S(1)} collective-permute-done((bf16[4,2,112,128]{3,2,1,0:T(8,128)(2,1)S(1)}, bf16[4,2,112,128]{3,2,1,0:T(8,128)(2,1)S(1)}, u32[]{:S(2)}, u32[]{:S(2)}) %collective-permute-start.4) | collective-permute-done | bytes 229408 | tf_op jit(solution)/shard_map/ppermute | solution.py:548
  28.3 1.6 %collective-permute-start.5 = (bf16[1,4,112,128]{3,2,1,0:T(8,128)(2,1)S(1)}, bf16[1,4,112,128]{3,2,1,0:T(8,128)(2,1)S(1)}, u32[]{:S(2)}, u32[]{:S(2)}) collective-permute-start(bf16[1,4,112,128]{3,2,1,0:T(8,128)(2,1)S(1)} %slice.98), channel_id=1, source_target_pairs={{0,4},{4,0},{8,12},{12,8},{16,20},{20,16},{24,28},{28,24},{1,5},{5... | collective-permute-start | bytes 344072 | tf_op jit(solution)/shard_map/ppermute | solution.py:548
  30.4 3.9 %slab_x.1 = (f32[13,2,80,1024]{3,2,1,0:T(8,128)S(1)}, f32[40,32,128]{2,1,0:T(8,128)S(1)}, bf16[8,256,256]{2,1,0:T(8,128)(2,1)S(1)}) custom-call(f32[9040,128]{1,0:T(8,128)S(1)} %slab_halo.1.rows_ref, bf16[80,240]{1,0:T(8,128)(2,1)S(1)} %copy-done.11, s32[32,80]{1,0:T(8,128)S(1)} %copy-done.4, bf16[48,256]{1,0:T(8,128)(2,1)S(1)} %copy-done.13), custom_call_target="tpu_custom_call" | custom-call | flops 5000000000 | bytes 1000000 | tf_op jit(solution)/shard_map/slab_x/pallas_call | solution.py:301
  34.3 6.0 %correlate.4 = (f32[1,32,1280]{2,1,0:T(8,128)S(1)}, f32[32,1280]{1,0:T(8,128)S(1)}, f32[2,32,1280]{2,1,0:T(8,128)S(1)}, f32[8,128]{1,0:T(8,128)S(1)}) custom-call(s32[1]{0:T(128)} %bitcast.place_ref, s32[1]{0:T(128)} %bitcast.1.tile_ref, bf16[4,4,112,128]{3,2,1,0:T(8,128)(2,1)S(1)} %pad_maximum_fusion.1.refs_0_.refs_1_, ...), custom_call_target="tpu_custom_call" | custom-call | flops 15000000512 | bytes 10000000 | tf_op jit(solution)/shard_map/correlate/pallas_call | solution.py:451
  40.3 1.6 %collective-permute-start.7 = (f32[2,32,1280]{2,1,0:T(8,128)S(1)}, f32[2,32,1280]{2,1,0:T(8,128)S(1)}, u32[]{:S(2)}, u32[]{:S(2)}) collective-permute-start(f32[2,32,1280]{2,1,0:T(8,128)S(1)} %get-tuple-element.47), channel_id=1, source_target_pairs={{0,2},{1,3},{2,0},{3,1},{4,6},{5,7},{6,4},{7,5},{8,10},{9,11},{10,... | collective-permute-start | bytes 983048 | tf_op jit(solution)/shard_map/ppermute | solution.py:645
  41.9 6.0 %correlate.5 = (f32[2,32,1280]{2,1,0:T(8,128)S(1)}, f32[32,1280]{1,0:T(8,128)S(1)}, f32[2,32,1280]{2,1,0:T(8,128)S(1)}, f32[8,128]{1,0:T(8,128)S(1)}) custom-call(s32[1]{0:T(128)} %bitcast.place_ref, s32[1]{0:T(128)} %bitcast.1.tile_ref, f32[1,32,1280]{2,1,0:T(8,128)S(1)} %get-tuple-element.45.refs_0_, ...), custom_call_target="tpu_custom_call" | custom-call | flops 15000000512 | bytes 10000000 | tf_op jit(solution)/shard_map/correlate/pallas_call | solution.py:451
  47.9 0.6 collective-permute-start.8
  48.5 0.7 collective-permute-done.7.refs_1_
  49.2 6.2 %correlate.6 = (f32[3,32,1280]{2,1,0:T(8,128)S(1)}, f32[32,1280]{1,0:T(8,128)S(1)}, f32[2,32,1280]{2,1,0:T(8,128)S(1)}, f32[8,128]{1,0:T(8,128)S(1)}) custom-call(s32[1]{0:T(128)} %bitcast.place_ref, s32[1]{0:T(128)} %bitcast.1.tile_ref, f32[2,32,1280]{2,1,0:T(8,128)S(1)} %get-tuple-element.51.refs_0_, ...), custom_call_target="tpu_custom_call" | custom-call | flops 15000000512 | bytes 10000000 | tf_op jit(solution)/shard_map/correlate/pallas_call | solution.py:451
  55.4 2.2 %collective-permute-start.9 = (f32[2,32,1280]{2,1,0:T(8,128)S(1)}, f32[2,32,1280]{2,1,0:T(8,128)S(1)}, u32[]{:S(2)}, u32[]{:S(2)}) collective-permute-start(f32[2,32,1280]{2,1,0:T(8,128)S(1)} %get-tuple-element.59), channel_id=1, source_target_pairs={{0,2},{1,3},{2,0},{3,1},{4,6},{5,7},{6,4},{7,5},{8,10},{9,11},{10,... | collective-permute-start | bytes 983048 | tf_op jit(solution)/shard_map/ppermute | solution.py:645
  57.8 6.0 %correlate.7 = (f32[4,32,1280]{2,1,0:T(8,128)S(1)}, f32[32,1280]{1,0:T(8,128)S(1)}, f32[2,32,1280]{2,1,0:T(8,128)S(1)}, f32[8,128]{1,0:T(8,128)S(1)}) custom-call(s32[1]{0:T(128)} %bitcast.place_ref, s32[1]{0:T(128)} %bitcast.1.tile_ref, f32[3,32,1280]{2,1,0:T(8,128)S(1)} %get-tuple-element.57.refs_0_, ...), custom_call_target="tpu_custom_call" | custom-call | flops 15000000512 | bytes 10000000 | tf_op jit(solution)/shard_map/correlate/pallas_call | solution.py:451
  64.1 1.7 %collective-permute-start.11 = (f32[3,4]{1,0:T(4,128)S(1)}, f32[3,4]{1,0:T(4,128)S(1)}, u32[]{:S(2)}, u32[]{:S(2)}) collective-permute-start(f32[3,4]{1,0:T(4,128)S(1)} %pad_maximum_fusion.5), channel_id=1, source_target_pairs={{0,4},{4,0},{8,12},{12,8},{16,20},{20,16},{24,28},{28,24},{1,5},{5... | collective-permute-start | bytes 152 | tf_op jit(solution)/shard_map/ppermute | solution.py:653
  65.8 1.9 %collective-permute-done.11 = f32[3,4]{1,0:T(4,128)S(1)} collective-permute-done((f32[3,4]{1,0:T(4,128)S(1)}, f32[3,4]{1,0:T(4,128)S(1)}, u32[]{:S(2)}, u32[]{:S(2)}) %collective-permute-start.11) | collective-permute-done | bytes 80 | tf_op jit(solution)/shard_map/ppermute | solution.py:653
  67.8 1.5 %collective-permute-start.12 = (f32[3,4]{1,0:T(4,128)S(1)}, f32[3,4]{1,0:T(4,128)S(1)}, u32[]{:S(2)}, u32[]{:S(2)}) collective-permute-start(f32[3,4]{1,0:T(4,128)S(1)} %select_add_fusion.2), channel_id=1, source_target_pairs={{0,8},{4,12},{8,0},{12,4},{16,24},{20,28},{24,16},{28,20},{1,9},{5... | collective-permute-start | bytes 152 | tf_op jit(solution)/shard_map/ppermute | solution.py:653
  69.3 2.0 %collective-permute-done.12.after_ref = f32[3,4]{1,0:T(4,128)S(1)} collective-permute-done((f32[3,4]{1,0:T(4,128)S(1)}, f32[3,4]{1,0:T(4,128)S(1)}, u32[]{:S(2)}, u32[]{:S(2)}) %collective-permute-start.12) | collective-permute-done | bytes 80 | tf_op jit(solution)/shard_map/ppermute | solution.py:653
  71.5 2.5 %collective-permute-done.14.refs_3_.refs_4_ = f32[2,32,1280]{2,1,0:T(8,128)S(1)} collective-permute-done((f32[2,32,1280]{2,1,0:T(8,128)S(1)}, f32[2,32,1280]{2,1,0:T(8,128)S(1)}, u32[]{:S(2)}, u32[]{:S(2)}) %collective-permute-start.14) | collective-permute-done | bytes 327712 | tf_op jit(solution)/shard_map/ppermute | solution.py:645
  74.1 1.8 %collective-permute-done.13 = f32[3,4]{1,0:T(4,128)S(1)} collective-permute-done((f32[3,4]{1,0:T(4,128)S(1)}, f32[3,4]{1,0:T(4,128)S(1)}, u32[]{:S(2)}, u32[]{:S(2)}) %collective-permute-start.13) | collective-permute-done | bytes 80 | tf_op jit(solution)/shard_map/ppermute | solution.py:653
  76.8 2.0 %collective-permute-start.16 = (f32[4,6]{1,0:T(4,128)S(1)}, f32[4,6]{1,0:T(4,128)S(1)}, u32[]{:S(2)}, u32[]{:S(2)}) collective-permute-start(f32[4,6]{1,0:T(4,128)S(1)} %pad_maximum_fusion.6), channel_id=1, source_target_pairs={{0,2},{1,3},{2,0},{3,1},{4,6},{5,7},{6,4},{7,5},{8,10},{9,11},{10,... | collective-permute-start | bytes 296 | tf_op jit(solution)/shard_map/ppermute | solution.py:579
  78.9 1.5 %collective-permute-done.16 = f32[4,6]{1,0:T(4,128)S(1)} collective-permute-done((f32[4,6]{1,0:T(4,128)S(1)}, f32[4,6]{1,0:T(4,128)S(1)}, u32[]{:S(2)}, u32[]{:S(2)}) %collective-permute-start.16) | collective-permute-done | bytes 128 | tf_op jit(solution)/shard_map/ppermute | solution.py:579
  80.4 1.5 %collective-permute-done.17 = f32[4,6]{1,0:T(4,128)S(1)} collective-permute-done((f32[4,6]{1,0:T(4,128)S(1)}, f32[4,6]{1,0:T(4,128)S(1)}, u32[]{:S(2)}, u32[]{:S(2)}) %collective-permute-start.17) | collective-permute-done | bytes 128 | tf_op jit(solution)/shard_map/ppermute | solution.py:579
  81.9 1.1 %copy-done.2 = f32[4,32,1280]{2,1,0:T(8,128)S(1)} copy-done((f32[4,32,1280]{2,1,0:T(8,128)S(1)}, f32[4,32,1280]{2,1,0:T(8,128)}, u32[]{:S(2)}) %copy-start.2) | copy-done | bytes 655384
  83.0 3.5 %combine.1 = (f32[32,1280]{1,0:T(8,128)}, f32[32,1280]{1,0:T(8,128)}, f32[4,32,1280]{2,1,0:T(8,128)}) custom-call(s32[1]{0:T(128)} %bitcast.place_ref, f32[16,6]{1,0:T(8,128)S(1)} %bitcast.27, f32[40,32,128]{2,1,0:T(8,128)S(1)} %get-tuple-element.41.refs_2_.refs_3_.mask_ref, f32[4,32,1280]{2,1,0:T(8,128)S(1)} %copy-done.2, ...), custom_call_target="tpu_custom_call" | custom-call | tf_op jit(solution)/shard_map/combine/pallas_call | solution.py:518
  (79 shorter events, 3.4 us)
Async XLA Ops:
  0.6 16.5 %copy-start = (f32[4,4096]{1,0:T(4,128)S(1)}, f32[4,4096]{1,0:T(4,128)}, u32[]{:S(2)}) copy-start(f32[4,4096]{1,0:T(4,128)} %param.17) | copy-start | bytes 196612
  2.6 14.4 %collective-permute-start.1 = (bf16[16,5120]{1,0:T(8,128)(2,1)S(1)}, bf16[16,5120]{1,0:T(8,128)(2,1)S(1)}, u32[]{:S(2)}, u32[]{:S(2)}) collective-permute-start(bf16[16,5120]{1,0:T(8,128)(2,1)S(1)} %constant_dynamic-slice_fusion), channel_id=1, source_target_pairs={{0,4},{4,8},{8,12},{12,16},{16,20},{20,24},{24,28},{1,5},{5,9},{9,... | collective-permute-start | bytes 491528 | tf_op jit(solution)/shard_map/ppermute | solution.py:587
  7.5 9.5 %collective-permute-start.2 = (bf16[16,5120]{1,0:T(8,128)(2,1)S(1)}, bf16[16,5120]{1,0:T(8,128)(2,1)S(1)}, u32[]{:S(2)}, u32[]{:S(2)}) collective-permute-start(bf16[16,5120]{1,0:T(8,128)(2,1)S(1)} %constant_dynamic-slice_fusion), channel_id=1, source_target_pairs={{4,0},{8,4},{12,8},{16,12},{20,16},{24,20},{28,24},{5,1},{9,5},{13... | collective-permute-start | bytes 491528 | tf_op jit(solution)/shard_map/ppermute | solution.py:587
  8.8 13.2 %collective-permute-start = (bf16[4,1,112,128]{3,2,1,0:T(8,128)(2,1)S(1)}, bf16[4,1,112,128]{3,2,1,0:T(8,128)(2,1)S(1)}, u32[]{:S(2)}, u32[]{:S(2)}) collective-permute-start(bf16[4,1,112,128]{3,2,1,0:T(8,128)(2,1)S(1)} %pad.4), channel_id=1, source_target_pairs={{0,16},{4,20},{8,24},{12,28},{16,0},{20,4},{24,8},{28,12},{1,17},{... | collective-permute-start | bytes 344072 | tf_op jit(solution)/shard_map/ppermute | solution.py:548
  15.4 1.8 %copy-start.15 = (s32[4]{0:T(128)S(1)}, s32[4]{0:T(128)}, u32[]{:S(2)}) copy-start(s32[4]{0:T(128)} %param.18) | copy-start | bytes 52
  15.4 6.7 %copy-start.6 = (bf16[240,512]{1,0:T(8,128)(2,1)S(1)}, bf16[240,512]{1,0:T(8,128)(2,1)}, u32[]{:S(2)}) copy-start(bf16[240,512]{1,0:T(8,128)(2,1)} %constant.50.clone.refs_1_.refs_3_) | copy-start | bytes 737284
  17.1 5.0 %collective-permute-start.3 = (bf16[2,16,5120]{2,1,0:T(8,128)(2,1)S(1)}, bf16[2,16,5120]{2,1,0:T(8,128)(2,1)S(1)}, u32[]{:S(2)}, u32[]{:S(2)}) collective-permute-start(bf16[2,16,5120]{2,1,0:T(8,128)(2,1)S(1)} %pad_maximum_fusion.2.refs_1_), channel_id=1, source_target_pairs={{0,1},{1,0},{2,3},{3,2},{4,5},{5,4},{6,7},{7,6},{8,9},{9,8},{10,11... | collective-permute-start | bytes 983048 | tf_op jit(solution)/shard_map/ppermute | solution.py:614
  22.0 8.4 %copy-start.4 = (s32[32,80]{1,0:T(8,128)S(1)}, s32[32,80]{1,0:T(8,128)}, u32[]{:S(2)}) copy-start(s32[32,80]{1,0:T(8,128)} %valid_ref.1) | copy-start | bytes 30724
  22.0 8.4 %copy-start.11 = (bf16[80,240]{1,0:T(8,128)(2,1)S(1)}, bf16[80,240]{1,0:T(8,128)(2,1)}, u32[]{:S(2)}) copy-start(bf16[80,240]{1,0:T(8,128)(2,1)} %constant.51.clone.x_ref) | copy-start | bytes 115204
  22.0 8.4 %copy-start.13 = (bf16[48,256]{1,0:T(8,128)(2,1)S(1)}, bf16[48,256]{1,0:T(8,128)(2,1)}, u32[]{:S(2)}) copy-start(bf16[48,256]{1,0:T(8,128)(2,1)} %constant.52.clone.tz_ref) | copy-start | bytes 73732
  22.0 6.1 %collective-permute-start.4 = (bf16[4,2,112,128]{3,2,1,0:T(8,128)(2,1)S(1)}, bf16[4,2,112,128]{3,2,1,0:T(8,128)(2,1)S(1)}, u32[]{:S(2)}, u32[]{:S(2)}) collective-permute-start(bf16[4,2,112,128]{3,2,1,0:T(8,128)(2,1)S(1)} %pad_maximum_fusion.3), channel_id=1, source_target_pairs={{0,8},{4,12},{8,0},{12,4},{16,24},{20,28},{24,16},{28,20},{1,9},{5... | collective-permute-start | bytes 688136 | tf_op jit(solution)/shard_map/ppermute | solution.py:548
  28.2 6.1 %copy-start.7 = (bf16[256,256]{1,0:T(8,128)(2,1)S(1)}, bf16[256,256]{1,0:T(8,128)(2,1)}, u32[]{:S(2)}) copy-start(bf16[256,256]{1,0:T(8,128)(2,1)} %constant.58.clone.refs_10_.refs_11_) | copy-start | bytes 393220
  28.2 6.1 %copy-start.8 = (bf16[160,208]{1,0:T(8,128)(2,1)S(1)}, bf16[160,208]{1,0:T(8,128)(2,1)}, u32[]{:S(2)}) copy-start(bf16[160,208]{1,0:T(8,128)(2,1)} %constant.57.clone.refs_9_.refs_10_) | copy-start | bytes 199684
  28.2 6.1 %copy-start.9 = (bf16[112,144]{1,0:T(8,128)(2,1)S(1)}, bf16[112,144]{1,0:T(8,128)(2,1)}, u32[]{:S(2)}) copy-start(bf16[112,144]{1,0:T(8,128)(2,1)} %constant.54.clone.refs_6_.refs_7_) | copy-start | bytes 96772
  28.3 6.1 %copy-start.10 = (bf16[80,144]{1,0:T(8,128)(2,1)S(1)}, bf16[80,144]{1,0:T(8,128)(2,1)}, u32[]{:S(2)}) copy-start(bf16[80,144]{1,0:T(8,128)(2,1)} %constant.55.clone.refs_7_.refs_8_) | copy-start | bytes 69124
  28.3 6.1 %copy-start.12 = (bf16[64,160]{1,0:T(8,128)(2,1)S(1)}, bf16[64,160]{1,0:T(8,128)(2,1)}, u32[]{:S(2)}) copy-start(bf16[64,160]{1,0:T(8,128)(2,1)} %constant.56.clone.refs_8_.refs_9_) | copy-start | bytes 61444
  28.3 6.1 %copy-start.14 = (f32[8,128]{1,0:T(8,128)S(1)}, f32[8,128]{1,0:T(8,128)}, u32[]{:S(2)}) copy-start(f32[8,128]{1,0:T(8,128)} %constant.53.clone.refs_5_.refs_6_) | copy-start | bytes 12292
  28.3 6.0 %collective-permute-start.5 = (bf16[1,4,112,128]{3,2,1,0:T(8,128)(2,1)S(1)}, bf16[1,4,112,128]{3,2,1,0:T(8,128)(2,1)S(1)}, u32[]{:S(2)}, u32[]{:S(2)}) collective-permute-start(bf16[1,4,112,128]{3,2,1,0:T(8,128)(2,1)S(1)} %slice.98), channel_id=1, source_target_pairs={{0,4},{4,0},{8,12},{12,8},{16,20},{20,16},{24,28},{28,24},{1,5},{5... | collective-permute-start | bytes 344072 | tf_op jit(solution)/shard_map/ppermute | solution.py:548
  29.9 12.1 %collective-permute-start.6 = (bf16[3,4,112,128]{3,2,1,0:T(8,128)(2,1)S(1)}, bf16[3,4,112,128]{3,2,1,0:T(8,128)(2,1)S(1)}, u32[]{:S(2)}, u32[]{:S(2)}) collective-permute-start(bf16[3,4,112,128]{3,2,1,0:T(8,128)(2,1)S(1)} %slice.99), channel_id=1, source_target_pairs={{0,4},{4,0},{8,12},{12,8},{16,20},{20,16},{24,28},{28,24},{1,5},{5... | collective-permute-start | bytes 1032200 | tf_op jit(solution)/shard_map/ppermute | solution.py:548
  40.3 8.8 %collective-permute-start.7 = (f32[2,32,1280]{2,1,0:T(8,128)S(1)}, f32[2,32,1280]{2,1,0:T(8,128)S(1)}, u32[]{:S(2)}, u32[]{:S(2)}) collective-permute-start(f32[2,32,1280]{2,1,0:T(8,128)S(1)} %get-tuple-element.47), channel_id=1, source_target_pairs={{0,2},{1,3},{2,0},{3,1},{4,6},{5,7},{6,4},{7,5},{8,10},{9,11},{10,... | collective-permute-start | bytes 983048 | tf_op jit(solution)/shard_map/ppermute | solution.py:645
  47.9 9.7 %collective-permute-start.8 = (f32[2,32,1280]{2,1,0:T(8,128)S(1)}, f32[2,32,1280]{2,1,0:T(8,128)S(1)}, u32[]{:S(2)}, u32[]{:S(2)}) collective-permute-start(f32[2,32,1280]{2,1,0:T(8,128)S(1)} %get-tuple-element.53), channel_id=1, source_target_pairs={{0,2},{1,3},{2,0},{3,1},{4,6},{5,7},{6,4},{7,5},{8,10},{9,11},{10,... | collective-permute-start | bytes 983048 | tf_op jit(solution)/shard_map/ppermute | solution.py:645
  55.4 8.5 %collective-permute-start.9 = (f32[2,32,1280]{2,1,0:T(8,128)S(1)}, f32[2,32,1280]{2,1,0:T(8,128)S(1)}, u32[]{:S(2)}, u32[]{:S(2)}) collective-permute-start(f32[2,32,1280]{2,1,0:T(8,128)S(1)} %get-tuple-element.59), channel_id=1, source_target_pairs={{0,2},{1,3},{2,0},{3,1},{4,6},{5,7},{6,4},{7,5},{8,10},{9,11},{10,... | collective-permute-start | bytes 983048 | tf_op jit(solution)/shard_map/ppermute | solution.py:645
  57.7 6.4 %collective-permute-start.10 = (f32[4,32,1280]{2,1,0:T(8,128)S(1)}, f32[4,32,1280]{2,1,0:T(8,128)S(1)}, u32[]{:S(2)}, u32[]{:S(2)}) collective-permute-start(f32[4,32,1280]{2,1,0:T(8,128)S(1)} %pad_maximum_fusion), channel_id=1, source_target_pairs={{0,1},{1,0},{2,3},{3,2},{4,5},{5,4},{6,7},{7,6},{8,9},{9,8},{10,11... | collective-permute-start | bytes 1966088 | tf_op jit(solution)/shard_map/ppermute | solution.py:648
  63.8 12.1 %copy-start.1 = (f32[4,32,1280]{2,1,0:T(8,128)}, f32[4,32,1280]{2,1,0:T(8,128)S(1)}, u32[]{:S(2)}) copy-start(f32[4,32,1280]{2,1,0:T(8,128)S(1)} %get-tuple-element.71.refs_0_) | copy-start | bytes 1966084
  63.9 10.2 %collective-permute-start.14 = (f32[2,32,1280]{2,1,0:T(8,128)S(1)}, f32[2,32,1280]{2,1,0:T(8,128)S(1)}, u32[]{:S(2)}, u32[]{:S(2)}) collective-permute-start(f32[2,32,1280]{2,1,0:T(8,128)S(1)} %get-tuple-element.69), channel_id=1, source_target_pairs={{0,2},{1,3},{2,0},{3,1},{4,6},{5,7},{6,4},{7,5},{8,10},{9,11},{10,... | collective-permute-start | bytes 983048 | tf_op jit(solution)/shard_map/ppermute | solution.py:645
  64.1 3.6 %collective-permute-start.11 = (f32[3,4]{1,0:T(4,128)S(1)}, f32[3,4]{1,0:T(4,128)S(1)}, u32[]{:S(2)}, u32[]{:S(2)}) collective-permute-start(f32[3,4]{1,0:T(4,128)S(1)} %pad_maximum_fusion.5), channel_id=1, source_target_pairs={{0,4},{4,0},{8,12},{12,8},{16,20},{20,16},{24,28},{28,24},{1,5},{5... | collective-permute-start | bytes 152 | tf_op jit(solution)/shard_map/ppermute | solution.py:653
  67.8 3.6 %collective-permute-start.12 = (f32[3,4]{1,0:T(4,128)S(1)}, f32[3,4]{1,0:T(4,128)S(1)}, u32[]{:S(2)}, u32[]{:S(2)}) collective-permute-start(f32[3,4]{1,0:T(4,128)S(1)} %select_add_fusion.2), channel_id=1, source_target_pairs={{0,8},{4,12},{8,0},{12,4},{16,24},{20,28},{24,16},{28,20},{1,9},{5... | collective-permute-start | bytes 152 | tf_op jit(solution)/shard_map/ppermute | solution.py:653
  71.4 4.5 %collective-permute-start.13 = (f32[3,4]{1,0:T(4,128)S(1)}, f32[3,4]{1,0:T(4,128)S(1)}, u32[]{:S(2)}, u32[]{:S(2)}) collective-permute-start(f32[3,4]{1,0:T(4,128)S(1)} %select_add_fusion.1), channel_id=1, source_target_pairs={{0,16},{4,20},{8,24},{12,28},{16,0},{20,4},{24,8},{28,12},{1,17},{... | collective-permute-start | bytes 152 | tf_op jit(solution)/shard_map/ppermute | solution.py:653
  75.9 6.0 %collective-permute-start.18 = (f32[4,32,1280]{2,1,0:T(8,128)S(1)}, f32[4,32,1280]{2,1,0:T(8,128)}, u32[]{:S(2)}, u32[]{:S(2)}) collective-permute-start(f32[4,32,1280]{2,1,0:T(8,128)S(1)} %pack.1), channel_id=1, source_target_pairs={{0,1},{1,0},{2,3},{3,2},{4,5},{5,4},{6,7},{7,6},{8,9},{9,8},{10,11... | collective-permute-start | bytes 1966088 | tf_op jit(solution)/shard_map/ppermute | solution.py:664
  76.3 2.6 %collective-permute-start.15 = (f32[4,6]{1,0:T(4,128)S(1)}, f32[4,6]{1,0:T(4,128)S(1)}, u32[]{:S(2)}, u32[]{:S(2)}) collective-permute-start(f32[4,6]{1,0:T(4,128)S(1)} %pad_maximum_fusion.6), channel_id=1, source_target_pairs={{0,1},{1,0},{2,3},{3,2},{4,5},{5,4},{6,7},{7,6},{8,9},{9,8},{10,11... | collective-permute-start | bytes 296 | tf_op jit(solution)/shard_map/ppermute | solution.py:579
  76.8 3.6 %collective-permute-start.16 = (f32[4,6]{1,0:T(4,128)S(1)}, f32[4,6]{1,0:T(4,128)S(1)}, u32[]{:S(2)}, u32[]{:S(2)}) collective-permute-start(f32[4,6]{1,0:T(4,128)S(1)} %pad_maximum_fusion.6), channel_id=1, source_target_pairs={{0,2},{1,3},{2,0},{3,1},{4,6},{5,7},{6,4},{7,5},{8,10},{9,11},{10,... | collective-permute-start | bytes 296 | tf_op jit(solution)/shard_map/ppermute | solution.py:579
  78.9 3.0 %collective-permute-start.17 = (f32[4,6]{1,0:T(4,128)S(1)}, f32[4,6]{1,0:T(4,128)S(1)}, u32[]{:S(2)}, u32[]{:S(2)}) collective-permute-start(f32[4,6]{1,0:T(4,128)S(1)} %pad_maximum_fusion.6), channel_id=1, source_target_pairs={{0,3},{1,2},{2,1},{3,0},{4,7},{5,6},{6,5},{7,4},{8,11},{9,10},{10,... | collective-permute-start | bytes 296 | tf_op jit(solution)/shard_map/ppermute | solution.py:579
  (3 other events, 3.0 us)

commit v15 on v13

--- a/solution.py
+++ b/solution.py
@@ -614,8 +614,8 @@
     far_swap = [(i, i ^ 2) for i in range(groups)]
     mines, sides, fars, stats = None, [], [], []
     for r in range(rots):
-        if r >= 2:
-            place, fars[r - 2] = lax.optimization_barrier((place, fars[r - 2]))
+        if r >= 3:
+            place, fars[r - 3] = lax.optimization_barrier((place, fars[r - 3]))
         mines, side, far, stat = correlate(
             mines, place, tile, held, r, lasts[min(r, 1)], max(r - 1, 0), mask, spec, tmpl_z, dims, tables
         )

time: 85.8 us -> 85 us (level)
    ppermute x4, waiting for transfers between devices: 2.1 us -> 1.07 us  [local(): fars.append(lax.ppermute(far, 'rot', far_swap))]
  transfers between devices with their start and end apart: 19 -> 19, of which waited for: 9 -> 9; matrix products, arithmetic and copies ran while one was open for 4% -> 4% of each run, Pallas kernels for 37% -> 38%
where the time goes in v15:
time: 85 us; the launch traced here: 84.6 us
  Pallas kernels  35.3 us (42%)
  starting transfers between devices  23.1 us (27%)
  waiting for transfers between devices  16.8 us (20%)
  local copies, waits for them, and re-layouts  5.23 us (6%)
  between operations  2.33 us (3%)
  other arithmetic  1.59 us (2%)
    pallas_call x4, Pallas kernels, correlate(): pl.pallas_call(functools.partial(corr_kernel, dims, rot, entry), out_shap...  24.3 us
    ppermute x4, waiting for transfers between devices, swap_blocks(): lax.ppermute(block, axis, [(i, i ^ step) for i in range(lax.axis_size(axi...  7.24 us
    ppermute x4, starting transfers between devices, swap_blocks(): lax.ppermute(block, axis, [(i, i ^ step) for i in range(lax.axis_size(axi...  6.86 us
    ppermute x3, waiting for transfers between devices, local(): partner = lax.ppermute(state, 'tile', [(i, i ^ step) for i in range(tiles)])  5.77 us
    ppermute x1, starting transfers between devices, neighbours(): lax.ppermute(block, axis, forward)  4.85 us
    ppermute x4, starting transfers between devices, local(): fars.append(lax.ppermute(far, 'rot', far_swap))  4.7 us
    pallas_call x1, Pallas kernels, slab_x(): pl.pallas_call(functools.partial(slab_x_kernel, dims), out_shape=(jax.Sha...  3.84 us
    pallas_call x2, Pallas kernels, slab_rows(): pl.pallas_call(functools.partial(slab_rows_kernel, dims), out_shape=jax.S...  3.67 us
  transfers between devices with their start and end apart: 19, of which 9 were waited for; matrix products, arithmetic and copies ran while one was open for 4% of the time, Pallas kernels for 38%

profile of v15, /device:TPU:0, one launch (start us, length us, event | category | flops | bytes accessed | tf_op | source)
XLA Modules:
  0.0 84.6 jit_solution(724780348951583470)
XLA Ops:
  0.7 1.0 %reshape.75 = bf16[4,1,108,128]{3,2,0,1:T(8,128)(2,1)S(1)} reshape(bf16[4,13824]{1,0:T(4,128)(2,1)} %param.15) | data formatting | bytes 221184 | tf_op jit(solution)/shard_map/reshape | solution.py:585
  1.7 0.9 %constant_dynamic-slice_fusion = bf16[16,5120]{1,0:T(8,128)(2,1)S(1)} fusion(bf16[32,5120]{1,0:T(8,128)(2,1)} %refs_0_.1, s32[]{:T(128)S(6)} %select_n.30), kind=kLoop, calls=%fused_computation.24 | loop fusion | bytes 327684 | tf_op jit(solution)/shard_map/dynamic_slice | solution.py:592
  2.6 4.9 %collective-permute-start.1 = (bf16[16,5120]{1,0:T(8,128)(2,1)S(1)}, bf16[16,5120]{1,0:T(8,128)(2,1)S(1)}, u32[]{:S(2)}, u32[]{:S(2)}) collective-permute-start(bf16[16,5120]{1,0:T(8,128)(2,1)S(1)} %constant_dynamic-slice_fusion), channel_id=1, source_target_pairs={{0,4},{4,8},{8,12},{12,16},{16,20},{20,24},{24,28},{1,5},{5,9},{9,... | collective-permute-start | bytes 491528 | tf_op jit(solution)/shard_map/ppermute | solution.py:568
  7.5 1.3 %collective-permute-start.2 = (bf16[16,5120]{1,0:T(8,128)(2,1)S(1)}, bf16[16,5120]{1,0:T(8,128)(2,1)S(1)}, u32[]{:S(2)}, u32[]{:S(2)}) collective-permute-start(bf16[16,5120]{1,0:T(8,128)(2,1)S(1)} %constant_dynamic-slice_fusion), channel_id=1, source_target_pairs={{4,0},{8,4},{12,8},{16,12},{20,16},{24,20},{28,24},{5,1},{9,5},{13... | collective-permute-start | bytes 491528 | tf_op jit(solution)/shard_map/ppermute | solution.py:568
  8.8 4.7 %collective-permute-start = (bf16[4,1,112,128]{3,2,1,0:T(8,128)(2,1)S(1)}, bf16[4,1,112,128]{3,2,1,0:T(8,128)(2,1)S(1)}, u32[]{:S(2)}, u32[]{:S(2)}) collective-permute-start(bf16[4,1,112,128]{3,2,1,0:T(8,128)(2,1)S(1)} %pad.4), channel_id=1, source_target_pairs={{0,16},{4,20},{8,24},{12,28},{16,0},{20,4},{24,8},{28,12},{1,17},{... | collective-permute-start | bytes 344072 | tf_op jit(solution)/shard_map/ppermute | solution.py:529
  13.5 1.0 %copy-done.1 = bf16[32,5120]{1,0:T(8,128)(2,1)S(1)} copy-done((bf16[32,5120]{1,0:T(8,128)(2,1)S(1)}, bf16[32,5120]{1,0:T(8,128)(2,1)}, u32[]{:S(2)}) %copy-start.1) | copy-done | bytes 327704
  14.4 0.9 %copy-done.3 = bf16[240,512]{1,0:T(8,128)(2,1)S(1)} copy-done((bf16[240,512]{1,0:T(8,128)(2,1)S(1)}, bf16[240,512]{1,0:T(8,128)(2,1)}, u32[]{:S(2)}) %copy-start.3) | copy-done | bytes 245784
  15.4 1.6 %slab_own.1.refs_0_ = f32[3616,128]{1,0:T(8,128)S(1)} custom-call(s32[1]{0:T(128)} %bitcast.place_ref, bf16[32,5120]{1,0:T(8,128)(2,1)S(1)} %copy-done.1, bf16[240,512]{1,0:T(8,128)(2,1)S(1)} %copy-done.3), custom_call_target="tpu_custom_call" | custom-call | flops 3200000000 | bytes 1000000 | tf_op jit(solution)/shard_map/slab_own/pallas_call | solution.py:248
  17.4 4.5 %collective-permute-done = bf16[4,1,112,128]{3,2,1,0:T(8,128)(2,1)S(1)} collective-permute-done((bf16[4,1,112,128]{3,2,1,0:T(8,128)(2,1)S(1)}, bf16[4,1,112,128]{3,2,1,0:T(8,128)(2,1)S(1)}, u32[]{:S(2)}, u32[]{:S(2)}) %collective-permute-start) | collective-permute-done | bytes 114720 | tf_op jit(solution)/shard_map/ppermute | solution.py:529
  22.1 2.1 %slab_halo.1.rows_ref = f32[9040,128]{1,0:T(8,128)S(1)} custom-call(s32[1]{0:T(128)} %bitcast.place_ref, f32[3616,128]{1,0:T(8,128)S(1)} %slab_own.1.refs_0_, bf16[2,16,5120]{2,1,0:T(8,128)(2,1)S(1)} %pad_maximum_fusion.3.refs_1_, bf16[2,16,5120]{2,1,0:T(8,128)(2,1)S(1)} %collective-permute-done.3.refs_2_, bf16[240,512]{1,0:T(8,128)(2,1)S(1)} %copy-done.4), custom_call_target="tpu_custom_call" | custom-call | flops 4800000000 | bytes 1000000 | tf_op jit(solution)/shard_map/slab_halo/pallas_call | solution.py:248
  25.4 2.7 %collective-permute-done.4 = bf16[4,2,112,128]{3,2,1,0:T(8,128)(2,1)S(1)} collective-permute-done((bf16[4,2,112,128]{3,2,1,0:T(8,128)(2,1)S(1)}, bf16[4,2,112,128]{3,2,1,0:T(8,128)(2,1)S(1)}, u32[]{:S(2)}, u32[]{:S(2)}) %collective-permute-start.4) | collective-permute-done | bytes 229408 | tf_op jit(solution)/shard_map/ppermute | solution.py:529
  28.3 1.6 %collective-permute-start.5 = (bf16[1,4,112,128]{3,2,1,0:T(8,128)(2,1)S(1)}, bf16[1,4,112,128]{3,2,1,0:T(8,128)(2,1)S(1)}, u32[]{:S(2)}, u32[]{:S(2)}) collective-permute-start(bf16[1,4,112,128]{3,2,1,0:T(8,128)(2,1)S(1)} %slice.110), channel_id=1, source_target_pairs={{0,4},{4,0},{8,12},{12,8},{16,20},{20,16},{24,28},{28,24},{1,5},{5... | collective-permute-start | bytes 344072 | tf_op jit(solution)/shard_map/ppermute | solution.py:529
  30.4 3.8 %slab_x.1 = (f32[13,2,80,1024]{3,2,1,0:T(8,128)S(1)}, f32[40,32,128]{2,1,0:T(8,128)S(1)}, bf16[8,256,256]{2,1,0:T(8,128)(2,1)S(1)}) custom-call(f32[9040,128]{1,0:T(8,128)S(1)} %slab_halo.1.rows_ref, bf16[80,240]{1,0:T(8,128)(2,1)S(1)} %copy-done.9, s32[32,80]{1,0:T(8,128)S(1)} %copy-done.2, bf16[48,256]{1,0:T(8,128)(2,1)S(1)} %copy-done.11), custom_call_target="tpu_custom_call" | custom-call | flops 5000000000 | bytes 1000000 | tf_op jit(solution)/shard_map/slab_x/pallas_call | solution.py:301
  34.3 6.0 %correlate.4 = (f32[1,32,1280]{2,1,0:T(8,128)S(1)}, f32[32,1280]{1,0:T(8,128)S(1)}, f32[2,32,1280]{2,1,0:T(8,128)S(1)}, f32[8,128]{1,0:T(8,128)S(1)}) custom-call(s32[1]{0:T(128)} %bitcast.place_ref, s32[1]{0:T(128)} %bitcast.1.tile_ref, bf16[4,4,112,128]{3,2,1,0:T(8,128)(2,1)S(1)} %pad_maximum_fusion.2.refs_0_.refs_1_, ...), custom_call_target="tpu_custom_call" | custom-call | flops 15000000512 | bytes 10000000 | tf_op jit(solution)/shard_map/correlate/pallas_call | solution.py:451
  40.3 1.6 %collective-permute-start.7 = (f32[2,32,1280]{2,1,0:T(8,128)S(1)}, f32[2,32,1280]{2,1,0:T(8,128)S(1)}, u32[]{:S(2)}, u32[]{:S(2)}) collective-permute-start(f32[2,32,1280]{2,1,0:T(8,128)S(1)} %get-tuple-element.45), channel_id=1, source_target_pairs={{0,2},{1,3},{2,0},{3,1},{4,6},{5,7},{6,4},{7,5},{8,10},{9,11},{10,... | collective-permute-start | bytes 983048 | tf_op jit(solution)/shard_map/ppermute | solution.py:626
  41.9 6.0 %correlate.5 = (f32[2,32,1280]{2,1,0:T(8,128)S(1)}, f32[32,1280]{1,0:T(8,128)S(1)}, f32[2,32,1280]{2,1,0:T(8,128)S(1)}, f32[8,128]{1,0:T(8,128)S(1)}) custom-call(s32[1]{0:T(128)} %bitcast.place_ref, s32[1]{0:T(128)} %bitcast.1.tile_ref, f32[1,32,1280]{2,1,0:T(8,128)S(1)} %get-tuple-element.43.refs_0_, ...), custom_call_target="tpu_custom_call" | custom-call | flops 15000000512 | bytes 10000000 | tf_op jit(solution)/shard_map/correlate/pallas_call | solution.py:451
  47.9 0.6 collective-permute-start.8
  48.5 6.2 %correlate.6 = (f32[3,32,1280]{2,1,0:T(8,128)S(1)}, f32[32,1280]{1,0:T(8,128)S(1)}, f32[2,32,1280]{2,1,0:T(8,128)S(1)}, f32[8,128]{1,0:T(8,128)S(1)}) custom-call(s32[1]{0:T(128)} %bitcast.place_ref, s32[1]{0:T(128)} %bitcast.1.tile_ref, f32[2,32,1280]{2,1,0:T(8,128)S(1)} %get-tuple-element.47.refs_0_, ...), custom_call_target="tpu_custom_call" | custom-call | flops 15000000512 | bytes 10000000 | tf_op jit(solution)/shard_map/correlate/pallas_call | solution.py:451
  54.8 1.6 %collective-permute-start.9 = (f32[2,32,1280]{2,1,0:T(8,128)S(1)}, f32[2,32,1280]{2,1,0:T(8,128)S(1)}, u32[]{:S(2)}, u32[]{:S(2)}) collective-permute-start(f32[2,32,1280]{2,1,0:T(8,128)S(1)} %get-tuple-element.55), channel_id=1, source_target_pairs={{0,2},{1,3},{2,0},{3,1},{4,6},{5,7},{6,4},{7,5},{8,10},{9,11},{10,... | collective-permute-start | bytes 983048 | tf_op jit(solution)/shard_map/ppermute | solution.py:626
  56.3 0.6 collective-permute-done.8.refs_2_
  57.1 6.0 %correlate.7 = (f32[4,32,1280]{2,1,0:T(8,128)S(1)}, f32[32,1280]{1,0:T(8,128)S(1)}, f32[2,32,1280]{2,1,0:T(8,128)S(1)}, f32[8,128]{1,0:T(8,128)S(1)}) custom-call(s32[1]{0:T(128)} %bitcast.place_ref, s32[1]{0:T(128)} %bitcast.1.tile_ref, f32[3,32,1280]{2,1,0:T(8,128)S(1)} %get-tuple-element.53.refs_0_, ...), custom_call_target="tpu_custom_call" | custom-call | flops 15000000512 | bytes 10000000 | tf_op jit(solution)/shard_map/correlate/pallas_call | solution.py:451
  63.1 1.0 %collective-permute-start.14 = (f32[2,32,1280]{2,1,0:T(8,128)S(1)}, f32[2,32,1280]{2,1,0:T(8,128)S(1)}, u32[]{:S(2)}, u32[]{:S(2)}) collective-permute-start(f32[2,32,1280]{2,1,0:T(8,128)S(1)} %get-tuple-element.65), channel_id=1, source_target_pairs={{0,2},{1,3},{2,0},{3,1},{4,6},{5,7},{6,4},{7,5},{8,10},{9,11},{10,... | collective-permute-start | bytes 983048 | tf_op jit(solution)/shard_map/ppermute | solution.py:626
  64.2 1.7 %collective-permute-start.11 = (f32[3,4]{1,0:T(4,128)S(1)}, f32[3,4]{1,0:T(4,128)S(1)}, u32[]{:S(2)}, u32[]{:S(2)}) collective-permute-start(f32[3,4]{1,0:T(4,128)S(1)} %pad_maximum_fusion.6), channel_id=1, source_target_pairs={{0,4},{4,0},{8,12},{12,8},{16,20},{20,16},{24,28},{28,24},{1,5},{5... | collective-permute-start | bytes 152 | tf_op jit(solution)/shard_map/ppermute | solution.py:634
  65.9 1.9 %collective-permute-done.11 = f32[3,4]{1,0:T(4,128)S(1)} collective-permute-done((f32[3,4]{1,0:T(4,128)S(1)}, f32[3,4]{1,0:T(4,128)S(1)}, u32[]{:S(2)}, u32[]{:S(2)}) %collective-permute-start.11) | collective-permute-done | bytes 80 | tf_op jit(solution)/shard_map/ppermute | solution.py:634
  67.9 1.5 %collective-permute-start.12 = (f32[3,4]{1,0:T(4,128)S(1)}, f32[3,4]{1,0:T(4,128)S(1)}, u32[]{:S(2)}, u32[]{:S(2)}) collective-permute-start(f32[3,4]{1,0:T(4,128)S(1)} %select_add_fusion.2), channel_id=1, source_target_pairs={{0,8},{4,12},{8,0},{12,4},{16,24},{20,28},{24,16},{28,20},{1,9},{5... | collective-permute-start | bytes 152 | tf_op jit(solution)/shard_map/ppermute | solution.py:634
  69.4 2.0 %collective-permute-done.12 = f32[3,4]{1,0:T(4,128)S(1)} collective-permute-done((f32[3,4]{1,0:T(4,128)S(1)}, f32[3,4]{1,0:T(4,128)S(1)}, u32[]{:S(2)}, u32[]{:S(2)}) %collective-permute-start.12) | collective-permute-done | bytes 80 | tf_op jit(solution)/shard_map/ppermute | solution.py:634
  73.3 0.9 %pad_maximum_fusion.1 = f32[4,32,1280]{2,1,0:T(8,128)} fusion(f32[1,32,1280]{2,1,0:T(8,128)S(1)} %slice_select_fusion, f32[1,32,1280]{2,1,0:T(8,128)S(1)} %slice.99, f32[1,32,1280]{2,1,0:T(8,128)S(1)} %bitcast.29, f32[1,32,1280]{2,1,0:T(8,128)S(1)} %bitcast.28), kind=kLoop, calls=%fused_computation.1 | loop fusion | flops 491520 | bytes 1310720 | tf_op jit(solution)/shard_map/stack | solution.py:637
  74.2 1.8 %collective-permute-done.13 = f32[3,4]{1,0:T(4,128)S(1)} collective-permute-done((f32[3,4]{1,0:T(4,128)S(1)}, f32[3,4]{1,0:T(4,128)S(1)}, u32[]{:S(2)}, u32[]{:S(2)}) %collective-permute-start.13) | collective-permute-done | bytes 80 | tf_op jit(solution)/shard_map/ppermute | solution.py:634
  76.9 1.1 %collective-permute-start.16 = (f32[4,6]{1,0:T(4,128)S(1)}, f32[4,6]{1,0:T(4,128)S(1)}, u32[]{:S(2)}, u32[]{:S(2)}) collective-permute-start(f32[4,6]{1,0:T(4,128)S(1)} %pad_maximum_fusion.7), channel_id=1, source_target_pairs={{0,2},{1,3},{2,0},{3,1},{4,6},{5,7},{6,4},{7,5},{8,10},{9,11},{10,... | collective-permute-start | bytes 296 | tf_op jit(solution)/shard_map/ppermute | solution.py:560
  78.4 2.1 %collective-permute-done.16 = f32[4,6]{1,0:T(4,128)S(1)} collective-permute-done((f32[4,6]{1,0:T(4,128)S(1)}, f32[4,6]{1,0:T(4,128)S(1)}, u32[]{:S(2)}, u32[]{:S(2)}) %collective-permute-start.16) | collective-permute-done | bytes 128 | tf_op jit(solution)/shard_map/ppermute | solution.py:560
  80.5 0.6 collective-permute-done.17
  81.1 3.5 %combine.1 = (f32[32,1280]{1,0:T(8,128)}, f32[32,1280]{1,0:T(8,128)}, f32[4,32,1280]{2,1,0:T(8,128)}) custom-call(s32[1]{0:T(128)} %bitcast.place_ref, f32[16,6]{1,0:T(8,128)S(1)} %bitcast.32, f32[40,32,128]{2,1,0:T(8,128)S(1)} %get-tuple-element.39.refs_2_.refs_3_.mask_ref, f32[4,32,1280]{2,1,0:T(8,128)S(1)} %get-tuple-element.67.refs_0_, ...), custom_call_target="tpu_custom_call" | custom-call | tf_op jit(solution)/shard_map/combine/pallas_call | solution.py:518
  (78 shorter events, 4.6 us)
Async XLA Ops:
  0.6 16.5 %copy-start = (f32[4,4096]{1,0:T(4,128)S(1)}, f32[4,4096]{1,0:T(4,128)}, u32[]{:S(2)}) copy-start(f32[4,4096]{1,0:T(4,128)} %param.17) | copy-start | bytes 196612
  2.6 14.4 %collective-permute-start.1 = (bf16[16,5120]{1,0:T(8,128)(2,1)S(1)}, bf16[16,5120]{1,0:T(8,128)(2,1)S(1)}, u32[]{:S(2)}, u32[]{:S(2)}) collective-permute-start(bf16[16,5120]{1,0:T(8,128)(2,1)S(1)} %constant_dynamic-slice_fusion), channel_id=1, source_target_pairs={{0,4},{4,8},{8,12},{12,16},{16,20},{20,24},{24,28},{1,5},{5,9},{9,... | collective-permute-start | bytes 491528 | tf_op jit(solution)/shard_map/ppermute | solution.py:568
  7.5 9.5 %collective-permute-start.2 = (bf16[16,5120]{1,0:T(8,128)(2,1)S(1)}, bf16[16,5120]{1,0:T(8,128)(2,1)S(1)}, u32[]{:S(2)}, u32[]{:S(2)}) collective-permute-start(bf16[16,5120]{1,0:T(8,128)(2,1)S(1)} %constant_dynamic-slice_fusion), channel_id=1, source_target_pairs={{4,0},{8,4},{12,8},{16,12},{20,16},{24,20},{28,24},{5,1},{9,5},{13... | collective-permute-start | bytes 491528 | tf_op jit(solution)/shard_map/ppermute | solution.py:568
  8.8 13.2 %collective-permute-start = (bf16[4,1,112,128]{3,2,1,0:T(8,128)(2,1)S(1)}, bf16[4,1,112,128]{3,2,1,0:T(8,128)(2,1)S(1)}, u32[]{:S(2)}, u32[]{:S(2)}) collective-permute-start(bf16[4,1,112,128]{3,2,1,0:T(8,128)(2,1)S(1)} %pad.4), channel_id=1, source_target_pairs={{0,16},{4,20},{8,24},{12,28},{16,0},{20,4},{24,8},{28,12},{1,17},{... | collective-permute-start | bytes 344072 | tf_op jit(solution)/shard_map/ppermute | solution.py:529
  13.5 1.0 %copy-start.1 = (bf16[32,5120]{1,0:T(8,128)(2,1)S(1)}, bf16[32,5120]{1,0:T(8,128)(2,1)}, u32[]{:S(2)}) copy-start(bf16[32,5120]{1,0:T(8,128)(2,1)} %refs_0_.1) | copy-start | bytes 983044
  15.4 1.8 %copy-start.13 = (s32[4]{0:T(128)S(1)}, s32[4]{0:T(128)}, u32[]{:S(2)}) copy-start(s32[4]{0:T(128)} %param.18) | copy-start | bytes 52
  15.4 6.7 %copy-start.4 = (bf16[240,512]{1,0:T(8,128)(2,1)S(1)}, bf16[240,512]{1,0:T(8,128)(2,1)}, u32[]{:S(2)}) copy-start(bf16[240,512]{1,0:T(8,128)(2,1)} %constant.52.clone.refs_1_.refs_3_) | copy-start | bytes 737284
  17.1 5.0 %collective-permute-start.3 = (bf16[2,16,5120]{2,1,0:T(8,128)(2,1)S(1)}, bf16[2,16,5120]{2,1,0:T(8,128)(2,1)S(1)}, u32[]{:S(2)}, u32[]{:S(2)}) collective-permute-start(bf16[2,16,5120]{2,1,0:T(8,128)(2,1)S(1)} %pad_maximum_fusion.3.refs_1_), channel_id=1, source_target_pairs={{0,1},{1,0},{2,3},{3,2},{4,5},{5,4},{6,7},{7,6},{8,9},{9,8},{10,11... | collective-permute-start | bytes 983048 | tf_op jit(solution)/shard_map/ppermute | solution.py:595
  22.0 8.4 %copy-start.2 = (s32[32,80]{1,0:T(8,128)S(1)}, s32[32,80]{1,0:T(8,128)}, u32[]{:S(2)}) copy-start(s32[32,80]{1,0:T(8,128)} %valid_ref.1) | copy-start | bytes 30724
  22.0 8.4 %copy-start.9 = (bf16[80,240]{1,0:T(8,128)(2,1)S(1)}, bf16[80,240]{1,0:T(8,128)(2,1)}, u32[]{:S(2)}) copy-start(bf16[80,240]{1,0:T(8,128)(2,1)} %constant.53.clone.x_ref) | copy-start | bytes 115204
  22.0 8.4 %copy-start.11 = (bf16[48,256]{1,0:T(8,128)(2,1)S(1)}, bf16[48,256]{1,0:T(8,128)(2,1)}, u32[]{:S(2)}) copy-start(bf16[48,256]{1,0:T(8,128)(2,1)} %constant.54.clone.tz_ref) | copy-start | bytes 73732
  22.0 6.1 %collective-permute-start.4 = (bf16[4,2,112,128]{3,2,1,0:T(8,128)(2,1)S(1)}, bf16[4,2,112,128]{3,2,1,0:T(8,128)(2,1)S(1)}, u32[]{:S(2)}, u32[]{:S(2)}) collective-permute-start(bf16[4,2,112,128]{3,2,1,0:T(8,128)(2,1)S(1)} %pad_maximum_fusion.4), channel_id=1, source_target_pairs={{0,8},{4,12},{8,0},{12,4},{16,24},{20,28},{24,16},{28,20},{1,9},{5... | collective-permute-start | bytes 688136 | tf_op jit(solution)/shard_map/ppermute | solution.py:529
  28.2 6.0 %copy-start.5 = (bf16[256,256]{1,0:T(8,128)(2,1)S(1)}, bf16[256,256]{1,0:T(8,128)(2,1)}, u32[]{:S(2)}) copy-start(bf16[256,256]{1,0:T(8,128)(2,1)} %constant.60.clone.refs_10_.refs_11_) | copy-start | bytes 393220
  28.2 6.0 %copy-start.6 = (bf16[160,208]{1,0:T(8,128)(2,1)S(1)}, bf16[160,208]{1,0:T(8,128)(2,1)}, u32[]{:S(2)}) copy-start(bf16[160,208]{1,0:T(8,128)(2,1)} %constant.59.clone.refs_9_.refs_10_) | copy-start | bytes 199684
  28.2 6.0 %copy-start.7 = (bf16[112,144]{1,0:T(8,128)(2,1)S(1)}, bf16[112,144]{1,0:T(8,128)(2,1)}, u32[]{:S(2)}) copy-start(bf16[112,144]{1,0:T(8,128)(2,1)} %constant.56.clone.refs_6_.refs_7_) | copy-start | bytes 96772
  28.3 6.0 %copy-start.8 = (bf16[80,144]{1,0:T(8,128)(2,1)S(1)}, bf16[80,144]{1,0:T(8,128)(2,1)}, u32[]{:S(2)}) copy-start(bf16[80,144]{1,0:T(8,128)(2,1)} %constant.57.clone.refs_7_.refs_8_) | copy-start | bytes 69124
  28.3 6.0 %copy-start.10 = (bf16[64,160]{1,0:T(8,128)(2,1)S(1)}, bf16[64,160]{1,0:T(8,128)(2,1)}, u32[]{:S(2)}) copy-start(bf16[64,160]{1,0:T(8,128)(2,1)} %constant.58.clone.refs_8_.refs_9_) | copy-start | bytes 61444
  28.3 6.0 %copy-start.12 = (f32[8,128]{1,0:T(8,128)S(1)}, f32[8,128]{1,0:T(8,128)}, u32[]{:S(2)}) copy-start(f32[8,128]{1,0:T(8,128)} %constant.55.clone.refs_5_.refs_6_) | copy-start | bytes 12292
  28.3 6.0 %collective-permute-start.5 = (bf16[1,4,112,128]{3,2,1,0:T(8,128)(2,1)S(1)}, bf16[1,4,112,128]{3,2,1,0:T(8,128)(2,1)S(1)}, u32[]{:S(2)}, u32[]{:S(2)}) collective-permute-start(bf16[1,4,112,128]{3,2,1,0:T(8,128)(2,1)S(1)} %slice.110), channel_id=1, source_target_pairs={{0,4},{4,0},{8,12},{12,8},{16,20},{20,16},{24,28},{28,24},{1,5},{5... | collective-permute-start | bytes 344072 | tf_op jit(solution)/shard_map/ppermute | solution.py:529
  29.9 12.1 %collective-permute-start.6 = (bf16[3,4,112,128]{3,2,1,0:T(8,128)(2,1)S(1)}, bf16[3,4,112,128]{3,2,1,0:T(8,128)(2,1)S(1)}, u32[]{:S(2)}, u32[]{:S(2)}) collective-permute-start(bf16[3,4,112,128]{3,2,1,0:T(8,128)(2,1)S(1)} %slice.111), channel_id=1, source_target_pairs={{0,4},{4,0},{8,12},{12,8},{16,20},{20,16},{24,28},{28,24},{1,5},{5... | collective-permute-start | bytes 1032200 | tf_op jit(solution)/shard_map/ppermute | solution.py:529
  40.3 16.0 %collective-permute-start.7 = (f32[2,32,1280]{2,1,0:T(8,128)S(1)}, f32[2,32,1280]{2,1,0:T(8,128)S(1)}, u32[]{:S(2)}, u32[]{:S(2)}) collective-permute-start(f32[2,32,1280]{2,1,0:T(8,128)S(1)} %get-tuple-element.45), channel_id=1, source_target_pairs={{0,2},{1,3},{2,0},{3,1},{4,6},{5,7},{6,4},{7,5},{8,10},{9,11},{10,... | collective-permute-start | bytes 983048 | tf_op jit(solution)/shard_map/ppermute | solution.py:626
  47.9 9.0 %collective-permute-start.8 = (f32[2,32,1280]{2,1,0:T(8,128)S(1)}, f32[2,32,1280]{2,1,0:T(8,128)S(1)}, u32[]{:S(2)}, u32[]{:S(2)}) collective-permute-start(f32[2,32,1280]{2,1,0:T(8,128)S(1)} %get-tuple-element.49), channel_id=1, source_target_pairs={{0,2},{1,3},{2,0},{3,1},{4,6},{5,7},{6,4},{7,5},{8,10},{9,11},{10,... | collective-permute-start | bytes 983048 | tf_op jit(solution)/shard_map/ppermute | solution.py:626
  54.8 9.3 %collective-permute-start.9 = (f32[2,32,1280]{2,1,0:T(8,128)S(1)}, f32[2,32,1280]{2,1,0:T(8,128)S(1)}, u32[]{:S(2)}, u32[]{:S(2)}) collective-permute-start(f32[2,32,1280]{2,1,0:T(8,128)S(1)} %get-tuple-element.55), channel_id=1, source_target_pairs={{0,2},{1,3},{2,0},{3,1},{4,6},{5,7},{6,4},{7,5},{8,10},{9,11},{10,... | collective-permute-start | bytes 983048 | tf_op jit(solution)/shard_map/ppermute | solution.py:626
  57.0 7.2 %collective-permute-start.10 = (f32[4,32,1280]{2,1,0:T(8,128)S(1)}, f32[4,32,1280]{2,1,0:T(8,128)S(1)}, u32[]{:S(2)}, u32[]{:S(2)}) collective-permute-start(f32[4,32,1280]{2,1,0:T(8,128)S(1)} %pad_maximum_fusion), channel_id=1, source_target_pairs={{0,1},{1,0},{2,3},{3,2},{4,5},{5,4},{6,7},{7,6},{8,9},{9,8},{10,11... | collective-permute-start | bytes 1966088 | tf_op jit(solution)/shard_map/ppermute | solution.py:629
  63.1 10.2 %collective-permute-start.14 = (f32[2,32,1280]{2,1,0:T(8,128)S(1)}, f32[2,32,1280]{2,1,0:T(8,128)S(1)}, u32[]{:S(2)}, u32[]{:S(2)}) collective-permute-start(f32[2,32,1280]{2,1,0:T(8,128)S(1)} %get-tuple-element.65), channel_id=1, source_target_pairs={{0,2},{1,3},{2,0},{3,1},{4,6},{5,7},{6,4},{7,5},{8,10},{9,11},{10,... | collective-permute-start | bytes 983048 | tf_op jit(solution)/shard_map/ppermute | solution.py:626
  64.2 3.6 %collective-permute-start.11 = (f32[3,4]{1,0:T(4,128)S(1)}, f32[3,4]{1,0:T(4,128)S(1)}, u32[]{:S(2)}, u32[]{:S(2)}) collective-permute-start(f32[3,4]{1,0:T(4,128)S(1)} %pad_maximum_fusion.6), channel_id=1, source_target_pairs={{0,4},{4,0},{8,12},{12,8},{16,20},{20,16},{24,28},{28,24},{1,5},{5... | collective-permute-start | bytes 152 | tf_op jit(solution)/shard_map/ppermute | solution.py:634
  67.9 3.6 %collective-permute-start.12 = (f32[3,4]{1,0:T(4,128)S(1)}, f32[3,4]{1,0:T(4,128)S(1)}, u32[]{:S(2)}, u32[]{:S(2)}) collective-permute-start(f32[3,4]{1,0:T(4,128)S(1)} %select_add_fusion.2), channel_id=1, source_target_pairs={{0,8},{4,12},{8,0},{12,4},{16,24},{20,28},{24,16},{28,20},{1,9},{5... | collective-permute-start | bytes 152 | tf_op jit(solution)/shard_map/ppermute | solution.py:634
  71.5 4.5 %collective-permute-start.13 = (f32[3,4]{1,0:T(4,128)S(1)}, f32[3,4]{1,0:T(4,128)S(1)}, u32[]{:S(2)}, u32[]{:S(2)}) collective-permute-start(f32[3,4]{1,0:T(4,128)S(1)} %select_add_fusion.1), channel_id=1, source_target_pairs={{0,16},{4,20},{8,24},{12,28},{16,0},{20,4},{24,8},{28,12},{1,17},{... | collective-permute-start | bytes 152 | tf_op jit(solution)/shard_map/ppermute | solution.py:634
  76.0 5.1 %collective-permute-start.18 = (f32[4,32,1280]{2,1,0:T(8,128)}, f32[4,32,1280]{2,1,0:T(8,128)}, u32[]{:S(2)}, u32[]{:S(2)}) collective-permute-start(f32[4,32,1280]{2,1,0:T(8,128)} %pad_maximum_fusion.1), channel_id=1, source_target_pairs={{0,1},{1,0},{2,3},{3,2},{4,5},{5,4},{6,7},{7,6},{8,9},{9,8},{10,11... | collective-permute-start | bytes 1966088 | tf_op jit(solution)/shard_map/ppermute | solution.py:646
  76.4 2.0 %collective-permute-start.15 = (f32[4,6]{1,0:T(4,128)S(1)}, f32[4,6]{1,0:T(4,128)S(1)}, u32[]{:S(2)}, u32[]{:S(2)}) collective-permute-start(f32[4,6]{1,0:T(4,128)S(1)} %pad_maximum_fusion.7), channel_id=1, source_target_pairs={{0,1},{1,0},{2,3},{3,2},{4,5},{5,4},{6,7},{7,6},{8,9},{9,8},{10,11... | collective-permute-start | bytes 296 | tf_op jit(solution)/shard_map/ppermute | solution.py:560
  76.9 3.6 %collective-permute-start.16 = (f32[4,6]{1,0:T(4,128)S(1)}, f32[4,6]{1,0:T(4,128)S(1)}, u32[]{:S(2)}, u32[]{:S(2)}) collective-permute-start(f32[4,6]{1,0:T(4,128)S(1)} %pad_maximum_fusion.7), channel_id=1, source_target_pairs={{0,2},{1,3},{2,0},{3,1},{4,6},{5,7},{6,4},{7,5},{8,10},{9,11},{10,... | collective-permute-start | bytes 296 | tf_op jit(solution)/shard_map/ppermute | solution.py:560
  78.1 3.0 %collective-permute-start.17 = (f32[4,6]{1,0:T(4,128)S(1)}, f32[4,6]{1,0:T(4,128)S(1)}, u32[]{:S(2)}, u32[]{:S(2)}) collective-permute-start(f32[4,6]{1,0:T(4,128)S(1)} %pad_maximum_fusion.7), channel_id=1, source_target_pairs={{0,3},{1,2},{2,1},{3,0},{4,7},{5,6},{6,5},{7,4},{8,11},{9,10},{10,... | collective-permute-start | bytes 296 | tf_op jit(solution)/shard_map/ppermute | solution.py:560
  (1 other events, 0.9 us)
